TPU v7x, 32 devices: a whole 2x2x4 slice. The times are simulated.
32 devices in a mesh: row: 4 (over y, x), col: 8 (over z, core).
Axes of the slice: x: 2, y: 2, z: 4, core: 2. Of those that a mesh axis runs over, the one named last changes fastest.
Arguments:
- image: bfloat16 [64, 512, 256], P('row', 'col'), may hold values from -7 to 7
- out_cotangent: bfloat16 [64, 512, 256], P('row', 'col'), may hold values from -6 to 6
- norm0_gain: bfloat16 [256], replicated, may hold values from 0.099609375 to 1.8984375
- w_expand: bfloat16 [256, 1024], replicated, may hold values from -0.375 to 0.375
- w_depth: bfloat16 [3, 3, 1024], replicated, may hold values from -2 to 2
- w_squeeze: bfloat16 [1024, 64], replicated, may hold values from -0.75 to 0.75
- w_excite: bfloat16 [64, 1024], replicated, may hold values from -3 to 3
- w_project: bfloat16 [1024, 256], replicated, may hold values from -0.1875 to 0.1875
- norm1_gain: bfloat16 [256], replicated, may hold values from 0.099609375 to 1.8984375
- w_qkv: bfloat16 [256, 768], replicated, may hold values from -0.375 to 0.375
- w_out: bfloat16 [256, 256], replicated, may hold values from -0.375 to 0.375
- attn_bias: float32 [8, 64, 64], replicated, may hold values from -2 to 250
Outputs:
- block_out: bfloat16 [64, 512, 256], P('row', 'col')
- grad_image: bfloat16 [64, 512, 256], P('row', 'col')
- grad_norm0: float32 [256], replicated
- grad_expand: float32 [256, 1024], replicated
- grad_depth: float32 [3, 3, 1024], replicated
- grad_squeeze: float32 [1024, 64], replicated
- grad_excite: float32 [64, 1024], replicated
- grad_project: float32 [1024, 256], replicated
- grad_norm1: float32 [256], replicated
- grad_qkv: float32 [256, 768], replicated
- grad_out_proj: float32 [256, 256], replicated
- grad_bias: float32 [8, 64, 64], replicated
All inputs are finite; a program needn't handle non-finite values.
Results may differ from a plain program's by a relative error of at most 0.015.
Values may be sent and summed in bfloat16 or wider, within the bound.
No kernel may reach another device: no remote copies, remote signals or barrier semaphores. Data moves between devices by JAX's collectives and lax.ppermute only.
A program may use at most 128 MiB of HBM per device.

v0:
```python
import functools
import math

import jax
import jax.numpy as jnp
from jax import lax
from jax.experimental import pallas as pl
from jax.experimental.pallas import tpu as pltpu
from jax.sharding import PartitionSpec as P

GRID = 8
AXES = ("row", "col")
BLOCK = 256
LANES = 128
SIDE = 16
GELU_A = math.sqrt(2.0 / math.pi)
GELU_B = GELU_A * 0.044715
F32 = jnp.float32
BF16 = jnp.bfloat16
PARAMS = pltpu.CompilerParams(vmem_limit_bytes=56 * 1024 * 1024)


def estimate(us):
    return pl.CostEstimate(flops=int(us * 1.1e9), bytes_accessed=int(us * 3.6e6), transcendentals=0)


def dot(left, right, contract=((1,), (0,))):
    return lax.dot_general(left, right, (contract, ((), ())), preferred_element_type=F32)


def dot_exact(vector, right, contract):
    tall = jnp.broadcast_to(vector, (8, vector.shape[1]))
    product = lax.dot_general(
        tall, right, (contract, ((), ())), precision=lax.Precision.HIGHEST, preferred_element_type=F32
    )
    return product[0:1]


def gelu_and_slope(x, with_slope=True):
    square = x * x
    t = jnp.tanh(x * (GELU_A + GELU_B * square))
    half = 0.5 + 0.5 * t
    value = x * half
    if not with_slope:
        return value, None
    slope = half + (value * (1.0 - t)) * (GELU_A + (3.0 * GELU_B) * square)
    return value, slope


def norm_rows(x):
    average = jnp.mean(x, axis=-1, keepdims=True)
    centered = x - average
    variance = jnp.mean(centered * centered, axis=-1, keepdims=True)
    rstd = lax.rsqrt(variance + 1e-05)
    return centered * rstd, rstd


def norm_rows_back(unit, rstd, gain, grad):
    unit_grad = grad * gain
    first = jnp.mean(unit_grad, axis=-1, keepdims=True)
    second = jnp.mean(unit_grad * unit, axis=-1, keepdims=True)
    return rstd * (unit_grad - first - unit * second)


def fold_rows(x):
    return jnp.sum(x.reshape(x.shape[0] // 8, 8, x.shape[1]), axis=0)


def whole(shape):
    return pl.BlockSpec(shape, lambda e: (0,) * len(shape))


def last_block(shape):
    lead = (0,) * (len(shape) - 1)
    return pl.BlockSpec(shape[:-1] + (BLOCK,), lambda e: lead + (e,))


def expand_kernel(
    image_ref, gain_ref, w_exp_ref,
    normed_ref, turned_ref, spread_ref, slope_ref,
    expanded_ref,
):
    rows, cols, channels = image_ref.shape

    @pl.when(pl.program_id(0) == 0)
    def _():
        gain = gain_ref[...].astype(F32)

        @pl.loop(0, rows // 4)
        def _(c):
            flat = image_ref[pl.ds(c * 4, 4)].reshape(4 * cols, channels)
            unit, _ = norm_rows(flat.astype(F32))
            at = pl.ds(pl.multiple_of(c * 4 * cols, 16), 4 * cols)
            normed_ref[at, :] = (unit * gain).astype(BF16)

        turned_ref[...] = normed_ref[...].T

    expanded_ref[...] = dot(normed_ref[...], w_exp_ref[...])

    @pl.loop(0, rows, unroll=4)
    def _(r):
        for h in range(BLOCK // LANES):
            lanes = slice(h * LANES, (h + 1) * LANES)
            x = expanded_ref[pl.ds(pl.multiple_of(r * cols, 16), cols), lanes]
            value, slope = gelu_and_slope(x)
            spread_ref[r, :, lanes] = value.astype(BF16)
            slope_ref[r, :, lanes] = slope.astype(BF16)


def run_expand(image, gain, w_expand):
    rows, cols, channels = image.shape
    expanded = w_expand.shape[1]
    return pl.pallas_call(
        expand_kernel,
        grid=(expanded // BLOCK,),
        in_specs=[whole(image.shape), whole(gain.shape), last_block(w_expand.shape)],
        out_specs=[
            whole((rows * cols, channels)), whole((channels, rows * cols)),
            last_block((rows, cols, expanded)), last_block((rows, cols, expanded)),
        ],
        out_shape=[
            jax.ShapeDtypeStruct((rows * cols, channels), BF16),
            jax.ShapeDtypeStruct((channels, rows * cols), BF16),
            jax.ShapeDtypeStruct((rows, cols, expanded), BF16),
            jax.ShapeDtypeStruct((rows, cols, expanded), BF16),
        ],
        scratch_shapes=[pltpu.VMEM((rows * cols, BLOCK), F32)],
        compiler_params=PARAMS,
        cost_estimate=estimate(14),
        name="expand",
    )(image, gain, w_expand)


def depthwise_kernel(
    up_ref, down_ref, side_ref, gain_ref, w_exp_ref, w_dep_ref, spread_ref,
    ring_ref, act_ref, pool_ref,
    ring_normed_ref, ring_wide_ref,
):
    rows, cols, _ = spread_ref.shape
    channels = up_ref.shape[2]
    over = 4 * cols
    side = 8

    @pl.when(pl.program_id(0) == 0)
    def _():
        gain = gain_ref[...].astype(F32)

        def put(at, values):
            unit, _ = norm_rows(values.astype(F32))
            ring_normed_ref[at : at + values.shape[0], :] = (unit * gain).astype(BF16)

        put(0, up_ref[...].reshape(2 * cols, channels))
        put(2 * cols, down_ref[...].reshape(2 * cols, channels))
        put(over, side_ref[...])

    ring_wide_ref[...] = dot(ring_normed_ref[...], w_exp_ref[...])
    tile = 32

    @pl.loop(0, ring_wide_ref.shape[0] // tile, unroll=True)
    def _(t):
        at = pl.ds(pl.multiple_of(t * tile, tile), tile)
        value, _ = gelu_and_slope(ring_wide_ref[at, :], False)
        low = value.astype(BF16)
        ring_ref[at, :] = low
        ring_wide_ref[at, :] = low.astype(F32)

    for h in range(BLOCK // LANES):
        lanes = slice(h * LANES, (h + 1) * LANES)
        taps = w_dep_ref[:, :, lanes].astype(F32)
        w = [[taps[a, b : b + 1] for b in range(3)] for a in range(3)]

        def line(r, main):
            at = pl.multiple_of(over + (r + 2) * side, side)
            return jnp.concatenate([main, ring_wide_ref[pl.ds(at, side), lanes]], axis=0)

        def conv(i, x, total):
            u = [x[0] * w[0][b] + x[1] * w[1][b] + x[2] * w[2][b] for b in range(3)]
            wide = cols + side
            pre = pltpu.roll(u[0], 1, 0) + u[1] + pltpu.roll(u[2], wide - 1, 0)
            value, _ = gelu_and_slope(pre[:cols], False)
            act_ref[i, :, lanes] = value.astype(BF16)
            return total + fold_rows(value)

        def step(i, carry):
            first, second, total = carry
            third = line(i + 1, spread_ref[i + 1, :, lanes].astype(F32))
            return second, third, conv(i, (first, second, third), total)

        carry = (
            line(-1, ring_wide_ref[cols : 2 * cols, lanes]),
            line(0, spread_ref[0, :, lanes].astype(F32)),
            jnp.zeros((8, LANES), F32),
        )
        first, second, total = lax.fori_loop(0, rows - 1, step, carry, unroll=5)
        third = line(rows, ring_wide_ref[2 * cols : 3 * cols, lanes])
        total = conv(rows - 1, (first, second, third), total)
        total = jnp.sum(total, axis=0, keepdims=True)
        pool_ref[:, :, lanes] = jnp.broadcast_to(total[None], (pool_ref.shape[0], 1, LANES))


def run_depthwise(count, up, down, side, gain, w_expand, w_depth, spread):
    rows, cols, expanded = spread.shape
    channels = up.shape[2]
    ring = 4 * cols + 8 * (rows + 4)
    return pl.pallas_call(
        depthwise_kernel,
        grid=(expanded // BLOCK,),
        in_specs=[
            whole(up.shape), whole(down.shape), whole(side.shape), whole(gain.shape),
            last_block(w_expand.shape), last_block(w_depth.shape), last_block(spread.shape),
        ],
        out_specs=[
            last_block((ring, expanded)), last_block(spread.shape), last_block((count, 1, expanded)),
        ],
        out_shape=[
            jax.ShapeDtypeStruct((ring, expanded), BF16),
            jax.ShapeDtypeStruct(spread.shape, BF16),
            jax.ShapeDtypeStruct((count, 1, expanded), F32),
        ],
        scratch_shapes=[pltpu.VMEM((ring, channels), BF16), pltpu.VMEM((ring, BLOCK), F32)],
        compiler_params=PARAMS,
        cost_estimate=estimate(1),
        name="depthwise",
    )(up, down, side, gain, w_expand, w_depth, spread)


def slope_kernel(flags_ref, ring_ref, w_dep_ref, spread_ref, main_ref, side_out_ref, wide_ref):
    rows, cols, _ = spread_ref.shape
    over = 4 * cols
    side = 8
    wide = cols + side

    for k, r in enumerate((0, 1, rows + 2, rows + 3)):
        wide_ref[r, :cols, :] = ring_ref[k * cols : (k + 1) * cols, :].astype(F32)
    sides = ring_ref[over:, :].astype(F32)
    for r in range(rows + 4):
        wide_ref[r, cols:, :] = sides[r * side : (r + 1) * side]

    @pl.loop(0, rows)
    def _(r):
        wide_ref[r + 2, :cols, :] = spread_ref[r].astype(F32)

    place = lax.broadcasted_iota(jnp.int32, (side, LANES), 0)
    side_mask = jnp.where(
        place == side - 1, flags_ref[2], jnp.where(place == 0, flags_ref[3], 1.0)
    ).astype(F32)

    @pl.loop(0, rows + 2)
    def _(i):
        keep = jnp.where(i == 0, flags_ref[0], jnp.where(i == rows + 1, flags_ref[1], 1.0))
        for h in range(BLOCK // LANES):
            lanes = slice(h * LANES, (h + 1) * LANES)
            taps = w_dep_ref[:, :, lanes].astype(F32)
            x = [wide_ref[i + a, :, lanes] for a in range(3)]
            u = [sum(x[a] * taps[a, b : b + 1] for a in range(3)) for b in range(3)]
            pre = pltpu.roll(u[0], 1, 0) + u[1] + pltpu.roll(u[2], wide - 1, 0)
            _, slope = gelu_and_slope(pre)
            slope = slope * keep
            main_ref[i, :, lanes] = slope[:cols].astype(BF16)
            side_out_ref[i, :, lanes] = slope[cols:] * side_mask


def run_slope(flags, ring, w_depth, spread):
    rows, cols, expanded = spread.shape
    return pl.pallas_call(
        slope_kernel,
        grid=(expanded // BLOCK,),
        in_specs=[
            pl.BlockSpec(memory_space=pltpu.SMEM),
            last_block(ring.shape), last_block(w_depth.shape), last_block(spread.shape),
        ],
        out_specs=[last_block((rows + 2, cols, expanded)), last_block((rows + 2, 8, expanded))],
        out_shape=[
            jax.ShapeDtypeStruct((rows + 2, cols, expanded), BF16),
            jax.ShapeDtypeStruct((rows + 2, 8, expanded), F32),
        ],
        scratch_shapes=[pltpu.VMEM((rows + 4, cols + 8, BLOCK), F32)],
        compiler_params=PARAMS,
        cost_estimate=estimate(13),
        name="slope",
    )(flags, ring, w_depth, spread)


def mix_kernel(
    cells_total, stride, bands,
    parts_ref, w_sq_ref, w_ex_ref, act_ref, image_ref, w_proj_ref, gain_ref, after_ref,
    pooled_ref, hidden_ref, gate_ref, mixed_ref, send_ref,
):
    step = pl.program_id(0)

    @pl.when(step == 0)
    def _():
        pooled = jnp.sum(parts_ref[...], axis=0) / cells_total
        hidden = dot_exact(pooled, w_sq_ref[...].astype(F32), ((1,), (0,)))
        silu = hidden * jax.nn.sigmoid(hidden)
        pooled_ref[...] = pooled
        hidden_ref[...] = hidden
        gate_ref[...] = jax.nn.sigmoid(dot_exact(silu, w_ex_ref[...].astype(F32), ((1,), (0,))))

    lines, cols, channels = image_ref.shape
    flat = act_ref[...].reshape(lines * cols, act_ref.shape[2])
    gated = (flat.astype(F32) * gate_ref[...]).astype(BF16)
    product = dot(gated, w_proj_ref[...])
    mixed = (image_ref[...].reshape(lines * cols, channels).astype(F32) + product).astype(BF16)
    mixed_ref[...] = mixed.reshape(lines, cols, channels)
    unit, _ = norm_rows(mixed.astype(F32))
    normed = (unit * gain_ref[...].astype(F32)).astype(BF16)
    for k in range(lines):
        line = step * lines + k
        for band in range(bands):
            start = k * cols + band * SIDE
            send_ref[lax.rem(line, stride) * bands + band, line // stride] = normed[
                start : start + SIDE
            ]


def run_mix(cells_total, stride, parts, w_squeeze, w_excite, act, image, w_project, gain, after):
    rows, cols, channels = image.shape
    expanded = act.shape[2]
    lines = 4
    bands = cols // SIDE
    block = lambda width: pl.BlockSpec((lines, cols, width), lambda r: (r, 0, 0))
    send = (stride * bands, rows // stride, SIDE, channels)
    return pl.pallas_call(
        functools.partial(mix_kernel, cells_total, stride, bands),
        grid=(rows // lines,),
        in_specs=[
            whole(parts.shape), whole(w_squeeze.shape), whole(w_excite.shape),
            block(expanded), block(channels), whole(w_project.shape), whole(gain.shape),
            pl.BlockSpec(memory_space=pl.ANY),
        ],
        out_specs=[
            whole((1, expanded)), whole((1, w_squeeze.shape[1])), whole((1, expanded)),
            block(channels), whole(send),
        ],
        out_shape=[
            jax.ShapeDtypeStruct((1, expanded), F32),
            jax.ShapeDtypeStruct((1, w_squeeze.shape[1]), F32),
            jax.ShapeDtypeStruct((1, expanded), F32),
            jax.ShapeDtypeStruct(image.shape, BF16),
            jax.ShapeDtypeStruct(send, BF16),
        ],
        compiler_params=PARAMS,
        cost_estimate=estimate(5),
        name="mix",
    )(parts, w_squeeze, w_excite, act, image, w_project, gain, after)


def attention_kernel(
    members, heads, lines,
    arrived_ref, cot_ref, w_qkv_ref, w_out_ref, bias_ref,
    x_ref, att_ref, grad_ref, packed_grad_ref, bias_out_ref,
    order_ref, packed_ref, att_grad_ref, bias_sum_ref,
):
    cells, channels = x_ref.shape
    groups = cells // members

    def places():
        for g in range(groups):
            for m in range(0, members, GRID):
                line, row = (m // GRID) % lines, m // GRID // lines
                start = (row * GRID * lines + line) * groups + g
                yield g * members + m, pl.ds(start, GRID, stride=lines * groups)

    for half in range(channels // LANES):
        lanes = slice(half * LANES, (half + 1) * LANES)
        order_ref[half] = arrived_ref[:, lanes].astype(F32)
        for g in range(groups):
            pieces = [order_ref[half, at, :] for k, at in places() if k // members == g]
            at = slice(g * members, (g + 1) * members)
            x_ref[at, lanes] = jnp.concatenate(pieces, axis=0).astype(BF16)
    dim = channels // heads
    per_half = LANES // dim
    halves = channels // LANES
    scale = dim ** (-0.5)
    packed_ref[...] = dot(x_ref[...], w_qkv_ref[...]).astype(BF16)
    att_grad_ref[...] = dot(cot_ref[...], w_out_ref[...], ((1,), (1,))).astype(BF16)
    bias_sum_ref[...] = jnp.zeros(bias_sum_ref.shape, F32)
    tall = per_half * members
    mask = (
        lax.broadcasted_iota(jnp.int32, (tall, LANES), 0) // members
        == lax.broadcasted_iota(jnp.int32, (tall, LANES), 1) // dim
    ).astype(F32).astype(BF16)
    owner = lax.broadcasted_iota(jnp.int32, (members, 2 * LANES), 1) % LANES // dim
    zero = jnp.zeros((members, LANES), BF16)

    def by_head(pair):
        return jnp.concatenate(
            [jnp.concatenate([v] * per_half, axis=0) * mask for v in pair], axis=1
        )

    def diagonal(pair):
        return jnp.concatenate(
            [
                jnp.concatenate([pair[0], zero], axis=1),
                jnp.concatenate([zero, pair[1]], axis=1),
            ],
            axis=0,
        )

    def collect(v):
        parts = [v[h * members : (h + 1) * members] for h in range(per_half)]
        picked = parts[-1]
        for h in range(per_half - 1):
            picked = jnp.where(owner == h, parts[h], picked)
        return [picked[:, :LANES], picked[:, LANES:]]

    def blocks(v):
        return [v[:members, :LANES], v[members:, LANES:]]

    def over_members(v, reduce):
        parted = v.reshape(per_half, members, 2 * members)
        small = reduce(parted, axis=1, keepdims=True)
        return jnp.broadcast_to(small, parted.shape).reshape(v.shape)

    def pair_step(g, carry):
        at = [pl.ds(pl.multiple_of((2 * g + k) * members, 16), members) for k in range(2)]
        for half in range(halves):
            def lanes(part):
                start = part * channels + half * LANES
                return slice(start, start + LANES)

            q, k, v = ([packed_ref[at[n], lanes(part)] for n in range(2)] for part in range(3))
            cot = [att_grad_ref[at[n], lanes(0)] for n in range(2)]
            q_diag, cot_diag = diagonal(q), diagonal(cot)
            k_tall, v_tall = by_head(k), by_head(v)
            scores = dot(k_tall, q_diag, ((1,), (1,))) * scale + bias_ref[half]
            grad_probs = dot(v_tall, cot_diag, ((1,), (1,)))
            lifted = jnp.exp(scores - over_members(scores, jnp.max))
            soft = lifted * (1.0 / over_members(lifted, jnp.sum))
            soft_low = soft.astype(BF16)
            grad_scores = soft * (grad_probs - over_members(grad_probs * soft, jnp.sum))
            bias_sum_ref[half] += grad_scores
            scaled = (grad_scores * scale).astype(BF16)
            attended = blocks(dot(soft_low, v_tall, ((0,), (0,))))
            grad_q = blocks(dot(scaled, k_tall, ((0,), (0,))))
            grad_v = collect(dot(soft_low, cot_diag))
            grad_k = collect(dot(scaled, q_diag))
            for n in range(2):
                att_ref[at[n], lanes(0)] = attended[n].astype(BF16)
                for part, value in enumerate((grad_q, grad_k, grad_v)):
                    packed_grad_ref[at[n], lanes(part)] = value[n].astype(BF16)
        return carry

    lax.fori_loop(0, cells // members // 2, pair_step, 0, unroll=2)
    grad = dot(packed_grad_ref[...], w_qkv_ref[...], ((1,), (1,)))
    for half in range(halves):
        lanes = slice(half * LANES, (half + 1) * LANES)
        for k, at in places():
            order_ref[half, at, :] = grad[k : k + GRID, lanes]
        grad_ref[:, lanes] = order_ref[half].astype(BF16)
    for half in range(halves):
        both = bias_sum_ref[half]
        bias_out_ref[half] = both[:, :members] + both[:, members:]


def run_attention(arrived, cot, w_qkv, w_out, bias_tall, heads, lines):
    cells, channels = cot.shape
    halves, tall, members2 = bias_tall.shape
    members = members2 // 2
    vmem = pl.BlockSpec(memory_space=pltpu.VMEM)
    return pl.pallas_call(
        functools.partial(attention_kernel, members, heads, lines),
        in_specs=[vmem] * 5,
        out_specs=[vmem] * 5,
        out_shape=[
            jax.ShapeDtypeStruct((cells, channels), BF16),
            jax.ShapeDtypeStruct((cells, channels), BF16),
            jax.ShapeDtypeStruct((cells, channels), BF16),
            jax.ShapeDtypeStruct((cells, 3 * channels), BF16),
            jax.ShapeDtypeStruct((halves, tall, members), F32),
        ],
        scratch_shapes=[
            pltpu.VMEM((channels // LANES, cells, LANES), F32),
            pltpu.VMEM((cells, 3 * channels), BF16),
            pltpu.VMEM((cells, channels), BF16),
            pltpu.VMEM(bias_tall.shape, F32),
        ],
        compiler_params=PARAMS,
        cost_estimate=estimate(14),
        name="attention",
    )(arrived.reshape(cells, channels), cot, w_qkv, w_out, bias_tall)


def attention_weights_kernel(x_ref, packed_grad_ref, att_ref, cot_ref, bias_ref, out_ref):
    channels = x_ref.shape[1]
    wide = 3 * channels
    out_ref[:, :wide] = dot(x_ref[...], packed_grad_ref[...], ((0,), (0,))).astype(BF16)
    out_ref[:, wide : wide + channels] = dot(att_ref[...], cot_ref[...], ((0,), (0,))).astype(BF16)
    bias = jnp.concatenate([bias_ref[half] for half in range(bias_ref.shape[0])], axis=1)
    out_ref[:, wide + channels :] = bias.astype(BF16)


def run_attention_weights(x, packed_grad, att, cot, bias):
    channels = x.shape[1]
    vmem = pl.BlockSpec(memory_space=pltpu.VMEM)
    width = 4 * channels + bias.shape[0] * bias.shape[2]
    return pl.pallas_call(
        attention_weights_kernel,
        in_specs=[vmem] * 5,
        out_specs=vmem,
        out_shape=jax.ShapeDtypeStruct((channels, width), BF16),
        compiler_params=PARAMS,
        cost_estimate=estimate(5),
        name="attention_weights",
    )(x, packed_grad, att, cot, bias)


def mixed_back_kernel(
    stride, bands,
    recv_ref, mixed_ref, cot_ref, gain_ref, act_ref, gate_ref, w_projt_ref,
    grad_ref, low_ref, norm_ref, project_ref, gate_grad_ref,
    turned_ref, total_ref,
):
    rows, cols, channels = mixed_ref.shape

    @pl.when(pl.program_id(0) == 0)
    def _():
        gain = gain_ref[...].astype(F32)
        lines = 4

        def some_rows(c, total):
            pieces = []
            for k in range(lines):
                i = c * lines + k
                a, p = lax.rem(i, stride), i // stride
                pieces += [recv_ref[a * bands + band, p] for band in range(bands)]
            grad = jnp.concatenate(pieces, axis=0).astype(F32)
            at = pl.ds(c * lines, lines)
            flat = lambda ref: ref[at].reshape(lines * cols, channels).astype(F32)
            unit, rstd = norm_rows(flat(mixed_ref))
            back = flat(cot_ref) + norm_rows_back(unit, rstd, gain, grad)
            grad_ref[at] = back.reshape(lines, cols, channels)
            low_ref[at] = back.astype(BF16).reshape(lines, cols, channels)
            return total + fold_rows(grad * unit)

        total = lax.fori_loop(
            0, rows // lines, some_rows, jnp.zeros((8, channels), F32), unroll=2
        )
        norm_ref[...] = jnp.sum(total, axis=0, keepdims=True)
        turned_ref[...] = low_ref[...].reshape(rows * cols, channels).T

    flat = act_ref[...].reshape(rows * cols, BLOCK)
    product = dot(turned_ref[...], flat)
    total = jnp.sum(product * w_projt_ref[...].astype(F32), axis=0, keepdims=True)
    step, steps = pl.program_id(0), pl.num_programs(0)
    total_ref[step] = total
    project_ref[...] = (product * gate_ref[...]).T.astype(BF16)

    @pl.when(step == steps - 1)
    def _():
        sums = [total_ref[e] for e in range(total_ref.shape[0])]
        high = [v.astype(BF16).astype(F32) for v in sums]
        terms = jnp.concatenate(high + [v - w for v, w in zip(sums, high)], axis=0)
        gate_grad_ref[...] = jnp.broadcast_to(terms.astype(BF16)[None], gate_grad_ref.shape)


def run_mixed_back(count, stride, recv, mixed, cot, gain, act, gate, w_project_t):
    rows, cols, channels = mixed.shape
    expanded = act.shape[2]
    return pl.pallas_call(
        functools.partial(mixed_back_kernel, stride, cols // SIDE),
        grid=(expanded // BLOCK,),
        in_specs=[
            whole(recv.shape), whole(mixed.shape), whole(cot.shape), whole(gain.shape),
            last_block(act.shape), last_block(gate.shape), last_block(w_project_t.shape),
        ],
        out_specs=[
            whole(mixed.shape), whole(mixed.shape), whole((1, channels)),
            last_block((BLOCK, expanded)), whole((count, 2 * expanded // BLOCK, BLOCK)),
        ],
        out_shape=[
            jax.ShapeDtypeStruct(mixed.shape, F32),
            jax.ShapeDtypeStruct(mixed.shape, BF16),
            jax.ShapeDtypeStruct((1, channels), F32),
            jax.ShapeDtypeStruct((BLOCK, expanded), BF16),
            jax.ShapeDtypeStruct((count, 2 * expanded // BLOCK, BLOCK), BF16),
        ],
        scratch_shapes=[
            pltpu.VMEM((channels, rows * cols), BF16),
            pltpu.VMEM((expanded // BLOCK, 1, BLOCK), F32),
        ],
        compiler_params=PARAMS,
        cost_estimate=estimate(7),
        name="mixed_back",
    )(recv, mixed, cot, gain, act, gate, w_project_t)


def unpack_kernel(
    place_ref, near_ref, far_ref, expand_ref, depth_ref, norm0_ref, norm1_ref, tail_ref
):
    expanded = expand_ref.shape[2]
    for pair, source in enumerate((near_ref, far_ref)):
        at = lax.rem(place_ref[0] + pair, 2)
        expand_ref[at] = source[:, :expanded].astype(F32)
        tail_ref[at] = source[:, expanded:].astype(F32)
    tail = tail_ref[0]
    pieces = expanded // LANES
    for t in range(9):
        for k in range(pieces):
            row = t * pieces + k
            lanes = slice(k * LANES, (k + 1) * LANES)
            depth_ref[t // 3, t % 3 : t % 3 + 1, lanes] = tail[row : row + 1]
    start = 9 * pieces
    half = norm0_ref.shape[1] // LANES
    for k in range(half):
        lanes = slice(k * LANES, (k + 1) * LANES)
        norm0_ref[:, lanes] = tail[start + k : start + k + 1]
        norm1_ref[:, lanes] = tail[start + half + k : start + half + k + 1]


def run_unpack(near, far, expanded):
    rows = near.shape[0]
    channels = 2 * rows
    place = (lax.axis_index("col") % 2).astype(jnp.int32).reshape(1)
    vmem = pl.BlockSpec(memory_space=pltpu.VMEM)
    return pl.pallas_call(
        unpack_kernel,
        in_specs=[pl.BlockSpec(memory_space=pltpu.SMEM), vmem, vmem],
        out_specs=[vmem] * 4,
        out_shape=[
            jax.ShapeDtypeStruct((2, rows, expanded), F32),
            jax.ShapeDtypeStruct((3, 3, expanded), F32),
            jax.ShapeDtypeStruct((1, channels), F32),
            jax.ShapeDtypeStruct((1, channels), F32),
        ],
        scratch_shapes=[pltpu.VMEM((2, rows, near.shape[1] - expanded), F32)],
        compiler_params=PARAMS,
        cost_estimate=estimate(2),
        name="unpack",
    )(place, near, far)


def expand_back_kernel(
    cells_total,
    parts_ref, hidden_ref, gate_all_ref, w_sq_ref, w_ex_ref,
    low_ref, up_ref, down_ref, side_ref, w_projt_ref, gate_ref, slope_ref, side_slope_ref,
    spread_slope_ref, spread_ref, w_dep_ref, turned_ref, w_exp_ref, gain_ref, norm1_ref,
    weights_ref, first_ref, logit_ref, pre_ref,
    main_ref, side_grad_ref, window_ref, expanded_ref, pool_ref, tail_ref, norm_ref,
):
    rows, cols, channels = low_ref.shape
    side = 8
    wide = cols + side
    step = pl.program_id(0)
    steps = pl.num_programs(0)

    @pl.when(step == 0)
    def _():
        gate = gate_all_ref[...]
        blocks = pool_ref.shape[0]
        terms = jnp.sum(parts_ref[...].astype(F32), axis=0)
        gate_grad = jnp.concatenate(
            [terms[e : e + 1] + terms[blocks + e : blocks + e + 1] for e in range(blocks)], axis=1
        )
        logit = gate_grad * gate * (1.0 - gate)
        hidden = hidden_ref[...]
        sig = jax.nn.sigmoid(hidden)
        pre = dot_exact(logit, w_ex_ref[...].astype(F32), ((1,), (1,))) * (
            sig + hidden * sig * (1.0 - sig)
        )
        logit_ref[...] = logit
        pre_ref[...] = pre
        pooled = dot_exact(pre, w_sq_ref[...].astype(F32), ((1,), (1,))) / cells_total
        for e in range(blocks):
            pool_ref[e] = pooled[:, e * BLOCK : (e + 1) * BLOCK]
        first_ref[...] = jnp.zeros(first_ref.shape, F32)
        tail_ref[...] = jnp.zeros(tail_ref.shape, F32)
        norm_ref[...] = jnp.zeros(norm_ref.shape, F32)

    w_projt = w_projt_ref[...]
    main_ref[pl.ds(0, cols), :] = dot(up_ref[0], w_projt)
    main_ref[pl.ds(cols, rows * cols), :] = dot(
        low_ref[...].reshape(rows * cols, channels), w_projt
    )
    main_ref[pl.ds((rows + 1) * cols, cols), :] = dot(down_ref[0], w_projt)
    side_grad_ref[...] = dot(side_ref[...], w_projt)

    @pl.loop(0, rows + 2, unroll=3)
    def _(i):
        for h in range(BLOCK // LANES):
            lanes = slice(h * LANES, (h + 1) * LANES)
            gate = gate_ref[:, lanes]
            pooled = pool_ref[step][:, lanes]
            gated = main_ref[pl.ds(pl.multiple_of(i * cols, 16), cols), lanes]
            main = (gated * gate + pooled) * slope_ref[i, :, lanes].astype(F32)
            gated = side_grad_ref[pl.ds(pl.multiple_of(i * side, side), side), lanes]
            edge = (gated * gate + pooled) * side_slope_ref[i, :, lanes]
            grad = jnp.concatenate([main, edge], axis=0)
            window_ref[0, i, :, lanes] = pltpu.roll(grad, wide - 1, 0)[:cols]
            window_ref[1, i, :, lanes] = grad[:cols]
            window_ref[2, i, :, lanes] = pltpu.roll(grad, 1, 0)[:cols]

    for h in range(BLOCK // LANES):
        lanes = slice(h * LANES, (h + 1) * LANES)
        taps = w_dep_ref[:, :, lanes].astype(F32)

        def back_row(i, sums):
            spread = spread_ref[i, :, lanes].astype(F32)
            total = jnp.zeros((cols, LANES), F32)
            new_sums = []
            for a in range(3):
                for b in range(3):
                    window = window_ref[b, i + 2 - a, :, lanes]
                    total = total + window * taps[a, b : b + 1]
                    new_sums.append(sums[a * 3 + b] + fold_rows(window * spread))
            grad = total * spread_slope_ref[i, :, lanes].astype(F32)
            expanded_ref[pl.ds(pl.multiple_of(i * cols, 16), cols), lanes] = grad.astype(BF16)
            return tuple(new_sums)

        sums = lax.fori_loop(0, rows, back_row, (jnp.zeros((8, LANES), F32),) * 9, unroll=2)
        for t in range(9):
            row = t * (steps * BLOCK // LANES) + step * (BLOCK // LANES) + h
            tail_ref[pl.ds(row, 1), :] = jnp.sum(sums[t], axis=0, keepdims=True)

    grad_expanded = expanded_ref[...]
    w_exp = w_exp_ref[...]
    weights = dot(turned_ref[...], grad_expanded)
    weights_ref[:, pl.ds(pl.multiple_of(step * BLOCK, BLOCK), BLOCK)] = weights.astype(BF16)
    norm_ref[...] += jnp.sum(weights * w_exp.astype(F32), axis=1, keepdims=True)
    first_ref[...] += dot(grad_expanded, w_exp, ((1,), (1,)))

    @pl.when(step == steps - 1)
    def _():
        norm = norm_ref[...].T[0:1] / gain_ref[...].astype(F32)
        start = 9 * steps * (BLOCK // LANES)
        for k in range(channels // LANES):
            piece = slice(k * LANES, (k + 1) * LANES)
            tail_ref[start + k : start + k + 1, :] = norm[:, piece]
            at = start + channels // LANES + k
            tail_ref[at : at + 1, :] = norm1_ref[:, piece]
        weights_ref[:, steps * BLOCK :] = tail_ref[...].astype(BF16)


def run_expand_back(
    cells_total, parts, hidden, gate, w_squeeze, w_excite, low, up, down, side,
    w_project_t, slope, side_slope, spread_slope, spread, w_depth, turned, w_expand, gain, norm1,
):
    rows, cols, channels = low.shape
    expanded = w_expand.shape[1]
    steps = expanded // BLOCK
    return pl.pallas_call(
        functools.partial(expand_back_kernel, cells_total),
        grid=(steps,),
        in_specs=[
            pl.BlockSpec(
                (parts.shape[0], 2 * steps, BLOCK), lambda e: (0, parts.shape[1] // (2 * steps) - 1, 0)
            ),
            whole(hidden.shape), whole(gate.shape),
            whole(w_squeeze.shape), whole(w_excite.shape),
            whole(low.shape), whole(up.shape), whole(down.shape), whole(side.shape),
            last_block(w_project_t.shape), last_block(gate.shape), last_block(slope.shape),
            last_block(side_slope.shape), last_block(spread_slope.shape), last_block(spread.shape),
            last_block(w_depth.shape), whole(turned.shape), last_block(w_expand.shape),
            whole(gain.shape), whole(norm1.shape),
        ],
        out_specs=[
            whole((channels, expanded + LANES)), whole((rows * cols, channels)),
            whole((1, expanded)), whole(hidden.shape),
        ],
        out_shape=[
            jax.ShapeDtypeStruct((channels, expanded + LANES), BF16),
            jax.ShapeDtypeStruct((rows * cols, channels), F32),
            jax.ShapeDtypeStruct((1, expanded), F32),
            jax.ShapeDtypeStruct(hidden.shape, F32),
        ],
        scratch_shapes=[
            pltpu.VMEM(((rows + 2) * cols, BLOCK), F32),
            pltpu.VMEM(((rows + 2) * 8, BLOCK), F32),
            pltpu.VMEM((3, rows + 2, cols, BLOCK), F32),
            pltpu.VMEM((rows * cols, BLOCK), BF16),
            pltpu.VMEM((steps, 1, BLOCK), F32),
            pltpu.VMEM((channels, LANES), F32),
            pltpu.VMEM((channels, LANES), F32),
        ],
        compiler_params=PARAMS,
        cost_estimate=estimate(14),
        name="expand_back",
    )(
        parts, hidden, gate, w_squeeze, w_excite, low, up, down, side, w_project_t, gate,
        slope, side_slope, spread_slope, spread, w_depth, turned, w_expand, gain, norm1,
    )


def image_back_kernel(image_ref, gain_ref, first_ref, mixed_ref, out_ref):
    unit, rstd = norm_rows(image_ref[...].astype(F32))
    grad = first_ref[...]
    back = mixed_ref[...] + norm_rows_back(unit, rstd, gain_ref[...].astype(F32), grad)
    out_ref[...] = back.astype(BF16)


def run_image_back(image, gain, first, mixed):
    cells, channels = image.shape
    block = pl.BlockSpec((cells // 4, channels), lambda r: (r, 0))
    return pl.pallas_call(
        image_back_kernel,
        grid=(4,),
        in_specs=[block, whole(gain.shape), block, block],
        out_specs=block,
        out_shape=jax.ShapeDtypeStruct((cells, channels), BF16),
        compiler_params=PARAMS,
        cost_estimate=estimate(4),
        name="image_back",
    )(image, gain, first, mixed)


def shift(cells, axis, step):
    count = lax.axis_size(axis)
    pairs = [(i, i + step) for i in range(count) if 0 <= i + step < count]
    return lax.ppermute(cells, axis, pairs)


def halo_rows(cells, width):
    up = shift(cells[cells.shape[0] - width :], "row", 1)
    down = shift(cells[:width], "row", -1)
    return up, down


def halo_sides(cells, up, down, width):
    rows, cols, channels = cells.shape
    first = jnp.concatenate([up[:, :width], cells[:, :width], down[:, :width]], axis=0)
    last = jnp.concatenate(
        [up[:, cols - width :], cells[:, cols - width :], down[:, cols - width :]], axis=0
    )
    left = shift(last, "col", 1)
    right = shift(first, "col", -1)
    gap = jnp.zeros((rows + 2 * width, 8 - 2 * width, channels), cells.dtype)
    side = jnp.concatenate([right, gap, left], axis=1)
    return side.reshape(-1, channels)


def hand_around(blocks):
    return lax.all_to_all(blocks, AXES, split_axis=0, concat_axis=0, tiled=True)


def sum_steps():
    return [("col", 1, 2), ("row", 1, lax.axis_size("row")), ("col", 2, lax.axis_size("col") // 2)]


def send_on(v, axis, stride, size, k):
    pairs = []
    for i in range(lax.axis_size(axis)):
        place = i // stride % size
        pairs.append((i, i + ((place + k) % size - place) * stride))
    return lax.ppermute(v, axis, pairs)


def sum_parts(matrix, axis, stride, size):
    place = lax.axis_index(axis) // stride % size
    parts = matrix.reshape(size, matrix.shape[0] // size, matrix.shape[1])
    part = lambda i: lax.dynamic_index_in_dim(parts, i % size, 0, False)
    total = part(place).astype(F32)
    for k in range(1, size):
        total = total + send_on(part(place + k), axis, stride, size, k).astype(F32)
    return total.astype(BF16)


def sum_shares(matrix):
    rows, columns = matrix.shape
    count = lax.axis_size("row") * lax.axis_size("col")
    pair = ("col", 1, 2)
    half = sum_parts(matrix, *pair)
    same_core = [list(range(k, count, 2)) for k in range(2)]

    def around(blocks):
        return lax.all_to_all(
            blocks, AXES, split_axis=0, concat_axis=0, tiled=True, axis_index_groups=same_core
        )

    arrived = around(half.reshape(count // 2, rows // count, columns))
    total = jnp.sum(arrived.astype(F32), axis=0).astype(BF16)
    sent = jnp.broadcast_to(total[None], (count // 2,) + total.shape)
    gathered = around(sent).reshape(rows // 2, columns)
    return gathered, send_on(gathered, *pair, 1)


def stack_kernel(*refs):
    for k, ref in enumerate(refs[:-1]):
        refs[-1][k] = ref[...]


def join_parts(blocks, axis, stride, size):
    arrived = [blocks] + [send_on(blocks, axis, stride, size, k) for k in range(1, size)]
    vmem = pl.BlockSpec(memory_space=pltpu.VMEM)
    stacked = pl.pallas_call(
        stack_kernel,
        in_specs=[vmem] * size,
        out_specs=vmem,
        out_shape=jax.ShapeDtypeStruct((size,) + blocks.shape, blocks.dtype),
        compiler_params=PARAMS,
        cost_estimate=estimate(1),
        name="stack",
    )(*arrived)
    return stacked.reshape((size * blocks.shape[0],) + blocks.shape[1:])


def unpack_weights_kernel(
    sizes, places_ref, near_ref, far_ref, qkv_ref, out_ref, bias_ref, project_ref
):
    channels = out_ref.shape[2]
    cuts = (0, 3 * channels, 4 * channels, 4 * channels + bias_ref.shape[2])
    pairs, over_row, rest = sizes
    for pair, source in enumerate((near_ref, far_ref)):
        for r in range(over_row):
            for c in range(rest):
                block = source[r * rest + c].astype(F32)
                at = lax.rem(places_ref[0] + pairs - pair, pairs)
                at = at * over_row + lax.rem(places_ref[1] + over_row - r, over_row)
                at = at * rest + lax.rem(places_ref[2] + rest - c, rest)
                for k, ref in enumerate((qkv_ref, out_ref, bias_ref)):
                    ref[at] = block[:, cuts[k] : cuts[k + 1]]
                for e in range(project_ref.shape[0]):
                    start = cuts[3] + e * channels
                    project_ref[e, at] = block[:, start : start + channels]


def run_unpack_weights(steps, near, far, channels, expanded, bias_width):
    count, rows, _ = near.shape
    count *= 2
    places = jnp.stack([lax.axis_index(axis) // stride % size for axis, stride, size in steps])
    vmem = pl.BlockSpec(memory_space=pltpu.VMEM)
    blocks = lambda width: jax.ShapeDtypeStruct((count, rows, width), F32)
    return pl.pallas_call(
        functools.partial(unpack_weights_kernel, tuple(size for _, _, size in steps)),
        in_specs=[pl.BlockSpec(memory_space=pltpu.SMEM), vmem, vmem],
        out_specs=[vmem] * 4,
        out_shape=[
            blocks(3 * channels), blocks(channels), blocks(bias_width),
            jax.ShapeDtypeStruct((expanded // BLOCK, count, rows, channels), F32),
        ],
        compiler_params=PARAMS,
        cost_estimate=estimate(2),
        name="unpack_weights",
    )(places.astype(jnp.int32), near, far)


def swap_groups(blocks, parity):
    groups = None
    if parity > 1:
        over_row = lax.axis_size("row")
        over_col = lax.axis_size("col")
        groups = [
            [r * over_col + c for r in range(over_row) for c in range(k, over_col, parity)]
            for k in range(parity)
        ]
    return lax.all_to_all(
        blocks, AXES, split_axis=0, concat_axis=0, tiled=True, axis_index_groups=groups
    )


def on_device(
    image, out_cotangent, norm0_gain, w_expand, w_depth, w_squeeze, w_excite, w_project,
    norm1_gain, w_qkv, w_out, attn_bias,
):
    rows, cols, channels = image.shape
    over_row = lax.axis_size("row")
    over_col = lax.axis_size("col")
    count = over_row * over_col
    cells_total = rows * cols * count
    stride = rows * over_row // GRID
    parity = over_col // GRID
    lines = rows // stride
    bands = cols // SIDE
    members = GRID * GRID
    expanded = w_expand.shape[1]

    def into_members(arrived):
        parted = arrived.reshape(over_row, GRID, lines, SIDE, channels)
        return parted.transpose(3, 0, 2, 1, 4).reshape(SIDE * members, channels)

    def out_of_members(values):
        parted = values.reshape(SIDE, over_row, lines, GRID, channels)
        return parted.transpose(1, 3, 2, 0, 4).reshape(-1, lines, SIDE, channels)

    row, col = lax.axis_index("row"), lax.axis_index("col")
    flags = jnp.stack([row > 0, row < over_row - 1, col > 0, col < over_col - 1]).astype(F32)
    gain_first = norm0_gain.reshape(1, channels)
    gain_second = norm1_gain.reshape(1, channels)
    w_project_t = w_project.T
    heads = attn_bias.shape[0]
    halves = channels // LANES
    bias_tall = attn_bias.transpose(0, 2, 1).reshape(halves, heads // halves * members, members)
    bias_tall = jnp.concatenate([bias_tall, bias_tall], axis=2)

    up, down = halo_rows(image, 2)
    normed_first, turned_first, spread, spread_slope = run_expand(image, gain_first, w_expand)
    up, down, spread = lax.optimization_barrier((up, down, spread))
    side = halo_sides(image, up, down, 2)
    cot_sent = (
        out_cotangent.reshape(lines, stride, bands, SIDE, channels)
        .transpose(1, 2, 0, 3, 4)
        .reshape(stride * bands, lines, SIDE, channels)
    )
    cot_members = into_members(swap_groups(cot_sent, parity))
    ring, act, pool = run_depthwise(count, up, down, side, gain_first, w_expand, w_depth, spread)
    pooled, hidden, gate, mixed, normed_sent = run_mix(
        cells_total, stride, hand_around(pool), w_squeeze, w_excite, act, image, w_project,
        gain_second, cot_members,
    )
    slope, side_slope = run_slope(flags, ring, w_depth, spread)
    normed_arrived = swap_groups(normed_sent, parity)
    normed_arrived, slope = lax.optimization_barrier((normed_arrived, slope))
    normed_members, attended, grad_normed, packed_grad, grad_bias = run_attention(
        normed_arrived, cot_members, w_qkv, w_out, bias_tall, heads, lines
    )
    grad_normed_home = swap_groups(grad_normed.reshape(normed_sent.shape), parity)
    weights = run_attention_weights(normed_members, packed_grad, attended, cot_members, grad_bias)
    grad_normed_home, weights = lax.optimization_barrier((grad_normed_home, weights))
    grad_mixed, grad_low, grad_norm1, grad_project, gate_grad = run_mixed_back(
        count, stride, grad_normed_home, mixed, out_cotangent, gain_second, act, gate, w_project_t
    )
    attended_sent = out_of_members(attended)
    if parity == 1:
        both = hand_around(
            jnp.concatenate([attended_sent.reshape(count, -1, channels), gate_grad], axis=1)
        )
        parts = both
        attended_home = both[:, : lines * SIDE].reshape(attended_sent.shape)
    else:
        parts = hand_around(gate_grad)
        attended_home = swap_groups(attended_sent, parity)
    up, down = halo_rows(grad_low, 1)
    side = halo_sides(grad_low, up, down, 1)
    weights = jnp.concatenate([weights, grad_project], axis=1)
    weights, _ = lax.optimization_barrier((weights, up))
    steps = sum_steps()
    for step in steps:
        weights = sum_parts(weights, *step)
    late, grad_first, logit, pre = run_expand_back(
        cells_total, parts, hidden, gate, w_squeeze, w_excite, grad_low, up, down, side,
        w_project_t, slope, side_slope, spread_slope, spread, w_depth, turned_first, w_expand,
        gain_first, grad_norm1,
    )
    weights, _ = lax.optimization_barrier((weights, late))
    weights = weights[None]
    for step in steps[:0:-1]:
        weights = join_parts(weights, *step)
    other = send_on(weights, *steps[0], 1)
    grad_qkv, grad_out_proj, grad_bias, grad_project = run_unpack_weights(
        steps, weights, other, channels, expanded, halves * members
    )
    grad_expand, grad_depth, grad_norm0, grad_norm1 = run_unpack(*sum_shares(late), expanded)
    grad_image = run_image_back(
        image.reshape(-1, channels), gain_first, grad_first, grad_mixed.reshape(-1, channels)
    )
    attended_map = (
        attended_home.reshape(stride, bands, lines, SIDE, channels)
        .transpose(2, 0, 1, 3, 4)
        .reshape(rows * cols, channels)
    )
    block_out = (mixed.reshape(-1, channels).astype(F32) + dot(attended_map, w_out)).astype(BF16)

    silu = jax.nn.silu(hidden)
    grad_squeeze = pooled.reshape(expanded, 1) * pre
    grad_excite = silu.reshape(-1, 1) * logit

    grad_bias = (
        grad_bias.reshape(heads // halves, members, halves, members)
        .transpose(2, 0, 3, 1)
        .reshape(attn_bias.shape)
    )
    return (
        block_out.reshape(image.shape),
        grad_image.reshape(image.shape),
        grad_norm0[0],
        grad_expand.reshape(w_expand.shape),
        grad_depth,
        grad_squeeze,
        grad_excite,
        grad_project.reshape(w_project.shape),
        grad_norm1[0],
        grad_qkv.reshape(w_qkv.shape),
        grad_out_proj.reshape(w_out.shape),
        grad_bias,
    )


def solution(mesh):
    cells = P("row", "col", None)
    return jax.shard_map(
        on_device,
        mesh=mesh,
        in_specs=(cells, cells) + (P(),) * 10,
        out_specs=(cells, cells) + (P(),) * 10,
        check_vma=False,
    )
```

profile of v0, /device:TPU:0, one launch (start us, length us, event | category | flops | bytes accessed | tf_op | source)
XLA Modules:
  0.0 222.3 jit_solution(13257412714031361762)
XLA Ops:
  0.7 0.9 fusion.15
  1.5 4.8 %collective-permute-start = (bf16[2,64,256]{2,1,0:T(8,128)(2,1)S(1)}, bf16[2,64,256]{2,1,0:T(8,128)(2,1)S(1)}, u32[]{:S(2)}, u32[]{:S(2)}) collective-permute-start(bf16[2,64,256]{2,1,0:T(8,128)(2,1)S(1)} %get-tuple-element.110), channel_id=1, source_target_pairs={{0,8},{8,16},{16,24},{1,9},{9,17},{17,25},{2,10},{10,18},{18,26},{... | collective-permute-start | bytes 196616 | tf_op jit(solution)/shard_map/ppermute | solution.py:810
  6.4 1.3 collective-permute-start.1
  7.7 1.9 copy.47
  9.6 7.0 %all-to-all-start.1 = ((bf16[32,2,16,256]{3,2,1,0:T(8,128)(2,1)}), bf16[32,2,16,256]{3,2,1,0:T(8,128)(2,1)S(1)}, u32[]{:S(2)}, u32[]{:S(2)}) async-start(bf16[32,2,16,256]{3,2,1,0:T(8,128)(2,1)} %bitcast.3), calls=%async_computation.1 | async-start | bytes 1048576 | tf_op jit(solution)/shard_map/all_to_all | solution.py:946
  17.2 7.3 %expand.1 = (bf16[1024,256]{1,0:T(8,128)(2,1)}, bf16[256,1024]{1,0:T(8,128)(2,1)}, bf16[16,64,1024]{2,1,0:T(8,128)(2,1)}, bf16[16,64,1024]{2,1,0:T(8,128)(2,1)}) custom-call(bf16[16,64,256]{2,1,0:T(8,128)(2,1)} %image_ref.3, bf16[1,256]{1,0:T(2,128)(2,1)} %reshape.136.gain_ref, bf16[256,1024]{1,0:T(8,128)(2,1)} %w_exp_ref.5), custom_call_target="tpu_custom_call" | custom-call | flops 15399999488 | bytes 50400000 | tf_op jit(solution)/shard_map/expand/pallas_call | solution.py:113
  24.5 0.9 fusion.14
  25.6 2.2 collective-permute-start.3
  27.8 1.3 collective-permute-start.2
  29.2 2.8 %collective-permute-done.2 = bf16[20,2,256]{2,0,1:T(8,128)(2,1)S(1)} collective-permute-done((bf16[20,2,256]{2,0,1:T(8,128)(2,1)S(1)}, bf16[20,2,256]{2,0,1:T(8,128)(2,1)S(1)}, u32[]{:S(2)}, u32[]{:S(2)}) %collective-permute-start.2) | collective-permute-done | bytes 20512 | tf_op jit(solution)/shard_map/ppermute | solution.py:810
  32.8 8.9 %depthwise.1 = (bf16[416,1024]{1,0:T(8,128)(2,1)}, bf16[16,64,1024]{2,1,0:T(8,128)(2,1)}, f32[32,1,1024]{2,1,0:T(1,128)}) custom-call(bf16[2,64,256]{2,1,0:T(8,128)(2,1)} %copy-done.17, bf16[2,64,256]{2,1,0:T(8,128)(2,1)} %copy-done.18, bf16[160,256]{1,0:T(8,128)(2,1)} %maximum_bitcast_fusion.side_ref, bf16[1,256]{1,0:T(2,128)(2,1)} %reshape.136.gain_ref, ...), custom_call_target="tpu_custom_call" | custom-call | flops 1100000000 | bytes 3600000 | tf_op jit(solution)/shard_map/depthwise/pallas_call | solution.py:205
  41.7 6.8 %all-to-all-start = ((f32[32,1,1024]{2,1,0:T(1,128)}), f32[32,1,1024]{2,1,0:T(1,128)S(1)}, u32[]{:S(2)}, u32[]{:S(2)}) async-start(f32[32,1,1024]{2,1,0:T(1,128)} %get-tuple-element.60), calls=%async_computation | async-start | bytes 262144 | tf_op jit(solution)/shard_map/all_to_all | solution.py:833
  48.5 0.8 copy.49.w_sq_ref
  50.6 0.8 pad_maximum_fusion.2.bias_ref
  51.4 1.1 copy.48
  52.5 4.1 %all-to-all-done.parts_ref = f32[32,1,1024]{2,1,0:T(1,128)S(1)} async-done(((f32[32,1,1024]{2,1,0:T(1,128)}), f32[32,1,1024]{2,1,0:T(1,128)S(1)}, u32[]{:S(2)}, u32[]{:S(2)}) %all-to-all-start) | async-done | bytes 131104 | tf_op jit(solution)/shard_map/all_to_all | solution.py:833
  57.3 5.4 %mix.1 = (f32[1,1024]{1,0:T(1,128)}, f32[1,64]{1,0:T(1,128)}, f32[1,1024]{1,0:T(1,128)}, bf16[16,64,256]{2,1,0:T(8,128)(2,1)}, bf16[32,2,16,256]{3,2,1,0:T(8,128)(2,1)}) custom-call(f32[32,1,1024]{2,1,0:T(1,128)} %copy-done.11, bf16[1024,64]{1,0:T(8,128)(2,1)} %copy.49.w_sq_ref, bf16[64,1024]{1,0:T(8,128)(2,1)} %w_ex_ref.3, ...), custom_call_target="tpu_custom_call" | custom-call | flops 5500000256 | bytes 18000000 | tf_op jit(solution)/shard_map/mix/pallas_call | solution.py:324
  62.7 2.6 %all-to-all-start.2 = ((bf16[32,2,16,256]{3,2,1,0:T(8,128)(2,1)}), bf16[32,2,16,256]{3,2,1,0:T(8,128)(2,1)S(1)}, u32[]{:S(2)}, u32[]{:S(2)}) async-start(bf16[32,2,16,256]{3,2,1,0:T(8,128)(2,1)} %get-tuple-element.63), calls=%async_computation.2 | async-start | bytes 1048576 | tf_op jit(solution)/shard_map/all_to_all | solution.py:946
  65.3 10.5 %slope.1 = (bf16[18,64,1024]{2,1,0:T(8,128)(2,1)}, f32[18,8,1024]{2,1,0:T(8,128)}) custom-call(f32[4]{0:T(128)} %add_convert_fusion.flags_ref, bf16[416,1024]{1,0:T(8,128)(2,1)} %get-tuple-element.64.ring_ref, bf16[3,3,1024]{2,1,0:T(4,128)(2,1)} %w_dep_ref.5, bf16[16,64,1024]{2,1,0:T(8,128)(2,1)} %get-tuple-element.59.spread_ref), custom_call_target="tpu_custom_call" | custom-call | flops 14300000256 | bytes 46800000 | tf_op jit(solution)/shard_map/slope/pallas_call | solution.py:265
  75.8 5.9 %all-to-all-done.2 = bf16[32,2,16,256]{3,2,1,0:T(8,128)(2,1)S(1)} async-done(((bf16[32,2,16,256]{3,2,1,0:T(8,128)(2,1)}), bf16[32,2,16,256]{3,2,1,0:T(8,128)(2,1)S(1)}, u32[]{:S(2)}, u32[]{:S(2)}) %all-to-all-start.2) | async-done | bytes 524320 | tf_op jit(solution)/shard_map/all_to_all | solution.py:946
  81.7 0.8 copy-done.7
  82.5 11.9 %attention.1 = (bf16[1024,256]{1,0:T(8,128)(2,1)}, bf16[1024,256]{1,0:T(8,128)(2,1)}, bf16[1024,256]{1,0:T(8,128)(2,1)}, bf16[1024,768]{1,0:T(8,128)(2,1)}, f32[2,256,64]{2,1,0:T(8,128)}) custom-call(bf16[1024,256]{1,0:T(8,128)(2,1)} %bitcast.114, bf16[1024,256]{1,0:T(8,128)(2,1)} %bitcast.109, bf16[256,768]{1,0:T(8,128)(2,1)} %w_qkv_ref.1, ...), custom_call_target="tpu_custom_call" | custom-call | flops 15399999488 | bytes 50400000 | tf_op jit(solution)/shard_map/attention/pallas_call | solution.py:462
  94.4 2.7 %all-to-all-start.3 = ((bf16[32,2,16,256]{3,2,1,0:T(8,128)(2,1)}), bf16[32,2,16,256]{3,2,1,0:T(8,128)(2,1)S(1)}, u32[]{:S(2)}, u32[]{:S(2)}) async-start(bf16[32,2,16,256]{3,2,1,0:T(8,128)(2,1)} %bitcast.112), calls=%async_computation.3 | async-start | bytes 1048576 | tf_op jit(solution)/shard_map/all_to_all | solution.py:946
  97.1 1.0 copy.52
  99.1 3.5 %attention_weights.1 = bf16[256,1152]{1,0:T(8,128)(2,1)} custom-call(bf16[1024,256]{1,0:T(8,128)(2,1)} %get-tuple-element.69.x_ref, bf16[1024,768]{1,0:T(8,128)(2,1)} %get-tuple-element.70.packed_grad_ref, bf16[1024,256]{1,0:T(8,128)(2,1)} %get-tuple-element.67.att_ref, bf16[1024,256]{1,0:T(8,128)(2,1)} %bitcast.110, f32[2,256,64]{2,1,0:T(8,128)} %get-tuple-element.71.bias_ref), custom_call_target="tpu_custom_call" | custom-call | flops 5500000256 | bytes 18000000 | tf_op jit(solution)/shard_map/attention_weights/pallas_call | solution.py:498
  102.6 10.9 %all-to-all-done.3.recv_ref = bf16[32,2,16,256]{3,2,1,0:T(8,128)(2,1)S(1)} async-done(((bf16[32,2,16,256]{3,2,1,0:T(8,128)(2,1)}), bf16[32,2,16,256]{3,2,1,0:T(8,128)(2,1)S(1)}, u32[]{:S(2)}, u32[]{:S(2)}) %all-to-all-start.3) | async-done | bytes 524320 | tf_op jit(solution)/shard_map/all_to_all | solution.py:946
  114.3 6.6 %mixed_back.1 = (f32[16,64,256]{2,1,0:T(8,128)}, bf16[16,64,256]{2,1,0:T(8,128)(2,1)}, f32[1,256]{1,0:T(1,128)}, bf16[256,1024]{1,0:T(8,128)(2,1)}, bf16[32,8,256]{2,1,0:T(8,128)(2,1)}) custom-call(bf16[32,2,16,256]{3,2,1,0:T(8,128)(2,1)} %copy-done.5, bf16[16,64,256]{2,1,0:T(8,128)(2,1)} %get-tuple-element.62.mixed_ref, bf16[16,64,256]{2,1,0:T(8,128)(2,1)} %cot_ref.1, ...), custom_call_target="tpu_custom_call" | custom-call | flops 7699999744 | bytes 25200000 | tf_op jit(solution)/shard_map/mixed_back/pallas_call | solution.py:561
  121.7 0.9 fusion.12
  122.6 1.9 pad_maximum_fusion.1
  124.5 2.6 %all-to-all-start.4 = ((bf16[32,40,256]{2,1,0:T(8,128)(2,1)}), bf16[32,40,256]{2,1,0:T(8,128)(2,1)S(1)}, u32[]{:S(2)}, u32[]{:S(2)}) async-start(bf16[32,40,256]{2,1,0:T(8,128)(2,1)} %pad_maximum_fusion.1), calls=%async_computation.4 | async-start | bytes 1310720 | tf_op jit(solution)/shard_map/all_to_all | solution.py:833
  127.1 3.5 %collective-permute-start.4 = (bf16[1,64,256]{2,1,0:T(8,128)(2,1)S(1)}, bf16[1,64,256]{2,1,0:T(8,128)(2,1)S(1)}, u32[]{:S(2)}, u32[]{:S(2)}) collective-permute-start(bf16[1,64,256]{2,1,0:T(8,128)(2,1)S(1)} %get-tuple-element.106), channel_id=1, source_target_pairs={{0,8},{8,16},{16,24},{1,9},{9,17},{17,25},{2,10},{10,18},{18,26},{... | collective-permute-start | bytes 98312 | tf_op jit(solution)/shard_map/ppermute | solution.py:810
  130.7 1.3 collective-permute-start.5
  132.4 4.2 %collective-permute-done.5.down_ref = bf16[1,64,256]{2,1,0:T(8,128)(2,1)S(1)} collective-permute-done((bf16[1,64,256]{2,1,0:T(8,128)(2,1)S(1)}, bf16[1,64,256]{2,1,0:T(8,128)(2,1)S(1)}, u32[]{:S(2)}, u32[]{:S(2)}) %collective-permute-start.5) | collective-permute-done | bytes 32800 | tf_op jit(solution)/shard_map/ppermute | solution.py:810
  136.6 1.3 collective-permute-start.7
  137.9 1.3 collective-permute-start.6
  140.1 3.4 %collective-permute-start.12 = (bf16[32,2176]{1,0:T(8,128)(2,1)S(1)}, bf16[32,2176]{1,0:T(8,128)(2,1)S(1)}, u32[]{:S(2)}, u32[]{:S(2)}) collective-permute-start(bf16[32,2176]{1,0:T(8,128)(2,1)S(1)} %get-tuple-element.102), channel_id=1, source_target_pairs={{0,16},{8,24},{16,0},{24,8},{1,17},{9,25},{17,1},{25,9},{2,18},{10... | collective-permute-start | bytes 417800 | tf_op jit(solution)/shard_map/ppermute | solution.py:845
  144.2 1.3 collective-permute-done.13
  145.5 1.7 collective-permute-done.12
  147.2 2.4 %collective-permute-done.11 = bf16[32,2176]{1,0:T(8,128)(2,1)S(1)} collective-permute-done((bf16[32,2176]{1,0:T(8,128)(2,1)S(1)}, bf16[32,2176]{1,0:T(8,128)(2,1)S(1)}, u32[]{:S(2)}, u32[]{:S(2)}) %collective-permute-start.11) | collective-permute-done | bytes 139296 | tf_op jit(solution)/shard_map/ppermute | solution.py:845
  149.7 6.4 %collective-permute-start.16 = (bf16[8,2176]{1,0:T(8,128)(2,1)S(1)}, bf16[8,2176]{1,0:T(8,128)(2,1)S(1)}, u32[]{:S(2)}, u32[]{:S(2)}) collective-permute-start(bf16[8,2176]{1,0:T(8,128)(2,1)S(1)} %get-tuple-element.112), channel_id=1, source_target_pairs={{0,6},{1,7},{2,0},{3,1},{4,2},{5,3},{6,4},{7,5},{8,14},{9,15},{10,... | collective-permute-start | bytes 104456 | tf_op jit(solution)/shard_map/ppermute | solution.py:845
  156.3 1.3 collective-permute-start.14
  157.6 0.8 copy-done
  158.4 16.4 %expand_back.1 = (bf16[256,1152]{1,0:T(8,128)(2,1)}, f32[1024,256]{1,0:T(8,128)}, f32[1,1024]{1,0:T(1,128)}, f32[1,64]{1,0:T(1,128)}) custom-call(bf16[32,40,256]{2,1,0:T(8,128)(2,1)} %copy-done, f32[1,64]{1,0:T(1,128)} %get-tuple-element.75.hidden_ref, f32[1,1024]{1,0:T(1,128)} %get-tuple-element.73.gate_ref.gate_all_ref, bf16[1024,64]{1,0:T(8,128)(2,1)} %copy.49.w_sq_ref, ...), custom_call_target="tpu_custom_call" | custom-call | flops 15399999488 | bytes 50400000 | tf_op jit(solution)/shard_map/expand_back/pallas_call | solution.py:742
  174.8 1.0 dynamic-slice_bitcast_fusion.1
  176.0 2.0 collective-permute-start.17
  178.0 1.1 collective-permute-start.18
  179.1 1.3 collective-permute-start.19
  180.4 1.8 fusion.3
  182.2 4.0 %all-to-all-start.5 = ((bf16[16,8,1152]{2,1,0:T(8,128)(2,1)}), bf16[16,8,1152]{2,1,0:T(8,128)(2,1)S(1)}, u32[]{:S(2)}, u32[]{:S(2)}) async-start(bf16[16,8,1152]{2,1,0:T(8,128)(2,1)} %fusion.3), calls=%async_computation.5 | async-start | bytes 589824 | tf_op jit(solution)/shard_map/all_to_all | solution.py:866
  187.5 1.5 stack.35
  189.0 1.9 collective-permute-start.20
  190.9 1.5 collective-permute-start.21
  192.4 1.5 collective-permute-start.22
  193.8 4.1 %image_back.1 = bf16[1024,256]{1,0:T(8,128)(2,1)} custom-call(bf16[1024,256]{1,0:T(8,128)(2,1)} %bitcast.119, bf16[1,256]{1,0:T(2,128)(2,1)} %reshape.136.gain_ref, f32[1024,256]{1,0:T(8,128)} %get-tuple-element.82.first_ref, f32[1024,256]{1,0:T(8,128)} %bitcast.133), custom_call_target="tpu_custom_call" | custom-call | flops 4400000000 | bytes 14400000 | tf_op jit(solution)/shard_map/image_back/pallas_call | solution.py:795
  198.7 4.6 %all-to-all-start.6 = ((bf16[16,8,1152]{2,1,0:T(8,128)(2,1)}), bf16[16,8,1152]{2,1,0:T(8,128)(2,1)S(1)}, u32[]{:S(2)}, u32[]{:S(2)}) async-start(bf16[16,8,1152]{2,1,0:T(8,128)(2,1)} %broadcast_in_dim.17), calls=%async_computation.6 | async-start | bytes 589824 | tf_op jit(solution)/shard_map/all_to_all | solution.py:866
  204.8 1.9 stack.36
  208.0 1.1 fusion
  209.1 4.0 %all-to-all-done.6 = bf16[16,8,1152]{2,1,0:T(8,128)(2,1)S(1)} async-done(((bf16[16,8,1152]{2,1,0:T(8,128)(2,1)}), bf16[16,8,1152]{2,1,0:T(8,128)(2,1)S(1)}, u32[]{:S(2)}, u32[]{:S(2)}) %all-to-all-start.6) | async-done | bytes 294944 | tf_op jit(solution)/shard_map/all_to_all | solution.py:866
  213.1 0.8 broadcast_multiply_fusion
  214.0 0.8 copy-done.21
  214.8 2.7 %unpack_weights.1 = (f32[32,8,768]{2,1,0:T(8,128)}, f32[32,8,256]{2,1,0:T(8,128)}, f32[32,8,128]{2,1,0:T(8,128)}, f32[4,32,8,256]{3,2,1,0:T(8,128)}) custom-call(s32[3]{0:T(128)} %pad_add_fusion.places_ref, bf16[16,8,2176]{2,1,0:T(8,128)(2,1)} %bitcast.128, bf16[16,8,2176]{2,1,0:T(8,128)(2,1)} %copy-done.21), custom_call_target="tpu_custom_call" | custom-call | flops 2200000000 | bytes 7200000 | tf_op jit(solution)/shard_map/unpack_weights/pallas_call | solution.py:923
  217.5 1.1 reshape.166
  218.6 0.8 copy.55
  220.2 2.1 unpack.1
  (132 shorter events, 13.8 us)
Async XLA Ops:
  0.6 16.0 %copy-start.29 = (bf16[256]{0:T(256)(128)(2,1)S(1)}, bf16[256]{0:T(256)(128)(2,1)}, u32[]{:S(2)}) copy-start(bf16[256]{0:T(256)(128)(2,1)} %param.14) | copy-start | bytes 1540
  1.5 23.9 %collective-permute-start = (bf16[2,64,256]{2,1,0:T(8,128)(2,1)S(1)}, bf16[2,64,256]{2,1,0:T(8,128)(2,1)S(1)}, u32[]{:S(2)}, u32[]{:S(2)}) collective-permute-start(bf16[2,64,256]{2,1,0:T(8,128)(2,1)S(1)} %get-tuple-element.110), channel_id=1, source_target_pairs={{0,8},{8,16},{16,24},{1,9},{9,17},{17,25},{2,10},{10,18},{18,26},{... | collective-permute-start | bytes 196616 | tf_op jit(solution)/shard_map/ppermute | solution.py:810
  6.4 19.1 %collective-permute-start.1 = (bf16[2,64,256]{2,1,0:T(8,128)(2,1)S(1)}, bf16[2,64,256]{2,1,0:T(8,128)(2,1)S(1)}, u32[]{:S(2)}, u32[]{:S(2)}) collective-permute-start(bf16[2,64,256]{2,1,0:T(8,128)(2,1)S(1)} %get-tuple-element.109), channel_id=1, source_target_pairs={{8,0},{16,8},{24,16},{9,1},{17,9},{25,17},{10,2},{18,10},{26,18},{... | collective-permute-start | bytes 196616 | tf_op jit(solution)/shard_map/ppermute | solution.py:810
  9.6 32.1 %all-to-all-start.1 = ((bf16[32,2,16,256]{3,2,1,0:T(8,128)(2,1)}), bf16[32,2,16,256]{3,2,1,0:T(8,128)(2,1)S(1)}, u32[]{:S(2)}, u32[]{:S(2)}) async-start(bf16[32,2,16,256]{3,2,1,0:T(8,128)(2,1)} %bitcast.3), calls=%async_computation.1 | async-start | bytes 1048576 | tf_op jit(solution)/shard_map/all_to_all | solution.py:946
  25.5 7.3 %copy-start.17 = (bf16[2,64,256]{2,1,0:T(8,128)(2,1)}, bf16[2,64,256]{2,1,0:T(8,128)(2,1)S(1)}, u32[]{:S(2)}) copy-start(bf16[2,64,256]{2,1,0:T(8,128)(2,1)S(1)} %collective-permute-done.up_ref) | copy-start | bytes 196612
  25.5 7.3 %copy-start.18 = (bf16[2,64,256]{2,1,0:T(8,128)(2,1)}, bf16[2,64,256]{2,1,0:T(8,128)(2,1)S(1)}, u32[]{:S(2)}) copy-start(bf16[2,64,256]{2,1,0:T(8,128)(2,1)S(1)} %collective-permute-done.1.down_ref) | copy-start | bytes 196612
  25.6 3.6 %collective-permute-start.3 = (bf16[20,2,256]{2,0,1:T(8,128)(2,1)S(1)}, bf16[20,2,256]{2,0,1:T(8,128)(2,1)S(1)}, u32[]{:S(2)}, u32[]{:S(2)}) collective-permute-start(bf16[20,2,256]{2,0,1:T(8,128)(2,1)S(1)} %pad_maximum_fusion.4), channel_id=1, source_target_pairs={{0,1},{1,2},{2,3},{3,4},{4,5},{5,6},{6,7},{8,9},{9,10},{10,11},{11... | collective-permute-start | bytes 61448 | tf_op jit(solution)/shard_map/ppermute | solution.py:810
  27.8 4.2 %collective-permute-start.2 = (bf16[20,2,256]{2,0,1:T(8,128)(2,1)S(1)}, bf16[20,2,256]{2,0,1:T(8,128)(2,1)S(1)}, u32[]{:S(2)}, u32[]{:S(2)}) collective-permute-start(bf16[20,2,256]{2,0,1:T(8,128)(2,1)S(1)} %pad_maximum_fusion.3), channel_id=1, source_target_pairs={{1,0},{2,1},{3,2},{4,3},{5,4},{6,5},{7,6},{9,8},{10,9},{11,10},{12... | collective-permute-start | bytes 61448 | tf_op jit(solution)/shard_map/ppermute | solution.py:810
  32.7 15.7 %copy-start.10 = (bf16[1024,64]{0,1:T(8,128)(2,1)S(1)}, bf16[1024,64]{0,1:T(8,128)(2,1)}, u32[]{:S(2)}) copy-start(bf16[1024,64]{0,1:T(8,128)(2,1)} %param.17) | copy-start | bytes 393220
  32.7 16.6 %copy-start.30 = (bf16[256]{0:T(256)(128)(2,1)S(1)}, bf16[256]{0:T(256)(128)(2,1)}, u32[]{:S(2)}) copy-start(bf16[256]{0:T(256)(128)(2,1)} %param.20) | copy-start | bytes 1540
  32.8 17.1 %copy-start.9 = (f32[8,64,64]{2,1,0:T(8,128)S(1)}, f32[8,64,64]{2,1,0:T(8,128)}, u32[]{:S(2)}) copy-start(f32[8,64,64]{2,1,0:T(8,128)} %param.23) | copy-start | bytes 393220
  41.7 15.0 %all-to-all-start = ((f32[32,1,1024]{2,1,0:T(1,128)}), f32[32,1,1024]{2,1,0:T(1,128)S(1)}, u32[]{:S(2)}, u32[]{:S(2)}) async-start(f32[32,1,1024]{2,1,0:T(1,128)} %get-tuple-element.60), calls=%async_computation | async-start | bytes 262144 | tf_op jit(solution)/shard_map/all_to_all | solution.py:833
  56.6 0.7 copy-start.11
  62.7 19.0 %all-to-all-start.2 = ((bf16[32,2,16,256]{3,2,1,0:T(8,128)(2,1)}), bf16[32,2,16,256]{3,2,1,0:T(8,128)(2,1)S(1)}, u32[]{:S(2)}, u32[]{:S(2)}) async-start(bf16[32,2,16,256]{3,2,1,0:T(8,128)(2,1)} %get-tuple-element.63), calls=%async_computation.2 | async-start | bytes 1048576 | tf_op jit(solution)/shard_map/all_to_all | solution.py:946
  81.7 0.8 copy-start.7
  94.4 2.8 %copy-start.3 = (bf16[1024,256]{1,0:T(8,128)(2,1)S(1)}, bf16[1024,256]{1,0:T(8,128)(2,1)}, u32[]{:S(2)}) copy-start(bf16[1024,256]{1,0:T(8,128)(2,1)} %w_proj_ref.1) | copy-start | bytes 1572868
  94.4 4.5 %copy-start.6 = (bf16[1024,256]{1,0:T(8,128)(2,1)S(1)}, bf16[1024,256]{1,0:T(8,128)(2,1)}, u32[]{:S(2)}) copy-start(bf16[1024,256]{1,0:T(8,128)(2,1)} %get-tuple-element.67.att_ref) | copy-start | bytes 1572868
  94.4 19.1 %all-to-all-start.3 = ((bf16[32,2,16,256]{3,2,1,0:T(8,128)(2,1)}), bf16[32,2,16,256]{3,2,1,0:T(8,128)(2,1)S(1)}, u32[]{:S(2)}, u32[]{:S(2)}) async-start(bf16[32,2,16,256]{3,2,1,0:T(8,128)(2,1)} %bitcast.112), calls=%async_computation.3 | async-start | bytes 1048576 | tf_op jit(solution)/shard_map/all_to_all | solution.py:946
  113.5 0.8 copy-start.5
  122.6 9.4 %copy-start.1 = (bf16[256,1152]{1,0:T(8,128)(2,1)S(1)}, bf16[256,1152]{1,0:T(8,128)(2,1)}, u32[]{:S(2)}) copy-start(bf16[256,1152]{1,0:T(8,128)(2,1)} %attention_weights.1) | copy-start | bytes 1769476
  122.6 9.4 %copy-start.2 = (bf16[256,1024]{1,0:T(8,128)(2,1)S(1)}, bf16[256,1024]{1,0:T(8,128)(2,1)}, u32[]{:S(2)}) copy-start(bf16[256,1024]{1,0:T(8,128)(2,1)} %get-tuple-element.92) | copy-start | bytes 1572868
  124.5 33.1 %all-to-all-start.4 = ((bf16[32,40,256]{2,1,0:T(8,128)(2,1)}), bf16[32,40,256]{2,1,0:T(8,128)(2,1)S(1)}, u32[]{:S(2)}, u32[]{:S(2)}) async-start(bf16[32,40,256]{2,1,0:T(8,128)(2,1)} %pad_maximum_fusion.1), calls=%async_computation.4 | async-start | bytes 1310720 | tf_op jit(solution)/shard_map/all_to_all | solution.py:833
  127.1 5.1 %collective-permute-start.4 = (bf16[1,64,256]{2,1,0:T(8,128)(2,1)S(1)}, bf16[1,64,256]{2,1,0:T(8,128)(2,1)S(1)}, u32[]{:S(2)}, u32[]{:S(2)}) collective-permute-start(bf16[1,64,256]{2,1,0:T(8,128)(2,1)S(1)} %get-tuple-element.106), channel_id=1, source_target_pairs={{0,8},{8,16},{16,24},{1,9},{9,17},{17,25},{2,10},{10,18},{18,26},{... | collective-permute-start | bytes 98312 | tf_op jit(solution)/shard_map/ppermute | solution.py:810
  130.7 5.9 %collective-permute-start.5 = (bf16[1,64,256]{2,1,0:T(8,128)(2,1)S(1)}, bf16[1,64,256]{2,1,0:T(8,128)(2,1)S(1)}, u32[]{:S(2)}, u32[]{:S(2)}) collective-permute-start(bf16[1,64,256]{2,1,0:T(8,128)(2,1)S(1)} %get-tuple-element.105), channel_id=1, source_target_pairs={{8,0},{16,8},{24,16},{9,1},{17,9},{25,17},{10,2},{18,10},{26,18},{... | collective-permute-start | bytes 98312 | tf_op jit(solution)/shard_map/ppermute | solution.py:810
  132.2 7.2 %copy-start.19 = (bf16[1,64,256]{2,1,0:T(8,128)(2,1)}, bf16[1,64,256]{2,1,0:T(8,128)(2,1)S(1)}, u32[]{:S(2)}) copy-start(bf16[1,64,256]{2,1,0:T(8,128)(2,1)S(1)} %collective-permute-done.4.up_ref) | copy-start | bytes 98308
  132.3 7.0 %collective-permute-start.10 = (bf16[128,2176]{1,0:T(8,128)(2,1)S(1)}, bf16[128,2176]{1,0:T(8,128)(2,1)S(1)}, u32[]{:S(2)}, u32[]{:S(2)}) collective-permute-start(bf16[128,2176]{1,0:T(8,128)(2,1)S(1)} %dynamic-slice_bitcast_fusion), channel_id=1, source_target_pairs={{0,1},{1,0},{2,3},{3,2},{4,5},{5,4},{6,7},{7,6},{8,9},{9,8},{10,11... | collective-permute-start | bytes 1671176 | tf_op jit(solution)/shard_map/ppermute | solution.py:845
  136.6 7.7 %copy-start.20 = (bf16[1,64,256]{2,1,0:T(8,128)(2,1)}, bf16[1,64,256]{2,1,0:T(8,128)(2,1)S(1)}, u32[]{:S(2)}) copy-start(bf16[1,64,256]{2,1,0:T(8,128)(2,1)S(1)} %collective-permute-done.5.down_ref) | copy-start | bytes 98308
  136.6 6.9 %collective-permute-start.7 = (bf16[18,1,256]{2,1,0:T(2,128)(2,1)S(1)}, bf16[18,1,256]{2,1,0:T(2,128)(2,1)S(1)}, u32[]{:S(2)}, u32[]{:S(2)}) collective-permute-start(bf16[18,1,256]{2,1,0:T(2,128)(2,1)S(1)} %pad_maximum_fusion.6), channel_id=1, source_target_pairs={{0,1},{1,2},{2,3},{3,4},{4,5},{5,6},{6,7},{8,9},{9,10},{10,11},{11... | collective-permute-start | bytes 27656 | tf_op jit(solution)/shard_map/ppermute | solution.py:810
  137.9 5.6 %collective-permute-start.6 = (bf16[18,1,256]{2,1,0:T(2,128)(2,1)S(1)}, bf16[18,1,256]{2,1,0:T(2,128)(2,1)S(1)}, u32[]{:S(2)}, u32[]{:S(2)}) collective-permute-start(bf16[18,1,256]{2,1,0:T(2,128)(2,1)S(1)} %pad_maximum_fusion.5), channel_id=1, source_target_pairs={{1,0},{2,1},{3,2},{4,3},{5,4},{6,5},{7,6},{9,8},{10,9},{11,10},{12... | collective-permute-start | bytes 27656 | tf_op jit(solution)/shard_map/ppermute | solution.py:810
  139.5 6.0 %collective-permute-start.13 = (bf16[32,2176]{1,0:T(8,128)(2,1)S(1)}, bf16[32,2176]{1,0:T(8,128)(2,1)S(1)}, u32[]{:S(2)}, u32[]{:S(2)}) collective-permute-start(bf16[32,2176]{1,0:T(8,128)(2,1)S(1)} %get-tuple-element.101), channel_id=1, source_target_pairs={{0,24},{8,0},{16,8},{24,16},{1,25},{9,1},{17,9},{25,17},{2,26},{10... | collective-permute-start | bytes 417800 | tf_op jit(solution)/shard_map/ppermute | solution.py:845
  140.1 7.1 %collective-permute-start.12 = (bf16[32,2176]{1,0:T(8,128)(2,1)S(1)}, bf16[32,2176]{1,0:T(8,128)(2,1)S(1)}, u32[]{:S(2)}, u32[]{:S(2)}) collective-permute-start(bf16[32,2176]{1,0:T(8,128)(2,1)S(1)} %get-tuple-element.102), channel_id=1, source_target_pairs={{0,16},{8,24},{16,0},{24,8},{1,17},{9,25},{17,1},{25,9},{2,18},{10... | collective-permute-start | bytes 417800 | tf_op jit(solution)/shard_map/ppermute | solution.py:845
  143.5 6.1 %collective-permute-start.11 = (bf16[32,2176]{1,0:T(8,128)(2,1)S(1)}, bf16[32,2176]{1,0:T(8,128)(2,1)S(1)}, u32[]{:S(2)}, u32[]{:S(2)}) collective-permute-start(bf16[32,2176]{1,0:T(8,128)(2,1)S(1)} %get-tuple-element.100), channel_id=1, source_target_pairs={{0,8},{8,16},{16,24},{24,0},{1,9},{9,17},{17,25},{25,1},{2,10},{10... | collective-permute-start | bytes 417800 | tf_op jit(solution)/shard_map/ppermute | solution.py:845
  149.7 26.2 %collective-permute-start.16 = (bf16[8,2176]{1,0:T(8,128)(2,1)S(1)}, bf16[8,2176]{1,0:T(8,128)(2,1)S(1)}, u32[]{:S(2)}, u32[]{:S(2)}) collective-permute-start(bf16[8,2176]{1,0:T(8,128)(2,1)S(1)} %get-tuple-element.112), channel_id=1, source_target_pairs={{0,6},{1,7},{2,0},{3,1},{4,2},{5,3},{6,4},{7,5},{8,14},{9,15},{10,... | collective-permute-start | bytes 104456 | tf_op jit(solution)/shard_map/ppermute | solution.py:845
  156.1 19.8 %collective-permute-start.15 = (bf16[8,2176]{1,0:T(8,128)(2,1)S(1)}, bf16[8,2176]{1,0:T(8,128)(2,1)S(1)}, u32[]{:S(2)}, u32[]{:S(2)}) collective-permute-start(bf16[8,2176]{1,0:T(8,128)(2,1)S(1)} %get-tuple-element.113), channel_id=1, source_target_pairs={{0,4},{1,5},{2,6},{3,7},{4,0},{5,1},{6,2},{7,3},{8,12},{9,13},{10,... | collective-permute-start | bytes 104456 | tf_op jit(solution)/shard_map/ppermute | solution.py:845
  156.3 19.6 %collective-permute-start.14 = (bf16[8,2176]{1,0:T(8,128)(2,1)S(1)}, bf16[8,2176]{1,0:T(8,128)(2,1)S(1)}, u32[]{:S(2)}, u32[]{:S(2)}) collective-permute-start(bf16[8,2176]{1,0:T(8,128)(2,1)S(1)} %get-tuple-element.111), channel_id=1, source_target_pairs={{0,2},{1,3},{2,4},{3,5},{4,6},{5,7},{6,0},{7,1},{8,10},{9,11},{10,... | collective-permute-start | bytes 104456 | tf_op jit(solution)/shard_map/ppermute | solution.py:845
  157.6 0.8 copy-start
  174.8 11.4 %copy-start.31 = (f32[1,64]{1,0:T(1,128)S(1)}, f32[1,64]{1,0:T(1,128)}, u32[]{:S(2)}) copy-start(f32[1,64]{1,0:T(1,128)} %get-tuple-element.75.hidden_ref) | copy-start | bytes 772
  175.8 4.6 %collective-permute-start.8 = (bf16[128,1152]{1,0:T(8,128)(2,1)S(1)}, bf16[128,1152]{1,0:T(8,128)(2,1)S(1)}, u32[]{:S(2)}, u32[]{:S(2)}) collective-permute-start(bf16[128,1152]{1,0:T(8,128)(2,1)S(1)} %dynamic-slice_bitcast_fusion.1), channel_id=1, source_target_pairs={{0,1},{1,0},{2,3},{3,2},{4,5},{5,4},{6,7},{7,6},{8,9},{9,8},{10,11... | collective-permute-start | bytes 884744 | tf_op jit(solution)/shard_map/ppermute | solution.py:845
  175.9 10.3 %copy-start.13 = (bf16[8,2176]{1,0:T(8,128)(2,1)}, bf16[8,2176]{1,0:T(8,128)(2,1)S(1)}, u32[]{:S(2)}) copy-start(bf16[8,2176]{1,0:T(8,128)(2,1)S(1)} %fusion.10) | copy-start | bytes 104452
  176.0 10.3 %collective-permute-start.17 = (bf16[1,8,2176]{2,1,0:T(8,128)(2,1)S(1)}, bf16[1,8,2176]{2,1,0:T(8,128)(2,1)S(1)}, u32[]{:S(2)}, u32[]{:S(2)}) collective-permute-start(bf16[1,8,2176]{2,1,0:T(8,128)(2,1)S(1)} %bitcast.120), channel_id=1, source_target_pairs={{0,2},{1,3},{2,4},{3,5},{4,6},{5,7},{6,0},{7,1},{8,10},{9,11},{10,... | collective-permute-start | bytes 104456 | tf_op jit(solution)/shard_map/ppermute | solution.py:845
  178.0 8.2 %collective-permute-start.18 = (bf16[1,8,2176]{2,1,0:T(8,128)(2,1)S(1)}, bf16[1,8,2176]{2,1,0:T(8,128)(2,1)S(1)}, u32[]{:S(2)}, u32[]{:S(2)}) collective-permute-start(bf16[1,8,2176]{2,1,0:T(8,128)(2,1)S(1)} %bitcast.121), channel_id=1, source_target_pairs={{0,4},{1,5},{2,6},{3,7},{4,0},{5,1},{6,2},{7,3},{8,12},{9,13},{10,... | collective-permute-start | bytes 104456 | tf_op jit(solution)/shard_map/ppermute | solution.py:845
  179.1 7.2 %collective-permute-start.19 = (bf16[1,8,2176]{2,1,0:T(8,128)(2,1)S(1)}, bf16[1,8,2176]{2,1,0:T(8,128)(2,1)S(1)}, u32[]{:S(2)}, u32[]{:S(2)}) collective-permute-start(bf16[1,8,2176]{2,1,0:T(8,128)(2,1)S(1)} %bitcast.122), channel_id=1, source_target_pairs={{0,6},{1,7},{2,0},{3,1},{4,2},{5,3},{6,4},{7,5},{8,14},{9,15},{10,... | collective-permute-start | bytes 104456 | tf_op jit(solution)/shard_map/ppermute | solution.py:845
  182.2 15.7 %all-to-all-start.5 = ((bf16[16,8,1152]{2,1,0:T(8,128)(2,1)}), bf16[16,8,1152]{2,1,0:T(8,128)(2,1)S(1)}, u32[]{:S(2)}, u32[]{:S(2)}) async-start(bf16[16,8,1152]{2,1,0:T(8,128)(2,1)} %fusion.3), calls=%async_computation.5 | async-start | bytes 589824 | tf_op jit(solution)/shard_map/all_to_all | solution.py:866
  186.2 0.6 copy-start.26
  186.3 0.6 copy-start.27
  186.9 0.6 copy-start.28
  189.0 14.4 %collective-permute-start.20 = (bf16[4,8,2176]{2,1,0:T(8,128)(2,1)}, bf16[4,8,2176]{2,1,0:T(8,128)(2,1)S(1)}, u32[]{:S(2)}, u32[]{:S(2)}) collective-permute-start(bf16[4,8,2176]{2,1,0:T(8,128)(2,1)} %bitcast.129), channel_id=1, source_target_pairs={{0,8},{8,16},{16,24},{24,0},{1,9},{9,17},{17,25},{25,1},{2,10},{10... | collective-permute-start | bytes 417800 | tf_op jit(solution)/shard_map/ppermute | solution.py:845
  190.9 12.5 %collective-permute-start.21 = (bf16[4,8,2176]{2,1,0:T(8,128)(2,1)}, bf16[4,8,2176]{2,1,0:T(8,128)(2,1)S(1)}, u32[]{:S(2)}, u32[]{:S(2)}) collective-permute-start(bf16[4,8,2176]{2,1,0:T(8,128)(2,1)} %bitcast.130), channel_id=1, source_target_pairs={{0,16},{8,24},{16,0},{24,8},{1,17},{9,25},{17,1},{25,9},{2,18},{10... | collective-permute-start | bytes 417800 | tf_op jit(solution)/shard_map/ppermute | solution.py:845
  192.4 11.1 %collective-permute-start.22 = (bf16[4,8,2176]{2,1,0:T(8,128)(2,1)}, bf16[4,8,2176]{2,1,0:T(8,128)(2,1)S(1)}, u32[]{:S(2)}, u32[]{:S(2)}) collective-permute-start(bf16[4,8,2176]{2,1,0:T(8,128)(2,1)} %bitcast.131), channel_id=1, source_target_pairs={{0,24},{8,0},{16,8},{24,16},{1,25},{9,1},{17,9},{25,17},{2,26},{10... | collective-permute-start | bytes 417800 | tf_op jit(solution)/shard_map/ppermute | solution.py:845
  198.7 14.4 %all-to-all-start.6 = ((bf16[16,8,1152]{2,1,0:T(8,128)(2,1)}), bf16[16,8,1152]{2,1,0:T(8,128)(2,1)S(1)}, u32[]{:S(2)}, u32[]{:S(2)}) async-start(bf16[16,8,1152]{2,1,0:T(8,128)(2,1)} %broadcast_in_dim.17), calls=%async_computation.6 | async-start | bytes 589824 | tf_op jit(solution)/shard_map/all_to_all | solution.py:866
  203.4 3.4 %copy-start.14 = (f32[1,1024]{1,0:T(1,128)S(1)}, f32[1,1024]{1,0:T(1,128)}, u32[]{:S(2)}) copy-start(f32[1,1024]{1,0:T(1,128)} %get-tuple-element.88) | copy-start | bytes 12292
  203.4 3.4 %copy-start.16 = (f32[1,64]{1,0:T(1,128)S(1)}, f32[1,64]{1,0:T(1,128)}, u32[]{:S(2)}) copy-start(f32[1,64]{1,0:T(1,128)} %get-tuple-element.89) | copy-start | bytes 772
  203.4 0.7 copy-start.23
  203.4 0.7 copy-start.24
  204.1 0.7 copy-start.25
  206.7 1.0 slice-start
  206.7 1.3 copy-start.4
  206.7 1.3 copy-start.12
  206.7 7.2 %collective-permute-start.23 = (bf16[16,8,2176]{2,1,0:T(8,128)(2,1)}, bf16[16,8,2176]{2,1,0:T(8,128)(2,1)S(1)}, u32[]{:S(2)}, u32[]{:S(2)}) collective-permute-start(bf16[16,8,2176]{2,1,0:T(8,128)(2,1)} %bitcast.127), channel_id=1, source_target_pairs={{0,1},{1,0},{2,3},{3,2},{4,5},{5,4},{6,7},{7,6},{8,9},{9,8},{10,11... | collective-permute-start | bytes 1671176 | tf_op jit(solution)/shard_map/ppermute | solution.py:845
  207.8 5.4 %copy-start.15 = (f32[1,1024]{1,0:T(1,128)S(1)}, f32[1,1024]{1,0:T(1,128)}, u32[]{:S(2)}) copy-start(f32[1,1024]{1,0:T(1,128)} %get-tuple-element.90) | copy-start | bytes 12292
  213.1 4.4 %copy-start.8 = (bf16[16,8,1152]{2,1,0:T(8,128)(2,1)}, bf16[16,8,1152]{2,1,0:T(8,128)(2,1)S(1)}, u32[]{:S(2)}) copy-start(bf16[16,8,1152]{2,1,0:T(8,128)(2,1)S(1)} %all-to-all-done.6) | copy-start | bytes 884740
  213.1 6.4 %collective-permute-start.9 = (bf16[128,1152]{1,0:T(8,128)(2,1)S(1)}, bf16[128,1152]{1,0:T(8,128)(2,1)S(1)}, u32[]{:S(2)}, u32[]{:S(2)}) collective-permute-start(bf16[128,1152]{1,0:T(8,128)(2,1)S(1)} %bitcast.115), channel_id=1, source_target_pairs={{0,1},{1,0},{2,3},{3,2},{4,5},{5,4},{6,7},{7,6},{8,9},{9,8},{10,11... | collective-permute-start | bytes 884744 | tf_op jit(solution)/shard_map/ppermute | solution.py:845
  214.0 0.8 copy-start.21
  219.5 0.7 copy-start.22
where the time goes:
time: 224 us; the launch traced here: 222 us
  Pallas kernels  82.9 us (37%)
  starting transfers between devices  68.9 us (31%)
  waiting for transfers between devices  37.4 us (17%)
  local copies, waits for them, and re-layouts  21.5 us (10%)
  other arithmetic  9.24 us (4%)
    ppermute x16, starting transfers between devices, send_on(): return lax.ppermute(v, axis, pairs)  21.5 us
    ppermute x8, starting transfers between devices, shift(): return lax.ppermute(cells, axis, pairs)  17 us
    all_to_all x3, waiting for transfers between devices, swap_groups(): lax.all_to_all(blocks, AXES, split_axis=0, concat_axis=0, tiled=True, axi...  16.8 us
    pallas_call x1, Pallas kernels, run_expand_back(): pl.pallas_call(functools.partial(expand_back_kernel, cells_total), grid=(...  16.4 us
    all_to_all x3, starting transfers between devices, swap_groups(): lax.all_to_all(blocks, AXES, split_axis=0, concat_axis=0, tiled=True, axi...  12.4 us
    pallas_call x1, Pallas kernels, run_attention(): pl.pallas_call(functools.partial(attention_kernel, members, heads, lines)...  11.9 us
    pallas_call x1, Pallas kernels, run_slope(): pl.pallas_call(slope_kernel, grid=(expanded // BLOCK,), in_specs=[pl.Bloc...  10.5 us
    all_to_all x2, starting transfers between devices, hand_around(): return lax.all_to_all(blocks, AXES, split_axis=0, concat_axis=0, tiled=True)  9.39 us
  transfers between devices with their start and end apart: 31, of which 10 were waited for; matrix products, arithmetic and copies ran while one was open for 9% of the time, Pallas kernels for 26%

commit v1 on v0

--- a/solution.py
+++ b/solution.py
@@ -348,9 +348,9 @@
 
 def attention_kernel(
     members, heads, lines,
-    arrived_ref, cot_ref, w_qkv_ref, w_out_ref, bias_ref,
+    arrived_ref, att_grad_ref, w_qkv_ref, bias_ref,
     x_ref, att_ref, grad_ref, packed_grad_ref, bias_out_ref,
-    order_ref, packed_ref, att_grad_ref, bias_sum_ref,
+    order_ref, packed_ref, bias_sum_ref,
 ):
     cells, channels = x_ref.shape
     groups = cells // members
@@ -374,7 +374,6 @@
     halves = channels // LANES
     scale = dim ** (-0.5)
     packed_ref[...] = dot(x_ref[...], w_qkv_ref[...]).astype(BF16)
-    att_grad_ref[...] = dot(cot_ref[...], w_out_ref[...], ((1,), (1,))).astype(BF16)
     bias_sum_ref[...] = jnp.zeros(bias_sum_ref.shape, F32)
     tall = per_half * members
     mask = (
@@ -454,14 +453,14 @@
         bias_out_ref[half] = both[:, :members] + both[:, members:]
 
 
-def run_attention(arrived, cot, w_qkv, w_out, bias_tall, heads, lines):
-    cells, channels = cot.shape
+def run_attention(arrived, att_grad, w_qkv, bias_tall, heads, lines):
+    cells, channels = att_grad.shape
     halves, tall, members2 = bias_tall.shape
     members = members2 // 2
     vmem = pl.BlockSpec(memory_space=pltpu.VMEM)
     return pl.pallas_call(
         functools.partial(attention_kernel, members, heads, lines),
-        in_specs=[vmem] * 5,
+        in_specs=[vmem] * 4,
         out_specs=[vmem] * 5,
         out_shape=[
             jax.ShapeDtypeStruct((cells, channels), BF16),
@@ -473,13 +472,12 @@
         scratch_shapes=[
             pltpu.VMEM((channels // LANES, cells, LANES), F32),
             pltpu.VMEM((cells, 3 * channels), BF16),
-            pltpu.VMEM((cells, channels), BF16),
             pltpu.VMEM(bias_tall.shape, F32),
         ],
         compiler_params=PARAMS,
         cost_estimate=estimate(14),
         name="attention",
-    )(arrived.reshape(cells, channels), cot, w_qkv, w_out, bias_tall)
+    )(arrived.reshape(cells, channels), att_grad, w_qkv, bias_tall)
 
 
 def attention_weights_kernel(x_ref, packed_grad_ref, att_ref, cot_ref, bias_ref, out_ref):
@@ -487,8 +485,11 @@
     wide = 3 * channels
     out_ref[:, :wide] = dot(x_ref[...], packed_grad_ref[...], ((0,), (0,))).astype(BF16)
     out_ref[:, wide : wide + channels] = dot(att_ref[...], cot_ref[...], ((0,), (0,))).astype(BF16)
-    bias = jnp.concatenate([bias_ref[half] for half in range(bias_ref.shape[0])], axis=1)
-    out_ref[:, wide + channels :] = bias.astype(BF16)
+    halves, tall, members = bias_ref.shape
+    for h in range(tall // members):
+        rows = slice(h * members, (h + 1) * members)
+        turned = jnp.concatenate([bias_ref[half, rows, :].T for half in range(halves)], axis=1)
+        out_ref[rows, wide + channels :] = turned.astype(BF16)
 
 
 def run_attention_weights(x, packed_grad, att, cot, bias):
@@ -509,7 +510,7 @@
 def mixed_back_kernel(
     stride, bands,
     recv_ref, mixed_ref, cot_ref, gain_ref, act_ref, gate_ref, w_projt_ref,
-    grad_ref, low_ref, norm_ref, project_ref, gate_grad_ref,
+    grad_ref, low_ref, norm_ref, project_ref, gate_grad_ref, lines_ref, sides_ref,
     turned_ref, total_ref,
 ):
     rows, cols, channels = mixed_ref.shape
@@ -538,6 +539,11 @@
             0, rows // lines, some_rows, jnp.zeros((8, channels), F32), unroll=2
         )
         norm_ref[...] = jnp.sum(total, axis=0, keepdims=True)
+        lines_ref[0] = low_ref[0]
+        lines_ref[1] = low_ref[rows - 1]
+        for i in range(rows):
+            sides_ref[0, i] = low_ref[i, 0:1, :]
+            sides_ref[1, i] = low_ref[i, cols - 1 : cols, :]
         turned_ref[...] = low_ref[...].reshape(rows * cols, channels).T
 
     flat = act_ref[...].reshape(rows * cols, BLOCK)
@@ -568,6 +574,7 @@
         out_specs=[
             whole(mixed.shape), whole(mixed.shape), whole((1, channels)),
             last_block((BLOCK, expanded)), whole((count, 2 * expanded // BLOCK, BLOCK)),
+            whole((2, cols, channels)), whole((2, rows, 1, channels)),
         ],
         out_shape=[
             jax.ShapeDtypeStruct(mixed.shape, F32),
@@ -575,6 +582,8 @@
             jax.ShapeDtypeStruct((1, channels), F32),
             jax.ShapeDtypeStruct((BLOCK, expanded), BF16),
             jax.ShapeDtypeStruct((count, 2 * expanded // BLOCK, BLOCK), BF16),
+            jax.ShapeDtypeStruct((2, cols, channels), BF16),
+            jax.ShapeDtypeStruct((2, rows, 1, channels), BF16),
         ],
         scratch_shapes=[
             pltpu.VMEM((channels, rows * cols), BF16),
@@ -810,23 +819,18 @@
     return lax.ppermute(cells, axis, pairs)
 
 
-def halo_rows(cells, width):
-    up = shift(cells[cells.shape[0] - width :], "row", 1)
-    down = shift(cells[:width], "row", -1)
-    return up, down
-
-
-def halo_sides(cells, up, down, width):
-    rows, cols, channels = cells.shape
-    first = jnp.concatenate([up[:, :width], cells[:, :width], down[:, :width]], axis=0)
-    last = jnp.concatenate(
-        [up[:, cols - width :], cells[:, cols - width :], down[:, cols - width :]], axis=0
-    )
+def halo_rows(top, bottom):
+    return shift(bottom, "row", 1), shift(top, "row", -1)
+
+
+def halo_sides(first, last, up, down):
+    width = up.shape[0]
+    first = jnp.concatenate([up[:, :width], first, down[:, :width]], axis=0)
+    last = jnp.concatenate([up[:, -width:], last, down[:, -width:]], axis=0)
     left = shift(last, "col", 1)
     right = shift(first, "col", -1)
-    gap = jnp.zeros((rows + 2 * width, 8 - 2 * width, channels), cells.dtype)
-    side = jnp.concatenate([right, gap, left], axis=1)
-    return side.reshape(-1, channels)
+    gap = jnp.zeros((first.shape[0], 8 - 2 * width, first.shape[2]), first.dtype)
+    return jnp.concatenate([right, gap, left], axis=1).reshape(-1, first.shape[2])
 
 
 def hand_around(blocks):
@@ -898,7 +902,8 @@
     sizes, places_ref, near_ref, far_ref, qkv_ref, out_ref, bias_ref, project_ref
 ):
     channels = out_ref.shape[2]
-    cuts = (0, 3 * channels, 4 * channels, 4 * channels + bias_ref.shape[2])
+    halves, members = bias_ref.shape[0], bias_ref.shape[3]
+    cuts = (0, 3 * channels, 4 * channels, 4 * channels + halves * members)
     pairs, over_row, rest = sizes
     for pair, source in enumerate((near_ref, far_ref)):
         for r in range(over_row):
@@ -907,14 +912,17 @@
                 at = lax.rem(places_ref[0] + pairs - pair, pairs)
                 at = at * over_row + lax.rem(places_ref[1] + over_row - r, over_row)
                 at = at * rest + lax.rem(places_ref[2] + rest - c, rest)
-                for k, ref in enumerate((qkv_ref, out_ref, bias_ref)):
-                    ref[at] = block[:, cuts[k] : cuts[k + 1]]
+                qkv_ref[at] = block[:, : cuts[1]]
+                out_ref[at] = block[:, cuts[1] : cuts[2]]
+                for half in range(halves):
+                    start = cuts[2] + half * members
+                    bias_ref[half, at] = block[:, start : start + members]
                 for e in range(project_ref.shape[0]):
                     start = cuts[3] + e * channels
                     project_ref[e, at] = block[:, start : start + channels]
 
 
-def run_unpack_weights(steps, near, far, channels, expanded, bias_width):
+def run_unpack_weights(steps, near, far, channels, expanded, halves, members):
     count, rows, _ = near.shape
     count *= 2
     places = jnp.stack([lax.axis_index(axis) // stride % size for axis, stride, size in steps])
@@ -925,7 +933,8 @@
         in_specs=[pl.BlockSpec(memory_space=pltpu.SMEM), vmem, vmem],
         out_specs=[vmem] * 4,
         out_shape=[
-            blocks(3 * channels), blocks(channels), blocks(bias_width),
+            blocks(3 * channels), blocks(channels),
+            jax.ShapeDtypeStruct((halves, count, rows, members), F32),
             jax.ShapeDtypeStruct((expanded // BLOCK, count, rows, channels), F32),
         ],
         compiler_params=PARAMS,
@@ -982,10 +991,10 @@
     bias_tall = attn_bias.transpose(0, 2, 1).reshape(halves, heads // halves * members, members)
     bias_tall = jnp.concatenate([bias_tall, bias_tall], axis=2)
 
-    up, down = halo_rows(image, 2)
+    up, down = halo_rows(image[:2], image[-2:])
     normed_first, turned_first, spread, spread_slope = run_expand(image, gain_first, w_expand)
     up, down, spread = lax.optimization_barrier((up, down, spread))
-    side = halo_sides(image, up, down, 2)
+    side = halo_sides(image[:, :2], image[:, -2:], up, down)
     cot_sent = (
         out_cotangent.reshape(lines, stride, bands, SIDE, channels)
         .transpose(1, 2, 0, 3, 4)
@@ -999,14 +1008,15 @@
     )
     slope, side_slope = run_slope(flags, ring, w_depth, spread)
     normed_arrived = swap_groups(normed_sent, parity)
-    normed_arrived, slope = lax.optimization_barrier((normed_arrived, slope))
+    att_grad = dot(cot_members, w_out, ((1,), (1,))).astype(BF16)
+    normed_arrived, slope, att_grad = lax.optimization_barrier((normed_arrived, slope, att_grad))
     normed_members, attended, grad_normed, packed_grad, grad_bias = run_attention(
-        normed_arrived, cot_members, w_qkv, w_out, bias_tall, heads, lines
+        normed_arrived, att_grad, w_qkv, bias_tall, heads, lines
     )
     grad_normed_home = swap_groups(grad_normed.reshape(normed_sent.shape), parity)
     weights = run_attention_weights(normed_members, packed_grad, attended, cot_members, grad_bias)
     grad_normed_home, weights = lax.optimization_barrier((grad_normed_home, weights))
-    grad_mixed, grad_low, grad_norm1, grad_project, gate_grad = run_mixed_back(
+    grad_mixed, grad_low, grad_norm1, grad_project, gate_grad, edge_lines, edge_sides = run_mixed_back(
         count, stride, grad_normed_home, mixed, out_cotangent, gain_second, act, gate, w_project_t
     )
     attended_sent = out_of_members(attended)
@@ -1019,12 +1029,12 @@
     else:
         parts = hand_around(gate_grad)
         attended_home = swap_groups(attended_sent, parity)
-    up, down = halo_rows(grad_low, 1)
-    side = halo_sides(grad_low, up, down, 1)
+    up, down = halo_rows(edge_lines[:1], edge_lines[1:])
+    side = halo_sides(edge_sides[0], edge_sides[1], up, down)
     weights = jnp.concatenate([weights, grad_project], axis=1)
     weights, _ = lax.optimization_barrier((weights, up))
     steps = sum_steps()
-    for step in steps:
+    for step in steps[:2]:
         weights = sum_parts(weights, *step)
     late, grad_first, logit, pre = run_expand_back(
         cells_total, parts, hidden, gate, w_squeeze, w_excite, grad_low, up, down, side,
@@ -1032,12 +1042,13 @@
         gain_first, grad_norm1,
     )
     weights, _ = lax.optimization_barrier((weights, late))
+    weights = sum_parts(weights, *steps[2])
     weights = weights[None]
     for step in steps[:0:-1]:
         weights = join_parts(weights, *step)
     other = send_on(weights, *steps[0], 1)
     grad_qkv, grad_out_proj, grad_bias, grad_project = run_unpack_weights(
-        steps, weights, other, channels, expanded, halves * members
+        steps, weights, other, channels, expanded, halves, members
     )
     grad_expand, grad_depth, grad_norm0, grad_norm1 = run_unpack(*sum_shares(late), expanded)
     grad_image = run_image_back(
@@ -1054,11 +1065,6 @@
     grad_squeeze = pooled.reshape(expanded, 1) * pre
     grad_excite = silu.reshape(-1, 1) * logit
 
-    grad_bias = (
-        grad_bias.reshape(heads // halves, members, halves, members)
-        .transpose(2, 0, 3, 1)
-        .reshape(attn_bias.shape)
-    )
     return (
         block_out.reshape(image.shape),
         grad_image.reshape(image.shape),
@@ -1071,7 +1077,7 @@
         grad_norm1[0],
         grad_qkv.reshape(w_qkv.shape),
         grad_out_proj.reshape(w_out.shape),
-        grad_bias,
+        grad_bias.reshape(attn_bias.shape),
     )
 
 

time: 224 us -> 228 us (1.018)
  waiting for transfers between devices: 37.4 us -> 46.5 us
  starting transfers between devices: 68.9 us -> 65.3 us
  local copies, waits for them, and re-layouts: 21.5 us -> 18.9 us
    ppermute x16, waiting for transfers between devices: 5.36 us -> 15.2 us  [send_on(): return lax.ppermute(v, axis, pairs)]
    ppermute x16, starting transfers between devices: 21.5 us -> 15.9 us  [send_on(): return lax.ppermute(v, axis, pairs)]
    all_to_all x2, starting transfers between devices: 9.39 us -> 13.5 us  [hand_around(): return lax.all_to_all(blocks, AXES, split_axis=0, concat_axis=0, tiled=True)]
    all_to_all x2, waiting for transfers between devices: 4.1 us -> 6.9 us  [hand_around(): return lax.all_to_all(blocks, AXES, split_axis=0, concat_axis=0, tiled=True)]
    unnamed x68 -> x74, local copies, waits for them, and re-layouts: 9.32 us -> 9.29 us
  transfers between devices with their start and end apart: 31 -> 31, of which waited for: 10 -> 12; matrix products, arithmetic and copies ran while one was open for 9% -> 9% of each run, Pallas kernels for 26% -> 18%
where the time goes in v1:
time: 228 us; the launch traced here: 227 us
  Pallas kernels  82.9 us (36%)
  starting transfers between devices  65.3 us (29%)
  waiting for transfers between devices  46.5 us (20%)
  local copies, waits for them, and re-layouts  18.9 us (8%)
  other arithmetic  9.32 us (4%)
    pallas_call x1, Pallas kernels, run_expand_back(): pl.pallas_call(functools.partial(expand_back_kernel, cells_total), grid=(...  16.3 us
    ppermute x16, starting transfers between devices, send_on(): return lax.ppermute(v, axis, pairs)  15.9 us
    all_to_all x3, waiting for transfers between devices, swap_groups(): lax.all_to_all(blocks, AXES, split_axis=0, concat_axis=0, tiled=True, axi...  15.5 us
    ppermute x16, waiting for transfers between devices, send_on(): return lax.ppermute(v, axis, pairs)  15.2 us
    ppermute x8, starting transfers between devices, shift(): return lax.ppermute(cells, axis, pairs)  15 us
    all_to_all x2, starting transfers between devices, hand_around(): return lax.all_to_all(blocks, AXES, split_axis=0, concat_axis=0, tiled=True)  13.5 us
    all_to_all x3, starting transfers between devices, swap_groups(): lax.all_to_all(blocks, AXES, split_axis=0, concat_axis=0, tiled=True, axi...  12.4 us
    pallas_call x1, Pallas kernels, run_attention(): pl.pallas_call(functools.partial(attention_kernel, members, heads, lines)...  11.8 us
  transfers between devices with their start and end apart: 31, of which 12 were waited for; matrix products, arithmetic and copies ran while one was open for 9% of the time, Pallas kernels for 18%

profile of v1, /device:TPU:0, one launch (start us, length us, event | category | flops | bytes accessed | tf_op | source)
XLA Modules:
  0.0 226.5 jit_solution(6023533912545935174)
XLA Ops:
  0.7 0.9 fusion.13
  1.6 4.8 %collective-permute-start = (bf16[2,64,256]{2,1,0:T(8,128)(2,1)S(1)}, bf16[2,64,256]{2,1,0:T(8,128)(2,1)S(1)}, u32[]{:S(2)}, u32[]{:S(2)}) collective-permute-start(bf16[2,64,256]{2,1,0:T(8,128)(2,1)S(1)} %get-tuple-element.112), channel_id=1, source_target_pairs={{0,8},{8,16},{16,24},{1,9},{9,17},{17,25},{2,10},{10,18},{18,26},{... | collective-permute-start | bytes 196616 | tf_op jit(solution)/shard_map/ppermute | solution.py:819
  6.4 1.3 collective-permute-start.1
  7.7 1.9 copy.57
  9.6 7.0 %all-to-all-start.1 = ((bf16[32,2,16,256]{3,2,1,0:T(8,128)(2,1)}), bf16[32,2,16,256]{3,2,1,0:T(8,128)(2,1)S(1)}, u32[]{:S(2)}, u32[]{:S(2)}) async-start(bf16[32,2,16,256]{3,2,1,0:T(8,128)(2,1)} %bitcast.3), calls=%async_computation.1 | async-start | bytes 1048576 | tf_op jit(solution)/shard_map/all_to_all | solution.py:955
  17.2 7.3 %expand.1 = (bf16[1024,256]{1,0:T(8,128)(2,1)}, bf16[256,1024]{1,0:T(8,128)(2,1)}, bf16[16,64,1024]{2,1,0:T(8,128)(2,1)}, bf16[16,64,1024]{2,1,0:T(8,128)(2,1)}) custom-call(bf16[16,64,256]{2,1,0:T(8,128)(2,1)} %image_ref.3, bf16[1,256]{1,0:T(2,128)(2,1)} %reshape.133.gain_ref, bf16[256,1024]{1,0:T(8,128)(2,1)} %w_exp_ref.5), custom_call_target="tpu_custom_call" | custom-call | flops 15399999488 | bytes 50400000 | tf_op jit(solution)/shard_map/expand/pallas_call | solution.py:113
  24.6 0.9 fusion.12
  25.6 2.2 collective-permute-start.3
  27.8 1.3 collective-permute-start.2
  29.2 2.8 %collective-permute-done.2 = bf16[20,2,256]{2,0,1:T(8,128)(2,1)S(1)} collective-permute-done((bf16[20,2,256]{2,0,1:T(8,128)(2,1)S(1)}, bf16[20,2,256]{2,0,1:T(8,128)(2,1)S(1)}, u32[]{:S(2)}, u32[]{:S(2)}) %collective-permute-start.2) | collective-permute-done | bytes 20512 | tf_op jit(solution)/shard_map/ppermute | solution.py:819
  32.8 8.9 %depthwise.1 = (bf16[416,1024]{1,0:T(8,128)(2,1)}, bf16[16,64,1024]{2,1,0:T(8,128)(2,1)}, f32[32,1,1024]{2,1,0:T(1,128)}) custom-call(bf16[2,64,256]{2,1,0:T(8,128)(2,1)} %copy-done.19, bf16[2,64,256]{2,1,0:T(8,128)(2,1)} %copy-done.20, bf16[160,256]{1,0:T(8,128)(2,1)} %maximum_bitcast_fusion.side_ref, bf16[1,256]{1,0:T(2,128)(2,1)} %reshape.133.gain_ref, ...), custom_call_target="tpu_custom_call" | custom-call | flops 1100000000 | bytes 3600000 | tf_op jit(solution)/shard_map/depthwise/pallas_call | solution.py:205
  41.7 6.8 %all-to-all-start = ((f32[32,1,1024]{2,1,0:T(1,128)}), f32[32,1,1024]{2,1,0:T(1,128)S(1)}, u32[]{:S(2)}, u32[]{:S(2)}) async-start(f32[32,1,1024]{2,1,0:T(1,128)} %get-tuple-element.63), calls=%async_computation | async-start | bytes 262144 | tf_op jit(solution)/shard_map/all_to_all | solution.py:837
  48.5 0.8 copy.59.w_sq_ref
  50.7 0.8 pad_maximum_fusion.2.bias_ref
  51.5 1.1 copy.58
  52.6 4.1 %all-to-all-done.parts_ref = f32[32,1,1024]{2,1,0:T(1,128)S(1)} async-done(((f32[32,1,1024]{2,1,0:T(1,128)}), f32[32,1,1024]{2,1,0:T(1,128)S(1)}, u32[]{:S(2)}, u32[]{:S(2)}) %all-to-all-start) | async-done | bytes 131104 | tf_op jit(solution)/shard_map/all_to_all | solution.py:837
  57.3 5.4 %mix.1 = (f32[1,1024]{1,0:T(1,128)}, f32[1,64]{1,0:T(1,128)}, f32[1,1024]{1,0:T(1,128)}, bf16[16,64,256]{2,1,0:T(8,128)(2,1)}, bf16[32,2,16,256]{3,2,1,0:T(8,128)(2,1)}) custom-call(f32[32,1,1024]{2,1,0:T(1,128)} %copy-done.13, bf16[1024,64]{1,0:T(8,128)(2,1)} %copy.59.w_sq_ref, bf16[64,1024]{1,0:T(8,128)(2,1)} %w_ex_ref.3, ...), custom_call_target="tpu_custom_call" | custom-call | flops 5500000256 | bytes 18000000 | tf_op jit(solution)/shard_map/mix/pallas_call | solution.py:324
  62.8 2.6 %all-to-all-start.2 = ((bf16[32,2,16,256]{3,2,1,0:T(8,128)(2,1)}), bf16[32,2,16,256]{3,2,1,0:T(8,128)(2,1)S(1)}, u32[]{:S(2)}, u32[]{:S(2)}) async-start(bf16[32,2,16,256]{3,2,1,0:T(8,128)(2,1)} %get-tuple-element.66), calls=%async_computation.2 | async-start | bytes 1048576 | tf_op jit(solution)/shard_map/all_to_all | solution.py:955
  65.4 10.5 %slope.1 = (bf16[18,64,1024]{2,1,0:T(8,128)(2,1)}, f32[18,8,1024]{2,1,0:T(8,128)}) custom-call(f32[4]{0:T(128)} %add_convert_fusion.flags_ref, bf16[416,1024]{1,0:T(8,128)(2,1)} %get-tuple-element.67.ring_ref, bf16[3,3,1024]{2,1,0:T(4,128)(2,1)} %w_dep_ref.5, bf16[16,64,1024]{2,1,0:T(8,128)(2,1)} %get-tuple-element.62.spread_ref), custom_call_target="tpu_custom_call" | custom-call | flops 14300000256 | bytes 46800000 | tf_op jit(solution)/shard_map/slope/pallas_call | solution.py:265
  75.9 1.1 convolution_convert_fusion.att_grad_ref
  77.0 4.7 %all-to-all-done.2 = bf16[32,2,16,256]{3,2,1,0:T(8,128)(2,1)S(1)} async-done(((bf16[32,2,16,256]{3,2,1,0:T(8,128)(2,1)}), bf16[32,2,16,256]{3,2,1,0:T(8,128)(2,1)S(1)}, u32[]{:S(2)}, u32[]{:S(2)}) %all-to-all-start.2) | async-done | bytes 524320 | tf_op jit(solution)/shard_map/all_to_all | solution.py:955
  82.5 11.8 %attention.1 = (bf16[1024,256]{1,0:T(8,128)(2,1)}, bf16[1024,256]{1,0:T(8,128)(2,1)}, bf16[1024,256]{1,0:T(8,128)(2,1)}, bf16[1024,768]{1,0:T(8,128)(2,1)}, f32[2,256,64]{2,1,0:T(8,128)}) custom-call(bf16[1024,256]{1,0:T(8,128)(2,1)} %bitcast.130, bf16[1024,256]{1,0:T(8,128)(2,1)} %convolution_convert_fusion.att_grad_ref, bf16[256,768]{1,0:T(8,128)(2,1)} %w_qkv_ref.1, ...), custom_call_target="tpu_custom_call" | custom-call | flops 15399999488 | bytes 50400000 | tf_op jit(solution)/shard_map/attention/pallas_call | solution.py:461
  94.4 2.7 %all-to-all-start.3 = ((bf16[32,2,16,256]{3,2,1,0:T(8,128)(2,1)}), bf16[32,2,16,256]{3,2,1,0:T(8,128)(2,1)S(1)}, u32[]{:S(2)}, u32[]{:S(2)}) async-start(bf16[32,2,16,256]{3,2,1,0:T(8,128)(2,1)} %bitcast.128), calls=%async_computation.3 | async-start | bytes 1048576 | tf_op jit(solution)/shard_map/all_to_all | solution.py:955
  97.1 1.0 copy.62
  99.2 3.5 %attention_weights.1 = bf16[256,1152]{1,0:T(8,128)(2,1)} custom-call(bf16[1024,256]{1,0:T(8,128)(2,1)} %get-tuple-element.73.x_ref, bf16[1024,768]{1,0:T(8,128)(2,1)} %get-tuple-element.74.packed_grad_ref, bf16[1024,256]{1,0:T(8,128)(2,1)} %get-tuple-element.71.att_ref, bf16[1024,256]{1,0:T(8,128)(2,1)} %bitcast.113, f32[2,256,64]{2,1,0:T(8,128)} %get-tuple-element.75.bias_ref), custom_call_target="tpu_custom_call" | custom-call | flops 5500000256 | bytes 18000000 | tf_op jit(solution)/shard_map/attention_weights/pallas_call | solution.py:499
  102.7 10.8 %all-to-all-done.3.recv_ref = bf16[32,2,16,256]{3,2,1,0:T(8,128)(2,1)S(1)} async-done(((bf16[32,2,16,256]{3,2,1,0:T(8,128)(2,1)}), bf16[32,2,16,256]{3,2,1,0:T(8,128)(2,1)S(1)}, u32[]{:S(2)}, u32[]{:S(2)}) %all-to-all-start.3) | async-done | bytes 524320 | tf_op jit(solution)/shard_map/all_to_all | solution.py:955
  114.3 6.7 %mixed_back.1 = (f32[16,64,256]{2,1,0:T(8,128)}, bf16[16,64,256]{2,1,0:T(8,128)(2,1)}, f32[1,256]{1,0:T(1,128)}, bf16[256,1024]{1,0:T(8,128)(2,1)}, bf16[32,8,25...) custom-call(bf16[32,2,16,256]{3,2,1,0:T(8,128)(2,1)} %copy-done.6, ...), custom_call_target="tpu_custom_call" | custom-call | flops 7699999744 | bytes 25200000 | tf_op jit(solution)/shard_map/mixed_back/pallas_call | solution.py:567
  121.8 1.5 collective-permute-start.4
  123.3 1.3 collective-permute-start.5
  124.6 1.2 pad_maximum_fusion
  126.0 1.0 collective-permute-start.10
  127.0 2.5 %collective-permute-done.5.down_ref = bf16[1,64,256]{2,1,0:T(8,128)(2,1)S(1)} collective-permute-done((bf16[1,64,256]{2,1,0:T(8,128)(2,1)S(1)}, bf16[1,64,256]{2,1,0:T(8,128)(2,1)S(1)}, u32[]{:S(2)}, u32[]{:S(2)}) %collective-permute-start.5) | collective-permute-done | bytes 32800 | tf_op jit(solution)/shard_map/ppermute | solution.py:819
  129.5 1.4 collective-permute-start.7
  130.9 1.3 collective-permute-start.6
  132.2 0.9 pad_maximum_fusion.1
  133.1 6.7 %all-to-all-start.4 = ((bf16[32,40,256]{2,1,0:T(8,128)(2,1)}), bf16[32,40,256]{2,1,0:T(8,128)(2,1)S(1)}, u32[]{:S(2)}, u32[]{:S(2)}) async-start(bf16[32,40,256]{2,1,0:T(8,128)(2,1)} %pad_maximum_fusion.1), calls=%async_computation.4 | async-start | bytes 1310720 | tf_op jit(solution)/shard_map/all_to_all | solution.py:837
  140.1 2.5 %collective-permute-start.13 = (bf16[32,2176]{1,0:T(8,128)(2,1)S(1)}, bf16[32,2176]{1,0:T(8,128)(2,1)S(1)}, u32[]{:S(2)}, u32[]{:S(2)}) collective-permute-start(bf16[32,2176]{1,0:T(8,128)(2,1)S(1)} %get-tuple-element.107), channel_id=1, source_target_pairs={{0,24},{8,0},{16,8},{24,16},{1,25},{9,1},{17,9},{25,17},{2,26},{10... | collective-permute-start | bytes 417800 | tf_op jit(solution)/shard_map/ppermute | solution.py:849
  144.4 6.3 %collective-permute-done.13 = bf16[32,2176]{1,0:T(8,128)(2,1)S(1)} collective-permute-done((bf16[32,2176]{1,0:T(8,128)(2,1)S(1)}, bf16[32,2176]{1,0:T(8,128)(2,1)S(1)}, u32[]{:S(2)}, u32[]{:S(2)}) %collective-permute-start.13) | collective-permute-done | bytes 139296 | tf_op jit(solution)/shard_map/ppermute | solution.py:849
  150.8 5.1 %collective-permute-done.11 = bf16[32,2176]{1,0:T(8,128)(2,1)S(1)} collective-permute-done((bf16[32,2176]{1,0:T(8,128)(2,1)S(1)}, bf16[32,2176]{1,0:T(8,128)(2,1)S(1)}, u32[]{:S(2)}, u32[]{:S(2)}) %collective-permute-start.11) | collective-permute-done | bytes 139296 | tf_op jit(solution)/shard_map/ppermute | solution.py:849
  156.0 2.8 %all-to-all-done.4.parts_ref = bf16[32,40,256]{2,1,0:T(8,128)(2,1)S(1)} async-done(((bf16[32,40,256]{2,1,0:T(8,128)(2,1)}), bf16[32,40,256]{2,1,0:T(8,128)(2,1)S(1)}, u32[]{:S(2)}, u32[]{:S(2)}) %all-to-all-start.4) | async-done | bytes 655392 | tf_op jit(solution)/shard_map/all_to_all | solution.py:837
  158.8 0.8 copy-done.1
  159.6 16.3 %expand_back.1 = (bf16[256,1152]{1,0:T(8,128)(2,1)}, f32[1024,256]{1,0:T(8,128)}, f32[1,1024]{1,0:T(1,128)}, f32[1,64]{1,0:T(1,128)}) custom-call(bf16[32,40,256]{2,1,0:T(8,128)(2,1)} %copy-done.1, f32[1,64]{1,0:T(1,128)} %get-tuple-element.79.hidden_ref, f32[1,1024]{1,0:T(1,128)} %get-tuple-element.77.gate_ref.gate_all_ref, ...), custom_call_target="tpu_custom_call" | custom-call | flops 15399999488 | bytes 50400000 | tf_op jit(solution)/shard_map/expand_back/pallas_call | solution.py:751
  176.0 1.2 collective-permute-start.16
  177.2 0.9 collective-permute-start.14
  178.1 1.0 dynamic-slice_bitcast_fusion.1
  180.0 2.1 collective-permute-done.15
  182.0 0.9 collective-permute-done.14
  183.1 1.9 collective-permute-start.18
  185.0 2.1 collective-permute-start.19
  187.1 1.8 fusion.3
  188.8 3.9 %all-to-all-start.5 = ((bf16[16,8,1152]{2,1,0:T(8,128)(2,1)}), bf16[16,8,1152]{2,1,0:T(8,128)(2,1)S(1)}, u32[]{:S(2)}, u32[]{:S(2)}) async-start(bf16[16,8,1152]{2,1,0:T(8,128)(2,1)} %fusion.3), calls=%async_computation.5 | async-start | bytes 589824 | tf_op jit(solution)/shard_map/all_to_all | solution.py:870
  194.0 1.5 stack.35
  195.5 1.9 collective-permute-start.20
  197.4 1.5 collective-permute-start.21
  198.9 1.5 collective-permute-start.22
  200.3 4.1 %image_back.1 = bf16[1024,256]{1,0:T(8,128)(2,1)} custom-call(bf16[1024,256]{1,0:T(8,128)(2,1)} %bitcast.134, bf16[1,256]{1,0:T(2,128)(2,1)} %reshape.133.gain_ref, f32[1024,256]{1,0:T(8,128)} %get-tuple-element.88.first_ref, f32[1024,256]{1,0:T(8,128)} %bitcast.146), custom_call_target="tpu_custom_call" | custom-call | flops 4400000000 | bytes 14400000 | tf_op jit(solution)/shard_map/image_back/pallas_call | solution.py:804
  205.2 4.6 %all-to-all-start.6 = ((bf16[16,8,1152]{2,1,0:T(8,128)(2,1)}), bf16[16,8,1152]{2,1,0:T(8,128)(2,1)S(1)}, u32[]{:S(2)}, u32[]{:S(2)}) async-start(bf16[16,8,1152]{2,1,0:T(8,128)(2,1)} %broadcast_in_dim.17), calls=%async_computation.6 | async-start | bytes 589824 | tf_op jit(solution)/shard_map/all_to_all | solution.py:870
  211.3 1.9 stack.36
  214.5 1.1 fusion
  215.6 3.6 %all-to-all-done.6 = bf16[16,8,1152]{2,1,0:T(8,128)(2,1)S(1)} async-done(((bf16[16,8,1152]{2,1,0:T(8,128)(2,1)}), bf16[16,8,1152]{2,1,0:T(8,128)(2,1)S(1)}, u32[]{:S(2)}, u32[]{:S(2)}) %all-to-all-start.6) | async-done | bytes 294944 | tf_op jit(solution)/shard_map/all_to_all | solution.py:870
  219.2 0.8 broadcast_multiply_fusion
  220.1 0.8 copy-done.23
  220.9 2.8 %unpack_weights.1 = (f32[32,8,768]{2,1,0:T(8,128)}, f32[32,8,256]{2,1,0:T(8,128)}, f32[2,32,8,64]{3,2,1,0:T(8,128)}, f32[4,32,8,256]{3,2,1,0:T(8,128)}) custom-call(s32[3]{0:T(128)} %pad_add_fusion.places_ref, bf16[16,8,2176]{2,1,0:T(8,128)(2,1)} %bitcast.141, bf16[16,8,2176]{2,1,0:T(8,128)(2,1)} %copy-done.23), custom_call_target="tpu_custom_call" | custom-call | flops 2200000000 | bytes 7200000 | tf_op jit(solution)/shard_map/unpack_weights/pallas_call | solution.py:931
  224.4 2.1 unpack.1
  (139 shorter events, 15.5 us)
Async XLA Ops:
  0.6 75.3 %copy-start = (bf16[256,256]{1,0:T(8,128)(2,1)S(1)}, bf16[256,256]{1,0:T(8,128)(2,1)}, u32[]{:S(2)}) copy-start(bf16[256,256]{1,0:T(8,128)(2,1)} %param.22) | copy-start | bytes 393220
  0.7 16.0 %copy-start.31 = (bf16[256]{0:T(256)(128)(2,1)S(1)}, bf16[256]{0:T(256)(128)(2,1)}, u32[]{:S(2)}) copy-start(bf16[256]{0:T(256)(128)(2,1)} %param.14) | copy-start | bytes 1540
  1.6 23.9 %collective-permute-start = (bf16[2,64,256]{2,1,0:T(8,128)(2,1)S(1)}, bf16[2,64,256]{2,1,0:T(8,128)(2,1)S(1)}, u32[]{:S(2)}, u32[]{:S(2)}) collective-permute-start(bf16[2,64,256]{2,1,0:T(8,128)(2,1)S(1)} %get-tuple-element.112), channel_id=1, source_target_pairs={{0,8},{8,16},{16,24},{1,9},{9,17},{17,25},{2,10},{10,18},{18,26},{... | collective-permute-start | bytes 196616 | tf_op jit(solution)/shard_map/ppermute | solution.py:819
  6.4 19.1 %collective-permute-start.1 = (bf16[2,64,256]{2,1,0:T(8,128)(2,1)S(1)}, bf16[2,64,256]{2,1,0:T(8,128)(2,1)S(1)}, u32[]{:S(2)}, u32[]{:S(2)}) collective-permute-start(bf16[2,64,256]{2,1,0:T(8,128)(2,1)S(1)} %get-tuple-element.111), channel_id=1, source_target_pairs={{8,0},{16,8},{24,16},{9,1},{17,9},{25,17},{10,2},{18,10},{26,18},{... | collective-permute-start | bytes 196616 | tf_op jit(solution)/shard_map/ppermute | solution.py:819
  9.6 32.1 %all-to-all-start.1 = ((bf16[32,2,16,256]{3,2,1,0:T(8,128)(2,1)}), bf16[32,2,16,256]{3,2,1,0:T(8,128)(2,1)S(1)}, u32[]{:S(2)}, u32[]{:S(2)}) async-start(bf16[32,2,16,256]{3,2,1,0:T(8,128)(2,1)} %bitcast.3), calls=%async_computation.1 | async-start | bytes 1048576 | tf_op jit(solution)/shard_map/all_to_all | solution.py:955
  25.5 7.3 %copy-start.19 = (bf16[2,64,256]{2,1,0:T(8,128)(2,1)}, bf16[2,64,256]{2,1,0:T(8,128)(2,1)S(1)}, u32[]{:S(2)}) copy-start(bf16[2,64,256]{2,1,0:T(8,128)(2,1)S(1)} %collective-permute-done.up_ref) | copy-start | bytes 196612
  25.5 7.3 %copy-start.20 = (bf16[2,64,256]{2,1,0:T(8,128)(2,1)}, bf16[2,64,256]{2,1,0:T(8,128)(2,1)S(1)}, u32[]{:S(2)}) copy-start(bf16[2,64,256]{2,1,0:T(8,128)(2,1)S(1)} %collective-permute-done.1.down_ref) | copy-start | bytes 196612
  25.6 3.6 %collective-permute-start.3 = (bf16[20,2,256]{2,0,1:T(8,128)(2,1)S(1)}, bf16[20,2,256]{2,0,1:T(8,128)(2,1)S(1)}, u32[]{:S(2)}, u32[]{:S(2)}) collective-permute-start(bf16[20,2,256]{2,0,1:T(8,128)(2,1)S(1)} %pad_maximum_fusion.4), channel_id=1, source_target_pairs={{0,1},{1,2},{2,3},{3,4},{4,5},{5,6},{6,7},{8,9},{9,10},{10,11},{11... | collective-permute-start | bytes 61448 | tf_op jit(solution)/shard_map/ppermute | solution.py:819
  27.8 4.2 %collective-permute-start.2 = (bf16[20,2,256]{2,0,1:T(8,128)(2,1)S(1)}, bf16[20,2,256]{2,0,1:T(8,128)(2,1)S(1)}, u32[]{:S(2)}, u32[]{:S(2)}) collective-permute-start(bf16[20,2,256]{2,0,1:T(8,128)(2,1)S(1)} %pad_maximum_fusion.3), channel_id=1, source_target_pairs={{1,0},{2,1},{3,2},{4,3},{5,4},{6,5},{7,6},{9,8},{10,9},{11,10},{12... | collective-permute-start | bytes 61448 | tf_op jit(solution)/shard_map/ppermute | solution.py:819
  32.8 15.7 %copy-start.11 = (bf16[1024,64]{0,1:T(8,128)(2,1)S(1)}, bf16[1024,64]{0,1:T(8,128)(2,1)}, u32[]{:S(2)}) copy-start(bf16[1024,64]{0,1:T(8,128)(2,1)} %param.17) | copy-start | bytes 393220
  32.8 16.6 %copy-start.32 = (bf16[256]{0:T(256)(128)(2,1)S(1)}, bf16[256]{0:T(256)(128)(2,1)}, u32[]{:S(2)}) copy-start(bf16[256]{0:T(256)(128)(2,1)} %param.20) | copy-start | bytes 1540
  32.8 17.1 %copy-start.10 = (f32[8,64,64]{2,1,0:T(8,128)S(1)}, f32[8,64,64]{2,1,0:T(8,128)}, u32[]{:S(2)}) copy-start(f32[8,64,64]{2,1,0:T(8,128)} %param.23) | copy-start | bytes 393220
  41.7 15.0 %all-to-all-start = ((f32[32,1,1024]{2,1,0:T(1,128)}), f32[32,1,1024]{2,1,0:T(1,128)S(1)}, u32[]{:S(2)}, u32[]{:S(2)}) async-start(f32[32,1,1024]{2,1,0:T(1,128)} %get-tuple-element.63), calls=%async_computation | async-start | bytes 262144 | tf_op jit(solution)/shard_map/all_to_all | solution.py:837
  56.7 0.7 copy-start.13
  62.8 19.0 %all-to-all-start.2 = ((bf16[32,2,16,256]{3,2,1,0:T(8,128)(2,1)}), bf16[32,2,16,256]{3,2,1,0:T(8,128)(2,1)S(1)}, u32[]{:S(2)}, u32[]{:S(2)}) async-start(bf16[32,2,16,256]{3,2,1,0:T(8,128)(2,1)} %get-tuple-element.66), calls=%async_computation.2 | async-start | bytes 1048576 | tf_op jit(solution)/shard_map/all_to_all | solution.py:955
  65.4 10.5 %copy-start.2 = (bf16[16,4,2,8,256]{4,3,2,1,0:T(8,128)(2,1)S(1)}, bf16[16,4,2,8,256]{4,3,2,1,0:T(8,128)(2,1)}, u32[]{:S(2)}) copy-start(bf16[16,4,2,8,256]{4,3,2,1,0:T(8,128)(2,1)} %copy.58) | copy-start | bytes 1572868
  81.8 0.8 copy-start.8
  94.4 2.8 %copy-start.4 = (bf16[1024,256]{1,0:T(8,128)(2,1)S(1)}, bf16[1024,256]{1,0:T(8,128)(2,1)}, u32[]{:S(2)}) copy-start(bf16[1024,256]{1,0:T(8,128)(2,1)} %w_proj_ref.1) | copy-start | bytes 1572868
  94.4 4.6 %copy-start.7 = (bf16[1024,256]{1,0:T(8,128)(2,1)S(1)}, bf16[1024,256]{1,0:T(8,128)(2,1)}, u32[]{:S(2)}) copy-start(bf16[1024,256]{1,0:T(8,128)(2,1)} %get-tuple-element.71.att_ref) | copy-start | bytes 1572868
  94.4 19.1 %all-to-all-start.3 = ((bf16[32,2,16,256]{3,2,1,0:T(8,128)(2,1)}), bf16[32,2,16,256]{3,2,1,0:T(8,128)(2,1)S(1)}, u32[]{:S(2)}, u32[]{:S(2)}) async-start(bf16[32,2,16,256]{3,2,1,0:T(8,128)(2,1)} %bitcast.128), calls=%async_computation.3 | async-start | bytes 1048576 | tf_op jit(solution)/shard_map/all_to_all | solution.py:955
  113.5 0.8 copy-start.6
  114.3 10.3 %copy-start.3 = (bf16[256,1152]{1,0:T(8,128)(2,1)S(1)}, bf16[256,1152]{1,0:T(8,128)(2,1)}, u32[]{:S(2)}) copy-start(bf16[256,1152]{1,0:T(8,128)(2,1)} %attention_weights.1) | copy-start | bytes 1769476
  121.0 4.8 %copy-start.15 = (bf16[2,16,1,256]{3,2,1,0:T(2,128)(2,1)S(1)}, bf16[2,16,1,256]{3,2,1,0:T(2,128)(2,1)}, u32[]{:S(2)}) copy-start(bf16[2,16,1,256]{3,2,1,0:T(2,128)(2,1)} %get-tuple-element.82) | copy-start | bytes 49156
  121.8 4.1 %collective-permute-start.4 = (bf16[1,64,256]{2,1,0:T(8,128)(2,1)S(1)}, bf16[1,64,256]{2,1,0:T(8,128)(2,1)S(1)}, u32[]{:S(2)}, u32[]{:S(2)}) collective-permute-start(bf16[1,64,256]{2,1,0:T(8,128)(2,1)S(1)} %get-tuple-element.117), channel_id=1, source_target_pairs={{0,8},{8,16},{16,24},{1,9},{9,17},{17,25},{2,10},{10,18},{18,26},{... | collective-permute-start | bytes 98312 | tf_op jit(solution)/shard_map/ppermute | solution.py:819
  123.3 6.2 %collective-permute-start.5 = (bf16[1,64,256]{2,1,0:T(8,128)(2,1)S(1)}, bf16[1,64,256]{2,1,0:T(8,128)(2,1)S(1)}, u32[]{:S(2)}, u32[]{:S(2)}) collective-permute-start(bf16[1,64,256]{2,1,0:T(8,128)(2,1)S(1)} %get-tuple-element.116), channel_id=1, source_target_pairs={{8,0},{16,8},{24,16},{9,1},{17,9},{25,17},{10,2},{18,10},{26,18},{... | collective-permute-start | bytes 98312 | tf_op jit(solution)/shard_map/ppermute | solution.py:819
  124.6 7.6 %copy-start.12 = (bf16[32,8,256]{2,1,0:T(8,128)(2,1)S(1)}, bf16[32,8,256]{2,1,0:T(8,128)(2,1)}, u32[]{:S(2)}) copy-start(bf16[32,8,256]{2,1,0:T(8,128)(2,1)} %get-tuple-element.78) | copy-start | bytes 393220
  125.9 7.2 %copy-start.21 = (bf16[1,64,256]{2,1,0:T(8,128)(2,1)}, bf16[1,64,256]{2,1,0:T(8,128)(2,1)S(1)}, u32[]{:S(2)}) copy-start(bf16[1,64,256]{2,1,0:T(8,128)(2,1)S(1)} %collective-permute-done.4.up_ref) | copy-start | bytes 98308
  126.0 13.9 %collective-permute-start.10 = (bf16[128,2176]{1,0:T(8,128)(2,1)S(1)}, bf16[128,2176]{1,0:T(8,128)(2,1)S(1)}, u32[]{:S(2)}, u32[]{:S(2)}) collective-permute-start(bf16[128,2176]{1,0:T(8,128)(2,1)S(1)} %dynamic-slice_bitcast_fusion), channel_id=1, source_target_pairs={{0,1},{1,0},{2,3},{3,2},{4,5},{5,4},{6,7},{7,6},{8,9},{9,8},{10,11... | collective-permute-start | bytes 1671176 | tf_op jit(solution)/shard_map/ppermute | solution.py:849
  129.5 3.6 %copy-start.22 = (bf16[1,64,256]{2,1,0:T(8,128)(2,1)}, bf16[1,64,256]{2,1,0:T(8,128)(2,1)S(1)}, u32[]{:S(2)}) copy-start(bf16[1,64,256]{2,1,0:T(8,128)(2,1)S(1)} %collective-permute-done.5.down_ref) | copy-start | bytes 98308
  129.5 10.3 %collective-permute-start.7 = (bf16[18,1,256]{2,0,1:T(8,128)(2,1)S(1)}, bf16[18,1,256]{2,0,1:T(8,128)(2,1)S(1)}, u32[]{:S(2)}, u32[]{:S(2)}) collective-permute-start(bf16[18,1,256]{2,0,1:T(8,128)(2,1)S(1)} %pad_maximum_fusion.6), channel_id=1, source_target_pairs={{0,1},{1,2},{2,3},{3,4},{4,5},{5,6},{6,7},{8,9},{9,10},{10,11},{11... | collective-permute-start | bytes 27656 | tf_op jit(solution)/shard_map/ppermute | solution.py:819
  130.9 8.9 %collective-permute-start.6 = (bf16[18,1,256]{2,0,1:T(8,128)(2,1)S(1)}, bf16[18,1,256]{2,0,1:T(8,128)(2,1)S(1)}, u32[]{:S(2)}, u32[]{:S(2)}) collective-permute-start(bf16[18,1,256]{2,0,1:T(8,128)(2,1)S(1)} %pad_maximum_fusion.5), channel_id=1, source_target_pairs={{1,0},{2,1},{3,2},{4,3},{5,4},{6,5},{7,6},{9,8},{10,9},{11,10},{12... | collective-permute-start | bytes 27656 | tf_op jit(solution)/shard_map/ppermute | solution.py:819
  133.1 25.7 %all-to-all-start.4 = ((bf16[32,40,256]{2,1,0:T(8,128)(2,1)}), bf16[32,40,256]{2,1,0:T(8,128)(2,1)S(1)}, u32[]{:S(2)}, u32[]{:S(2)}) async-start(bf16[32,40,256]{2,1,0:T(8,128)(2,1)} %pad_maximum_fusion.1), calls=%async_computation.4 | async-start | bytes 1310720 | tf_op jit(solution)/shard_map/all_to_all | solution.py:837
  140.1 10.7 %collective-permute-start.13 = (bf16[32,2176]{1,0:T(8,128)(2,1)S(1)}, bf16[32,2176]{1,0:T(8,128)(2,1)S(1)}, u32[]{:S(2)}, u32[]{:S(2)}) collective-permute-start(bf16[32,2176]{1,0:T(8,128)(2,1)S(1)} %get-tuple-element.107), channel_id=1, source_target_pairs={{0,24},{8,0},{16,8},{24,16},{1,25},{9,1},{17,9},{25,17},{2,26},{10... | collective-permute-start | bytes 417800 | tf_op jit(solution)/shard_map/ppermute | solution.py:849
  142.6 8.1 %collective-permute-start.12 = (bf16[32,2176]{1,0:T(8,128)(2,1)S(1)}, bf16[32,2176]{1,0:T(8,128)(2,1)S(1)}, u32[]{:S(2)}, u32[]{:S(2)}) collective-permute-start(bf16[32,2176]{1,0:T(8,128)(2,1)S(1)} %get-tuple-element.108), channel_id=1, source_target_pairs={{0,16},{8,24},{16,0},{24,8},{1,17},{9,25},{17,1},{25,9},{2,18},{10... | collective-permute-start | bytes 417800 | tf_op jit(solution)/shard_map/ppermute | solution.py:849
  143.2 12.7 %collective-permute-start.11 = (bf16[32,2176]{1,0:T(8,128)(2,1)S(1)}, bf16[32,2176]{1,0:T(8,128)(2,1)S(1)}, u32[]{:S(2)}, u32[]{:S(2)}) collective-permute-start(bf16[32,2176]{1,0:T(8,128)(2,1)S(1)} %get-tuple-element.106), channel_id=1, source_target_pairs={{0,8},{8,16},{16,24},{24,0},{1,9},{9,17},{17,25},{25,1},{2,10},{10... | collective-permute-start | bytes 417800 | tf_op jit(solution)/shard_map/ppermute | solution.py:849
  158.8 0.8 copy-start.1
  175.9 16.8 %copy-start.33 = (f32[1,64]{1,0:T(1,128)S(1)}, f32[1,64]{1,0:T(1,128)}, u32[]{:S(2)}) copy-start(f32[1,64]{1,0:T(1,128)} %get-tuple-element.79.hidden_ref) | copy-start | bytes 772
  176.0 4.0 %collective-permute-start.16 = (bf16[8,2176]{1,0:T(8,128)(2,1)S(1)}, bf16[8,2176]{1,0:T(8,128)(2,1)S(1)}, u32[]{:S(2)}, u32[]{:S(2)}) collective-permute-start(bf16[8,2176]{1,0:T(8,128)(2,1)S(1)} %get-tuple-element.114), channel_id=1, source_target_pairs={{0,6},{1,7},{2,0},{3,1},{4,2},{5,3},{6,4},{7,5},{8,14},{9,15},{10,... | collective-permute-start | bytes 104456 | tf_op jit(solution)/shard_map/ppermute | solution.py:849
  177.2 4.8 %collective-permute-start.15 = (bf16[8,2176]{1,0:T(8,128)(2,1)S(1)}, bf16[8,2176]{1,0:T(8,128)(2,1)S(1)}, u32[]{:S(2)}, u32[]{:S(2)}) collective-permute-start(bf16[8,2176]{1,0:T(8,128)(2,1)S(1)} %get-tuple-element.115), channel_id=1, source_target_pairs={{0,4},{1,5},{2,6},{3,7},{4,0},{5,1},{6,2},{7,3},{8,12},{9,13},{10,... | collective-permute-start | bytes 104456 | tf_op jit(solution)/shard_map/ppermute | solution.py:849
  177.2 5.7 %collective-permute-start.14 = (bf16[8,2176]{1,0:T(8,128)(2,1)S(1)}, bf16[8,2176]{1,0:T(8,128)(2,1)S(1)}, u32[]{:S(2)}, u32[]{:S(2)}) collective-permute-start(bf16[8,2176]{1,0:T(8,128)(2,1)S(1)} %get-tuple-element.113), channel_id=1, source_target_pairs={{0,2},{1,3},{2,4},{3,5},{4,6},{5,7},{6,0},{7,1},{8,10},{9,11},{10,... | collective-permute-start | bytes 104456 | tf_op jit(solution)/shard_map/ppermute | solution.py:849
  179.1 8.0 %collective-permute-start.8 = (bf16[128,1152]{1,0:T(8,128)(2,1)S(1)}, bf16[128,1152]{1,0:T(8,128)(2,1)S(1)}, u32[]{:S(2)}, u32[]{:S(2)}) collective-permute-start(bf16[128,1152]{1,0:T(8,128)(2,1)S(1)} %dynamic-slice_bitcast_fusion.1), channel_id=1, source_target_pairs={{0,1},{1,0},{2,3},{3,2},{4,5},{5,4},{6,7},{7,6},{8,9},{9,8},{10,11... | collective-permute-start | bytes 884744 | tf_op jit(solution)/shard_map/ppermute | solution.py:849
  183.0 9.8 %copy-start.14 = (bf16[1,8,2176]{2,1,0:T(8,128)(2,1)}, bf16[1,8,2176]{2,1,0:T(8,128)(2,1)S(1)}, u32[]{:S(2)}) copy-start(bf16[1,8,2176]{2,1,0:T(8,128)(2,1)S(1)} %fusion.10.refs_0_) | copy-start | bytes 104452
  183.0 9.8 %collective-permute-start.17 = (bf16[1,8,2176]{2,1,0:T(8,128)(2,1)S(1)}, bf16[1,8,2176]{2,1,0:T(8,128)(2,1)S(1)}, u32[]{:S(2)}, u32[]{:S(2)}) collective-permute-start(bf16[1,8,2176]{2,1,0:T(8,128)(2,1)S(1)} %fusion.10.refs_0_), channel_id=1, source_target_pairs={{0,2},{1,3},{2,4},{3,5},{4,6},{5,7},{6,0},{7,1},{8,10},{9,11},{10,... | collective-permute-start | bytes 104456 | tf_op jit(solution)/shard_map/ppermute | solution.py:849
  183.1 9.7 %collective-permute-start.18 = (bf16[1,8,2176]{2,1,0:T(8,128)(2,1)S(1)}, bf16[1,8,2176]{2,1,0:T(8,128)(2,1)S(1)}, u32[]{:S(2)}, u32[]{:S(2)}) collective-permute-start(bf16[1,8,2176]{2,1,0:T(8,128)(2,1)S(1)} %fusion.10.refs_0_), channel_id=1, source_target_pairs={{0,4},{1,5},{2,6},{3,7},{4,0},{5,1},{6,2},{7,3},{8,12},{9,13},{10,... | collective-permute-start | bytes 104456 | tf_op jit(solution)/shard_map/ppermute | solution.py:849
  185.0 7.8 %collective-permute-start.19 = (bf16[1,8,2176]{2,1,0:T(8,128)(2,1)S(1)}, bf16[1,8,2176]{2,1,0:T(8,128)(2,1)S(1)}, u32[]{:S(2)}, u32[]{:S(2)}) collective-permute-start(bf16[1,8,2176]{2,1,0:T(8,128)(2,1)S(1)} %fusion.10.refs_0_), channel_id=1, source_target_pairs={{0,6},{1,7},{2,0},{3,1},{4,2},{5,3},{6,4},{7,5},{8,14},{9,15},{10,... | collective-permute-start | bytes 104456 | tf_op jit(solution)/shard_map/ppermute | solution.py:849
  188.8 15.6 %all-to-all-start.5 = ((bf16[16,8,1152]{2,1,0:T(8,128)(2,1)}), bf16[16,8,1152]{2,1,0:T(8,128)(2,1)S(1)}, u32[]{:S(2)}, u32[]{:S(2)}) async-start(bf16[16,8,1152]{2,1,0:T(8,128)(2,1)} %fusion.3), calls=%async_computation.5 | async-start | bytes 589824 | tf_op jit(solution)/shard_map/all_to_all | solution.py:870
  192.7 0.6 copy-start.28
  195.5 14.4 %collective-permute-start.20 = (bf16[4,8,2176]{2,1,0:T(8,128)(2,1)}, bf16[4,8,2176]{2,1,0:T(8,128)(2,1)S(1)}, u32[]{:S(2)}, u32[]{:S(2)}) collective-permute-start(bf16[4,8,2176]{2,1,0:T(8,128)(2,1)} %bitcast.142), channel_id=1, source_target_pairs={{0,8},{8,16},{16,24},{24,0},{1,9},{9,17},{17,25},{25,1},{2,10},{10... | collective-permute-start | bytes 417800 | tf_op jit(solution)/shard_map/ppermute | solution.py:849
  197.4 12.5 %collective-permute-start.21 = (bf16[4,8,2176]{2,1,0:T(8,128)(2,1)}, bf16[4,8,2176]{2,1,0:T(8,128)(2,1)S(1)}, u32[]{:S(2)}, u32[]{:S(2)}) collective-permute-start(bf16[4,8,2176]{2,1,0:T(8,128)(2,1)} %bitcast.143), channel_id=1, source_target_pairs={{0,16},{8,24},{16,0},{24,8},{1,17},{9,25},{17,1},{25,9},{2,18},{10... | collective-permute-start | bytes 417800 | tf_op jit(solution)/shard_map/ppermute | solution.py:849
  198.9 11.1 %collective-permute-start.22 = (bf16[4,8,2176]{2,1,0:T(8,128)(2,1)}, bf16[4,8,2176]{2,1,0:T(8,128)(2,1)S(1)}, u32[]{:S(2)}, u32[]{:S(2)}) collective-permute-start(bf16[4,8,2176]{2,1,0:T(8,128)(2,1)} %bitcast.144), channel_id=1, source_target_pairs={{0,24},{8,0},{16,8},{24,16},{1,25},{9,1},{17,9},{25,17},{2,26},{10... | collective-permute-start | bytes 417800 | tf_op jit(solution)/shard_map/ppermute | solution.py:849
  205.2 14.0 %all-to-all-start.6 = ((bf16[16,8,1152]{2,1,0:T(8,128)(2,1)}), bf16[16,8,1152]{2,1,0:T(8,128)(2,1)S(1)}, u32[]{:S(2)}, u32[]{:S(2)}) async-start(bf16[16,8,1152]{2,1,0:T(8,128)(2,1)} %broadcast_in_dim.17), calls=%async_computation.6 | async-start | bytes 589824 | tf_op jit(solution)/shard_map/all_to_all | solution.py:870
  209.9 3.4 %copy-start.16 = (f32[1,1024]{1,0:T(1,128)S(1)}, f32[1,1024]{1,0:T(1,128)}, u32[]{:S(2)}) copy-start(f32[1,1024]{1,0:T(1,128)} %get-tuple-element.94) | copy-start | bytes 12292
  209.9 3.4 %copy-start.18 = (f32[1,64]{1,0:T(1,128)S(1)}, f32[1,64]{1,0:T(1,128)}, u32[]{:S(2)}) copy-start(f32[1,64]{1,0:T(1,128)} %get-tuple-element.95) | copy-start | bytes 772
  209.9 0.7 copy-start.25
  209.9 0.7 copy-start.26
  210.6 0.7 copy-start.27
  213.2 1.1 slice-start
  213.2 1.3 copy-start.5
  213.2 6.8 %collective-permute-start.23 = (bf16[16,8,2176]{2,1,0:T(8,128)(2,1)}, bf16[16,8,2176]{2,1,0:T(8,128)(2,1)S(1)}, u32[]{:S(2)}, u32[]{:S(2)}) collective-permute-start(bf16[16,8,2176]{2,1,0:T(8,128)(2,1)} %bitcast.140), channel_id=1, source_target_pairs={{0,1},{1,0},{2,3},{3,2},{4,5},{5,4},{6,7},{7,6},{8,9},{9,8},{10,11... | collective-permute-start | bytes 1671176 | tf_op jit(solution)/shard_map/ppermute | solution.py:849
  214.3 4.9 %copy-start.17 = (f32[1,1024]{1,0:T(1,128)S(1)}, f32[1,1024]{1,0:T(1,128)}, u32[]{:S(2)}) copy-start(f32[1,1024]{1,0:T(1,128)} %get-tuple-element.96) | copy-start | bytes 12292
  219.2 4.4 %copy-start.9 = (bf16[16,8,1152]{2,1,0:T(8,128)(2,1)}, bf16[16,8,1152]{2,1,0:T(8,128)(2,1)S(1)}, u32[]{:S(2)}) copy-start(bf16[16,8,1152]{2,1,0:T(8,128)(2,1)S(1)} %all-to-all-done.6) | copy-start | bytes 884740
  219.2 4.4 %collective-permute-start.9 = (bf16[128,1152]{1,0:T(8,128)(2,1)S(1)}, bf16[128,1152]{1,0:T(8,128)(2,1)S(1)}, u32[]{:S(2)}, u32[]{:S(2)}) collective-permute-start(bf16[128,1152]{1,0:T(8,128)(2,1)S(1)} %bitcast.131), channel_id=1, source_target_pairs={{0,1},{1,0},{2,3},{3,2},{4,5},{5,4},{6,7},{7,6},{8,9},{9,8},{10,11... | collective-permute-start | bytes 884744 | tf_op jit(solution)/shard_map/ppermute | solution.py:849
  220.1 0.8 copy-start.23
  223.7 0.7 copy-start.24
  (2 other events, 1.2 us)

commit v2 on v1

--- a/solution.py
+++ b/solution.py
@@ -646,7 +646,7 @@
     low_ref, up_ref, down_ref, side_ref, w_projt_ref, gate_ref, slope_ref, side_slope_ref,
     spread_slope_ref, spread_ref, w_dep_ref, turned_ref, w_exp_ref, gain_ref, norm1_ref,
     weights_ref, first_ref, logit_ref, pre_ref,
-    main_ref, side_grad_ref, window_ref, expanded_ref, pool_ref, tail_ref, norm_ref,
+    main_ref, side_grad_ref, window_ref, expanded_ref, pool_ref, tail_ref, norm_ref, weights_sum_ref,
 ):
     rows, cols, channels = low_ref.shape
     side = 8
@@ -678,15 +678,14 @@
         norm_ref[...] = jnp.zeros(norm_ref.shape, F32)
 
     w_projt = w_projt_ref[...]
-    main_ref[pl.ds(0, cols), :] = dot(up_ref[0], w_projt)
-    main_ref[pl.ds(cols, rows * cols), :] = dot(
-        low_ref[...].reshape(rows * cols, channels), w_projt
-    )
-    main_ref[pl.ds((rows + 1) * cols, cols), :] = dot(down_ref[0], w_projt)
-    side_grad_ref[...] = dot(side_ref[...], w_projt)
-
-    @pl.loop(0, rows + 2, unroll=3)
-    def _(i):
+    w_exp = w_exp_ref[...]
+    two = 2 * cols
+
+    def gate_rows(p):
+        at = pl.ds(pl.multiple_of(cols + p * two, 16), two)
+        main_ref[at, :] = dot(low_ref[pl.ds(2 * p, 2)].reshape(two, channels), w_projt)
+
+    def window_row(i):
         for h in range(BLOCK // LANES):
             lanes = slice(h * LANES, (h + 1) * LANES)
             gate = gate_ref[:, lanes]
@@ -700,34 +699,64 @@
             window_ref[1, i, :, lanes] = grad[:cols]
             window_ref[2, i, :, lanes] = pltpu.roll(grad, 1, 0)[:cols]
 
+    side_grad_ref[...] = dot(side_ref[...], w_projt)
+    main_ref[pl.ds(0, cols), :] = dot(up_ref[0], w_projt)
+    main_ref[pl.ds((rows + 1) * cols, cols), :] = dot(down_ref[0], w_projt)
+    gate_rows(0)
+    window_row(0)
+    window_row(rows + 1)
+
+    @pl.loop(0, rows // 2 - 1)
+    def _(p):
+        window_row(2 * p + 1)
+        window_row(2 * p + 2)
+        gate_rows(p + 1)
+
+    window_row(rows - 1)
+    window_row(rows)
+
+    weights_sum_ref[...] = jnp.zeros(weights_sum_ref.shape, F32)
+
+    def back_rows(p, sums):
+        sums = list(sums)
+        for r in range(2):
+            i = 2 * p + r
+            for h in range(BLOCK // LANES):
+                lanes = slice(h * LANES, (h + 1) * LANES)
+                taps = w_dep_ref[:, :, lanes].astype(F32)
+                spread = spread_ref[i, :, lanes].astype(F32)
+                total = jnp.zeros((cols, LANES), F32)
+                for a in range(3):
+                    for b in range(3):
+                        window = window_ref[b, i + 2 - a, :, lanes]
+                        total = total + window * taps[a, b : b + 1]
+                        sums[h * 9 + a * 3 + b] += fold_rows(window * spread)
+                grad = total * spread_slope_ref[i, :, lanes].astype(F32)
+                at = pl.ds(pl.multiple_of(i * cols, 16), cols)
+                expanded_ref[at, lanes] = grad.astype(BF16)
+        return tuple(sums)
+
+    def use_rows(p):
+        at = pl.ds(pl.multiple_of(p * two, LANES), two)
+        grad = expanded_ref[at, :]
+        first_ref[at, :] += dot(grad, w_exp, ((1,), (1,)))
+        weights_sum_ref[...] += dot(turned_ref[:, at], grad)
+
+    def back_step(p, sums):
+        use_rows(p - 1)
+        return back_rows(p, sums)
+
+    sums = back_rows(0, (jnp.zeros((8, LANES), F32),) * (9 * BLOCK // LANES))
+    sums = lax.fori_loop(1, rows // 2, back_step, sums)
+    use_rows(rows // 2 - 1)
     for h in range(BLOCK // LANES):
-        lanes = slice(h * LANES, (h + 1) * LANES)
-        taps = w_dep_ref[:, :, lanes].astype(F32)
-
-        def back_row(i, sums):
-            spread = spread_ref[i, :, lanes].astype(F32)
-            total = jnp.zeros((cols, LANES), F32)
-            new_sums = []
-            for a in range(3):
-                for b in range(3):
-                    window = window_ref[b, i + 2 - a, :, lanes]
-                    total = total + window * taps[a, b : b + 1]
-                    new_sums.append(sums[a * 3 + b] + fold_rows(window * spread))
-            grad = total * spread_slope_ref[i, :, lanes].astype(F32)
-            expanded_ref[pl.ds(pl.multiple_of(i * cols, 16), cols), lanes] = grad.astype(BF16)
-            return tuple(new_sums)
-
-        sums = lax.fori_loop(0, rows, back_row, (jnp.zeros((8, LANES), F32),) * 9, unroll=2)
         for t in range(9):
             row = t * (steps * BLOCK // LANES) + step * (BLOCK // LANES) + h
-            tail_ref[pl.ds(row, 1), :] = jnp.sum(sums[t], axis=0, keepdims=True)
-
-    grad_expanded = expanded_ref[...]
-    w_exp = w_exp_ref[...]
-    weights = dot(turned_ref[...], grad_expanded)
+            tail_ref[pl.ds(row, 1), :] = jnp.sum(sums[h * 9 + t], axis=0, keepdims=True)
+
+    weights = weights_sum_ref[...]
     weights_ref[:, pl.ds(pl.multiple_of(step * BLOCK, BLOCK), BLOCK)] = weights.astype(BF16)
     norm_ref[...] += jnp.sum(weights * w_exp.astype(F32), axis=1, keepdims=True)
-    first_ref[...] += dot(grad_expanded, w_exp, ((1,), (1,)))
 
     @pl.when(step == steps - 1)
     def _():
@@ -781,6 +810,7 @@
             pltpu.VMEM((steps, 1, BLOCK), F32),
             pltpu.VMEM((channels, LANES), F32),
             pltpu.VMEM((channels, LANES), F32),
+            pltpu.VMEM((channels, BLOCK), F32),
         ],
         compiler_params=PARAMS,
         cost_estimate=estimate(14),
@@ -1030,11 +1060,12 @@
         parts = hand_around(gate_grad)
         attended_home = swap_groups(attended_sent, parity)
     up, down = halo_rows(edge_lines[:1], edge_lines[1:])
+    edge_sides, parts = lax.optimization_barrier((edge_sides, parts))
     side = halo_sides(edge_sides[0], edge_sides[1], up, down)
     weights = jnp.concatenate([weights, grad_project], axis=1)
     weights, _ = lax.optimization_barrier((weights, up))
     steps = sum_steps()
-    for step in steps[:2]:
+    for step in steps:
         weights = sum_parts(weights, *step)
     late, grad_first, logit, pre = run_expand_back(
         cells_total, parts, hidden, gate, w_squeeze, w_excite, grad_low, up, down, side,
@@ -1042,7 +1073,6 @@
         gain_first, grad_norm1,
     )
     weights, _ = lax.optimization_barrier((weights, late))
-    weights = sum_parts(weights, *steps[2])
     weights = weights[None]
     for step in steps[:0:-1]:
         weights = join_parts(weights, *step)

time: 228 us -> 235 us (1.031)
  Pallas kernels: 82.9 us -> 90.3 us
    ppermute x16, waiting for transfers between devices: 15.2 us -> 4.7 us  [send_on(): return lax.ppermute(v, axis, pairs)]
    pallas_call x1, Pallas kernels: 16.3 us -> 23.8 us  [run_expand_back(): pl.pallas_call(functools.partial(expand_back_kernel, cells_total), grid=(...]
    all_to_all x2, waiting for transfers between devices: 6.9 us -> 12.7 us  [hand_around(): return lax.all_to_all(blocks, AXES, split_axis=0, concat_axis=0, tiled=True)]
    ppermute x8, waiting for transfers between devices: 5.31 us -> 10.1 us  [shift(): return lax.ppermute(cells, axis, pairs)]
    ppermute x16, starting transfers between devices: 15.9 us -> 19.4 us  [send_on(): return lax.ppermute(v, axis, pairs)]
    all_to_all x2, starting transfers between devices: 13.5 us -> 11.1 us  [hand_around(): return lax.all_to_all(blocks, AXES, split_axis=0, concat_axis=0, tiled=True)]
  transfers between devices with their start and end apart: 31 -> 31, of which waited for: 12 -> 11; matrix products, arithmetic and copies ran while one was open for 9% -> 8% of each run, Pallas kernels for 18% -> 17%
where the time goes in v2:
time: 235 us; the launch traced here: 233 us
  Pallas kernels  90.3 us (38%)
  starting transfers between devices  67.2 us (29%)
  waiting for transfers between devices  44.4 us (19%)
  local copies, waits for them, and re-layouts  18.4 us (8%)
  other arithmetic  9.3 us (4%)
    pallas_call x1, Pallas kernels, run_expand_back(): pl.pallas_call(functools.partial(expand_back_kernel, cells_total), grid=(...  23.8 us
    ppermute x16, starting transfers between devices, send_on(): return lax.ppermute(v, axis, pairs)  19.4 us
    all_to_all x3, waiting for transfers between devices, swap_groups(): lax.all_to_all(blocks, AXES, split_axis=0, concat_axis=0, tiled=True, axi...  15.5 us
    ppermute x8, starting transfers between devices, shift(): return lax.ppermute(cells, axis, pairs)  15.3 us
    all_to_all x2, waiting for transfers between devices, hand_around(): return lax.all_to_all(blocks, AXES, split_axis=0, concat_axis=0, tiled=True)  12.7 us
    all_to_all x3, starting transfers between devices, swap_groups(): lax.all_to_all(blocks, AXES, split_axis=0, concat_axis=0, tiled=True, axi...  12.4 us
    pallas_call x1, Pallas kernels, run_attention(): pl.pallas_call(functools.partial(attention_kernel, members, heads, lines)...  11.8 us
    all_to_all x2, starting transfers between devices, hand_around(): return lax.all_to_all(blocks, AXES, split_axis=0, concat_axis=0, tiled=True)  11.1 us
  transfers between devices with their start and end apart: 31, of which 11 were waited for; matrix products, arithmetic and copies ran while one was open for 8% of the time, Pallas kernels for 17%

profile of v2, /device:TPU:0, one launch (start us, length us, event | category | flops | bytes accessed | tf_op | source)
XLA Modules:
  0.0 233.2 jit_solution(14281973570293245395)
XLA Ops:
  0.7 0.9 fusion.13
  1.6 4.8 %collective-permute-start = (bf16[2,64,256]{2,1,0:T(8,128)(2,1)S(1)}, bf16[2,64,256]{2,1,0:T(8,128)(2,1)S(1)}, u32[]{:S(2)}, u32[]{:S(2)}) collective-permute-start(bf16[2,64,256]{2,1,0:T(8,128)(2,1)S(1)} %get-tuple-element.116), channel_id=1, source_target_pairs={{0,8},{8,16},{16,24},{1,9},{9,17},{17,25},{2,10},{10,18},{18,26},{... | collective-permute-start | bytes 196616 | tf_op jit(solution)/shard_map/ppermute | solution.py:849
  6.4 1.3 collective-permute-start.1
  7.7 1.9 copy.57
  9.6 7.0 %all-to-all-start.1 = ((bf16[32,2,16,256]{3,2,1,0:T(8,128)(2,1)}), bf16[32,2,16,256]{3,2,1,0:T(8,128)(2,1)S(1)}, u32[]{:S(2)}, u32[]{:S(2)}) async-start(bf16[32,2,16,256]{3,2,1,0:T(8,128)(2,1)} %bitcast.3), calls=%async_computation.1 | async-start | bytes 1048576 | tf_op jit(solution)/shard_map/all_to_all | solution.py:985
  17.2 7.3 %expand.1 = (bf16[1024,256]{1,0:T(8,128)(2,1)}, bf16[256,1024]{1,0:T(8,128)(2,1)}, bf16[16,64,1024]{2,1,0:T(8,128)(2,1)}, bf16[16,64,1024]{2,1,0:T(8,128)(2,1)}) custom-call(bf16[16,64,256]{2,1,0:T(8,128)(2,1)} %image_ref.3, bf16[1,256]{1,0:T(2,128)(2,1)} %reshape.133.gain_ref, bf16[256,1024]{1,0:T(8,128)(2,1)} %w_exp_ref.5), custom_call_target="tpu_custom_call" | custom-call | flops 15399999488 | bytes 50400000 | tf_op jit(solution)/shard_map/expand/pallas_call | solution.py:113
  24.6 0.9 fusion.12
  25.6 2.2 collective-permute-start.3
  27.8 1.3 collective-permute-start.2
  29.2 2.8 %collective-permute-done.2 = bf16[20,2,256]{2,0,1:T(8,128)(2,1)S(1)} collective-permute-done((bf16[20,2,256]{2,0,1:T(8,128)(2,1)S(1)}, bf16[20,2,256]{2,0,1:T(8,128)(2,1)S(1)}, u32[]{:S(2)}, u32[]{:S(2)}) %collective-permute-start.2) | collective-permute-done | bytes 20512 | tf_op jit(solution)/shard_map/ppermute | solution.py:849
  32.8 8.9 %depthwise.1 = (bf16[416,1024]{1,0:T(8,128)(2,1)}, bf16[16,64,1024]{2,1,0:T(8,128)(2,1)}, f32[32,1,1024]{2,1,0:T(1,128)}) custom-call(bf16[2,64,256]{2,1,0:T(8,128)(2,1)} %copy-done.19, bf16[2,64,256]{2,1,0:T(8,128)(2,1)} %copy-done.20, bf16[160,256]{1,0:T(8,128)(2,1)} %maximum_bitcast_fusion.side_ref, bf16[1,256]{1,0:T(2,128)(2,1)} %reshape.133.gain_ref, ...), custom_call_target="tpu_custom_call" | custom-call | flops 1100000000 | bytes 3600000 | tf_op jit(solution)/shard_map/depthwise/pallas_call | solution.py:205
  41.7 6.8 %all-to-all-start = ((f32[32,1,1024]{2,1,0:T(1,128)}), f32[32,1,1024]{2,1,0:T(1,128)S(1)}, u32[]{:S(2)}, u32[]{:S(2)}) async-start(f32[32,1,1024]{2,1,0:T(1,128)} %get-tuple-element.65), calls=%async_computation | async-start | bytes 262144 | tf_op jit(solution)/shard_map/all_to_all | solution.py:867
  48.5 0.8 copy.59.w_sq_ref
  50.7 0.8 pad_maximum_fusion.2.bias_ref
  51.5 1.1 copy.58
  52.6 4.1 %all-to-all-done.parts_ref = f32[32,1,1024]{2,1,0:T(1,128)S(1)} async-done(((f32[32,1,1024]{2,1,0:T(1,128)}), f32[32,1,1024]{2,1,0:T(1,128)S(1)}, u32[]{:S(2)}, u32[]{:S(2)}) %all-to-all-start) | async-done | bytes 131104 | tf_op jit(solution)/shard_map/all_to_all | solution.py:867
  57.3 5.4 %mix.1 = (f32[1,1024]{1,0:T(1,128)}, f32[1,64]{1,0:T(1,128)}, f32[1,1024]{1,0:T(1,128)}, bf16[16,64,256]{2,1,0:T(8,128)(2,1)}, bf16[32,2,16,256]{3,2,1,0:T(8,128)(2,1)}) custom-call(f32[32,1,1024]{2,1,0:T(1,128)} %copy-done.13, bf16[1024,64]{1,0:T(8,128)(2,1)} %copy.59.w_sq_ref, bf16[64,1024]{1,0:T(8,128)(2,1)} %w_ex_ref.3, ...), custom_call_target="tpu_custom_call" | custom-call | flops 5500000256 | bytes 18000000 | tf_op jit(solution)/shard_map/mix/pallas_call | solution.py:324
  62.8 2.6 %all-to-all-start.2 = ((bf16[32,2,16,256]{3,2,1,0:T(8,128)(2,1)}), bf16[32,2,16,256]{3,2,1,0:T(8,128)(2,1)S(1)}, u32[]{:S(2)}, u32[]{:S(2)}) async-start(bf16[32,2,16,256]{3,2,1,0:T(8,128)(2,1)} %get-tuple-element.68), calls=%async_computation.2 | async-start | bytes 1048576 | tf_op jit(solution)/shard_map/all_to_all | solution.py:985
  65.4 10.5 %slope.1 = (bf16[18,64,1024]{2,1,0:T(8,128)(2,1)}, f32[18,8,1024]{2,1,0:T(8,128)}) custom-call(f32[4]{0:T(128)} %add_convert_fusion.flags_ref, bf16[416,1024]{1,0:T(8,128)(2,1)} %get-tuple-element.69.ring_ref, bf16[3,3,1024]{2,1,0:T(4,128)(2,1)} %w_dep_ref.5, bf16[16,64,1024]{2,1,0:T(8,128)(2,1)} %get-tuple-element.64.spread_ref), custom_call_target="tpu_custom_call" | custom-call | flops 14300000256 | bytes 46800000 | tf_op jit(solution)/shard_map/slope/pallas_call | solution.py:265
  75.9 1.1 convolution_convert_fusion.att_grad_ref
  77.0 4.7 %all-to-all-done.2 = bf16[32,2,16,256]{3,2,1,0:T(8,128)(2,1)S(1)} async-done(((bf16[32,2,16,256]{3,2,1,0:T(8,128)(2,1)}), bf16[32,2,16,256]{3,2,1,0:T(8,128)(2,1)S(1)}, u32[]{:S(2)}, u32[]{:S(2)}) %all-to-all-start.2) | async-done | bytes 524320 | tf_op jit(solution)/shard_map/all_to_all | solution.py:985
  82.5 11.8 %attention.1 = (bf16[1024,256]{1,0:T(8,128)(2,1)}, bf16[1024,256]{1,0:T(8,128)(2,1)}, bf16[1024,256]{1,0:T(8,128)(2,1)}, bf16[1024,768]{1,0:T(8,128)(2,1)}, f32[2,256,64]{2,1,0:T(8,128)}) custom-call(bf16[1024,256]{1,0:T(8,128)(2,1)} %bitcast.128, bf16[1024,256]{1,0:T(8,128)(2,1)} %convolution_convert_fusion.att_grad_ref, bf16[256,768]{1,0:T(8,128)(2,1)} %w_qkv_ref.1, ...), custom_call_target="tpu_custom_call" | custom-call | flops 15399999488 | bytes 50400000 | tf_op jit(solution)/shard_map/attention/pallas_call | solution.py:461
  94.4 2.8 %all-to-all-start.3 = ((bf16[32,2,16,256]{3,2,1,0:T(8,128)(2,1)}), bf16[32,2,16,256]{3,2,1,0:T(8,128)(2,1)S(1)}, u32[]{:S(2)}, u32[]{:S(2)}) async-start(bf16[32,2,16,256]{3,2,1,0:T(8,128)(2,1)} %bitcast.126), calls=%async_computation.3 | async-start | bytes 1048576 | tf_op jit(solution)/shard_map/all_to_all | solution.py:985
  97.2 1.0 copy.62
  99.3 3.4 %attention_weights.1 = bf16[256,1152]{1,0:T(8,128)(2,1)} custom-call(bf16[1024,256]{1,0:T(8,128)(2,1)} %get-tuple-element.75.x_ref, bf16[1024,768]{1,0:T(8,128)(2,1)} %get-tuple-element.76.packed_grad_ref, bf16[1024,256]{1,0:T(8,128)(2,1)} %get-tuple-element.73.att_ref, bf16[1024,256]{1,0:T(8,128)(2,1)} %bitcast.113, f32[2,256,64]{2,1,0:T(8,128)} %get-tuple-element.77.bias_ref), custom_call_target="tpu_custom_call" | custom-call | flops 5500000256 | bytes 18000000 | tf_op jit(solution)/shard_map/attention_weights/pallas_call | solution.py:499
  102.7 10.8 %all-to-all-done.3.recv_ref = bf16[32,2,16,256]{3,2,1,0:T(8,128)(2,1)S(1)} async-done(((bf16[32,2,16,256]{3,2,1,0:T(8,128)(2,1)}), bf16[32,2,16,256]{3,2,1,0:T(8,128)(2,1)S(1)}, u32[]{:S(2)}, u32[]{:S(2)}) %all-to-all-start.3) | async-done | bytes 524320 | tf_op jit(solution)/shard_map/all_to_all | solution.py:985
  114.3 6.7 %mixed_back.1 = (f32[16,64,256]{2,1,0:T(8,128)}, bf16[16,64,256]{2,1,0:T(8,128)(2,1)}, f32[1,256]{1,0:T(1,128)}, bf16[256,1024]{1,0:T(8,128)(2,1)}, bf16[32,8,25...) custom-call(bf16[32,2,16,256]{3,2,1,0:T(8,128)(2,1)} %copy-done.6, ...), custom_call_target="tpu_custom_call" | custom-call | flops 7699999744 | bytes 25200000 | tf_op jit(solution)/shard_map/mixed_back/pallas_call | solution.py:567
  121.8 1.5 collective-permute-start.4
  123.3 1.2 pad_maximum_fusion
  124.9 0.8 dynamic-slice_bitcast_fusion
  126.3 0.9 pad_maximum_fusion.1
  127.2 4.3 %all-to-all-start.4 = ((bf16[32,40,256]{2,1,0:T(8,128)(2,1)}), bf16[32,40,256]{2,1,0:T(8,128)(2,1)S(1)}, u32[]{:S(2)}, u32[]{:S(2)}) async-start(bf16[32,40,256]{2,1,0:T(8,128)(2,1)} %pad_maximum_fusion.1), calls=%async_computation.4 | async-start | bytes 1310720 | tf_op jit(solution)/shard_map/all_to_all | solution.py:867
  131.5 1.3 collective-permute-start.5
  132.9 5.3 %collective-permute-done.5.down_ref = bf16[1,64,256]{2,1,0:T(8,128)(2,1)S(1)} collective-permute-done((bf16[1,64,256]{2,1,0:T(8,128)(2,1)S(1)}, bf16[1,64,256]{2,1,0:T(8,128)(2,1)S(1)}, u32[]{:S(2)}, u32[]{:S(2)}) %collective-permute-start.5) | collective-permute-done | bytes 32800 | tf_op jit(solution)/shard_map/ppermute | solution.py:849
  138.8 3.3 %collective-permute-start.12 = (bf16[32,2176]{1,0:T(8,128)(2,1)S(1)}, bf16[32,2176]{1,0:T(8,128)(2,1)S(1)}, u32[]{:S(2)}, u32[]{:S(2)}) collective-permute-start(bf16[32,2176]{1,0:T(8,128)(2,1)S(1)} %get-tuple-element.112), channel_id=1, source_target_pairs={{0,16},{8,24},{16,0},{24,8},{1,17},{9,25},{17,1},{25,9},{2,18},{10... | collective-permute-start | bytes 417800 | tf_op jit(solution)/shard_map/ppermute | solution.py:879
  142.1 8.6 %all-to-all-done.4.parts_ref = bf16[32,40,256]{2,1,0:T(8,128)(2,1)S(1)} async-done(((bf16[32,40,256]{2,1,0:T(8,128)(2,1)}), bf16[32,40,256]{2,1,0:T(8,128)(2,1)S(1)}, u32[]{:S(2)}, u32[]{:S(2)}) %all-to-all-start.4) | async-done | bytes 655392 | tf_op jit(solution)/shard_map/all_to_all | solution.py:867
  150.8 1.7 collective-permute-start.7
  152.5 1.3 collective-permute-start.6
  153.9 1.6 collective-permute-done.6
  156.3 23.8 %expand_back.1 = (bf16[256,1152]{1,0:T(8,128)(2,1)}, f32[1024,256]{1,0:T(8,128)}, f32[1,1024]{1,0:T(1,128)}, f32[1,64]{1,0:T(1,128)}) custom-call(bf16[32,40,256]{2,1,0:T(8,128)(2,1)} %copy-done.1, f32[1,64]{1,0:T(1,128)} %get-tuple-element.83.hidden_ref, f32[1,1024]{1,0:T(1,128)} %get-tuple-element.79.gate_ref.gate_all_ref, ...), custom_call_target="tpu_custom_call" | custom-call | flops 15399999488 | bytes 50400000 | tf_op jit(solution)/shard_map/expand_back/pallas_call | solution.py:780
  180.0 1.0 dynamic-slice_bitcast_fusion.1
  181.0 2.0 collective-permute-start.8
  183.3 1.6 collective-permute-start.15
  184.9 1.0 collective-permute-start.14
  185.9 1.7 fusion.3
  187.7 5.4 %all-to-all-start.5 = ((bf16[16,8,1152]{2,1,0:T(8,128)(2,1)}), bf16[16,8,1152]{2,1,0:T(8,128)(2,1)S(1)}, u32[]{:S(2)}, u32[]{:S(2)}) async-start(bf16[16,8,1152]{2,1,0:T(8,128)(2,1)} %fusion.3), calls=%async_computation.5 | async-start | bytes 589824 | tf_op jit(solution)/shard_map/all_to_all | solution.py:900
  193.2 2.0 collective-permute-start.17
  195.2 2.4 %collective-permute-start.18 = (bf16[1,8,2176]{2,1,0:T(8,128)(2,1)S(1)}, bf16[1,8,2176]{2,1,0:T(8,128)(2,1)S(1)}, u32[]{:S(2)}, u32[]{:S(2)}) collective-permute-start(bf16[1,8,2176]{2,1,0:T(8,128)(2,1)S(1)} %bitcast.134), channel_id=1, source_target_pairs={{0,4},{1,5},{2,6},{3,7},{4,0},{5,1},{6,2},{7,3},{8,12},{9,13},{10,... | collective-permute-start | bytes 104456 | tf_op jit(solution)/shard_map/ppermute | solution.py:879
  197.6 1.5 collective-permute-start.19
  199.0 1.1 fusion
  200.1 2.9 %collective-permute-done.17.refs_1_ = bf16[1,8,2176]{2,1,0:T(8,128)(2,1)S(1)} collective-permute-done((bf16[1,8,2176]{2,1,0:T(8,128)(2,1)S(1)}, bf16[1,8,2176]{2,1,0:T(8,128)(2,1)S(1)}, u32[]{:S(2)}, u32[]{:S(2)}) %collective-permute-start.17) | collective-permute-done | bytes 34848 | tf_op jit(solution)/shard_map/ppermute | solution.py:879
  203.0 1.8 collective-permute-done.18.refs_2_
  206.0 1.5 stack.35
  207.5 1.5 collective-permute-start.20
  209.0 1.5 collective-permute-start.21
  210.4 1.5 collective-permute-start.22
  212.7 3.5 %all-to-all-start.6 = ((bf16[16,8,1152]{2,1,0:T(8,128)(2,1)}), bf16[16,8,1152]{2,1,0:T(8,128)(2,1)S(1)}, u32[]{:S(2)}, u32[]{:S(2)}) async-start(bf16[16,8,1152]{2,1,0:T(8,128)(2,1)} %broadcast_in_dim.17), calls=%async_computation.6 | async-start | bytes 589824 | tf_op jit(solution)/shard_map/all_to_all | solution.py:900
  218.4 2.0 stack.36
  220.4 4.1 %image_back.1 = bf16[1024,256]{1,0:T(8,128)(2,1)} custom-call(bf16[1024,256]{1,0:T(8,128)(2,1)} %bitcast.132, bf16[1,256]{1,0:T(2,128)(2,1)} %reshape.133.gain_ref, f32[1024,256]{1,0:T(8,128)} %get-tuple-element.92.first_ref, f32[1024,256]{1,0:T(8,128)} %bitcast.148), custom_call_target="tpu_custom_call" | custom-call | flops 4400000000 | bytes 14400000 | tf_op jit(solution)/shard_map/image_back/pallas_call | solution.py:834
  224.5 1.4 all-to-all-done.6
  225.9 0.8 broadcast_multiply_fusion
  226.8 0.8 copy-done.23
  227.6 2.8 %unpack_weights.1 = (f32[32,8,768]{2,1,0:T(8,128)}, f32[32,8,256]{2,1,0:T(8,128)}, f32[2,32,8,64]{3,2,1,0:T(8,128)}, f32[4,32,8,256]{3,2,1,0:T(8,128)}) custom-call(s32[3]{0:T(128)} %pad_add_fusion.places_ref, bf16[16,8,2176]{2,1,0:T(8,128)(2,1)} %bitcast.143, bf16[16,8,2176]{2,1,0:T(8,128)(2,1)} %copy-done.23), custom_call_target="tpu_custom_call" | custom-call | flops 2200000000 | bytes 7200000 | tf_op jit(solution)/shard_map/unpack_weights/pallas_call | solution.py:961
  231.1 2.1 unpack.1
  (139 shorter events, 14.6 us)
Async XLA Ops:
  0.6 75.3 %copy-start = (bf16[256,256]{1,0:T(8,128)(2,1)S(1)}, bf16[256,256]{1,0:T(8,128)(2,1)}, u32[]{:S(2)}) copy-start(bf16[256,256]{1,0:T(8,128)(2,1)} %param.22) | copy-start | bytes 393220
  0.7 16.0 %copy-start.31 = (bf16[256]{0:T(256)(128)(2,1)S(1)}, bf16[256]{0:T(256)(128)(2,1)}, u32[]{:S(2)}) copy-start(bf16[256]{0:T(256)(128)(2,1)} %param.14) | copy-start | bytes 1540
  1.6 23.9 %collective-permute-start = (bf16[2,64,256]{2,1,0:T(8,128)(2,1)S(1)}, bf16[2,64,256]{2,1,0:T(8,128)(2,1)S(1)}, u32[]{:S(2)}, u32[]{:S(2)}) collective-permute-start(bf16[2,64,256]{2,1,0:T(8,128)(2,1)S(1)} %get-tuple-element.116), channel_id=1, source_target_pairs={{0,8},{8,16},{16,24},{1,9},{9,17},{17,25},{2,10},{10,18},{18,26},{... | collective-permute-start | bytes 196616 | tf_op jit(solution)/shard_map/ppermute | solution.py:849
  6.4 19.1 %collective-permute-start.1 = (bf16[2,64,256]{2,1,0:T(8,128)(2,1)S(1)}, bf16[2,64,256]{2,1,0:T(8,128)(2,1)S(1)}, u32[]{:S(2)}, u32[]{:S(2)}) collective-permute-start(bf16[2,64,256]{2,1,0:T(8,128)(2,1)S(1)} %get-tuple-element.115), channel_id=1, source_target_pairs={{8,0},{16,8},{24,16},{9,1},{17,9},{25,17},{10,2},{18,10},{26,18},{... | collective-permute-start | bytes 196616 | tf_op jit(solution)/shard_map/ppermute | solution.py:849
  9.6 32.1 %all-to-all-start.1 = ((bf16[32,2,16,256]{3,2,1,0:T(8,128)(2,1)}), bf16[32,2,16,256]{3,2,1,0:T(8,128)(2,1)S(1)}, u32[]{:S(2)}, u32[]{:S(2)}) async-start(bf16[32,2,16,256]{3,2,1,0:T(8,128)(2,1)} %bitcast.3), calls=%async_computation.1 | async-start | bytes 1048576 | tf_op jit(solution)/shard_map/all_to_all | solution.py:985
  25.5 7.3 %copy-start.19 = (bf16[2,64,256]{2,1,0:T(8,128)(2,1)}, bf16[2,64,256]{2,1,0:T(8,128)(2,1)S(1)}, u32[]{:S(2)}) copy-start(bf16[2,64,256]{2,1,0:T(8,128)(2,1)S(1)} %collective-permute-done.up_ref) | copy-start | bytes 196612
  25.5 7.3 %copy-start.20 = (bf16[2,64,256]{2,1,0:T(8,128)(2,1)}, bf16[2,64,256]{2,1,0:T(8,128)(2,1)S(1)}, u32[]{:S(2)}) copy-start(bf16[2,64,256]{2,1,0:T(8,128)(2,1)S(1)} %collective-permute-done.1.down_ref) | copy-start | bytes 196612
  25.6 3.6 %collective-permute-start.3 = (bf16[20,2,256]{2,0,1:T(8,128)(2,1)S(1)}, bf16[20,2,256]{2,0,1:T(8,128)(2,1)S(1)}, u32[]{:S(2)}, u32[]{:S(2)}) collective-permute-start(bf16[20,2,256]{2,0,1:T(8,128)(2,1)S(1)} %pad_maximum_fusion.4), channel_id=1, source_target_pairs={{0,1},{1,2},{2,3},{3,4},{4,5},{5,6},{6,7},{8,9},{9,10},{10,11},{11... | collective-permute-start | bytes 61448 | tf_op jit(solution)/shard_map/ppermute | solution.py:849
  27.8 4.2 %collective-permute-start.2 = (bf16[20,2,256]{2,0,1:T(8,128)(2,1)S(1)}, bf16[20,2,256]{2,0,1:T(8,128)(2,1)S(1)}, u32[]{:S(2)}, u32[]{:S(2)}) collective-permute-start(bf16[20,2,256]{2,0,1:T(8,128)(2,1)S(1)} %pad_maximum_fusion.3), channel_id=1, source_target_pairs={{1,0},{2,1},{3,2},{4,3},{5,4},{6,5},{7,6},{9,8},{10,9},{11,10},{12... | collective-permute-start | bytes 61448 | tf_op jit(solution)/shard_map/ppermute | solution.py:849
  32.8 15.7 %copy-start.11 = (bf16[1024,64]{0,1:T(8,128)(2,1)S(1)}, bf16[1024,64]{0,1:T(8,128)(2,1)}, u32[]{:S(2)}) copy-start(bf16[1024,64]{0,1:T(8,128)(2,1)} %param.17) | copy-start | bytes 393220
  32.8 16.6 %copy-start.32 = (bf16[256]{0:T(256)(128)(2,1)S(1)}, bf16[256]{0:T(256)(128)(2,1)}, u32[]{:S(2)}) copy-start(bf16[256]{0:T(256)(128)(2,1)} %param.20) | copy-start | bytes 1540
  32.8 17.1 %copy-start.10 = (f32[8,64,64]{2,1,0:T(8,128)S(1)}, f32[8,64,64]{2,1,0:T(8,128)}, u32[]{:S(2)}) copy-start(f32[8,64,64]{2,1,0:T(8,128)} %param.23) | copy-start | bytes 393220
  41.7 15.0 %all-to-all-start = ((f32[32,1,1024]{2,1,0:T(1,128)}), f32[32,1,1024]{2,1,0:T(1,128)S(1)}, u32[]{:S(2)}, u32[]{:S(2)}) async-start(f32[32,1,1024]{2,1,0:T(1,128)} %get-tuple-element.65), calls=%async_computation | async-start | bytes 262144 | tf_op jit(solution)/shard_map/all_to_all | solution.py:867
  56.7 0.7 copy-start.13
  62.8 19.0 %all-to-all-start.2 = ((bf16[32,2,16,256]{3,2,1,0:T(8,128)(2,1)}), bf16[32,2,16,256]{3,2,1,0:T(8,128)(2,1)S(1)}, u32[]{:S(2)}, u32[]{:S(2)}) async-start(bf16[32,2,16,256]{3,2,1,0:T(8,128)(2,1)} %get-tuple-element.68), calls=%async_computation.2 | async-start | bytes 1048576 | tf_op jit(solution)/shard_map/all_to_all | solution.py:985
  65.4 10.5 %copy-start.2 = (bf16[16,4,2,8,256]{4,3,2,1,0:T(8,128)(2,1)S(1)}, bf16[16,4,2,8,256]{4,3,2,1,0:T(8,128)(2,1)}, u32[]{:S(2)}) copy-start(bf16[16,4,2,8,256]{4,3,2,1,0:T(8,128)(2,1)} %copy.58) | copy-start | bytes 1572868
  81.8 0.8 copy-start.8
  94.4 2.8 %copy-start.4 = (bf16[1024,256]{1,0:T(8,128)(2,1)S(1)}, bf16[1024,256]{1,0:T(8,128)(2,1)}, u32[]{:S(2)}) copy-start(bf16[1024,256]{1,0:T(8,128)(2,1)} %w_proj_ref.1) | copy-start | bytes 1572868
  94.4 4.6 %copy-start.33 = (f32[1,64]{1,0:T(1,128)S(1)}, f32[1,64]{1,0:T(1,128)}, u32[]{:S(2)}) copy-start(f32[1,64]{1,0:T(1,128)} %get-tuple-element.83.hidden_ref) | copy-start | bytes 772
  94.4 4.6 %copy-start.7 = (bf16[1024,256]{1,0:T(8,128)(2,1)S(1)}, bf16[1024,256]{1,0:T(8,128)(2,1)}, u32[]{:S(2)}) copy-start(bf16[1024,256]{1,0:T(8,128)(2,1)} %get-tuple-element.73.att_ref) | copy-start | bytes 1572868
  94.4 19.1 %all-to-all-start.3 = ((bf16[32,2,16,256]{3,2,1,0:T(8,128)(2,1)}), bf16[32,2,16,256]{3,2,1,0:T(8,128)(2,1)S(1)}, u32[]{:S(2)}, u32[]{:S(2)}) async-start(bf16[32,2,16,256]{3,2,1,0:T(8,128)(2,1)} %bitcast.126), calls=%async_computation.3 | async-start | bytes 1048576 | tf_op jit(solution)/shard_map/all_to_all | solution.py:985
  113.5 0.8 copy-start.6
  114.3 9.0 %copy-start.3 = (bf16[256,1152]{1,0:T(8,128)(2,1)S(1)}, bf16[256,1152]{1,0:T(8,128)(2,1)}, u32[]{:S(2)}) copy-start(bf16[256,1152]{1,0:T(8,128)(2,1)} %attention_weights.1) | copy-start | bytes 1769476
  121.8 3.1 %collective-permute-start.4 = (bf16[1,64,256]{2,1,0:T(8,128)(2,1)S(1)}, bf16[1,64,256]{2,1,0:T(8,128)(2,1)S(1)}, u32[]{:S(2)}, u32[]{:S(2)}) collective-permute-start(bf16[1,64,256]{2,1,0:T(8,128)(2,1)S(1)} %get-tuple-element.121), channel_id=1, source_target_pairs={{0,8},{8,16},{16,24},{1,9},{9,17},{17,25},{2,10},{10,18},{18,26},{... | collective-permute-start | bytes 98312 | tf_op jit(solution)/shard_map/ppermute | solution.py:849
  123.3 3.0 %copy-start.12 = (bf16[32,8,256]{2,1,0:T(8,128)(2,1)S(1)}, bf16[32,8,256]{2,1,0:T(8,128)(2,1)}, u32[]{:S(2)}) copy-start(bf16[32,8,256]{2,1,0:T(8,128)(2,1)} %get-tuple-element.80) | copy-start | bytes 393220
  124.9 8.0 %copy-start.21 = (bf16[1,64,256]{2,1,0:T(8,128)(2,1)}, bf16[1,64,256]{2,1,0:T(8,128)(2,1)S(1)}, u32[]{:S(2)}) copy-start(bf16[1,64,256]{2,1,0:T(8,128)(2,1)S(1)} %collective-permute-done.4.up_ref) | copy-start | bytes 98308
  125.7 12.5 %collective-permute-start.10 = (bf16[128,2176]{1,0:T(8,128)(2,1)}, bf16[128,2176]{1,0:T(8,128)(2,1)S(1)}, u32[]{:S(2)}, u32[]{:S(2)}) collective-permute-start(bf16[128,2176]{1,0:T(8,128)(2,1)} %dynamic-slice_bitcast_fusion), channel_id=1, source_target_pairs={{0,1},{1,0},{2,3},{3,2},{4,5},{5,4},{6,7},{7,6},{8,9},{9,8},{10,11... | collective-permute-start | bytes 1671176 | tf_op jit(solution)/shard_map/ppermute | solution.py:879
  127.2 23.5 %all-to-all-start.4 = ((bf16[32,40,256]{2,1,0:T(8,128)(2,1)}), bf16[32,40,256]{2,1,0:T(8,128)(2,1)S(1)}, u32[]{:S(2)}, u32[]{:S(2)}) async-start(bf16[32,40,256]{2,1,0:T(8,128)(2,1)} %pad_maximum_fusion.1), calls=%async_computation.4 | async-start | bytes 1310720 | tf_op jit(solution)/shard_map/all_to_all | solution.py:867
  131.5 19.2 %copy-start.15 = (bf16[2,16,1,256]{3,2,1,0:T(2,128)(2,1)S(1)}, bf16[2,16,1,256]{3,2,1,0:T(2,128)(2,1)}, u32[]{:S(2)}) copy-start(bf16[2,16,1,256]{3,2,1,0:T(2,128)(2,1)} %get-tuple-element.86) | copy-start | bytes 49156
  131.5 6.6 %collective-permute-start.5 = (bf16[1,64,256]{2,1,0:T(8,128)(2,1)S(1)}, bf16[1,64,256]{2,1,0:T(8,128)(2,1)S(1)}, u32[]{:S(2)}, u32[]{:S(2)}) collective-permute-start(bf16[1,64,256]{2,1,0:T(8,128)(2,1)S(1)} %get-tuple-element.120), channel_id=1, source_target_pairs={{8,0},{16,8},{24,16},{9,1},{17,9},{25,17},{10,2},{18,10},{26,18},{... | collective-permute-start | bytes 98312 | tf_op jit(solution)/shard_map/ppermute | solution.py:849
  138.2 12.6 %copy-start.22 = (bf16[1,64,256]{2,1,0:T(8,128)(2,1)}, bf16[1,64,256]{2,1,0:T(8,128)(2,1)S(1)}, u32[]{:S(2)}) copy-start(bf16[1,64,256]{2,1,0:T(8,128)(2,1)S(1)} %collective-permute-done.5.down_ref) | copy-start | bytes 98308
  138.4 15.4 %collective-permute-start.13 = (bf16[32,2176]{1,0:T(8,128)(2,1)S(1)}, bf16[32,2176]{1,0:T(8,128)(2,1)S(1)}, u32[]{:S(2)}, u32[]{:S(2)}) collective-permute-start(bf16[32,2176]{1,0:T(8,128)(2,1)S(1)} %get-tuple-element.111), channel_id=1, source_target_pairs={{0,24},{8,0},{16,8},{24,16},{1,25},{9,1},{17,9},{25,17},{2,26},{10... | collective-permute-start | bytes 417800 | tf_op jit(solution)/shard_map/ppermute | solution.py:879
  138.8 15.0 %collective-permute-start.12 = (bf16[32,2176]{1,0:T(8,128)(2,1)S(1)}, bf16[32,2176]{1,0:T(8,128)(2,1)S(1)}, u32[]{:S(2)}, u32[]{:S(2)}) collective-permute-start(bf16[32,2176]{1,0:T(8,128)(2,1)S(1)} %get-tuple-element.112), channel_id=1, source_target_pairs={{0,16},{8,24},{16,0},{24,8},{1,17},{9,25},{17,1},{25,9},{2,18},{10... | collective-permute-start | bytes 417800 | tf_op jit(solution)/shard_map/ppermute | solution.py:879
  142.1 11.7 %collective-permute-start.11 = (bf16[32,2176]{1,0:T(8,128)(2,1)S(1)}, bf16[32,2176]{1,0:T(8,128)(2,1)S(1)}, u32[]{:S(2)}, u32[]{:S(2)}) collective-permute-start(bf16[32,2176]{1,0:T(8,128)(2,1)S(1)} %get-tuple-element.110), channel_id=1, source_target_pairs={{0,8},{8,16},{16,24},{24,0},{1,9},{9,17},{17,25},{25,1},{2,10},{10... | collective-permute-start | bytes 417800 | tf_op jit(solution)/shard_map/ppermute | solution.py:879
  150.7 5.6 %copy-start.1 = (bf16[32,40,256]{2,1,0:T(8,128)(2,1)}, bf16[32,40,256]{2,1,0:T(8,128)(2,1)S(1)}, u32[]{:S(2)}) copy-start(bf16[32,40,256]{2,1,0:T(8,128)(2,1)S(1)} %all-to-all-done.4.parts_ref) | copy-start | bytes 1966084
  150.8 3.1 %collective-permute-start.7 = (bf16[18,1,256]{2,0,1:T(8,128)(2,1)S(1)}, bf16[18,1,256]{2,0,1:T(8,128)(2,1)S(1)}, u32[]{:S(2)}, u32[]{:S(2)}) collective-permute-start(bf16[18,1,256]{2,0,1:T(8,128)(2,1)S(1)} %pad_maximum_fusion.6), channel_id=1, source_target_pairs={{0,1},{1,2},{2,3},{3,4},{4,5},{5,6},{6,7},{8,9},{9,10},{10,11},{11... | collective-permute-start | bytes 27656 | tf_op jit(solution)/shard_map/ppermute | solution.py:849
  152.5 3.1 %collective-permute-start.6 = (bf16[18,1,256]{2,0,1:T(8,128)(2,1)S(1)}, bf16[18,1,256]{2,0,1:T(8,128)(2,1)S(1)}, u32[]{:S(2)}, u32[]{:S(2)}) collective-permute-start(bf16[18,1,256]{2,0,1:T(8,128)(2,1)S(1)} %pad_maximum_fusion.5), channel_id=1, source_target_pairs={{1,0},{2,1},{3,2},{4,3},{5,4},{6,5},{7,6},{9,8},{10,9},{11,10},{12... | collective-permute-start | bytes 27656 | tf_op jit(solution)/shard_map/ppermute | solution.py:849
  181.0 4.9 %collective-permute-start.8 = (bf16[128,1152]{1,0:T(8,128)(2,1)S(1)}, bf16[128,1152]{1,0:T(8,128)(2,1)S(1)}, u32[]{:S(2)}, u32[]{:S(2)}) collective-permute-start(bf16[128,1152]{1,0:T(8,128)(2,1)S(1)} %dynamic-slice_bitcast_fusion.1), channel_id=1, source_target_pairs={{0,1},{1,0},{2,3},{3,2},{4,5},{5,4},{6,7},{7,6},{8,9},{9,8},{10,11... | collective-permute-start | bytes 884744 | tf_op jit(solution)/shard_map/ppermute | solution.py:879
  183.1 10.0 %collective-permute-start.16 = (bf16[8,2176]{1,0:T(8,128)(2,1)S(1)}, bf16[8,2176]{1,0:T(8,128)(2,1)S(1)}, u32[]{:S(2)}, u32[]{:S(2)}) collective-permute-start(bf16[8,2176]{1,0:T(8,128)(2,1)S(1)} %get-tuple-element.118), channel_id=1, source_target_pairs={{0,6},{1,7},{2,0},{3,1},{4,2},{5,3},{6,4},{7,5},{8,14},{9,15},{10,... | collective-permute-start | bytes 104456 | tf_op jit(solution)/shard_map/ppermute | solution.py:879
  183.3 9.8 %collective-permute-start.15 = (bf16[8,2176]{1,0:T(8,128)(2,1)S(1)}, bf16[8,2176]{1,0:T(8,128)(2,1)S(1)}, u32[]{:S(2)}, u32[]{:S(2)}) collective-permute-start(bf16[8,2176]{1,0:T(8,128)(2,1)S(1)} %get-tuple-element.119), channel_id=1, source_target_pairs={{0,4},{1,5},{2,6},{3,7},{4,0},{5,1},{6,2},{7,3},{8,12},{9,13},{10,... | collective-permute-start | bytes 104456 | tf_op jit(solution)/shard_map/ppermute | solution.py:879
  184.9 8.3 %slice-start = ((bf16[32,40,256]{2,1,0:T(8,128)(2,1)}), bf16[32,32,256]{2,1,0:T(8,128)(2,1)S(1)}, s32[]{:S(2)}) async-start(bf16[32,40,256]{2,1,0:T(8,128)(2,1)} %copy-done.1), calls=%async_computation.7 | async-start | bytes 1048576 | tf_op jit(solution)/shard_map/slice | solution.py:1058
  184.9 8.2 %collective-permute-start.14 = (bf16[8,2176]{1,0:T(8,128)(2,1)S(1)}, bf16[8,2176]{1,0:T(8,128)(2,1)S(1)}, u32[]{:S(2)}, u32[]{:S(2)}) collective-permute-start(bf16[8,2176]{1,0:T(8,128)(2,1)S(1)} %get-tuple-element.117), channel_id=1, source_target_pairs={{0,2},{1,3},{2,4},{3,5},{4,6},{5,7},{6,0},{7,1},{8,10},{9,11},{10,... | collective-permute-start | bytes 104456 | tf_op jit(solution)/shard_map/ppermute | solution.py:879
  187.7 11.3 %copy-start.5 = (bf16[16,64,256]{2,1,0:T(8,128)(2,1)S(1)}, bf16[16,64,256]{2,1,0:T(8,128)(2,1)}, u32[]{:S(2)}) copy-start(bf16[16,64,256]{2,1,0:T(8,128)(2,1)} %get-tuple-element.67.mixed_ref) | copy-start | bytes 1572868
  187.7 24.2 %all-to-all-start.5 = ((bf16[16,8,1152]{2,1,0:T(8,128)(2,1)}), bf16[16,8,1152]{2,1,0:T(8,128)(2,1)S(1)}, u32[]{:S(2)}, u32[]{:S(2)}) async-start(bf16[16,8,1152]{2,1,0:T(8,128)(2,1)} %fusion.3), calls=%async_computation.5 | async-start | bytes 589824 | tf_op jit(solution)/shard_map/all_to_all | solution.py:900
  193.1 7.0 %copy-start.14 = (bf16[8,2176]{1,0:T(8,128)(2,1)}, bf16[8,2176]{1,0:T(8,128)(2,1)S(1)}, u32[]{:S(2)}) copy-start(bf16[8,2176]{1,0:T(8,128)(2,1)S(1)} %fusion.10) | copy-start | bytes 104452
  193.2 9.8 %collective-permute-start.17 = (bf16[1,8,2176]{2,1,0:T(8,128)(2,1)S(1)}, bf16[1,8,2176]{2,1,0:T(8,128)(2,1)S(1)}, u32[]{:S(2)}, u32[]{:S(2)}) collective-permute-start(bf16[1,8,2176]{2,1,0:T(8,128)(2,1)S(1)} %bitcast.133), channel_id=1, source_target_pairs={{0,2},{1,3},{2,4},{3,5},{4,6},{5,7},{6,0},{7,1},{8,10},{9,11},{10,... | collective-permute-start | bytes 104456 | tf_op jit(solution)/shard_map/ppermute | solution.py:879
  195.2 9.6 %collective-permute-start.18 = (bf16[1,8,2176]{2,1,0:T(8,128)(2,1)S(1)}, bf16[1,8,2176]{2,1,0:T(8,128)(2,1)S(1)}, u32[]{:S(2)}, u32[]{:S(2)}) collective-permute-start(bf16[1,8,2176]{2,1,0:T(8,128)(2,1)S(1)} %bitcast.134), channel_id=1, source_target_pairs={{0,4},{1,5},{2,6},{3,7},{4,0},{5,1},{6,2},{7,3},{8,12},{9,13},{10,... | collective-permute-start | bytes 104456 | tf_op jit(solution)/shard_map/ppermute | solution.py:879
  197.6 7.2 %collective-permute-start.19 = (bf16[1,8,2176]{2,1,0:T(8,128)(2,1)S(1)}, bf16[1,8,2176]{2,1,0:T(8,128)(2,1)S(1)}, u32[]{:S(2)}, u32[]{:S(2)}) collective-permute-start(bf16[1,8,2176]{2,1,0:T(8,128)(2,1)S(1)} %bitcast.135), channel_id=1, source_target_pairs={{0,6},{1,7},{2,0},{3,1},{4,2},{5,3},{6,4},{7,5},{8,14},{9,15},{10,... | collective-permute-start | bytes 104456 | tf_op jit(solution)/shard_map/ppermute | solution.py:879
  200.1 16.1 %copy-start.16 = (f32[1,1024]{1,0:T(1,128)S(1)}, f32[1,1024]{1,0:T(1,128)}, u32[]{:S(2)}) copy-start(f32[1,1024]{1,0:T(1,128)} %get-tuple-element.98) | copy-start | bytes 12292
  200.1 16.1 %copy-start.18 = (f32[1,64]{1,0:T(1,128)S(1)}, f32[1,64]{1,0:T(1,128)}, u32[]{:S(2)}) copy-start(f32[1,64]{1,0:T(1,128)} %get-tuple-element.99) | copy-start | bytes 772
  203.0 1.8 copy-start.28
  207.5 9.5 %collective-permute-start.20 = (bf16[4,8,2176]{2,1,0:T(8,128)(2,1)}, bf16[4,8,2176]{2,1,0:T(8,128)(2,1)S(1)}, u32[]{:S(2)}, u32[]{:S(2)}) collective-permute-start(bf16[4,8,2176]{2,1,0:T(8,128)(2,1)} %bitcast.144), channel_id=1, source_target_pairs={{0,8},{8,16},{16,24},{24,0},{1,9},{9,17},{17,25},{25,1},{2,10},{10... | collective-permute-start | bytes 417800 | tf_op jit(solution)/shard_map/ppermute | solution.py:879
  209.0 8.1 %collective-permute-start.21 = (bf16[4,8,2176]{2,1,0:T(8,128)(2,1)}, bf16[4,8,2176]{2,1,0:T(8,128)(2,1)S(1)}, u32[]{:S(2)}, u32[]{:S(2)}) collective-permute-start(bf16[4,8,2176]{2,1,0:T(8,128)(2,1)} %bitcast.145), channel_id=1, source_target_pairs={{0,16},{8,24},{16,0},{24,8},{1,17},{9,25},{17,1},{25,9},{2,18},{10... | collective-permute-start | bytes 417800 | tf_op jit(solution)/shard_map/ppermute | solution.py:879
  210.4 6.6 %collective-permute-start.22 = (bf16[4,8,2176]{2,1,0:T(8,128)(2,1)}, bf16[4,8,2176]{2,1,0:T(8,128)(2,1)S(1)}, u32[]{:S(2)}, u32[]{:S(2)}) collective-permute-start(bf16[4,8,2176]{2,1,0:T(8,128)(2,1)} %bitcast.146), channel_id=1, source_target_pairs={{0,24},{8,0},{16,8},{24,16},{1,25},{9,1},{17,9},{25,17},{2,26},{10... | collective-permute-start | bytes 417800 | tf_op jit(solution)/shard_map/ppermute | solution.py:879
  212.7 13.2 %all-to-all-start.6 = ((bf16[16,8,1152]{2,1,0:T(8,128)(2,1)}), bf16[16,8,1152]{2,1,0:T(8,128)(2,1)S(1)}, u32[]{:S(2)}, u32[]{:S(2)}) async-start(bf16[16,8,1152]{2,1,0:T(8,128)(2,1)} %broadcast_in_dim.17), calls=%async_computation.6 | async-start | bytes 589824 | tf_op jit(solution)/shard_map/all_to_all | solution.py:900
  217.0 0.7 copy-start.25
  217.1 0.7 copy-start.26
  217.8 0.7 copy-start.27
  220.4 6.4 %collective-permute-start.23 = (bf16[16,8,2176]{2,1,0:T(8,128)(2,1)}, bf16[16,8,2176]{2,1,0:T(8,128)(2,1)S(1)}, u32[]{:S(2)}, u32[]{:S(2)}) collective-permute-start(bf16[16,8,2176]{2,1,0:T(8,128)(2,1)} %bitcast.142), channel_id=1, source_target_pairs={{0,1},{1,0},{2,3},{3,2},{4,5},{5,4},{6,7},{7,6},{8,9},{9,8},{10,11... | collective-permute-start | bytes 1671176 | tf_op jit(solution)/shard_map/ppermute | solution.py:879
  220.4 5.6 %copy-start.17 = (f32[1,1024]{1,0:T(1,128)S(1)}, f32[1,1024]{1,0:T(1,128)}, u32[]{:S(2)}) copy-start(f32[1,1024]{1,0:T(1,128)} %get-tuple-element.100) | copy-start | bytes 12292
  225.9 4.4 %copy-start.9 = (bf16[16,8,1152]{2,1,0:T(8,128)(2,1)}, bf16[16,8,1152]{2,1,0:T(8,128)(2,1)S(1)}, u32[]{:S(2)}) copy-start(bf16[16,8,1152]{2,1,0:T(8,128)(2,1)S(1)} %all-to-all-done.6) | copy-start | bytes 884740
  225.9 4.4 %collective-permute-start.9 = (bf16[128,1152]{1,0:T(8,128)(2,1)S(1)}, bf16[128,1152]{1,0:T(8,128)(2,1)S(1)}, u32[]{:S(2)}, u32[]{:S(2)}) collective-permute-start(bf16[128,1152]{1,0:T(8,128)(2,1)S(1)} %bitcast.129), channel_id=1, source_target_pairs={{0,1},{1,0},{2,3},{3,2},{4,5},{5,4},{6,7},{7,6},{8,9},{9,8},{10,11... | collective-permute-start | bytes 884744 | tf_op jit(solution)/shard_map/ppermute | solution.py:879
  226.8 0.8 copy-start.23
  230.4 0.7 copy-start.24
  (2 other events, 1.2 us)

commit v3 on v1

--- a/solution.py
+++ b/solution.py
@@ -17,7 +17,7 @@
 GELU_B = GELU_A * 0.044715
 F32 = jnp.float32
 BF16 = jnp.bfloat16
-PARAMS = pltpu.CompilerParams(vmem_limit_bytes=56 * 1024 * 1024)
+PARAMS = pltpu.CompilerParams(vmem_limit_bytes=24 * 1024 * 1024)
 
 
 def estimate(us):
@@ -510,7 +510,7 @@
 def mixed_back_kernel(
     stride, bands,
     recv_ref, mixed_ref, cot_ref, gain_ref, act_ref, gate_ref, w_projt_ref,
-    grad_ref, low_ref, norm_ref, project_ref, gate_grad_ref, lines_ref, sides_ref,
+    grad_ref, low_ref, norm_ref, project_ref, gate_grad_ref,
     turned_ref, total_ref,
 ):
     rows, cols, channels = mixed_ref.shape
@@ -539,11 +539,6 @@
             0, rows // lines, some_rows, jnp.zeros((8, channels), F32), unroll=2
         )
         norm_ref[...] = jnp.sum(total, axis=0, keepdims=True)
-        lines_ref[0] = low_ref[0]
-        lines_ref[1] = low_ref[rows - 1]
-        for i in range(rows):
-            sides_ref[0, i] = low_ref[i, 0:1, :]
-            sides_ref[1, i] = low_ref[i, cols - 1 : cols, :]
         turned_ref[...] = low_ref[...].reshape(rows * cols, channels).T
 
     flat = act_ref[...].reshape(rows * cols, BLOCK)
@@ -574,7 +569,6 @@
         out_specs=[
             whole(mixed.shape), whole(mixed.shape), whole((1, channels)),
             last_block((BLOCK, expanded)), whole((count, 2 * expanded // BLOCK, BLOCK)),
-            whole((2, cols, channels)), whole((2, rows, 1, channels)),
         ],
         out_shape=[
             jax.ShapeDtypeStruct(mixed.shape, F32),
@@ -582,8 +576,6 @@
             jax.ShapeDtypeStruct((1, channels), F32),
             jax.ShapeDtypeStruct((BLOCK, expanded), BF16),
             jax.ShapeDtypeStruct((count, 2 * expanded // BLOCK, BLOCK), BF16),
-            jax.ShapeDtypeStruct((2, cols, channels), BF16),
-            jax.ShapeDtypeStruct((2, rows, 1, channels), BF16),
         ],
         scratch_shapes=[
             pltpu.VMEM((channels, rows * cols), BF16),
@@ -819,18 +811,23 @@
     return lax.ppermute(cells, axis, pairs)
 
 
-def halo_rows(top, bottom):
-    return shift(bottom, "row", 1), shift(top, "row", -1)
-
-
-def halo_sides(first, last, up, down):
-    width = up.shape[0]
-    first = jnp.concatenate([up[:, :width], first, down[:, :width]], axis=0)
-    last = jnp.concatenate([up[:, -width:], last, down[:, -width:]], axis=0)
+def halo_rows(cells, width):
+    up = shift(cells[cells.shape[0] - width :], "row", 1)
+    down = shift(cells[:width], "row", -1)
+    return up, down
+
+
+def halo_sides(cells, up, down, width):
+    rows, cols, channels = cells.shape
+    first = jnp.concatenate([up[:, :width], cells[:, :width], down[:, :width]], axis=0)
+    last = jnp.concatenate(
+        [up[:, cols - width :], cells[:, cols - width :], down[:, cols - width :]], axis=0
+    )
     left = shift(last, "col", 1)
     right = shift(first, "col", -1)
-    gap = jnp.zeros((first.shape[0], 8 - 2 * width, first.shape[2]), first.dtype)
-    return jnp.concatenate([right, gap, left], axis=1).reshape(-1, first.shape[2])
+    gap = jnp.zeros((rows + 2 * width, 8 - 2 * width, channels), cells.dtype)
+    side = jnp.concatenate([right, gap, left], axis=1)
+    return side.reshape(-1, channels)
 
 
 def hand_around(blocks):
@@ -991,10 +988,10 @@
     bias_tall = attn_bias.transpose(0, 2, 1).reshape(halves, heads // halves * members, members)
     bias_tall = jnp.concatenate([bias_tall, bias_tall], axis=2)
 
-    up, down = halo_rows(image[:2], image[-2:])
+    up, down = halo_rows(image, 2)
     normed_first, turned_first, spread, spread_slope = run_expand(image, gain_first, w_expand)
     up, down, spread = lax.optimization_barrier((up, down, spread))
-    side = halo_sides(image[:, :2], image[:, -2:], up, down)
+    side = halo_sides(image, up, down, 2)
     cot_sent = (
         out_cotangent.reshape(lines, stride, bands, SIDE, channels)
         .transpose(1, 2, 0, 3, 4)
@@ -1016,7 +1013,7 @@
     grad_normed_home = swap_groups(grad_normed.reshape(normed_sent.shape), parity)
     weights = run_attention_weights(normed_members, packed_grad, attended, cot_members, grad_bias)
     grad_normed_home, weights = lax.optimization_barrier((grad_normed_home, weights))
-    grad_mixed, grad_low, grad_norm1, grad_project, gate_grad, edge_lines, edge_sides = run_mixed_back(
+    grad_mixed, grad_low, grad_norm1, grad_project, gate_grad = run_mixed_back(
         count, stride, grad_normed_home, mixed, out_cotangent, gain_second, act, gate, w_project_t
     )
     attended_sent = out_of_members(attended)
@@ -1029,12 +1026,12 @@
     else:
         parts = hand_around(gate_grad)
         attended_home = swap_groups(attended_sent, parity)
-    up, down = halo_rows(edge_lines[:1], edge_lines[1:])
-    side = halo_sides(edge_sides[0], edge_sides[1], up, down)
+    up, down = halo_rows(grad_low, 1)
+    side = halo_sides(grad_low, up, down, 1)
     weights = jnp.concatenate([weights, grad_project], axis=1)
     weights, _ = lax.optimization_barrier((weights, up))
     steps = sum_steps()
-    for step in steps[:2]:
+    for step in steps:
         weights = sum_parts(weights, *step)
     late, grad_first, logit, pre = run_expand_back(
         cells_total, parts, hidden, gate, w_squeeze, w_excite, grad_low, up, down, side,
@@ -1042,7 +1039,6 @@
         gain_first, grad_norm1,
     )
     weights, _ = lax.optimization_barrier((weights, late))
-    weights = sum_parts(weights, *steps[2])
     weights = weights[None]
     for step in steps[:0:-1]:
         weights = join_parts(weights, *step)

time: 228 us -> 224 us (0.982)
  local copies, waits for them, and re-layouts: 18.9 us -> 43.5 us
  Pallas kernels: 82.9 us -> 60.2 us
  waiting for transfers between devices: 46.5 us -> 41.1 us
  other arithmetic: 9.32 us -> 4.93 us
  starting transfers between devices: 65.3 us -> 69.5 us
    unnamed x74 -> x108, local copies, waits for them, and re-layouts: 9.29 us -> 36.7 us
    ppermute x16, waiting for transfers between devices: 15.2 us -> 6 us  [send_on(): return lax.ppermute(v, axis, pairs)]
    all_to_all x2, waiting for transfers between devices: 3.6 us -> 11.7 us  [around(): lax.all_to_all(blocks, AXES, split_axis=0, concat_axis=0, tiled=True, axi...]
    ppermute x16, starting transfers between devices: 15.9 us -> 21.5 us  [send_on(): return lax.ppermute(v, axis, pairs)]
    all_to_all x3, waiting for transfers between devices: 15.5 us -> 11 us  [swap_groups(): lax.all_to_all(blocks, AXES, split_axis=0, concat_axis=0, tiled=True, axi...]
    all_to_all x2, starting transfers between devices: 13.5 us -> 9.36 us  [hand_around(): return lax.all_to_all(blocks, AXES, split_axis=0, concat_axis=0, tiled=True)]
    pallas_call x1, Pallas kernels: 6.72 us -> 3.25 us  [run_mixed_back(): pl.pallas_call(functools.partial(mixed_back_kernel, stride, cols // SIDE)...]
    pallas_call x2, Pallas kernels: 3.43 us -> 0.05 us  [join_parts(): pl.pallas_call(stack_kernel, in_specs=[vmem] * size, out_specs=vmem, out_...]
  transfers between devices with their start and end apart: 31 -> 31, of which waited for: 12 -> 10; matrix products, arithmetic and copies ran while one was open for 9% -> 5% of each run, Pallas kernels for 18% -> 19%
where the time goes in v3:
time: 224 us; the launch traced here: 222 us
  starting transfers between devices  69.5 us (31%)
  Pallas kernels  60.2 us (27%)
  local copies, waits for them, and re-layouts  43.5 us (19%)
  waiting for transfers between devices  41.1 us (18%)
  other arithmetic  4.93 us (2%)
    unnamed x108, local copies, waits for them, and re-layouts  36.7 us
    ppermute x16, starting transfers between devices, send_on(): return lax.ppermute(v, axis, pairs)  21.5 us
    ppermute x8, starting transfers between devices, shift(): return lax.ppermute(cells, axis, pairs)  17.2 us
    all_to_all x3, starting transfers between devices, swap_groups(): lax.all_to_all(blocks, AXES, split_axis=0, concat_axis=0, tiled=True, axi...  13.9 us
    pallas_call x1, Pallas kernels, run_expand_back(): pl.pallas_call(functools.partial(expand_back_kernel, cells_total), grid=(...  13.6 us
    all_to_all x2, waiting for transfers between devices, around(): lax.all_to_all(blocks, AXES, split_axis=0, concat_axis=0, tiled=True, axi...  11.7 us
    all_to_all x3, waiting for transfers between devices, swap_groups(): lax.all_to_all(blocks, AXES, split_axis=0, concat_axis=0, tiled=True, axi...  11 us
    pallas_call x1, Pallas kernels, run_attention(): pl.pallas_call(functools.partial(attention_kernel, members, heads, lines)...  10.4 us
  transfers between devices with their start and end apart: 31, of which 10 were waited for; matrix products, arithmetic and copies ran while one was open for 5% of the time, Pallas kernels for 19%

profile of v3, /device:TPU:0, one launch (start us, length us, event | category | flops | bytes accessed | tf_op | source)
XLA Modules:
  0.0 222.4 jit_solution(11890771878845186640)
XLA Ops:
  1.7 4.8 %collective-permute-start = (bf16[2,64,256]{2,1,0:T(8,128)(2,1)S(1)}, bf16[2,64,256]{2,1,0:T(8,128)(2,1)S(1)}, u32[]{:S(2)}, u32[]{:S(2)}) collective-permute-start(bf16[2,64,256]{2,1,0:T(8,128)(2,1)S(1)} %get-tuple-element.112), channel_id=1, source_target_pairs={{0,8},{8,16},{16,24},{1,9},{9,17},{17,25},{2,10},{10,18},{18,26},{... | collective-permute-start | bytes 196616 | tf_op jit(solution)/shard_map/ppermute | solution.py:811
  6.5 1.3 collective-permute-start.1
  7.8 1.9 copy.45
  9.7 7.0 %all-to-all-start.1 = ((bf16[32,2,16,256]{3,2,1,0:T(8,128)(2,1)}), bf16[32,2,16,256]{3,2,1,0:T(8,128)(2,1)S(1)}, u32[]{:S(2)}, u32[]{:S(2)}) async-start(bf16[32,2,16,256]{3,2,1,0:T(8,128)(2,1)} %bitcast.3), calls=%async_computation.1 | async-start | bytes 1048576 | tf_op jit(solution)/shard_map/all_to_all | solution.py:952
  16.8 5.8 %expand.1 = (bf16[1024,256]{1,0:T(8,128)(2,1)}, bf16[256,1024]{1,0:T(8,128)(2,1)S(1)}, bf16[16,64,1024]{2,1,0:T(8,128)(2,1)S(1)}, bf16[16,64,1024]{2,1,0:T(8,128)(2,1)S(1)}) custom-call(bf16[16,64,256]{2,1,0:T(8,128)(2,1)S(1)} %copy-done.10, bf16[1,256]{1,0:T(2,128)(2,1)S(1)} %reshape.133.gain_ref, bf16[256,1024]{1,0:T(8,128)(2,1)S(1)} %copy-done.14), custom_call_target="tpu_custom_call" | custom-call | flops 15399999488 | bytes 50400000 | tf_op jit(solution)/shard_map/expand/pallas_call | solution.py:113
  22.6 1.3 copy-done.40
  24.9 2.2 collective-permute-start.3
  27.1 1.3 collective-permute-start.2
  28.5 2.8 %collective-permute-done.2 = bf16[20,2,256]{2,0,1:T(8,128)(2,1)S(1)} collective-permute-done((bf16[20,2,256]{2,0,1:T(8,128)(2,1)S(1)}, bf16[20,2,256]{2,0,1:T(8,128)(2,1)S(1)}, u32[]{:S(2)}, u32[]{:S(2)}) %collective-permute-start.2) | collective-permute-done | bytes 20512 | tf_op jit(solution)/shard_map/ppermute | solution.py:811
  31.5 8.0 %depthwise.1 = (bf16[416,1024]{1,0:T(8,128)(2,1)S(1)}, bf16[16,64,1024]{2,1,0:T(8,128)(2,1)S(1)}, f32[32,1,1024]{2,1,0:T(1,128)}) custom-call(bf16[2,64,256]{2,1,0:T(8,128)(2,1)S(1)} %collective-permute-done.up_ref, bf16[2,64,256]{2,1,0:T(8,128)(2,1)S(1)} %collective-permute-done.1.down_ref, bf16[160,256]{1,0:T(8,128)(2,1)S(1)} %maximum_bitcast_fusion.side_ref, ...), custom_call_target="tpu_custom_call" | custom-call | flops 1100000000 | bytes 3600000 | tf_op jit(solution)/shard_map/depthwise/pallas_call | solution.py:205
  39.5 1.3 copy-done.22
  40.9 1.4 copy-done.25
  43.9 6.7 %all-to-all-start = ((f32[32,1,1024]{2,1,0:T(1,128)}), f32[32,1,1024]{2,1,0:T(1,128)S(1)}, u32[]{:S(2)}, u32[]{:S(2)}) async-start(f32[32,1,1024]{2,1,0:T(1,128)} %get-tuple-element.61), calls=%async_computation | async-start | bytes 262144 | tf_op jit(solution)/shard_map/all_to_all | solution.py:834
  51.0 1.3 copy.48
  53.4 5.4 %all-to-all-done.parts_ref = f32[32,1,1024]{2,1,0:T(1,128)S(1)} async-done(((f32[32,1,1024]{2,1,0:T(1,128)}), f32[32,1,1024]{2,1,0:T(1,128)S(1)}, u32[]{:S(2)}, u32[]{:S(2)}) %all-to-all-start) | async-done | bytes 131104 | tf_op jit(solution)/shard_map/all_to_all | solution.py:834
  58.9 1.6 copy-done.26
  60.5 3.4 %mix.1 = (f32[1,1024]{1,0:T(1,128)S(1)}, f32[1,64]{1,0:T(1,128)S(1)}, f32[1,1024]{1,0:T(1,128)S(1)}, bf16[16,64,256]{2,1,0:T(8,128)(2,1)S(1)}, bf16[32,2,16,256]{3,2,1,0:T(8,128)(2,1)}) custom-call(f32[32,1,1024]{2,1,0:T(1,128)S(1)} %all-to-all-done.parts_ref, bf16[1024,64]{1,0:T(8,128)(2,1)S(1)} %copy.47.w_sq_ref, bf16[64,1024]{1,0:T(8,128)(2,1)S(1)} %copy-done.17, ...), custom_call_target="tpu_custom_call" | custom-call | flops 5500000256 | bytes 18000000 | tf_op jit(solution)/shard_map/mix/pallas_call | solution.py:324
  63.8 2.6 %all-to-all-start.2 = ((bf16[32,2,16,256]{3,2,1,0:T(8,128)(2,1)}), bf16[32,2,16,256]{3,2,1,0:T(8,128)(2,1)S(1)}, u32[]{:S(2)}, u32[]{:S(2)}) async-start(bf16[32,2,16,256]{3,2,1,0:T(8,128)(2,1)} %get-tuple-element.64), calls=%async_computation.2 | async-start | bytes 1048576 | tf_op jit(solution)/shard_map/all_to_all | solution.py:952
  66.5 1.6 copy-done.23
  68.0 1.2 copy-done.29
  69.2 9.5 %slope.1 = (bf16[18,64,1024]{2,1,0:T(8,128)(2,1)S(1)}, f32[18,8,1024]{2,1,0:T(8,128)S(1)}) custom-call(f32[4]{0:T(128)S(1)} %add_convert_fusion.flags_ref, bf16[416,1024]{1,0:T(8,128)(2,1)S(1)} %copy-done.29, bf16[3,3,1024]{2,1,0:T(4,128)(2,1)S(1)} %copy-done.19, bf16[16,64,1024]{2,1,0:T(8,128)(2,1)S(1)} %copy-done.23), custom_call_target="tpu_custom_call" | custom-call | flops 14300000256 | bytes 46800000 | tf_op jit(solution)/shard_map/slope/pallas_call | solution.py:265
  78.7 1.4 copy-done.36
  81.3 1.5 all-to-all-done.2
  84.8 10.4 %attention.1 = (bf16[1024,256]{1,0:T(8,128)(2,1)S(1)}, bf16[1024,256]{1,0:T(8,128)(2,1)S(1)}, bf16[1024,256]{1,0:T(8,128)(2,1)}, bf16[1024,768]{1,0:T(8,128)(2,1)S(1)}, f32[2,256,64]{2,1,0:T(8,128)S(1)}) custom-call(bf16[1024,256]{1,0:T(8,128)(2,1)S(1)} %bitcast.103, bf16[1024,256]{1,0:T(8,128)(2,1)S(1)} %convolution_convert_fusion.att_grad_ref, ...), custom_call_target="tpu_custom_call" | custom-call | flops 15399999488 | bytes 50400000 | tf_op jit(solution)/shard_map/attention/pallas_call | solution.py:461
  95.1 1.2 copy-done.32
  97.8 4.3 %all-to-all-start.3 = ((bf16[32,2,16,256]{3,2,1,0:T(8,128)(2,1)}), bf16[32,2,16,256]{3,2,1,0:T(8,128)(2,1)S(1)}, u32[]{:S(2)}, u32[]{:S(2)}) async-start(bf16[32,2,16,256]{3,2,1,0:T(8,128)(2,1)} %bitcast.18), calls=%async_computation.3 | async-start | bytes 1048576 | tf_op jit(solution)/shard_map/all_to_all | solution.py:952
  102.7 1.1 copy.49
  103.8 1.0 copy-done.6
  104.8 1.4 copy-done.33
  109.0 9.5 %all-to-all-done.3.recv_ref = bf16[32,2,16,256]{3,2,1,0:T(8,128)(2,1)S(1)} async-done(((bf16[32,2,16,256]{3,2,1,0:T(8,128)(2,1)}), bf16[32,2,16,256]{3,2,1,0:T(8,128)(2,1)S(1)}, u32[]{:S(2)}, u32[]{:S(2)}) %all-to-all-start.3) | async-done | bytes 524320 | tf_op jit(solution)/shard_map/all_to_all | solution.py:952
  119.2 1.0 copy-done.4
  120.3 1.6 copy-done.27
  121.9 3.2 %mixed_back.1 = (f32[16,64,256]{2,1,0:T(8,128)S(1)}, bf16[16,64,256]{2,1,0:T(8,128)(2,1)S(1)}, f32[1,256]{1,0:T(1,128)S(1)}, bf16[256,1024]{1,0:T(8,128)(2,1)S(1)}, bf16[32,8,256]{2,1,0:T(8,128)(2,1)S(1)}) custom-call(bf16[32,2,16,256]{3,2,1,0:T(8,128)(2,1)S(1)} %copy-done.4, bf16[16,64,256]{2,1,0:T(8,128)(2,1)S(1)} %get-tuple-element.63.mixed_ref, ...), custom_call_target="tpu_custom_call" | custom-call | flops 7699999744 | bytes 25200000 | tf_op jit(solution)/shard_map/mixed_back/pallas_call | solution.py:562
  127.8 2.6 %all-to-all-start.4 = ((bf16[32,40,256]{2,1,0:T(8,128)(2,1)}), bf16[32,40,256]{2,1,0:T(8,128)(2,1)S(1)}, u32[]{:S(2)}, u32[]{:S(2)}) async-start(bf16[32,40,256]{2,1,0:T(8,128)(2,1)} %pad_maximum_fusion.1), calls=%async_computation.4 | async-start | bytes 1310720 | tf_op jit(solution)/shard_map/all_to_all | solution.py:834
  130.4 3.5 %collective-permute-start.4 = (bf16[1,64,256]{2,1,0:T(8,128)(2,1)S(1)}, bf16[1,64,256]{2,1,0:T(8,128)(2,1)S(1)}, u32[]{:S(2)}, u32[]{:S(2)}) collective-permute-start(bf16[1,64,256]{2,1,0:T(8,128)(2,1)S(1)} %get-tuple-element.108), channel_id=1, source_target_pairs={{0,8},{8,16},{16,24},{1,9},{9,17},{17,25},{2,10},{10,18},{18,26},{... | collective-permute-start | bytes 98312 | tf_op jit(solution)/shard_map/ppermute | solution.py:811
  134.0 1.5 collective-permute-start.5
  135.7 4.2 %collective-permute-done.5.down_ref = bf16[1,64,256]{2,1,0:T(8,128)(2,1)S(1)} collective-permute-done((bf16[1,64,256]{2,1,0:T(8,128)(2,1)S(1)}, bf16[1,64,256]{2,1,0:T(8,128)(2,1)S(1)}, u32[]{:S(2)}, u32[]{:S(2)}) %collective-permute-start.5) | collective-permute-done | bytes 32800 | tf_op jit(solution)/shard_map/ppermute | solution.py:811
  139.9 1.3 collective-permute-start.7
  141.3 1.3 collective-permute-start.6
  143.5 3.4 %collective-permute-start.12 = (bf16[32,2176]{1,0:T(8,128)(2,1)S(1)}, bf16[32,2176]{1,0:T(8,128)(2,1)S(1)}, u32[]{:S(2)}, u32[]{:S(2)}) collective-permute-start(bf16[32,2176]{1,0:T(8,128)(2,1)S(1)} %get-tuple-element.104), channel_id=1, source_target_pairs={{0,16},{8,24},{16,0},{24,8},{1,17},{9,25},{17,1},{25,9},{2,18},{10... | collective-permute-start | bytes 417800 | tf_op jit(solution)/shard_map/ppermute | solution.py:846
  147.0 1.9 collective-permute-done.13
  148.9 1.7 collective-permute-done.12
  150.5 2.4 %collective-permute-done.11 = bf16[32,2176]{1,0:T(8,128)(2,1)S(1)} collective-permute-done((bf16[32,2176]{1,0:T(8,128)(2,1)S(1)}, bf16[32,2176]{1,0:T(8,128)(2,1)S(1)}, u32[]{:S(2)}, u32[]{:S(2)}) %collective-permute-start.11) | collective-permute-done | bytes 139296 | tf_op jit(solution)/shard_map/ppermute | solution.py:846
  153.0 6.4 %collective-permute-start.16 = (bf16[8,2176]{1,0:T(8,128)(2,1)S(1)}, bf16[8,2176]{1,0:T(8,128)(2,1)S(1)}, u32[]{:S(2)}, u32[]{:S(2)}) collective-permute-start(bf16[8,2176]{1,0:T(8,128)(2,1)S(1)} %get-tuple-element.114), channel_id=1, source_target_pairs={{0,6},{1,7},{2,0},{3,1},{4,2},{5,3},{6,4},{7,5},{8,14},{9,15},{10,... | collective-permute-start | bytes 104456 | tf_op jit(solution)/shard_map/ppermute | solution.py:846
  159.6 1.3 collective-permute-start.14
  162.0 1.6 copy-done.24
  163.6 1.7 copy-done.37
  165.3 1.6 copy-done.41
  166.9 1.1 copy-done.43
  169.0 13.6 %expand_back.1 = (bf16[256,1152]{1,0:T(8,128)(2,1)S(1)}, f32[1024,256]{1,0:T(8,128)S(1)}, f32[1,1024]{1,0:T(1,128)S(1)}, f32[1,64]{1,0:T(1,128)S(1)}) custom-call(bf16[32,40,256]{2,1,0:T(8,128)(2,1)S(1)} %all-to-all-done.4.parts_ref, f32[1,64]{1,0:T(1,128)S(1)} %get-tuple-element.77.hidden_ref, f32[1,1024]{1,0:T(1,128)S(1)} %get-tuple-element.75.gate_ref.gate_all_ref, ...), custom_call_target="tpu_custom_call" | custom-call | flops 15399999488 | bytes 50400000 | tf_op jit(solution)/shard_map/expand_back/pallas_call | solution.py:743
  183.8 2.0 collective-permute-start.17
  185.8 1.1 collective-permute-start.18
  186.9 1.3 collective-permute-start.19
  189.0 4.0 %all-to-all-start.5 = ((bf16[16,8,1152]{2,1,0:T(8,128)(2,1)}), bf16[16,8,1152]{2,1,0:T(8,128)(2,1)S(1)}, u32[]{:S(2)}, u32[]{:S(2)}) async-start(bf16[16,8,1152]{2,1,0:T(8,128)(2,1)} %fusion.3), calls=%async_computation.5 | async-start | bytes 589824 | tf_op jit(solution)/shard_map/all_to_all | solution.py:867
  193.1 2.0 collective-permute-start.20
  195.1 1.5 collective-permute-start.21
  196.6 1.5 collective-permute-start.22
  198.0 2.2 %image_back.1 = bf16[1024,256]{1,0:T(8,128)(2,1)} custom-call(bf16[1024,256]{1,0:T(8,128)(2,1)S(1)} %bitcast.106, bf16[1,256]{1,0:T(2,128)(2,1)S(1)} %reshape.133.gain_ref, f32[1024,256]{1,0:T(8,128)S(1)} %copy-done.31, f32[1024,256]{1,0:T(8,128)S(1)} %bitcast.120), custom_call_target="tpu_custom_call" | custom-call | flops 4400000000 | bytes 14400000 | tf_op jit(solution)/shard_map/image_back/pallas_call | solution.py:796
  200.3 4.0 %all-to-all-done.5 = bf16[16,8,1152]{2,1,0:T(8,128)(2,1)S(1)} async-done(((bf16[16,8,1152]{2,1,0:T(8,128)(2,1)}), bf16[16,8,1152]{2,1,0:T(8,128)(2,1)S(1)}, u32[]{:S(2)}, u32[]{:S(2)}) %all-to-all-start.5) | async-done | bytes 294944 | tf_op jit(solution)/shard_map/all_to_all | solution.py:867
  205.1 3.5 %all-to-all-start.6 = ((bf16[16,8,1152]{2,1,0:T(8,128)(2,1)}), bf16[16,8,1152]{2,1,0:T(8,128)(2,1)S(1)}, u32[]{:S(2)}, u32[]{:S(2)}) async-start(bf16[16,8,1152]{2,1,0:T(8,128)(2,1)} %broadcast_in_dim.17), calls=%async_computation.6 | async-start | bytes 589824 | tf_op jit(solution)/shard_map/all_to_all | solution.py:867
  209.7 1.1 fusion
  210.8 7.6 %all-to-all-done.6 = bf16[16,8,1152]{2,1,0:T(8,128)(2,1)S(1)} async-done(((bf16[16,8,1152]{2,1,0:T(8,128)(2,1)}), bf16[16,8,1152]{2,1,0:T(8,128)(2,1)S(1)}, u32[]{:S(2)}, u32[]{:S(2)}) %all-to-all-start.6) | async-done | bytes 294944 | tf_op jit(solution)/shard_map/all_to_all | solution.py:867
  219.2 2.1 unpack_weights.1
  221.3 1.1 unpack.1
  (170 shorter events, 24.5 us)
Async XLA Ops:
  0.6 80.3 %copy-start = (bf16[256,256]{1,0:T(8,128)(2,1)S(1)}, bf16[256,256]{1,0:T(8,128)(2,1)}, u32[]{:S(2)}) copy-start(bf16[256,256]{1,0:T(8,128)(2,1)} %param.22) | copy-start | bytes 393220
  0.7 16.1 %copy-start.10 = (bf16[16,64,256]{2,1,0:T(8,128)(2,1)S(1)}, bf16[16,64,256]{2,1,0:T(8,128)(2,1)}, u32[]{:S(2)}) copy-start(bf16[16,64,256]{2,1,0:T(8,128)(2,1)} %image_ref.3) | copy-start | bytes 1572868
  0.7 16.1 %copy-start.50 = (bf16[256]{0:T(256)(128)(2,1)S(1)}, bf16[256]{0:T(256)(128)(2,1)}, u32[]{:S(2)}) copy-start(bf16[256]{0:T(256)(128)(2,1)} %param.14) | copy-start | bytes 1540
  0.7 16.1 %copy-start.14 = (bf16[256,1024]{1,0:T(8,128)(2,1)S(1)}, bf16[256,1024]{1,0:T(8,128)(2,1)}, u32[]{:S(2)}) copy-start(bf16[256,1024]{1,0:T(8,128)(2,1)} %w_exp_ref.5) | copy-start | bytes 1572868
  1.7 23.1 %collective-permute-start = (bf16[2,64,256]{2,1,0:T(8,128)(2,1)S(1)}, bf16[2,64,256]{2,1,0:T(8,128)(2,1)S(1)}, u32[]{:S(2)}, u32[]{:S(2)}) collective-permute-start(bf16[2,64,256]{2,1,0:T(8,128)(2,1)S(1)} %get-tuple-element.112), channel_id=1, source_target_pairs={{0,8},{8,16},{16,24},{1,9},{9,17},{17,25},{2,10},{10,18},{18,26},{... | collective-permute-start | bytes 196616 | tf_op jit(solution)/shard_map/ppermute | solution.py:811
  6.5 18.3 %collective-permute-start.1 = (bf16[2,64,256]{2,1,0:T(8,128)(2,1)S(1)}, bf16[2,64,256]{2,1,0:T(8,128)(2,1)S(1)}, u32[]{:S(2)}, u32[]{:S(2)}) collective-permute-start(bf16[2,64,256]{2,1,0:T(8,128)(2,1)S(1)} %get-tuple-element.111), channel_id=1, source_target_pairs={{8,0},{16,8},{24,16},{9,1},{17,9},{25,17},{10,2},{18,10},{26,18},{... | collective-permute-start | bytes 196616 | tf_op jit(solution)/shard_map/ppermute | solution.py:811
  9.7 33.4 %all-to-all-start.1 = ((bf16[32,2,16,256]{3,2,1,0:T(8,128)(2,1)}), bf16[32,2,16,256]{3,2,1,0:T(8,128)(2,1)S(1)}, u32[]{:S(2)}, u32[]{:S(2)}) async-start(bf16[32,2,16,256]{3,2,1,0:T(8,128)(2,1)} %bitcast.3), calls=%async_computation.1 | async-start | bytes 1048576 | tf_op jit(solution)/shard_map/all_to_all | solution.py:952
  16.8 14.7 %copy-start.19 = (bf16[3,3,1024]{2,1,0:T(4,128)(2,1)S(1)}, bf16[3,3,1024]{2,1,0:T(4,128)(2,1)}, u32[]{:S(2)}) copy-start(bf16[3,3,1024]{2,1,0:T(4,128)(2,1)} %w_dep_ref.5) | copy-start | bytes 55300
  22.6 1.3 copy-start.40
  24.9 3.6 %collective-permute-start.3 = (bf16[20,2,256]{2,0,1:T(8,128)(2,1)S(1)}, bf16[20,2,256]{2,0,1:T(8,128)(2,1)S(1)}, u32[]{:S(2)}, u32[]{:S(2)}) collective-permute-start(bf16[20,2,256]{2,0,1:T(8,128)(2,1)S(1)} %pad_maximum_fusion.4), channel_id=1, source_target_pairs={{0,1},{1,2},{2,3},{3,4},{4,5},{5,6},{6,7},{8,9},{9,10},{10,11},{11... | collective-permute-start | bytes 61448 | tf_op jit(solution)/shard_map/ppermute | solution.py:811
  27.1 4.3 %collective-permute-start.2 = (bf16[20,2,256]{2,0,1:T(8,128)(2,1)S(1)}, bf16[20,2,256]{2,0,1:T(8,128)(2,1)S(1)}, u32[]{:S(2)}, u32[]{:S(2)}) collective-permute-start(bf16[20,2,256]{2,0,1:T(8,128)(2,1)S(1)} %pad_maximum_fusion.3), channel_id=1, source_target_pairs={{1,0},{2,1},{3,2},{4,3},{5,4},{6,5},{7,6},{9,8},{10,9},{11,10},{12... | collective-permute-start | bytes 61448 | tf_op jit(solution)/shard_map/ppermute | solution.py:811
  31.5 19.3 %copy-start.49 = (bf16[1024,64]{0,1:T(8,128)(2,1)S(1)}, bf16[1024,64]{0,1:T(8,128)(2,1)}, u32[]{:S(2)}) copy-start(bf16[1024,64]{0,1:T(8,128)(2,1)} %param.17) | copy-start | bytes 393220
  31.5 19.4 %copy-start.51 = (bf16[256]{0:T(256)(128)(2,1)S(1)}, bf16[256]{0:T(256)(128)(2,1)}, u32[]{:S(2)}) copy-start(bf16[256]{0:T(256)(128)(2,1)} %param.20) | copy-start | bytes 1540
  39.5 1.3 copy-start.22
  40.9 1.4 copy-start.25
  43.9 14.9 %all-to-all-start = ((f32[32,1,1024]{2,1,0:T(1,128)}), f32[32,1,1024]{2,1,0:T(1,128)S(1)}, u32[]{:S(2)}, u32[]{:S(2)}) async-start(f32[32,1,1024]{2,1,0:T(1,128)} %get-tuple-element.61), calls=%async_computation | async-start | bytes 262144 | tf_op jit(solution)/shard_map/all_to_all | solution.py:834
  50.7 2.5 %copy-start.47 = (bf16[32,2,16,256]{3,2,1,0:T(8,128)(2,1)S(1)}, bf16[32,2,16,256]{3,2,1,0:T(8,128)(2,1)}, u32[]{:S(2)}) copy-start(bf16[32,2,16,256]{3,2,1,0:T(8,128)(2,1)} %copy-done.46) | copy-start | bytes 1572868
  50.7 8.2 %copy-start.1 = (bf16[1024,256]{1,0:T(8,128)(2,1)S(1)}, bf16[1024,256]{1,0:T(8,128)(2,1)}, u32[]{:S(2)}) copy-start(bf16[1024,256]{1,0:T(8,128)(2,1)} %w_proj_ref.1) | copy-start | bytes 1572868
  50.7 8.2 %copy-start.17 = (bf16[64,1024]{1,0:T(8,128)(2,1)S(1)}, bf16[64,1024]{1,0:T(8,128)(2,1)}, u32[]{:S(2)}) copy-start(bf16[64,1024]{1,0:T(8,128)(2,1)} %w_ex_ref.3) | copy-start | bytes 393220
  50.9 12.9 %copy-start.7 = (bf16[1024,64]{1,0:T(8,128)(2,1)}, bf16[1024,64]{1,0:T(8,128)(2,1)S(1)}, u32[]{:S(2)}) copy-start(bf16[1024,64]{1,0:T(8,128)(2,1)S(1)} %copy.47.w_sq_ref) | copy-start | bytes 393220
  58.9 1.6 copy-start.26
  63.8 19.0 %all-to-all-start.2 = ((bf16[32,2,16,256]{3,2,1,0:T(8,128)(2,1)}), bf16[32,2,16,256]{3,2,1,0:T(8,128)(2,1)S(1)}, u32[]{:S(2)}, u32[]{:S(2)}) async-start(bf16[32,2,16,256]{3,2,1,0:T(8,128)(2,1)} %get-tuple-element.64), calls=%async_computation.2 | async-start | bytes 1048576 | tf_op jit(solution)/shard_map/all_to_all | solution.py:952
  66.5 1.6 copy-start.23
  68.0 1.2 copy-start.29
  78.7 1.4 copy-start.36
  95.1 1.2 copy-start.32
  97.8 6.0 %copy-start.5 = (bf16[1024,256]{1,0:T(8,128)(2,1)}, bf16[1024,256]{1,0:T(8,128)(2,1)S(1)}, u32[]{:S(2)}) copy-start(bf16[1024,256]{1,0:T(8,128)(2,1)S(1)} %get-tuple-element.69.att_ref) | copy-start | bytes 1572868
  97.8 20.7 %all-to-all-start.3 = ((bf16[32,2,16,256]{3,2,1,0:T(8,128)(2,1)}), bf16[32,2,16,256]{3,2,1,0:T(8,128)(2,1)S(1)}, u32[]{:S(2)}, u32[]{:S(2)}) async-start(bf16[32,2,16,256]{3,2,1,0:T(8,128)(2,1)} %bitcast.18), calls=%async_computation.3 | async-start | bytes 1048576 | tf_op jit(solution)/shard_map/all_to_all | solution.py:952
  104.8 1.4 copy-start.33
  108.2 11.0 %copy-start.2 = (bf16[16,64,256]{2,1,0:T(8,128)(2,1)S(1)}, bf16[16,64,256]{2,1,0:T(8,128)(2,1)}, u32[]{:S(2)}) copy-start(bf16[16,64,256]{2,1,0:T(8,128)(2,1)} %cot_ref.1) | copy-start | bytes 1572868
  120.3 1.6 copy-start.27
  121.9 5.1 %copy-start.48 = (bf16[16,4,2,8,256]{4,0,2,3,1:T(8,128)(2,1)S(1)}, bf16[16,4,2,8,256]{4,0,2,3,1:T(8,128)(2,1)}, u32[]{:S(2)}) copy-start(bf16[16,4,2,8,256]{4,0,2,3,1:T(8,128)(2,1)} %copy.49) | copy-start | bytes 1572868
  127.8 33.1 %all-to-all-start.4 = ((bf16[32,40,256]{2,1,0:T(8,128)(2,1)}), bf16[32,40,256]{2,1,0:T(8,128)(2,1)S(1)}, u32[]{:S(2)}, u32[]{:S(2)}) async-start(bf16[32,40,256]{2,1,0:T(8,128)(2,1)} %pad_maximum_fusion.1), calls=%async_computation.4 | async-start | bytes 1310720 | tf_op jit(solution)/shard_map/all_to_all | solution.py:834
  130.4 5.1 %collective-permute-start.4 = (bf16[1,64,256]{2,1,0:T(8,128)(2,1)S(1)}, bf16[1,64,256]{2,1,0:T(8,128)(2,1)S(1)}, u32[]{:S(2)}, u32[]{:S(2)}) collective-permute-start(bf16[1,64,256]{2,1,0:T(8,128)(2,1)S(1)} %get-tuple-element.108), channel_id=1, source_target_pairs={{0,8},{8,16},{16,24},{1,9},{9,17},{17,25},{2,10},{10,18},{18,26},{... | collective-permute-start | bytes 98312 | tf_op jit(solution)/shard_map/ppermute | solution.py:811
  134.0 5.9 %collective-permute-start.5 = (bf16[1,64,256]{2,1,0:T(8,128)(2,1)S(1)}, bf16[1,64,256]{2,1,0:T(8,128)(2,1)S(1)}, u32[]{:S(2)}, u32[]{:S(2)}) collective-permute-start(bf16[1,64,256]{2,1,0:T(8,128)(2,1)S(1)} %get-tuple-element.107), channel_id=1, source_target_pairs={{8,0},{16,8},{24,16},{9,1},{17,9},{25,17},{10,2},{18,10},{26,18},{... | collective-permute-start | bytes 98312 | tf_op jit(solution)/shard_map/ppermute | solution.py:811
  135.6 6.9 %collective-permute-start.10 = (bf16[128,2176]{1,0:T(8,128)(2,1)S(1)}, bf16[128,2176]{1,0:T(8,128)(2,1)S(1)}, u32[]{:S(2)}, u32[]{:S(2)}) collective-permute-start(bf16[128,2176]{1,0:T(8,128)(2,1)S(1)} %dynamic-slice_bitcast_fusion), channel_id=1, source_target_pairs={{0,1},{1,0},{2,3},{3,2},{4,5},{5,4},{6,7},{7,6},{8,9},{9,8},{10,11... | collective-permute-start | bytes 1671176 | tf_op jit(solution)/shard_map/ppermute | solution.py:846
  139.9 6.9 %collective-permute-start.7 = (bf16[18,1,256]{2,1,0:T(2,128)(2,1)S(1)}, bf16[18,1,256]{2,1,0:T(2,128)(2,1)S(1)}, u32[]{:S(2)}, u32[]{:S(2)}) collective-permute-start(bf16[18,1,256]{2,1,0:T(2,128)(2,1)S(1)} %pad_maximum_fusion.6), channel_id=1, source_target_pairs={{0,1},{1,2},{2,3},{3,4},{4,5},{5,6},{6,7},{8,9},{9,10},{10,11},{11... | collective-permute-start | bytes 27656 | tf_op jit(solution)/shard_map/ppermute | solution.py:811
  141.3 5.6 %collective-permute-start.6 = (bf16[18,1,256]{2,1,0:T(2,128)(2,1)S(1)}, bf16[18,1,256]{2,1,0:T(2,128)(2,1)S(1)}, u32[]{:S(2)}, u32[]{:S(2)}) collective-permute-start(bf16[18,1,256]{2,1,0:T(2,128)(2,1)S(1)} %pad_maximum_fusion.5), channel_id=1, source_target_pairs={{1,0},{2,1},{3,2},{4,3},{5,4},{6,5},{7,6},{9,8},{10,9},{11,10},{12... | collective-permute-start | bytes 27656 | tf_op jit(solution)/shard_map/ppermute | solution.py:811
  142.8 18.2 %copy-start.8 = (bf16[1024,64]{1,0:T(8,128)(2,1)S(1)}, bf16[1024,64]{1,0:T(8,128)(2,1)}, u32[]{:S(2)}) copy-start(bf16[1024,64]{1,0:T(8,128)(2,1)} %copy-done.7) | copy-start | bytes 393220
  142.8 18.2 %copy-start.13 = (bf16[16,64,256]{2,1,0:T(8,128)(2,1)S(1)}, bf16[16,64,256]{2,1,0:T(8,128)(2,1)}, u32[]{:S(2)}) copy-start(bf16[16,64,256]{2,1,0:T(8,128)(2,1)} %copy-done.12) | copy-start | bytes 1572868
  142.8 18.2 %copy-start.18 = (bf16[64,1024]{1,0:T(8,128)(2,1)S(1)}, bf16[64,1024]{1,0:T(8,128)(2,1)}, u32[]{:S(2)}) copy-start(bf16[64,1024]{1,0:T(8,128)(2,1)} %w_ex_ref.3) | copy-start | bytes 393220
  142.9 6.0 %collective-permute-start.13 = (bf16[32,2176]{1,0:T(8,128)(2,1)S(1)}, bf16[32,2176]{1,0:T(8,128)(2,1)S(1)}, u32[]{:S(2)}, u32[]{:S(2)}) collective-permute-start(bf16[32,2176]{1,0:T(8,128)(2,1)S(1)} %get-tuple-element.103), channel_id=1, source_target_pairs={{0,24},{8,0},{16,8},{24,16},{1,25},{9,1},{17,9},{25,17},{2,26},{10... | collective-permute-start | bytes 417800 | tf_op jit(solution)/shard_map/ppermute | solution.py:846
  143.5 7.1 %collective-permute-start.12 = (bf16[32,2176]{1,0:T(8,128)(2,1)S(1)}, bf16[32,2176]{1,0:T(8,128)(2,1)S(1)}, u32[]{:S(2)}, u32[]{:S(2)}) collective-permute-start(bf16[32,2176]{1,0:T(8,128)(2,1)S(1)} %get-tuple-element.104), channel_id=1, source_target_pairs={{0,16},{8,24},{16,0},{24,8},{1,17},{9,25},{17,1},{25,9},{2,18},{10... | collective-permute-start | bytes 417800 | tf_op jit(solution)/shard_map/ppermute | solution.py:846
  146.9 6.1 %collective-permute-start.11 = (bf16[32,2176]{1,0:T(8,128)(2,1)S(1)}, bf16[32,2176]{1,0:T(8,128)(2,1)S(1)}, u32[]{:S(2)}, u32[]{:S(2)}) collective-permute-start(bf16[32,2176]{1,0:T(8,128)(2,1)S(1)} %get-tuple-element.102), channel_id=1, source_target_pairs={{0,8},{8,16},{16,24},{24,0},{1,9},{9,17},{17,25},{25,1},{2,10},{10... | collective-permute-start | bytes 417800 | tf_op jit(solution)/shard_map/ppermute | solution.py:846
  153.0 30.7 %collective-permute-start.16 = (bf16[8,2176]{1,0:T(8,128)(2,1)S(1)}, bf16[8,2176]{1,0:T(8,128)(2,1)S(1)}, u32[]{:S(2)}, u32[]{:S(2)}) collective-permute-start(bf16[8,2176]{1,0:T(8,128)(2,1)S(1)} %get-tuple-element.114), channel_id=1, source_target_pairs={{0,6},{1,7},{2,0},{3,1},{4,2},{5,3},{6,4},{7,5},{8,14},{9,15},{10,... | collective-permute-start | bytes 104456 | tf_op jit(solution)/shard_map/ppermute | solution.py:846
  159.4 24.3 %collective-permute-start.15 = (bf16[8,2176]{1,0:T(8,128)(2,1)S(1)}, bf16[8,2176]{1,0:T(8,128)(2,1)S(1)}, u32[]{:S(2)}, u32[]{:S(2)}) collective-permute-start(bf16[8,2176]{1,0:T(8,128)(2,1)S(1)} %get-tuple-element.115), channel_id=1, source_target_pairs={{0,4},{1,5},{2,6},{3,7},{4,0},{5,1},{6,2},{7,3},{8,12},{9,13},{10,... | collective-permute-start | bytes 104456 | tf_op jit(solution)/shard_map/ppermute | solution.py:846
  159.6 24.1 %collective-permute-start.14 = (bf16[8,2176]{1,0:T(8,128)(2,1)S(1)}, bf16[8,2176]{1,0:T(8,128)(2,1)S(1)}, u32[]{:S(2)}, u32[]{:S(2)}) collective-permute-start(bf16[8,2176]{1,0:T(8,128)(2,1)S(1)} %get-tuple-element.113), channel_id=1, source_target_pairs={{0,2},{1,3},{2,4},{3,5},{4,6},{5,7},{6,0},{7,1},{8,10},{9,11},{10,... | collective-permute-start | bytes 104456 | tf_op jit(solution)/shard_map/ppermute | solution.py:846
  162.0 1.6 copy-start.24
  163.6 1.7 copy-start.37
  165.3 1.6 copy-start.41
  183.6 4.6 %collective-permute-start.8 = (bf16[128,1152]{1,0:T(8,128)(2,1)S(1)}, bf16[128,1152]{1,0:T(8,128)(2,1)S(1)}, u32[]{:S(2)}, u32[]{:S(2)}) collective-permute-start(bf16[128,1152]{1,0:T(8,128)(2,1)S(1)} %dynamic-slice_bitcast_fusion.1), channel_id=1, source_target_pairs={{0,1},{1,0},{2,3},{3,2},{4,5},{5,4},{6,7},{7,6},{8,9},{9,8},{10,11... | collective-permute-start | bytes 884744 | tf_op jit(solution)/shard_map/ppermute | solution.py:846
  183.8 9.3 %collective-permute-start.17 = (bf16[1,8,2176]{2,1,0:T(8,128)(2,1)S(1)}, bf16[1,8,2176]{2,1,0:T(8,128)(2,1)S(1)}, u32[]{:S(2)}, u32[]{:S(2)}) collective-permute-start(bf16[1,8,2176]{2,1,0:T(8,128)(2,1)S(1)} %bitcast.107), channel_id=1, source_target_pairs={{0,2},{1,3},{2,4},{3,5},{4,6},{5,7},{6,0},{7,1},{8,10},{9,11},{10,... | collective-permute-start | bytes 104456 | tf_op jit(solution)/shard_map/ppermute | solution.py:846
  185.8 7.3 %collective-permute-start.18 = (bf16[1,8,2176]{2,1,0:T(8,128)(2,1)S(1)}, bf16[1,8,2176]{2,1,0:T(8,128)(2,1)S(1)}, u32[]{:S(2)}, u32[]{:S(2)}) collective-permute-start(bf16[1,8,2176]{2,1,0:T(8,128)(2,1)S(1)} %bitcast.108), channel_id=1, source_target_pairs={{0,4},{1,5},{2,6},{3,7},{4,0},{5,1},{6,2},{7,3},{8,12},{9,13},{10,... | collective-permute-start | bytes 104456 | tf_op jit(solution)/shard_map/ppermute | solution.py:846
  186.9 6.2 %collective-permute-start.19 = (bf16[1,8,2176]{2,1,0:T(8,128)(2,1)S(1)}, bf16[1,8,2176]{2,1,0:T(8,128)(2,1)S(1)}, u32[]{:S(2)}, u32[]{:S(2)}) collective-permute-start(bf16[1,8,2176]{2,1,0:T(8,128)(2,1)S(1)} %bitcast.109), channel_id=1, source_target_pairs={{0,6},{1,7},{2,0},{3,1},{4,2},{5,3},{6,4},{7,5},{8,14},{9,15},{10,... | collective-permute-start | bytes 104456 | tf_op jit(solution)/shard_map/ppermute | solution.py:846
  189.0 15.3 %all-to-all-start.5 = ((bf16[16,8,1152]{2,1,0:T(8,128)(2,1)}), bf16[16,8,1152]{2,1,0:T(8,128)(2,1)S(1)}, u32[]{:S(2)}, u32[]{:S(2)}) async-start(bf16[16,8,1152]{2,1,0:T(8,128)(2,1)} %fusion.3), calls=%async_computation.5 | async-start | bytes 589824 | tf_op jit(solution)/shard_map/all_to_all | solution.py:867
  193.0 5.0 %copy-start.11 = (bf16[16,64,256]{2,1,0:T(8,128)(2,1)S(1)}, bf16[16,64,256]{2,1,0:T(8,128)(2,1)}, u32[]{:S(2)}) copy-start(bf16[16,64,256]{2,1,0:T(8,128)(2,1)} %image_ref.3) | copy-start | bytes 1572868
  193.0 5.0 %copy-start.21 = (f32[16,64,256]{2,1,0:T(8,128)S(1)}, f32[16,64,256]{2,1,0:T(8,128)}, u32[]{:S(2)}) copy-start(f32[16,64,256]{2,1,0:T(8,128)} %copy-done.20) | copy-start | bytes 3145732
  193.1 5.0 %copy-start.31 = (f32[1024,256]{1,0:T(8,128)S(1)}, f32[1024,256]{1,0:T(8,128)}, u32[]{:S(2)}) copy-start(f32[1024,256]{1,0:T(8,128)} %copy-done.30) | copy-start | bytes 3145732
  193.1 15.5 %collective-permute-start.20 = (bf16[4,8,2176]{2,1,0:T(8,128)(2,1)S(1)}, bf16[4,8,2176]{2,1,0:T(8,128)(2,1)S(1)}, u32[]{:S(2)}, u32[]{:S(2)}) collective-permute-start(bf16[4,8,2176]{2,1,0:T(8,128)(2,1)S(1)} %bitcast.116), channel_id=1, source_target_pairs={{0,8},{8,16},{16,24},{24,0},{1,9},{9,17},{17,25},{25,1},{2,10},{10... | collective-permute-start | bytes 417800 | tf_op jit(solution)/shard_map/ppermute | solution.py:846
  195.1 13.5 %collective-permute-start.21 = (bf16[4,8,2176]{2,1,0:T(8,128)(2,1)S(1)}, bf16[4,8,2176]{2,1,0:T(8,128)(2,1)S(1)}, u32[]{:S(2)}, u32[]{:S(2)}) collective-permute-start(bf16[4,8,2176]{2,1,0:T(8,128)(2,1)S(1)} %bitcast.117), channel_id=1, source_target_pairs={{0,16},{8,24},{16,0},{24,8},{1,17},{9,25},{17,1},{25,9},{2,18},{10... | collective-permute-start | bytes 417800 | tf_op jit(solution)/shard_map/ppermute | solution.py:846
  196.6 12.1 %collective-permute-start.22 = (bf16[4,8,2176]{2,1,0:T(8,128)(2,1)S(1)}, bf16[4,8,2176]{2,1,0:T(8,128)(2,1)S(1)}, u32[]{:S(2)}, u32[]{:S(2)}) collective-permute-start(bf16[4,8,2176]{2,1,0:T(8,128)(2,1)S(1)} %bitcast.118), channel_id=1, source_target_pairs={{0,24},{8,0},{16,8},{24,16},{1,25},{9,1},{17,9},{25,17},{2,26},{10... | collective-permute-start | bytes 417800 | tf_op jit(solution)/shard_map/ppermute | solution.py:846
  205.1 13.4 %all-to-all-start.6 = ((bf16[16,8,1152]{2,1,0:T(8,128)(2,1)}), bf16[16,8,1152]{2,1,0:T(8,128)(2,1)S(1)}, u32[]{:S(2)}, u32[]{:S(2)}) async-start(bf16[16,8,1152]{2,1,0:T(8,128)(2,1)} %broadcast_in_dim.17), calls=%async_computation.6 | async-start | bytes 589824 | tf_op jit(solution)/shard_map/all_to_all | solution.py:867
  208.7 10.5 %collective-permute-start.23 = (bf16[16,8,2176]{2,1,0:T(8,128)(2,1)S(1)}, bf16[16,8,2176]{2,1,0:T(8,128)(2,1)S(1)}, u32[]{:S(2)}, u32[]{:S(2)}) collective-permute-start(bf16[16,8,2176]{2,1,0:T(8,128)(2,1)S(1)} %bitcast.114), channel_id=1, source_target_pairs={{0,1},{1,0},{2,3},{3,2},{4,5},{5,4},{6,7},{7,6},{8,9},{9,8},{10,11... | collective-permute-start | bytes 1671176 | tf_op jit(solution)/shard_map/ppermute | solution.py:846
  218.4 2.9 %collective-permute-start.9 = (bf16[128,1152]{1,0:T(8,128)(2,1)S(1)}, bf16[128,1152]{1,0:T(8,128)(2,1)S(1)}, u32[]{:S(2)}, u32[]{:S(2)}) collective-permute-start(bf16[128,1152]{1,0:T(8,128)(2,1)S(1)} %bitcast.104), channel_id=1, source_target_pairs={{0,1},{1,0},{2,3},{3,2},{4,5},{5,4},{6,7},{7,6},{8,9},{9,8},{10,11... | collective-permute-start | bytes 884744 | tf_op jit(solution)/shard_map/ppermute | solution.py:846
  (19 other events, 17.5 us)

commit v4 on v3

--- a/solution.py
+++ b/solution.py
@@ -17,7 +17,8 @@
 GELU_B = GELU_A * 0.044715
 F32 = jnp.float32
 BF16 = jnp.bfloat16
-PARAMS = pltpu.CompilerParams(vmem_limit_bytes=24 * 1024 * 1024)
+PARAMS = pltpu.CompilerParams(vmem_limit_bytes=56 * 1024 * 1024)
+SMALL = pltpu.CompilerParams(vmem_limit_bytes=24 * 1024 * 1024)
 
 
 def estimate(us):
@@ -340,7 +341,7 @@
             jax.ShapeDtypeStruct(image.shape, BF16),
             jax.ShapeDtypeStruct(send, BF16),
         ],
-        compiler_params=PARAMS,
+        compiler_params=SMALL,
         cost_estimate=estimate(5),
         name="mix",
     )(parts, w_squeeze, w_excite, act, image, w_project, gain, after)
@@ -626,7 +627,7 @@
             jax.ShapeDtypeStruct((1, channels), F32),
         ],
         scratch_shapes=[pltpu.VMEM((2, rows, near.shape[1] - expanded), F32)],
-        compiler_params=PARAMS,
+        compiler_params=SMALL,
         cost_estimate=estimate(2),
         name="unpack",
     )(place, near, far)
@@ -799,7 +800,7 @@
         in_specs=[block, whole(gain.shape), block, block],
         out_specs=block,
         out_shape=jax.ShapeDtypeStruct((cells, channels), BF16),
-        compiler_params=PARAMS,
+        compiler_params=SMALL,
         cost_estimate=estimate(4),
         name="image_back",
     )(image, gain, first, mixed)
@@ -888,7 +889,7 @@
         in_specs=[vmem] * size,
         out_specs=vmem,
         out_shape=jax.ShapeDtypeStruct((size,) + blocks.shape, blocks.dtype),
-        compiler_params=PARAMS,
+        compiler_params=SMALL,
         cost_estimate=estimate(1),
         name="stack",
     )(*arrived)
@@ -934,7 +935,7 @@
             jax.ShapeDtypeStruct((halves, count, rows, members), F32),
             jax.ShapeDtypeStruct((expanded // BLOCK, count, rows, channels), F32),
         ],
-        compiler_params=PARAMS,
+        compiler_params=SMALL,
         cost_estimate=estimate(2),
         name="unpack_weights",
     )(places.astype(jnp.int32), near, far)

time: 224 us -> 217 us (0.969)
  local copies, waits for them, and re-layouts: 43.5 us -> 15.7 us
  Pallas kernels: 60.2 us -> 73.8 us
  other arithmetic: 4.93 us -> 9.66 us
  waiting for transfers between devices: 41.1 us -> 44.9 us
    unnamed x108 -> x66, local copies, waits for them, and re-layouts: 36.7 us -> 7.71 us
    all_to_all x3, waiting for transfers between devices: 11 us -> 16.2 us  [swap_groups(): lax.all_to_all(blocks, AXES, split_axis=0, concat_axis=0, tiled=True, axi...]
    pallas_call x1, Pallas kernels: 3.25 us -> 6.63 us  [run_mixed_back(): pl.pallas_call(functools.partial(mixed_back_kernel, stride, cols // SIDE)...]
    pallas_call x1, Pallas kernels: 13.6 us -> 16.4 us  [run_expand_back(): pl.pallas_call(functools.partial(expand_back_kernel, cells_total), grid=(...]
    pallas_call x1, Pallas kernels: 0.74 us -> 3.45 us  [run_attention_weights(): pl.pallas_call(attention_weights_kernel, in_specs=[vmem] * 5, out_specs=v...]
  transfers between devices with their start and end apart: 31 -> 31, of which waited for: 10 -> 10; matrix products, arithmetic and copies ran while one was open for 5% -> 8% of each run, Pallas kernels for 19% -> 24%
where the time goes in v4:
time: 217 us; the launch traced here: 216 us
  Pallas kernels  73.8 us (34%)
  starting transfers between devices  68 us (31%)
  waiting for transfers between devices  44.9 us (21%)
  local copies, waits for them, and re-layouts  15.7 us (7%)
  other arithmetic  9.66 us (4%)
  matrix products  2.21 us (1%)
    ppermute x16, starting transfers between devices, send_on(): return lax.ppermute(v, axis, pairs)  21.5 us
    ppermute x8, starting transfers between devices, shift(): return lax.ppermute(cells, axis, pairs)  17.2 us
    pallas_call x1, Pallas kernels, run_expand_back(): pl.pallas_call(functools.partial(expand_back_kernel, cells_total), grid=(...  16.4 us
    all_to_all x3, waiting for transfers between devices, swap_groups(): lax.all_to_all(blocks, AXES, split_axis=0, concat_axis=0, tiled=True, axi...  16.2 us
    all_to_all x3, starting transfers between devices, swap_groups(): lax.all_to_all(blocks, AXES, split_axis=0, concat_axis=0, tiled=True, axi...  12.3 us
    pallas_call x1, Pallas kernels, run_attention(): pl.pallas_call(functools.partial(attention_kernel, members, heads, lines)...  11.8 us
    all_to_all x2, waiting for transfers between devices, around(): lax.all_to_all(blocks, AXES, split_axis=0, concat_axis=0, tiled=True, axi...  11.2 us
    pallas_call x1, Pallas kernels, run_slope(): pl.pallas_call(slope_kernel, grid=(expanded // BLOCK,), in_specs=[pl.Bloc...  10.5 us
  transfers between devices with their start and end apart: 31, of which 10 were waited for; matrix products, arithmetic and copies ran while one was open for 8% of the time, Pallas kernels for 24%

profile of v4, /device:TPU:0, one launch (start us, length us, event | category | flops | bytes accessed | tf_op | source)
XLA Modules:
  0.0 215.6 jit_solution(172882030863314548)
XLA Ops:
  0.7 0.9 fusion.15
  1.6 4.8 %collective-permute-start = (bf16[2,64,256]{2,1,0:T(8,128)(2,1)S(1)}, bf16[2,64,256]{2,1,0:T(8,128)(2,1)S(1)}, u32[]{:S(2)}, u32[]{:S(2)}) collective-permute-start(bf16[2,64,256]{2,1,0:T(8,128)(2,1)S(1)} %get-tuple-element.112), channel_id=1, source_target_pairs={{0,8},{8,16},{16,24},{1,9},{9,17},{17,25},{2,10},{10,18},{18,26},{... | collective-permute-start | bytes 196616 | tf_op jit(solution)/shard_map/ppermute | solution.py:812
  6.4 1.3 collective-permute-start.1
  7.7 1.9 copy.45
  9.6 7.0 %all-to-all-start.1 = ((bf16[32,2,16,256]{3,2,1,0:T(8,128)(2,1)}), bf16[32,2,16,256]{3,2,1,0:T(8,128)(2,1)S(1)}, u32[]{:S(2)}, u32[]{:S(2)}) async-start(bf16[32,2,16,256]{3,2,1,0:T(8,128)(2,1)} %bitcast.3), calls=%async_computation.1 | async-start | bytes 1048576 | tf_op jit(solution)/shard_map/all_to_all | solution.py:953
  17.2 7.4 %expand.1 = (bf16[1024,256]{1,0:T(8,128)(2,1)}, bf16[256,1024]{1,0:T(8,128)(2,1)}, bf16[16,64,1024]{2,1,0:T(8,128)(2,1)}, bf16[16,64,1024]{2,1,0:T(8,128)(2,1)}) custom-call(bf16[16,64,256]{2,1,0:T(8,128)(2,1)} %image_ref.3, bf16[1,256]{1,0:T(2,128)(2,1)} %reshape.133.gain_ref, bf16[256,1024]{1,0:T(8,128)(2,1)} %w_exp_ref.5), custom_call_target="tpu_custom_call" | custom-call | flops 15399999488 | bytes 50400000 | tf_op jit(solution)/shard_map/expand/pallas_call | solution.py:114
  24.8 2.2 %collective-permute-start.3 = (bf16[20,2,256]{2,0,1:T(8,128)(2,1)S(1)}, bf16[20,2,256]{2,0,1:T(8,128)(2,1)S(1)}, u32[]{:S(2)}, u32[]{:S(2)}) collective-permute-start(bf16[20,2,256]{2,0,1:T(8,128)(2,1)S(1)} %pad_maximum_fusion.4), channel_id=1, source_target_pairs={{0,1},{1,2},{2,3},{3,4},{4,5},{5,6},{6,7},{8,9},{9,10},{10,11},{11... | collective-permute-start | bytes 61448 | tf_op jit(solution)/shard_map/ppermute | solution.py:812
  27.0 1.3 collective-permute-start.2
  28.4 2.8 %collective-permute-done.2 = bf16[20,2,256]{2,0,1:T(8,128)(2,1)S(1)} collective-permute-done((bf16[20,2,256]{2,0,1:T(8,128)(2,1)S(1)}, bf16[20,2,256]{2,0,1:T(8,128)(2,1)S(1)}, u32[]{:S(2)}, u32[]{:S(2)}) %collective-permute-start.2) | collective-permute-done | bytes 20512 | tf_op jit(solution)/shard_map/ppermute | solution.py:812
  32.0 8.9 %depthwise.1 = (bf16[416,1024]{1,0:T(8,128)(2,1)}, bf16[16,64,1024]{2,1,0:T(8,128)(2,1)}, f32[32,1,1024]{2,1,0:T(1,128)}) custom-call(bf16[2,64,256]{2,1,0:T(8,128)(2,1)} %copy-done.25, bf16[2,64,256]{2,1,0:T(8,128)(2,1)} %copy-done.26, bf16[160,256]{1,0:T(8,128)(2,1)} %maximum_bitcast_fusion.side_ref, bf16[1,256]{1,0:T(2,128)(2,1)} %reshape.133.gain_ref, ...), custom_call_target="tpu_custom_call" | custom-call | flops 1100000000 | bytes 3600000 | tf_op jit(solution)/shard_map/depthwise/pallas_call | solution.py:206
  40.9 6.8 %all-to-all-start = ((f32[32,1,1024]{2,1,0:T(1,128)}), f32[32,1,1024]{2,1,0:T(1,128)S(1)}, u32[]{:S(2)}, u32[]{:S(2)}) async-start(f32[32,1,1024]{2,1,0:T(1,128)} %get-tuple-element.61), calls=%async_computation | async-start | bytes 262144 | tf_op jit(solution)/shard_map/all_to_all | solution.py:835
  48.8 0.8 pad_maximum_fusion.2.bias_ref
  49.9 6.0 %all-to-all-done.parts_ref = f32[32,1,1024]{2,1,0:T(1,128)S(1)} async-done(((f32[32,1,1024]{2,1,0:T(1,128)}), f32[32,1,1024]{2,1,0:T(1,128)S(1)}, u32[]{:S(2)}, u32[]{:S(2)}) %all-to-all-start) | async-done | bytes 131104 | tf_op jit(solution)/shard_map/all_to_all | solution.py:835
  55.9 1.6 copy-done.13
  57.5 3.4 %mix.1 = (f32[1,1024]{1,0:T(1,128)S(1)}, f32[1,64]{1,0:T(1,128)S(1)}, f32[1,1024]{1,0:T(1,128)S(1)}, bf16[16,64,256]{2,1,0:T(8,128)(2,1)S(1)}, bf16[32,2,16,256]{3,2,1,0:T(8,128)(2,1)}) custom-call(f32[32,1,1024]{2,1,0:T(1,128)S(1)} %all-to-all-done.parts_ref, bf16[1024,64]{1,0:T(8,128)(2,1)S(1)} %copy.47.w_sq_ref, bf16[64,1024]{1,0:T(8,128)(2,1)S(1)} %copy-done.7, ...), custom_call_target="tpu_custom_call" | custom-call | flops 5500000256 | bytes 18000000 | tf_op jit(solution)/shard_map/mix/pallas_call | solution.py:325
  60.9 0.8 copy-done.3
  62.8 2.6 %all-to-all-start.2 = ((bf16[32,2,16,256]{3,2,1,0:T(8,128)(2,1)}), bf16[32,2,16,256]{3,2,1,0:T(8,128)(2,1)S(1)}, u32[]{:S(2)}, u32[]{:S(2)}) async-start(bf16[32,2,16,256]{3,2,1,0:T(8,128)(2,1)} %get-tuple-element.64), calls=%async_computation.2 | async-start | bytes 1048576 | tf_op jit(solution)/shard_map/all_to_all | solution.py:953
  65.4 10.5 %slope.1 = (bf16[18,64,1024]{2,1,0:T(8,128)(2,1)}, f32[18,8,1024]{2,1,0:T(8,128)}) custom-call(f32[4]{0:T(128)} %add_convert_fusion.flags_ref, bf16[416,1024]{1,0:T(8,128)(2,1)} %get-tuple-element.65.ring_ref, bf16[3,3,1024]{2,1,0:T(4,128)(2,1)} %w_dep_ref.5, bf16[16,64,1024]{2,1,0:T(8,128)(2,1)} %get-tuple-element.60.spread_ref), custom_call_target="tpu_custom_call" | custom-call | flops 14300000256 | bytes 46800000 | tf_op jit(solution)/shard_map/slope/pallas_call | solution.py:266
  75.9 1.1 convolution_convert_fusion.att_grad_ref
  77.0 4.8 %all-to-all-done.2 = bf16[32,2,16,256]{3,2,1,0:T(8,128)(2,1)S(1)} async-done(((bf16[32,2,16,256]{3,2,1,0:T(8,128)(2,1)}), bf16[32,2,16,256]{3,2,1,0:T(8,128)(2,1)S(1)}, u32[]{:S(2)}, u32[]{:S(2)}) %all-to-all-start.2) | async-done | bytes 524320 | tf_op jit(solution)/shard_map/all_to_all | solution.py:953
  81.7 0.8 copy-done.20
  82.5 11.8 %attention.1 = (bf16[1024,256]{1,0:T(8,128)(2,1)}, bf16[1024,256]{1,0:T(8,128)(2,1)}, bf16[1024,256]{1,0:T(8,128)(2,1)}, bf16[1024,768]{1,0:T(8,128)(2,1)}, f32[2,256,64]{2,1,0:T(8,128)}) custom-call(bf16[1024,256]{1,0:T(8,128)(2,1)} %bitcast.129, bf16[1024,256]{1,0:T(8,128)(2,1)} %convolution_convert_fusion.att_grad_ref, bf16[256,768]{1,0:T(8,128)(2,1)} %w_qkv_ref.1, ...), custom_call_target="tpu_custom_call" | custom-call | flops 15399999488 | bytes 50400000 | tf_op jit(solution)/shard_map/attention/pallas_call | solution.py:462
  94.3 2.7 %all-to-all-start.3 = ((bf16[32,2,16,256]{3,2,1,0:T(8,128)(2,1)}), bf16[32,2,16,256]{3,2,1,0:T(8,128)(2,1)S(1)}, u32[]{:S(2)}, u32[]{:S(2)}) async-start(bf16[32,2,16,256]{3,2,1,0:T(8,128)(2,1)} %bitcast.127), calls=%async_computation.3 | async-start | bytes 1048576 | tf_op jit(solution)/shard_map/all_to_all | solution.py:953
  97.1 1.0 copy.50
  98.6 3.4 %attention_weights.1 = bf16[256,1152]{1,0:T(8,128)(2,1)} custom-call(bf16[1024,256]{1,0:T(8,128)(2,1)} %get-tuple-element.71.x_ref, bf16[1024,768]{1,0:T(8,128)(2,1)} %get-tuple-element.72.packed_grad_ref, bf16[1024,256]{1,0:T(8,128)(2,1)} %get-tuple-element.69.att_ref, bf16[1024,256]{1,0:T(8,128)(2,1)} %bitcast.95, f32[2,256,64]{2,1,0:T(8,128)} %get-tuple-element.73.bias_ref), custom_call_target="tpu_custom_call" | custom-call | flops 5500000256 | bytes 18000000 | tf_op jit(solution)/shard_map/attention_weights/pallas_call | solution.py:500
  102.0 11.4 %all-to-all-done.3.recv_ref = bf16[32,2,16,256]{3,2,1,0:T(8,128)(2,1)S(1)} async-done(((bf16[32,2,16,256]{3,2,1,0:T(8,128)(2,1)}), bf16[32,2,16,256]{3,2,1,0:T(8,128)(2,1)S(1)}, u32[]{:S(2)}, u32[]{:S(2)}) %all-to-all-start.3) | async-done | bytes 524320 | tf_op jit(solution)/shard_map/all_to_all | solution.py:953
  113.4 0.8 copy-done.18
  114.2 6.6 %mixed_back.1 = (f32[16,64,256]{2,1,0:T(8,128)}, bf16[16,64,256]{2,1,0:T(8,128)(2,1)}, f32[1,256]{1,0:T(1,128)}, bf16[256,1024]{1,0:T(8,128)(2,1)}, bf16[32,8,256]{2,1,0:T(8,128)(2,1)}) custom-call(bf16[32,2,16,256]{3,2,1,0:T(8,128)(2,1)} %copy-done.18, bf16[16,64,256]{2,1,0:T(8,128)(2,1)} %copy-done.3, bf16[16,64,256]{2,1,0:T(8,128)(2,1)} %cot_ref.1, ...), custom_call_target="tpu_custom_call" | custom-call | flops 7699999744 | bytes 25200000 | tf_op jit(solution)/shard_map/mixed_back/pallas_call | solution.py:563
  121.6 0.9 fusion.12
  122.6 1.8 pad_maximum_fusion.1
  124.4 2.6 %all-to-all-start.4 = ((bf16[32,40,256]{2,1,0:T(8,128)(2,1)}), bf16[32,40,256]{2,1,0:T(8,128)(2,1)S(1)}, u32[]{:S(2)}, u32[]{:S(2)}) async-start(bf16[32,40,256]{2,1,0:T(8,128)(2,1)} %pad_maximum_fusion.1), calls=%async_computation.4 | async-start | bytes 1310720 | tf_op jit(solution)/shard_map/all_to_all | solution.py:835
  127.0 3.5 %collective-permute-start.4 = (bf16[1,64,256]{2,1,0:T(8,128)(2,1)S(1)}, bf16[1,64,256]{2,1,0:T(8,128)(2,1)S(1)}, u32[]{:S(2)}, u32[]{:S(2)}) collective-permute-start(bf16[1,64,256]{2,1,0:T(8,128)(2,1)S(1)} %get-tuple-element.108), channel_id=1, source_target_pairs={{0,8},{8,16},{16,24},{1,9},{9,17},{17,25},{2,10},{10,18},{18,26},{... | collective-permute-start | bytes 98312 | tf_op jit(solution)/shard_map/ppermute | solution.py:812
  130.6 1.3 collective-permute-start.5
  131.9 1.1 pad_maximum_fusion
  133.2 3.3 %collective-permute-done.5.down_ref = bf16[1,64,256]{2,1,0:T(8,128)(2,1)S(1)} collective-permute-done((bf16[1,64,256]{2,1,0:T(8,128)(2,1)S(1)}, bf16[1,64,256]{2,1,0:T(8,128)(2,1)S(1)}, u32[]{:S(2)}, u32[]{:S(2)}) %collective-permute-start.5) | collective-permute-done | bytes 32800 | tf_op jit(solution)/shard_map/ppermute | solution.py:812
  136.5 1.3 collective-permute-start.7
  137.9 1.5 collective-permute-start.6
  139.6 1.5 collective-permute-start.13
  141.0 2.5 %collective-permute-start.12 = (bf16[32,2176]{1,0:T(8,128)(2,1)S(1)}, bf16[32,2176]{1,0:T(8,128)(2,1)S(1)}, u32[]{:S(2)}, u32[]{:S(2)}) collective-permute-start(bf16[32,2176]{1,0:T(8,128)(2,1)S(1)} %get-tuple-element.104), channel_id=1, source_target_pairs={{0,16},{8,24},{16,0},{24,8},{1,17},{9,25},{17,1},{25,9},{2,18},{10... | collective-permute-start | bytes 417800 | tf_op jit(solution)/shard_map/ppermute | solution.py:847
  144.3 1.5 collective-permute-done.13
  145.8 1.5 collective-permute-done.12
  147.3 2.4 %collective-permute-done.11 = bf16[32,2176]{1,0:T(8,128)(2,1)S(1)} collective-permute-done((bf16[32,2176]{1,0:T(8,128)(2,1)S(1)}, bf16[32,2176]{1,0:T(8,128)(2,1)S(1)}, u32[]{:S(2)}, u32[]{:S(2)}) %collective-permute-start.11) | collective-permute-done | bytes 139296 | tf_op jit(solution)/shard_map/ppermute | solution.py:847
  149.7 6.4 %collective-permute-start.16 = (bf16[8,2176]{1,0:T(8,128)(2,1)S(1)}, bf16[8,2176]{1,0:T(8,128)(2,1)S(1)}, u32[]{:S(2)}, u32[]{:S(2)}) collective-permute-start(bf16[8,2176]{1,0:T(8,128)(2,1)S(1)} %get-tuple-element.114), channel_id=1, source_target_pairs={{0,6},{1,7},{2,0},{3,1},{4,2},{5,3},{6,4},{7,5},{8,14},{9,15},{10,... | collective-permute-start | bytes 104456 | tf_op jit(solution)/shard_map/ppermute | solution.py:847
  156.4 1.3 collective-permute-start.14
  157.7 0.8 copy-done.16
  158.5 16.4 %expand_back.1 = (bf16[256,1152]{1,0:T(8,128)(2,1)}, f32[1024,256]{1,0:T(8,128)}, f32[1,1024]{1,0:T(1,128)}, f32[1,64]{1,0:T(1,128)}) custom-call(bf16[32,40,256]{2,1,0:T(8,128)(2,1)} %copy-done.16, f32[1,64]{1,0:T(1,128)} %copy-done.11, f32[1,1024]{1,0:T(1,128)} %copy-done.15, bf16[1024,64]{1,0:T(8,128)(2,1)} %copy-done.5, bf16[64,1024]{1,0:T(8,128)(2,1)} %w_ex_ref.3, ...), custom_call_target="tpu_custom_call" | custom-call | flops 15399999488 | bytes 50400000 | tf_op jit(solution)/shard_map/expand_back/pallas_call | solution.py:744
  174.9 1.0 dynamic-slice_bitcast_fusion.1
  176.0 2.0 collective-permute-start.17
  178.1 1.1 collective-permute-start.18
  179.2 1.3 collective-permute-start.19
  180.5 1.8 fusion.3
  182.3 4.0 %all-to-all-start.5 = ((bf16[16,8,1152]{2,1,0:T(8,128)(2,1)}), bf16[16,8,1152]{2,1,0:T(8,128)(2,1)S(1)}, u32[]{:S(2)}, u32[]{:S(2)}) async-start(bf16[16,8,1152]{2,1,0:T(8,128)(2,1)} %fusion.3), calls=%async_computation.5 | async-start | bytes 589824 | tf_op jit(solution)/shard_map/all_to_all | solution.py:868
  186.4 2.0 collective-permute-start.20
  188.3 1.5 collective-permute-start.21
  189.8 1.5 collective-permute-start.22
  191.3 2.3 %image_back.1 = bf16[1024,256]{1,0:T(8,128)(2,1)} custom-call(bf16[1024,256]{1,0:T(8,128)(2,1)S(1)} %bitcast.99, bf16[1,256]{1,0:T(2,128)(2,1)S(1)} %copy-done.9, f32[1024,256]{1,0:T(8,128)S(1)} %copy-done.14, f32[1024,256]{1,0:T(8,128)S(1)} %bitcast.111), custom_call_target="tpu_custom_call" | custom-call | flops 4400000000 | bytes 14400000 | tf_op jit(solution)/shard_map/image_back/pallas_call | solution.py:797
  193.5 4.0 %all-to-all-done.5 = bf16[16,8,1152]{2,1,0:T(8,128)(2,1)S(1)} async-done(((bf16[16,8,1152]{2,1,0:T(8,128)(2,1)}), bf16[16,8,1152]{2,1,0:T(8,128)(2,1)S(1)}, u32[]{:S(2)}, u32[]{:S(2)}) %all-to-all-start.5) | async-done | bytes 294944 | tf_op jit(solution)/shard_map/all_to_all | solution.py:868
  198.3 3.5 %all-to-all-start.6 = ((bf16[16,8,1152]{2,1,0:T(8,128)(2,1)}), bf16[16,8,1152]{2,1,0:T(8,128)(2,1)S(1)}, u32[]{:S(2)}, u32[]{:S(2)}) async-start(bf16[16,8,1152]{2,1,0:T(8,128)(2,1)} %broadcast_in_dim.17), calls=%async_computation.6 | async-start | bytes 589824 | tf_op jit(solution)/shard_map/all_to_all | solution.py:868
  202.5 0.8 broadcast_multiply_fusion.1
  203.4 1.1 fusion
  204.5 7.2 %all-to-all-done.6 = bf16[16,8,1152]{2,1,0:T(8,128)(2,1)S(1)} async-done(((bf16[16,8,1152]{2,1,0:T(8,128)(2,1)}), bf16[16,8,1152]{2,1,0:T(8,128)(2,1)S(1)}, u32[]{:S(2)}, u32[]{:S(2)}) %all-to-all-start.6) | async-done | bytes 294944 | tf_op jit(solution)/shard_map/all_to_all | solution.py:868
  211.7 0.8 broadcast_multiply_fusion
  212.5 2.1 unpack_weights.1
  214.6 1.1 unpack.1
  (129 shorter events, 8.1 us)
Async XLA Ops:
  0.6 75.2 %copy-start = (bf16[256,256]{1,0:T(8,128)(2,1)S(1)}, bf16[256,256]{1,0:T(8,128)(2,1)}, u32[]{:S(2)}) copy-start(bf16[256,256]{1,0:T(8,128)(2,1)} %param.22) | copy-start | bytes 393220
  0.7 16.0 %copy-start.29 = (bf16[256]{0:T(256)(128)(2,1)S(1)}, bf16[256]{0:T(256)(128)(2,1)}, u32[]{:S(2)}) copy-start(bf16[256]{0:T(256)(128)(2,1)} %param.14) | copy-start | bytes 1540
  1.6 23.1 %collective-permute-start = (bf16[2,64,256]{2,1,0:T(8,128)(2,1)S(1)}, bf16[2,64,256]{2,1,0:T(8,128)(2,1)S(1)}, u32[]{:S(2)}, u32[]{:S(2)}) collective-permute-start(bf16[2,64,256]{2,1,0:T(8,128)(2,1)S(1)} %get-tuple-element.112), channel_id=1, source_target_pairs={{0,8},{8,16},{16,24},{1,9},{9,17},{17,25},{2,10},{10,18},{18,26},{... | collective-permute-start | bytes 196616 | tf_op jit(solution)/shard_map/ppermute | solution.py:812
  6.4 18.3 %collective-permute-start.1 = (bf16[2,64,256]{2,1,0:T(8,128)(2,1)S(1)}, bf16[2,64,256]{2,1,0:T(8,128)(2,1)S(1)}, u32[]{:S(2)}, u32[]{:S(2)}) collective-permute-start(bf16[2,64,256]{2,1,0:T(8,128)(2,1)S(1)} %get-tuple-element.111), channel_id=1, source_target_pairs={{8,0},{16,8},{24,16},{9,1},{17,9},{25,17},{10,2},{18,10},{26,18},{... | collective-permute-start | bytes 196616 | tf_op jit(solution)/shard_map/ppermute | solution.py:812
  9.6 31.3 %all-to-all-start.1 = ((bf16[32,2,16,256]{3,2,1,0:T(8,128)(2,1)}), bf16[32,2,16,256]{3,2,1,0:T(8,128)(2,1)S(1)}, u32[]{:S(2)}, u32[]{:S(2)}) async-start(bf16[32,2,16,256]{3,2,1,0:T(8,128)(2,1)} %bitcast.3), calls=%async_computation.1 | async-start | bytes 1048576 | tf_op jit(solution)/shard_map/all_to_all | solution.py:953
  17.2 7.4 %copy-start.6 = (bf16[16,64,256]{2,1,0:T(8,128)(2,1)S(1)}, bf16[16,64,256]{2,1,0:T(8,128)(2,1)}, u32[]{:S(2)}) copy-start(bf16[16,64,256]{2,1,0:T(8,128)(2,1)} %image_ref.3) | copy-start | bytes 1572868
  24.7 7.3 %copy-start.25 = (bf16[2,64,256]{2,1,0:T(8,128)(2,1)}, bf16[2,64,256]{2,1,0:T(8,128)(2,1)S(1)}, u32[]{:S(2)}) copy-start(bf16[2,64,256]{2,1,0:T(8,128)(2,1)S(1)} %collective-permute-done.up_ref) | copy-start | bytes 196612
  24.7 7.3 %copy-start.26 = (bf16[2,64,256]{2,1,0:T(8,128)(2,1)}, bf16[2,64,256]{2,1,0:T(8,128)(2,1)S(1)}, u32[]{:S(2)}) copy-start(bf16[2,64,256]{2,1,0:T(8,128)(2,1)S(1)} %collective-permute-done.1.down_ref) | copy-start | bytes 196612
  24.8 3.6 %collective-permute-start.3 = (bf16[20,2,256]{2,0,1:T(8,128)(2,1)S(1)}, bf16[20,2,256]{2,0,1:T(8,128)(2,1)S(1)}, u32[]{:S(2)}, u32[]{:S(2)}) collective-permute-start(bf16[20,2,256]{2,0,1:T(8,128)(2,1)S(1)} %pad_maximum_fusion.4), channel_id=1, source_target_pairs={{0,1},{1,2},{2,3},{3,4},{4,5},{5,6},{6,7},{8,9},{9,10},{10,11},{11... | collective-permute-start | bytes 61448 | tf_op jit(solution)/shard_map/ppermute | solution.py:812
  27.0 4.2 %collective-permute-start.2 = (bf16[20,2,256]{2,0,1:T(8,128)(2,1)S(1)}, bf16[20,2,256]{2,0,1:T(8,128)(2,1)S(1)}, u32[]{:S(2)}, u32[]{:S(2)}) collective-permute-start(bf16[20,2,256]{2,0,1:T(8,128)(2,1)S(1)} %pad_maximum_fusion.3), channel_id=1, source_target_pairs={{1,0},{2,1},{3,2},{4,3},{5,4},{6,5},{7,6},{9,8},{10,9},{11,10},{12... | collective-permute-start | bytes 61448 | tf_op jit(solution)/shard_map/ppermute | solution.py:812
  32.0 15.8 %copy-start.22 = (bf16[1024,64]{0,1:T(8,128)(2,1)S(1)}, bf16[1024,64]{0,1:T(8,128)(2,1)}, u32[]{:S(2)}) copy-start(bf16[1024,64]{0,1:T(8,128)(2,1)} %param.17) | copy-start | bytes 393220
  32.0 15.9 %copy-start.30 = (bf16[256]{0:T(256)(128)(2,1)S(1)}, bf16[256]{0:T(256)(128)(2,1)}, u32[]{:S(2)}) copy-start(bf16[256]{0:T(256)(128)(2,1)} %param.20) | copy-start | bytes 1540
  32.0 16.0 %copy-start.21 = (f32[8,64,64]{2,1,0:T(8,128)S(1)}, f32[8,64,64]{2,1,0:T(8,128)}, u32[]{:S(2)}) copy-start(f32[8,64,64]{2,1,0:T(8,128)} %param.23) | copy-start | bytes 393220
  40.9 15.0 %all-to-all-start = ((f32[32,1,1024]{2,1,0:T(1,128)}), f32[32,1,1024]{2,1,0:T(1,128)S(1)}, u32[]{:S(2)}, u32[]{:S(2)}) async-start(f32[32,1,1024]{2,1,0:T(1,128)} %get-tuple-element.61), calls=%async_computation | async-start | bytes 262144 | tf_op jit(solution)/shard_map/all_to_all | solution.py:835
  47.7 8.2 %copy-start.2 = (bf16[1024,256]{1,0:T(8,128)(2,1)S(1)}, bf16[1024,256]{1,0:T(8,128)(2,1)}, u32[]{:S(2)}) copy-start(bf16[1024,256]{1,0:T(8,128)(2,1)} %w_proj_ref.1) | copy-start | bytes 1572868
  47.8 8.2 %copy-start.7 = (bf16[64,1024]{1,0:T(8,128)(2,1)S(1)}, bf16[64,1024]{1,0:T(8,128)(2,1)}, u32[]{:S(2)}) copy-start(bf16[64,1024]{1,0:T(8,128)(2,1)} %w_ex_ref.3) | copy-start | bytes 393220
  48.0 12.9 %copy-start.5 = (bf16[1024,64]{1,0:T(8,128)(2,1)}, bf16[1024,64]{1,0:T(8,128)(2,1)S(1)}, u32[]{:S(2)}) copy-start(bf16[1024,64]{1,0:T(8,128)(2,1)S(1)} %copy.47.w_sq_ref) | copy-start | bytes 393220
  48.0 12.9 %copy-start.10 = (bf16[1,256]{1,0:T(2,128)(2,1)}, bf16[1,256]{1,0:T(2,128)(2,1)S(1)}, u32[]{:S(2)}) copy-start(bf16[1,256]{1,0:T(2,128)(2,1)S(1)} %reshape.135.gain_ref) | copy-start | bytes 1540
  49.9 26.0 %copy-start.1 = (bf16[16,4,2,8,256]{4,3,2,1,0:T(8,128)(2,1)}, bf16[16,4,2,8,256]{4,3,2,1,0:T(8,128)(2,1)S(1)}, u32[]{:S(2)}) copy-start(bf16[16,4,2,8,256]{4,3,2,1,0:T(8,128)(2,1)S(1)} %copy.46) | copy-start | bytes 1572868
  55.9 1.6 copy-start.13
  60.9 0.8 copy-start.3
  61.7 0.5 copy-start.11
  62.2 0.6 copy-start.15
  62.8 19.0 %all-to-all-start.2 = ((bf16[32,2,16,256]{3,2,1,0:T(8,128)(2,1)}), bf16[32,2,16,256]{3,2,1,0:T(8,128)(2,1)S(1)}, u32[]{:S(2)}, u32[]{:S(2)}) async-start(bf16[32,2,16,256]{3,2,1,0:T(8,128)(2,1)} %get-tuple-element.64), calls=%async_computation.2 | async-start | bytes 1048576 | tf_op jit(solution)/shard_map/all_to_all | solution.py:953
  81.7 0.8 copy-start.20
  94.3 3.9 %copy-start.19 = (bf16[1024,256]{1,0:T(8,128)(2,1)S(1)}, bf16[1024,256]{1,0:T(8,128)(2,1)}, u32[]{:S(2)}) copy-start(bf16[1024,256]{1,0:T(8,128)(2,1)} %get-tuple-element.69.att_ref) | copy-start | bytes 1572868
  94.3 19.1 %all-to-all-start.3 = ((bf16[32,2,16,256]{3,2,1,0:T(8,128)(2,1)}), bf16[32,2,16,256]{3,2,1,0:T(8,128)(2,1)S(1)}, u32[]{:S(2)}, u32[]{:S(2)}) async-start(bf16[32,2,16,256]{3,2,1,0:T(8,128)(2,1)} %bitcast.127), calls=%async_computation.3 | async-start | bytes 1048576 | tf_op jit(solution)/shard_map/all_to_all | solution.py:953
  113.4 0.8 copy-start.18
  122.5 9.3 %copy-start.17 = (bf16[256,1152]{1,0:T(8,128)(2,1)S(1)}, bf16[256,1152]{1,0:T(8,128)(2,1)}, u32[]{:S(2)}) copy-start(bf16[256,1152]{1,0:T(8,128)(2,1)} %attention_weights.1) | copy-start | bytes 1769476
  124.4 33.3 %all-to-all-start.4 = ((bf16[32,40,256]{2,1,0:T(8,128)(2,1)}), bf16[32,40,256]{2,1,0:T(8,128)(2,1)S(1)}, u32[]{:S(2)}, u32[]{:S(2)}) async-start(bf16[32,40,256]{2,1,0:T(8,128)(2,1)} %pad_maximum_fusion.1), calls=%async_computation.4 | async-start | bytes 1310720 | tf_op jit(solution)/shard_map/all_to_all | solution.py:835
  127.0 6.0 %collective-permute-start.4 = (bf16[1,64,256]{2,1,0:T(8,128)(2,1)S(1)}, bf16[1,64,256]{2,1,0:T(8,128)(2,1)S(1)}, u32[]{:S(2)}, u32[]{:S(2)}) collective-permute-start(bf16[1,64,256]{2,1,0:T(8,128)(2,1)S(1)} %get-tuple-element.108), channel_id=1, source_target_pairs={{0,8},{8,16},{16,24},{1,9},{9,17},{17,25},{2,10},{10,18},{18,26},{... | collective-permute-start | bytes 98312 | tf_op jit(solution)/shard_map/ppermute | solution.py:812
  130.6 5.9 %collective-permute-start.5 = (bf16[1,64,256]{2,1,0:T(8,128)(2,1)S(1)}, bf16[1,64,256]{2,1,0:T(8,128)(2,1)S(1)}, u32[]{:S(2)}, u32[]{:S(2)}) collective-permute-start(bf16[1,64,256]{2,1,0:T(8,128)(2,1)S(1)} %get-tuple-element.107), channel_id=1, source_target_pairs={{8,0},{16,8},{24,16},{9,1},{17,9},{25,17},{10,2},{18,10},{26,18},{... | collective-permute-start | bytes 98312 | tf_op jit(solution)/shard_map/ppermute | solution.py:812
  133.0 6.5 %copy-start.27 = (bf16[1,64,256]{2,1,0:T(8,128)(2,1)}, bf16[1,64,256]{2,1,0:T(8,128)(2,1)S(1)}, u32[]{:S(2)}) copy-start(bf16[1,64,256]{2,1,0:T(8,128)(2,1)S(1)} %collective-permute-done.4.up_ref) | copy-start | bytes 98308
  133.1 6.3 %collective-permute-start.10 = (bf16[128,2176]{1,0:T(8,128)(2,1)S(1)}, bf16[128,2176]{1,0:T(8,128)(2,1)S(1)}, u32[]{:S(2)}, u32[]{:S(2)}) collective-permute-start(bf16[128,2176]{1,0:T(8,128)(2,1)S(1)} %dynamic-slice_bitcast_fusion), channel_id=1, source_target_pairs={{0,1},{1,0},{2,3},{3,2},{4,5},{5,4},{6,7},{7,6},{8,9},{9,8},{10,11... | collective-permute-start | bytes 1671176 | tf_op jit(solution)/shard_map/ppermute | solution.py:847
  136.5 7.8 %copy-start.28 = (bf16[1,64,256]{2,1,0:T(8,128)(2,1)}, bf16[1,64,256]{2,1,0:T(8,128)(2,1)S(1)}, u32[]{:S(2)}) copy-start(bf16[1,64,256]{2,1,0:T(8,128)(2,1)S(1)} %collective-permute-done.5.down_ref) | copy-start | bytes 98308
  136.5 7.0 %collective-permute-start.7 = (bf16[18,1,256]{2,1,0:T(2,128)(2,1)S(1)}, bf16[18,1,256]{2,1,0:T(2,128)(2,1)S(1)}, u32[]{:S(2)}, u32[]{:S(2)}) collective-permute-start(bf16[18,1,256]{2,1,0:T(2,128)(2,1)S(1)} %pad_maximum_fusion.6), channel_id=1, source_target_pairs={{0,1},{1,2},{2,3},{3,4},{4,5},{5,6},{6,7},{8,9},{9,10},{10,11},{11... | collective-permute-start | bytes 27656 | tf_op jit(solution)/shard_map/ppermute | solution.py:812
  137.9 5.7 %collective-permute-start.6 = (bf16[18,1,256]{2,1,0:T(2,128)(2,1)S(1)}, bf16[18,1,256]{2,1,0:T(2,128)(2,1)S(1)}, u32[]{:S(2)}, u32[]{:S(2)}) collective-permute-start(bf16[18,1,256]{2,1,0:T(2,128)(2,1)S(1)} %pad_maximum_fusion.5), channel_id=1, source_target_pairs={{1,0},{2,1},{3,2},{4,3},{5,4},{6,5},{7,6},{9,8},{10,9},{11,10},{12... | collective-permute-start | bytes 27656 | tf_op jit(solution)/shard_map/ppermute | solution.py:812
  139.6 6.2 %collective-permute-start.13 = (bf16[32,2176]{1,0:T(8,128)(2,1)S(1)}, bf16[32,2176]{1,0:T(8,128)(2,1)S(1)}, u32[]{:S(2)}, u32[]{:S(2)}) collective-permute-start(bf16[32,2176]{1,0:T(8,128)(2,1)S(1)} %get-tuple-element.103), channel_id=1, source_target_pairs={{0,24},{8,0},{16,8},{24,16},{1,25},{9,1},{17,9},{25,17},{2,26},{10... | collective-permute-start | bytes 417800 | tf_op jit(solution)/shard_map/ppermute | solution.py:847
  141.0 6.2 %collective-permute-start.12 = (bf16[32,2176]{1,0:T(8,128)(2,1)S(1)}, bf16[32,2176]{1,0:T(8,128)(2,1)S(1)}, u32[]{:S(2)}, u32[]{:S(2)}) collective-permute-start(bf16[32,2176]{1,0:T(8,128)(2,1)S(1)} %get-tuple-element.104), channel_id=1, source_target_pairs={{0,16},{8,24},{16,0},{24,8},{1,17},{9,25},{17,1},{25,9},{2,18},{10... | collective-permute-start | bytes 417800 | tf_op jit(solution)/shard_map/ppermute | solution.py:847
  143.6 6.1 %collective-permute-start.11 = (bf16[32,2176]{1,0:T(8,128)(2,1)S(1)}, bf16[32,2176]{1,0:T(8,128)(2,1)S(1)}, u32[]{:S(2)}, u32[]{:S(2)}) collective-permute-start(bf16[32,2176]{1,0:T(8,128)(2,1)S(1)} %get-tuple-element.102), channel_id=1, source_target_pairs={{0,8},{8,16},{16,24},{24,0},{1,9},{9,17},{17,25},{25,1},{2,10},{10... | collective-permute-start | bytes 417800 | tf_op jit(solution)/shard_map/ppermute | solution.py:847
  149.7 26.2 %collective-permute-start.16 = (bf16[8,2176]{1,0:T(8,128)(2,1)S(1)}, bf16[8,2176]{1,0:T(8,128)(2,1)S(1)}, u32[]{:S(2)}, u32[]{:S(2)}) collective-permute-start(bf16[8,2176]{1,0:T(8,128)(2,1)S(1)} %get-tuple-element.114), channel_id=1, source_target_pairs={{0,6},{1,7},{2,0},{3,1},{4,2},{5,3},{6,4},{7,5},{8,14},{9,15},{10,... | collective-permute-start | bytes 104456 | tf_op jit(solution)/shard_map/ppermute | solution.py:847
  156.2 19.8 %collective-permute-start.15 = (bf16[8,2176]{1,0:T(8,128)(2,1)S(1)}, bf16[8,2176]{1,0:T(8,128)(2,1)S(1)}, u32[]{:S(2)}, u32[]{:S(2)}) collective-permute-start(bf16[8,2176]{1,0:T(8,128)(2,1)S(1)} %get-tuple-element.115), channel_id=1, source_target_pairs={{0,4},{1,5},{2,6},{3,7},{4,0},{5,1},{6,2},{7,3},{8,12},{9,13},{10,... | collective-permute-start | bytes 104456 | tf_op jit(solution)/shard_map/ppermute | solution.py:847
  156.4 19.6 %collective-permute-start.14 = (bf16[8,2176]{1,0:T(8,128)(2,1)S(1)}, bf16[8,2176]{1,0:T(8,128)(2,1)S(1)}, u32[]{:S(2)}, u32[]{:S(2)}) collective-permute-start(bf16[8,2176]{1,0:T(8,128)(2,1)S(1)} %get-tuple-element.113), channel_id=1, source_target_pairs={{0,2},{1,3},{2,4},{3,5},{4,6},{5,7},{6,0},{7,1},{8,10},{9,11},{10,... | collective-permute-start | bytes 104456 | tf_op jit(solution)/shard_map/ppermute | solution.py:847
  157.7 0.8 copy-start.16
  174.9 11.4 %copy-start.12 = (f32[1,64]{1,0:T(1,128)S(1)}, f32[1,64]{1,0:T(1,128)}, u32[]{:S(2)}) copy-start(f32[1,64]{1,0:T(1,128)} %copy-done.11) | copy-start | bytes 772
  175.9 4.6 %collective-permute-start.8 = (bf16[128,1152]{1,0:T(8,128)(2,1)S(1)}, bf16[128,1152]{1,0:T(8,128)(2,1)S(1)}, u32[]{:S(2)}, u32[]{:S(2)}) collective-permute-start(bf16[128,1152]{1,0:T(8,128)(2,1)S(1)} %dynamic-slice_bitcast_fusion.1), channel_id=1, source_target_pairs={{0,1},{1,0},{2,3},{3,2},{4,5},{5,4},{6,7},{7,6},{8,9},{9,8},{10,11... | collective-permute-start | bytes 884744 | tf_op jit(solution)/shard_map/ppermute | solution.py:847
  176.0 10.3 %collective-permute-start.17 = (bf16[1,8,2176]{2,1,0:T(8,128)(2,1)S(1)}, bf16[1,8,2176]{2,1,0:T(8,128)(2,1)S(1)}, u32[]{:S(2)}, u32[]{:S(2)}) collective-permute-start(bf16[1,8,2176]{2,1,0:T(8,128)(2,1)S(1)} %bitcast.100), channel_id=1, source_target_pairs={{0,2},{1,3},{2,4},{3,5},{4,6},{5,7},{6,0},{7,1},{8,10},{9,11},{10,... | collective-permute-start | bytes 104456 | tf_op jit(solution)/shard_map/ppermute | solution.py:847
  178.1 8.3 %collective-permute-start.18 = (bf16[1,8,2176]{2,1,0:T(8,128)(2,1)S(1)}, bf16[1,8,2176]{2,1,0:T(8,128)(2,1)S(1)}, u32[]{:S(2)}, u32[]{:S(2)}) collective-permute-start(bf16[1,8,2176]{2,1,0:T(8,128)(2,1)S(1)} %bitcast.101), channel_id=1, source_target_pairs={{0,4},{1,5},{2,6},{3,7},{4,0},{5,1},{6,2},{7,3},{8,12},{9,13},{10,... | collective-permute-start | bytes 104456 | tf_op jit(solution)/shard_map/ppermute | solution.py:847
  179.2 7.2 %collective-permute-start.19 = (bf16[1,8,2176]{2,1,0:T(8,128)(2,1)S(1)}, bf16[1,8,2176]{2,1,0:T(8,128)(2,1)S(1)}, u32[]{:S(2)}, u32[]{:S(2)}) collective-permute-start(bf16[1,8,2176]{2,1,0:T(8,128)(2,1)S(1)} %bitcast.102), channel_id=1, source_target_pairs={{0,6},{1,7},{2,0},{3,1},{4,2},{5,3},{6,4},{7,5},{8,14},{9,15},{10,... | collective-permute-start | bytes 104456 | tf_op jit(solution)/shard_map/ppermute | solution.py:847
  182.3 15.3 %all-to-all-start.5 = ((bf16[16,8,1152]{2,1,0:T(8,128)(2,1)}), bf16[16,8,1152]{2,1,0:T(8,128)(2,1)S(1)}, u32[]{:S(2)}, u32[]{:S(2)}) async-start(bf16[16,8,1152]{2,1,0:T(8,128)(2,1)} %fusion.3), calls=%async_computation.5 | async-start | bytes 589824 | tf_op jit(solution)/shard_map/all_to_all | solution.py:868
  186.3 5.0 %copy-start.8 = (f32[16,64,256]{2,1,0:T(8,128)S(1)}, f32[16,64,256]{2,1,0:T(8,128)}, u32[]{:S(2)}) copy-start(f32[16,64,256]{2,1,0:T(8,128)} %get-tuple-element.85) | copy-start | bytes 3145732
  186.3 5.0 %copy-start.9 = (bf16[1,256]{1,0:T(2,128)(2,1)S(1)}, bf16[1,256]{1,0:T(2,128)(2,1)}, u32[]{:S(2)}) copy-start(bf16[1,256]{1,0:T(2,128)(2,1)} %reshape.133.gain_ref) | copy-start | bytes 1540
  186.3 5.0 %copy-start.14 = (f32[1024,256]{1,0:T(8,128)S(1)}, f32[1024,256]{1,0:T(8,128)}, u32[]{:S(2)}) copy-start(f32[1024,256]{1,0:T(8,128)} %get-tuple-element.84.first_ref) | copy-start | bytes 3145732
  186.4 15.5 %collective-permute-start.20 = (bf16[4,8,2176]{2,1,0:T(8,128)(2,1)S(1)}, bf16[4,8,2176]{2,1,0:T(8,128)(2,1)S(1)}, u32[]{:S(2)}, u32[]{:S(2)}) collective-permute-start(bf16[4,8,2176]{2,1,0:T(8,128)(2,1)S(1)} %bitcast.107), channel_id=1, source_target_pairs={{0,8},{8,16},{16,24},{24,0},{1,9},{9,17},{17,25},{25,1},{2,10},{10... | collective-permute-start | bytes 417800 | tf_op jit(solution)/shard_map/ppermute | solution.py:847
  188.3 13.5 %collective-permute-start.21 = (bf16[4,8,2176]{2,1,0:T(8,128)(2,1)S(1)}, bf16[4,8,2176]{2,1,0:T(8,128)(2,1)S(1)}, u32[]{:S(2)}, u32[]{:S(2)}) collective-permute-start(bf16[4,8,2176]{2,1,0:T(8,128)(2,1)S(1)} %bitcast.108), channel_id=1, source_target_pairs={{0,16},{8,24},{16,0},{24,8},{1,17},{9,25},{17,1},{25,9},{2,18},{10... | collective-permute-start | bytes 417800 | tf_op jit(solution)/shard_map/ppermute | solution.py:847
  189.8 12.1 %collective-permute-start.22 = (bf16[4,8,2176]{2,1,0:T(8,128)(2,1)S(1)}, bf16[4,8,2176]{2,1,0:T(8,128)(2,1)S(1)}, u32[]{:S(2)}, u32[]{:S(2)}) collective-permute-start(bf16[4,8,2176]{2,1,0:T(8,128)(2,1)S(1)} %bitcast.109), channel_id=1, source_target_pairs={{0,24},{8,0},{16,8},{24,16},{1,25},{9,1},{17,9},{25,17},{2,26},{10... | collective-permute-start | bytes 417800 | tf_op jit(solution)/shard_map/ppermute | solution.py:847
  198.3 13.4 %all-to-all-start.6 = ((bf16[16,8,1152]{2,1,0:T(8,128)(2,1)}), bf16[16,8,1152]{2,1,0:T(8,128)(2,1)S(1)}, u32[]{:S(2)}, u32[]{:S(2)}) async-start(bf16[16,8,1152]{2,1,0:T(8,128)(2,1)} %broadcast_in_dim.17), calls=%async_computation.6 | async-start | bytes 589824 | tf_op jit(solution)/shard_map/all_to_all | solution.py:868
  201.9 0.7 copy-start.24
  202.0 1.4 slice-start
  202.0 1.4 copy-start.4
  202.0 10.5 %collective-permute-start.23 = (bf16[16,8,2176]{2,1,0:T(8,128)(2,1)S(1)}, bf16[16,8,2176]{2,1,0:T(8,128)(2,1)S(1)}, u32[]{:S(2)}, u32[]{:S(2)}) collective-permute-start(bf16[16,8,2176]{2,1,0:T(8,128)(2,1)S(1)} %bitcast.105), channel_id=1, source_target_pairs={{0,1},{1,0},{2,3},{3,2},{4,5},{5,4},{6,7},{7,6},{8,9},{9,8},{10,11... | collective-permute-start | bytes 1671176 | tf_op jit(solution)/shard_map/ppermute | solution.py:847
  203.3 8.4 %copy-start.23 = (f32[1,1024]{1,0:T(1,128)S(1)}, f32[1,1024]{1,0:T(1,128)}, u32[]{:S(2)}) copy-start(f32[1,1024]{1,0:T(1,128)} %get-tuple-element.92) | copy-start | bytes 12292
  211.7 2.9 %collective-permute-start.9 = (bf16[128,1152]{1,0:T(8,128)(2,1)S(1)}, bf16[128,1152]{1,0:T(8,128)(2,1)S(1)}, u32[]{:S(2)}, u32[]{:S(2)}) collective-permute-start(bf16[128,1152]{1,0:T(8,128)(2,1)S(1)} %bitcast.97), channel_id=1, source_target_pairs={{0,1},{1,0},{2,3},{3,2},{4,5},{5,4},{6,7},{7,6},{8,9},{9,8},{10,11... | collective-permute-start | bytes 884744 | tf_op jit(solution)/shard_map/ppermute | solution.py:847

commit v5 on v4

--- a/solution.py
+++ b/solution.py
@@ -78,7 +78,7 @@
 
 def expand_kernel(
     image_ref, gain_ref, w_exp_ref,
-    normed_ref, turned_ref, spread_ref, slope_ref,
+    normed_ref, spread_ref, pre_ref,
     expanded_ref,
 ):
     rows, cols, channels = image_ref.shape
@@ -94,8 +94,6 @@
             at = pl.ds(pl.multiple_of(c * 4 * cols, 16), 4 * cols)
             normed_ref[at, :] = (unit * gain).astype(BF16)
 
-        turned_ref[...] = normed_ref[...].T
-
     expanded_ref[...] = dot(normed_ref[...], w_exp_ref[...])
 
     @pl.loop(0, rows, unroll=4)
@@ -103,9 +101,9 @@
         for h in range(BLOCK // LANES):
             lanes = slice(h * LANES, (h + 1) * LANES)
             x = expanded_ref[pl.ds(pl.multiple_of(r * cols, 16), cols), lanes]
-            value, slope = gelu_and_slope(x)
+            value, _ = gelu_and_slope(x, False)
             spread_ref[r, :, lanes] = value.astype(BF16)
-            slope_ref[r, :, lanes] = slope.astype(BF16)
+            pre_ref[r, :, lanes] = x.astype(BF16)
 
 
 def run_expand(image, gain, w_expand):
@@ -116,12 +114,11 @@
         grid=(expanded // BLOCK,),
         in_specs=[whole(image.shape), whole(gain.shape), last_block(w_expand.shape)],
         out_specs=[
-            whole((rows * cols, channels)), whole((channels, rows * cols)),
+            whole((rows * cols, channels)),
             last_block((rows, cols, expanded)), last_block((rows, cols, expanded)),
         ],
         out_shape=[
             jax.ShapeDtypeStruct((rows * cols, channels), BF16),
-            jax.ShapeDtypeStruct((channels, rows * cols), BF16),
             jax.ShapeDtypeStruct((rows, cols, expanded), BF16),
             jax.ShapeDtypeStruct((rows, cols, expanded), BF16),
         ],
@@ -225,8 +222,23 @@
     )(up, down, side, gain, w_expand, w_depth, spread)
 
 
-def slope_kernel(flags_ref, ring_ref, w_dep_ref, spread_ref, main_ref, side_out_ref, wide_ref):
+def slope_kernel(
+    flags_ref, ring_ref, w_dep_ref, spread_ref, pre_ref, normed_ref,
+    main_ref, side_out_ref, spread_slope_ref, turned_ref, wide_ref,
+):
     rows, cols, _ = spread_ref.shape
+
+    @pl.when(pl.program_id(0) == 0)
+    def _():
+        turned_ref[...] = normed_ref[...].T
+
+    @pl.loop(0, rows, unroll=4)
+    def _(r):
+        for h in range(BLOCK // LANES):
+            lanes = slice(h * LANES, (h + 1) * LANES)
+            _, slope = gelu_and_slope(pre_ref[r, :, lanes].astype(F32))
+            spread_slope_ref[r, :, lanes] = slope.astype(BF16)
+
     over = 4 * cols
     side = 8
     wide = cols + side
@@ -261,7 +273,7 @@
             side_out_ref[i, :, lanes] = slope[cols:] * side_mask
 
 
-def run_slope(flags, ring, w_depth, spread):
+def run_slope(flags, ring, w_depth, spread, pre, normed):
     rows, cols, expanded = spread.shape
     return pl.pallas_call(
         slope_kernel,
@@ -269,17 +281,23 @@
         in_specs=[
             pl.BlockSpec(memory_space=pltpu.SMEM),
             last_block(ring.shape), last_block(w_depth.shape), last_block(spread.shape),
-        ],
-        out_specs=[last_block((rows + 2, cols, expanded)), last_block((rows + 2, 8, expanded))],
+            last_block(pre.shape), whole(normed.shape),
+        ],
+        out_specs=[
+            last_block((rows + 2, cols, expanded)), last_block((rows + 2, 8, expanded)),
+            last_block(pre.shape), whole(normed.shape[::-1]),
+        ],
         out_shape=[
             jax.ShapeDtypeStruct((rows + 2, cols, expanded), BF16),
             jax.ShapeDtypeStruct((rows + 2, 8, expanded), F32),
+            jax.ShapeDtypeStruct(pre.shape, BF16),
+            jax.ShapeDtypeStruct(normed.shape[::-1], BF16),
         ],
         scratch_shapes=[pltpu.VMEM((rows + 4, cols + 8, BLOCK), F32)],
         compiler_params=PARAMS,
         cost_estimate=estimate(13),
         name="slope",
-    )(flags, ring, w_depth, spread)
+    )(flags, ring, w_depth, spread, pre, normed)
 
 
 def mix_kernel(
@@ -341,7 +359,7 @@
             jax.ShapeDtypeStruct(image.shape, BF16),
             jax.ShapeDtypeStruct(send, BF16),
         ],
-        compiler_params=SMALL,
+        compiler_params=PARAMS,
         cost_estimate=estimate(5),
         name="mix",
     )(parts, w_squeeze, w_excite, act, image, w_project, gain, after)
@@ -511,7 +529,7 @@
 def mixed_back_kernel(
     stride, bands,
     recv_ref, mixed_ref, cot_ref, gain_ref, act_ref, gate_ref, w_projt_ref,
-    grad_ref, low_ref, norm_ref, project_ref, gate_grad_ref,
+    low_ref, norm_ref, project_ref, gate_grad_ref,
     turned_ref, total_ref,
 ):
     rows, cols, channels = mixed_ref.shape
@@ -532,7 +550,6 @@
             flat = lambda ref: ref[at].reshape(lines * cols, channels).astype(F32)
             unit, rstd = norm_rows(flat(mixed_ref))
             back = flat(cot_ref) + norm_rows_back(unit, rstd, gain, grad)
-            grad_ref[at] = back.reshape(lines, cols, channels)
             low_ref[at] = back.astype(BF16).reshape(lines, cols, channels)
             return total + fold_rows(grad * unit)
 
@@ -568,11 +585,10 @@
             last_block(act.shape), last_block(gate.shape), last_block(w_project_t.shape),
         ],
         out_specs=[
-            whole(mixed.shape), whole(mixed.shape), whole((1, channels)),
+            whole(mixed.shape), whole((1, channels)),
             last_block((BLOCK, expanded)), whole((count, 2 * expanded // BLOCK, BLOCK)),
         ],
         out_shape=[
-            jax.ShapeDtypeStruct(mixed.shape, F32),
             jax.ShapeDtypeStruct(mixed.shape, BF16),
             jax.ShapeDtypeStruct((1, channels), F32),
             jax.ShapeDtypeStruct((BLOCK, expanded), BF16),
@@ -787,7 +803,7 @@
 def image_back_kernel(image_ref, gain_ref, first_ref, mixed_ref, out_ref):
     unit, rstd = norm_rows(image_ref[...].astype(F32))
     grad = first_ref[...]
-    back = mixed_ref[...] + norm_rows_back(unit, rstd, gain_ref[...].astype(F32), grad)
+    back = mixed_ref[...].astype(F32) + norm_rows_back(unit, rstd, gain_ref[...].astype(F32), grad)
     out_ref[...] = back.astype(BF16)
 
 
@@ -990,7 +1006,7 @@
     bias_tall = jnp.concatenate([bias_tall, bias_tall], axis=2)
 
     up, down = halo_rows(image, 2)
-    normed_first, turned_first, spread, spread_slope = run_expand(image, gain_first, w_expand)
+    normed_first, spread, pre_spread = run_expand(image, gain_first, w_expand)
     up, down, spread = lax.optimization_barrier((up, down, spread))
     side = halo_sides(image, up, down, 2)
     cot_sent = (
@@ -1004,7 +1020,9 @@
         cells_total, stride, hand_around(pool), w_squeeze, w_excite, act, image, w_project,
         gain_second, cot_members,
     )
-    slope, side_slope = run_slope(flags, ring, w_depth, spread)
+    slope, side_slope, spread_slope, turned_first = run_slope(
+        flags, ring, w_depth, spread, pre_spread, normed_first
+    )
     normed_arrived = swap_groups(normed_sent, parity)
     att_grad = dot(cot_members, w_out, ((1,), (1,))).astype(BF16)
     normed_arrived, slope, att_grad = lax.optimization_barrier((normed_arrived, slope, att_grad))
@@ -1014,7 +1032,7 @@
     grad_normed_home = swap_groups(grad_normed.reshape(normed_sent.shape), parity)
     weights = run_attention_weights(normed_members, packed_grad, attended, cot_members, grad_bias)
     grad_normed_home, weights = lax.optimization_barrier((grad_normed_home, weights))
-    grad_mixed, grad_low, grad_norm1, grad_project, gate_grad = run_mixed_back(
+    grad_low, grad_norm1, grad_project, gate_grad = run_mixed_back(
         count, stride, grad_normed_home, mixed, out_cotangent, gain_second, act, gate, w_project_t
     )
     attended_sent = out_of_members(attended)
@@ -1049,7 +1067,7 @@
     )
     grad_expand, grad_depth, grad_norm0, grad_norm1 = run_unpack(*sum_shares(late), expanded)
     grad_image = run_image_back(
-        image.reshape(-1, channels), gain_first, grad_first, grad_mixed.reshape(-1, channels)
+        image.reshape(-1, channels), gain_first, grad_first, grad_low.reshape(-1, channels)
     )
     attended_map = (
         attended_home.reshape(stride, bands, lines, SIDE, channels)

time: 217 us -> 217 us (level)
  waiting for transfers between devices: 44.9 us -> 40.7 us
  Pallas kernels: 73.8 us -> 77.7 us
    all_to_all x3, waiting for transfers between devices: 16.2 us -> 12.9 us  [swap_groups(): lax.all_to_all(blocks, AXES, split_axis=0, concat_axis=0, tiled=True, axi...]
    pallas_call x1, Pallas kernels: 10.5 us -> 13.7 us  [run_slope(): pl.pallas_call(slope_kernel, grid=(expanded // BLOCK,), in_specs=[pl.Bloc...]
    unnamed x66 -> x58, local copies, waits for them, and re-layouts: 7.71 us -> 5.53 us
  transfers between devices with their start and end apart: 31 -> 31, of which waited for: 10 -> 11; matrix products, arithmetic and copies ran while one was open for 8% -> 9% of each run, Pallas kernels for 24% -> 25%
where the time goes in v5:
time: 217 us; the launch traced here: 216 us
  Pallas kernels  77.7 us (36%)
  starting transfers between devices  69.6 us (32%)
  waiting for transfers between devices  40.7 us (19%)
  local copies, waits for them, and re-layouts  15.7 us (7%)
  other arithmetic  8.71 us (4%)
  matrix products  2.22 us (1%)
    ppermute x16, starting transfers between devices, send_on(): return lax.ppermute(v, axis, pairs)  21.5 us
    ppermute x8, starting transfers between devices, shift(): return lax.ppermute(cells, axis, pairs)  17.2 us
    pallas_call x1, Pallas kernels, run_expand_back(): pl.pallas_call(functools.partial(expand_back_kernel, cells_total), grid=(...  16.2 us
    all_to_all x3, starting transfers between devices, swap_groups(): lax.all_to_all(blocks, AXES, split_axis=0, concat_axis=0, tiled=True, axi...  14 us
    pallas_call x1, Pallas kernels, run_slope(): pl.pallas_call(slope_kernel, grid=(expanded // BLOCK,), in_specs=[pl.Bloc...  13.7 us
    all_to_all x3, waiting for transfers between devices, swap_groups(): lax.all_to_all(blocks, AXES, split_axis=0, concat_axis=0, tiled=True, axi...  12.9 us
    pallas_call x1, Pallas kernels, run_attention(): pl.pallas_call(functools.partial(attention_kernel, members, heads, lines)...  11.8 us
    all_to_all x2, waiting for transfers between devices, around(): lax.all_to_all(blocks, AXES, split_axis=0, concat_axis=0, tiled=True, axi...  11.2 us
  transfers between devices with their start and end apart: 31, of which 11 were waited for; matrix products, arithmetic and copies ran while one was open for 9% of the time, Pallas kernels for 25%

profile of v5, /device:TPU:0, one launch (start us, length us, event | category | flops | bytes accessed | tf_op | source)
XLA Modules:
  0.0 216.0 jit_solution(6477401774922383085)
XLA Ops:
  0.7 0.9 fusion.15
  1.6 4.8 %collective-permute-start = (bf16[2,64,256]{2,1,0:T(8,128)(2,1)S(1)}, bf16[2,64,256]{2,1,0:T(8,128)(2,1)S(1)}, u32[]{:S(2)}, u32[]{:S(2)}) collective-permute-start(bf16[2,64,256]{2,1,0:T(8,128)(2,1)S(1)} %get-tuple-element.114), channel_id=1, source_target_pairs={{0,8},{8,16},{16,24},{1,9},{9,17},{17,25},{2,10},{10,18},{18,26},{... | collective-permute-start | bytes 196616 | tf_op jit(solution)/shard_map/ppermute | solution.py:828
  6.4 1.3 collective-permute-start.1
  7.7 1.9 copy.45
  9.6 7.0 %all-to-all-start.1 = ((bf16[32,2,16,256]{3,2,1,0:T(8,128)(2,1)}), bf16[32,2,16,256]{3,2,1,0:T(8,128)(2,1)S(1)}, u32[]{:S(2)}, u32[]{:S(2)}) async-start(bf16[32,2,16,256]{3,2,1,0:T(8,128)(2,1)} %bitcast.3), calls=%async_computation.1 | async-start | bytes 1048576 | tf_op jit(solution)/shard_map/all_to_all | solution.py:969
  17.2 6.5 %expand.1 = (bf16[1024,256]{1,0:T(8,128)(2,1)}, bf16[16,64,1024]{2,1,0:T(8,128)(2,1)}, bf16[16,64,1024]{2,1,0:T(8,128)(2,1)}) custom-call(bf16[16,64,256]{2,1,0:T(8,128)(2,1)} %image_ref.3, bf16[1,256]{1,0:T(2,128)(2,1)} %reshape.133.gain_ref, bf16[256,1024]{1,0:T(8,128)(2,1)} %w_exp_ref.5), custom_call_target="tpu_custom_call" | custom-call | flops 15399999488 | bytes 50400000 | tf_op jit(solution)/shard_map/expand/pallas_call | solution.py:112
  23.7 0.9 fusion.14
  24.7 2.1 collective-permute-start.3
  26.9 1.3 collective-permute-start.2
  28.3 2.8 %collective-permute-done.2 = bf16[20,2,256]{2,0,1:T(8,128)(2,1)S(1)} collective-permute-done((bf16[20,2,256]{2,0,1:T(8,128)(2,1)S(1)}, bf16[20,2,256]{2,0,1:T(8,128)(2,1)S(1)}, u32[]{:S(2)}, u32[]{:S(2)}) %collective-permute-start.2) | collective-permute-done | bytes 20512 | tf_op jit(solution)/shard_map/ppermute | solution.py:828
  31.9 8.9 %depthwise.1 = (bf16[416,1024]{1,0:T(8,128)(2,1)}, bf16[16,64,1024]{2,1,0:T(8,128)(2,1)}, f32[32,1,1024]{2,1,0:T(1,128)}) custom-call(bf16[2,64,256]{2,1,0:T(8,128)(2,1)} %copy-done.20, bf16[2,64,256]{2,1,0:T(8,128)(2,1)} %copy-done.21, bf16[160,256]{1,0:T(8,128)(2,1)} %maximum_bitcast_fusion.side_ref, bf16[1,256]{1,0:T(2,128)(2,1)} %reshape.133.gain_ref, ...), custom_call_target="tpu_custom_call" | custom-call | flops 1100000000 | bytes 3600000 | tf_op jit(solution)/shard_map/depthwise/pallas_call | solution.py:203
  40.9 6.8 %all-to-all-start = ((f32[32,1,1024]{2,1,0:T(1,128)}), f32[32,1,1024]{2,1,0:T(1,128)S(1)}, u32[]{:S(2)}, u32[]{:S(2)}) async-start(f32[32,1,1024]{2,1,0:T(1,128)} %get-tuple-element.62), calls=%async_computation | async-start | bytes 262144 | tf_op jit(solution)/shard_map/all_to_all | solution.py:851
  47.7 0.8 copy.47.w_sq_ref
  49.9 0.8 pad_maximum_fusion.2.bias_ref
  50.7 1.1 copy.46
  51.8 4.0 %all-to-all-done.parts_ref = f32[32,1,1024]{2,1,0:T(1,128)S(1)} async-done(((f32[32,1,1024]{2,1,0:T(1,128)}), f32[32,1,1024]{2,1,0:T(1,128)S(1)}, u32[]{:S(2)}, u32[]{:S(2)}) %all-to-all-start) | async-done | bytes 131104 | tf_op jit(solution)/shard_map/all_to_all | solution.py:851
  56.5 5.4 %mix.1 = (f32[1,1024]{1,0:T(1,128)}, f32[1,64]{1,0:T(1,128)}, f32[1,1024]{1,0:T(1,128)}, bf16[16,64,256]{2,1,0:T(8,128)(2,1)}, bf16[32,2,16,256]{3,2,1,0:T(8,128)(2,1)}) custom-call(f32[32,1,1024]{2,1,0:T(1,128)} %copy-done.16, bf16[1024,64]{1,0:T(8,128)(2,1)} %copy.47.w_sq_ref, bf16[64,1024]{1,0:T(8,128)(2,1)} %w_ex_ref.3, ...), custom_call_target="tpu_custom_call" | custom-call | flops 5500000256 | bytes 18000000 | tf_op jit(solution)/shard_map/mix/pallas_call | solution.py:343
  61.9 2.6 %all-to-all-start.2 = ((bf16[32,2,16,256]{3,2,1,0:T(8,128)(2,1)}), bf16[32,2,16,256]{3,2,1,0:T(8,128)(2,1)S(1)}, u32[]{:S(2)}, u32[]{:S(2)}) async-start(bf16[32,2,16,256]{3,2,1,0:T(8,128)(2,1)} %get-tuple-element.65), calls=%async_computation.2 | async-start | bytes 1048576 | tf_op jit(solution)/shard_map/all_to_all | solution.py:969
  64.6 13.7 %slope.1 = (bf16[18,64,1024]{2,1,0:T(8,128)(2,1)}, f32[18,8,1024]{2,1,0:T(8,128)}, bf16[16,64,1024]{2,1,0:T(8,128)(2,1)}, bf16[256,1024]{1,0:T(8,128)(2,1)}) custom-call(f32[4]{0:T(128)} %add_convert_fusion.flags_ref, bf16[416,1024]{1,0:T(8,128)(2,1)} %get-tuple-element.66.ring_ref, bf16[3,3,1024]{2,1,0:T(4,128)(2,1)} %w_dep_ref.5, ...), custom_call_target="tpu_custom_call" | custom-call | flops 14300000256 | bytes 46800000 | tf_op jit(solution)/shard_map/slope/pallas_call | solution.py:278
  78.3 1.1 convolution_convert_fusion.att_grad_ref
  79.4 1.5 all-to-all-done.2
  80.9 0.8 copy-done.13
  81.7 11.8 %attention.1 = (bf16[1024,256]{1,0:T(8,128)(2,1)}, bf16[1024,256]{1,0:T(8,128)(2,1)}, bf16[1024,256]{1,0:T(8,128)(2,1)}, bf16[1024,768]{1,0:T(8,128)(2,1)}, f32[2,256,64]{2,1,0:T(8,128)}) custom-call(bf16[1024,256]{1,0:T(8,128)(2,1)} %bitcast.128, bf16[1024,256]{1,0:T(8,128)(2,1)} %convolution_convert_fusion.att_grad_ref, bf16[256,768]{1,0:T(8,128)(2,1)} %w_qkv_ref.1, ...), custom_call_target="tpu_custom_call" | custom-call | flops 15399999488 | bytes 50400000 | tf_op jit(solution)/shard_map/attention/pallas_call | solution.py:480
  93.5 4.4 %all-to-all-start.3 = ((bf16[32,2,16,256]{3,2,1,0:T(8,128)(2,1)}), bf16[32,2,16,256]{3,2,1,0:T(8,128)(2,1)S(1)}, u32[]{:S(2)}, u32[]{:S(2)}) async-start(bf16[32,2,16,256]{3,2,1,0:T(8,128)(2,1)} %bitcast.126), calls=%async_computation.3 | async-start | bytes 1048576 | tf_op jit(solution)/shard_map/all_to_all | solution.py:969
  97.9 1.0 copy.50
  99.3 3.5 %attention_weights.1 = bf16[256,1152]{1,0:T(8,128)(2,1)} custom-call(bf16[1024,256]{1,0:T(8,128)(2,1)} %get-tuple-element.74.x_ref, bf16[1024,768]{1,0:T(8,128)(2,1)} %get-tuple-element.75.packed_grad_ref, bf16[1024,256]{1,0:T(8,128)(2,1)} %get-tuple-element.72.att_ref, bf16[1024,256]{1,0:T(8,128)(2,1)} %bitcast.113, f32[2,256,64]{2,1,0:T(8,128)} %get-tuple-element.76.bias_ref), custom_call_target="tpu_custom_call" | custom-call | flops 5500000256 | bytes 18000000 | tf_op jit(solution)/shard_map/attention_weights/pallas_call | solution.py:518
  102.8 11.4 %all-to-all-done.3.recv_ref = bf16[32,2,16,256]{3,2,1,0:T(8,128)(2,1)S(1)} async-done(((bf16[32,2,16,256]{3,2,1,0:T(8,128)(2,1)}), bf16[32,2,16,256]{3,2,1,0:T(8,128)(2,1)S(1)}, u32[]{:S(2)}, u32[]{:S(2)}) %all-to-all-start.3) | async-done | bytes 524320 | tf_op jit(solution)/shard_map/all_to_all | solution.py:969
  114.2 0.8 copy-done.11
  115.0 6.3 %mixed_back.1 = (bf16[16,64,256]{2,1,0:T(8,128)(2,1)}, f32[1,256]{1,0:T(1,128)}, bf16[256,1024]{1,0:T(8,128)(2,1)}, bf16[32,8,256]{2,1,0:T(8,128)(2,1)}) custom-call(bf16[32,2,16,256]{3,2,1,0:T(8,128)(2,1)} %copy-done.11, bf16[16,64,256]{2,1,0:T(8,128)(2,1)} %get-tuple-element.64.mixed_ref, bf16[16,64,256]{2,1,0:T(8,128)(2,1)} %cot_ref.1, ...), custom_call_target="tpu_custom_call" | custom-call | flops 7699999744 | bytes 25200000 | tf_op jit(solution)/shard_map/mixed_back/pallas_call | solution.py:580
  121.3 0.8 fusion.13
  122.1 0.9 fusion.12
  123.0 1.9 pad_maximum_fusion.1
  124.9 2.6 %all-to-all-start.4 = ((bf16[32,40,256]{2,1,0:T(8,128)(2,1)}), bf16[32,40,256]{2,1,0:T(8,128)(2,1)S(1)}, u32[]{:S(2)}, u32[]{:S(2)}) async-start(bf16[32,40,256]{2,1,0:T(8,128)(2,1)} %pad_maximum_fusion.1), calls=%async_computation.4 | async-start | bytes 1310720 | tf_op jit(solution)/shard_map/all_to_all | solution.py:851
  127.5 3.5 %collective-permute-start.4 = (bf16[1,64,256]{2,1,0:T(8,128)(2,1)S(1)}, bf16[1,64,256]{2,1,0:T(8,128)(2,1)S(1)}, u32[]{:S(2)}, u32[]{:S(2)}) collective-permute-start(bf16[1,64,256]{2,1,0:T(8,128)(2,1)S(1)} %get-tuple-element.110), channel_id=1, source_target_pairs={{0,8},{8,16},{16,24},{1,9},{9,17},{17,25},{2,10},{10,18},{18,26},{... | collective-permute-start | bytes 98312 | tf_op jit(solution)/shard_map/ppermute | solution.py:828
  131.0 1.3 collective-permute-start.5
  132.7 4.2 %collective-permute-done.5.down_ref = bf16[1,64,256]{2,1,0:T(8,128)(2,1)S(1)} collective-permute-done((bf16[1,64,256]{2,1,0:T(8,128)(2,1)S(1)}, bf16[1,64,256]{2,1,0:T(8,128)(2,1)S(1)}, u32[]{:S(2)}, u32[]{:S(2)}) %collective-permute-start.5) | collective-permute-done | bytes 32800 | tf_op jit(solution)/shard_map/ppermute | solution.py:828
  137.0 1.3 collective-permute-start.7
  138.3 1.5 collective-permute-start.6
  140.6 3.4 %collective-permute-start.12 = (bf16[32,2176]{1,0:T(8,128)(2,1)S(1)}, bf16[32,2176]{1,0:T(8,128)(2,1)S(1)}, u32[]{:S(2)}, u32[]{:S(2)}) collective-permute-start(bf16[32,2176]{1,0:T(8,128)(2,1)S(1)} %get-tuple-element.106), channel_id=1, source_target_pairs={{0,16},{8,24},{16,0},{24,8},{1,17},{9,25},{17,1},{25,9},{2,18},{10... | collective-permute-start | bytes 417800 | tf_op jit(solution)/shard_map/ppermute | solution.py:863
  144.8 1.5 collective-permute-done.13
  146.2 1.5 collective-permute-done.12
  147.7 2.4 %collective-permute-done.11 = bf16[32,2176]{1,0:T(8,128)(2,1)S(1)} collective-permute-done((bf16[32,2176]{1,0:T(8,128)(2,1)S(1)}, bf16[32,2176]{1,0:T(8,128)(2,1)S(1)}, u32[]{:S(2)}, u32[]{:S(2)}) %collective-permute-start.11) | collective-permute-done | bytes 139296 | tf_op jit(solution)/shard_map/ppermute | solution.py:863
  150.2 6.4 %collective-permute-start.16 = (bf16[8,2176]{1,0:T(8,128)(2,1)S(1)}, bf16[8,2176]{1,0:T(8,128)(2,1)S(1)}, u32[]{:S(2)}, u32[]{:S(2)}) collective-permute-start(bf16[8,2176]{1,0:T(8,128)(2,1)S(1)} %get-tuple-element.116), channel_id=1, source_target_pairs={{0,6},{1,7},{2,0},{3,1},{4,2},{5,3},{6,4},{7,5},{8,14},{9,15},{10,... | collective-permute-start | bytes 104456 | tf_op jit(solution)/shard_map/ppermute | solution.py:863
  156.8 1.3 collective-permute-start.14
  158.1 0.8 copy-done.5
  158.9 16.2 %expand_back.1 = (bf16[256,1152]{1,0:T(8,128)(2,1)}, f32[1024,256]{1,0:T(8,128)}, f32[1,1024]{1,0:T(1,128)}, f32[1,64]{1,0:T(1,128)}) custom-call(bf16[32,40,256]{2,1,0:T(8,128)(2,1)} %copy-done.5, f32[1,64]{1,0:T(1,128)} %get-tuple-element.80.hidden_ref, f32[1,1024]{1,0:T(1,128)} %get-tuple-element.78.gate_ref.gate_all_ref, ...), custom_call_target="tpu_custom_call" | custom-call | flops 15399999488 | bytes 50400000 | tf_op jit(solution)/shard_map/expand_back/pallas_call | solution.py:760
  175.2 1.0 dynamic-slice_bitcast_fusion.1
  176.3 2.0 collective-permute-start.17
  178.4 1.1 collective-permute-start.18
  179.5 1.3 collective-permute-start.19
  180.8 1.8 fusion.3
  182.6 4.0 %all-to-all-start.5 = ((bf16[16,8,1152]{2,1,0:T(8,128)(2,1)}), bf16[16,8,1152]{2,1,0:T(8,128)(2,1)S(1)}, u32[]{:S(2)}, u32[]{:S(2)}) async-start(bf16[16,8,1152]{2,1,0:T(8,128)(2,1)} %fusion.3), calls=%async_computation.5 | async-start | bytes 589824 | tf_op jit(solution)/shard_map/all_to_all | solution.py:884
  186.7 2.0 collective-permute-start.20
  188.7 1.5 collective-permute-start.21
  190.2 1.5 collective-permute-start.22
  191.6 2.2 %image_back.1 = bf16[1024,256]{1,0:T(8,128)(2,1)} custom-call(bf16[1024,256]{1,0:T(8,128)(2,1)S(1)} %bitcast.95, bf16[1,256]{1,0:T(2,128)(2,1)S(1)} %copy-done.3, f32[1024,256]{1,0:T(8,128)S(1)} %copy-done.4, bf16[1024,256]{1,0:T(8,128)(2,1)S(1)} %bitcast.100), custom_call_target="tpu_custom_call" | custom-call | flops 4400000000 | bytes 14400000 | tf_op jit(solution)/shard_map/image_back/pallas_call | solution.py:813
  193.9 4.0 %all-to-all-done.5 = bf16[16,8,1152]{2,1,0:T(8,128)(2,1)S(1)} async-done(((bf16[16,8,1152]{2,1,0:T(8,128)(2,1)}), bf16[16,8,1152]{2,1,0:T(8,128)(2,1)S(1)}, u32[]{:S(2)}, u32[]{:S(2)}) %all-to-all-start.5) | async-done | bytes 294944 | tf_op jit(solution)/shard_map/all_to_all | solution.py:884
  198.7 3.5 %all-to-all-start.6 = ((bf16[16,8,1152]{2,1,0:T(8,128)(2,1)}), bf16[16,8,1152]{2,1,0:T(8,128)(2,1)S(1)}, u32[]{:S(2)}, u32[]{:S(2)}) async-start(bf16[16,8,1152]{2,1,0:T(8,128)(2,1)} %broadcast_in_dim.17), calls=%async_computation.6 | async-start | bytes 589824 | tf_op jit(solution)/shard_map/all_to_all | solution.py:884
  202.9 0.8 broadcast_multiply_fusion.1
  203.8 1.1 fusion
  204.8 7.2 %all-to-all-done.6 = bf16[16,8,1152]{2,1,0:T(8,128)(2,1)S(1)} async-done(((bf16[16,8,1152]{2,1,0:T(8,128)(2,1)}), bf16[16,8,1152]{2,1,0:T(8,128)(2,1)S(1)}, u32[]{:S(2)}, u32[]{:S(2)}) %all-to-all-start.6) | async-done | bytes 294944 | tf_op jit(solution)/shard_map/all_to_all | solution.py:884
  212.0 0.8 broadcast_multiply_fusion
  212.8 2.1 unpack_weights.1
  214.9 1.1 unpack.1
  (121 shorter events, 7.9 us)
Async XLA Ops:
  0.6 77.6 %copy-start = (bf16[256,256]{1,0:T(8,128)(2,1)S(1)}, bf16[256,256]{1,0:T(8,128)(2,1)}, u32[]{:S(2)}) copy-start(bf16[256,256]{1,0:T(8,128)(2,1)} %param.22) | copy-start | bytes 393220
  0.7 16.0 %copy-start.24 = (bf16[256]{0:T(256)(128)(2,1)S(1)}, bf16[256]{0:T(256)(128)(2,1)}, u32[]{:S(2)}) copy-start(bf16[256]{0:T(256)(128)(2,1)} %param.14) | copy-start | bytes 1540
  1.6 23.0 %collective-permute-start = (bf16[2,64,256]{2,1,0:T(8,128)(2,1)S(1)}, bf16[2,64,256]{2,1,0:T(8,128)(2,1)S(1)}, u32[]{:S(2)}, u32[]{:S(2)}) collective-permute-start(bf16[2,64,256]{2,1,0:T(8,128)(2,1)S(1)} %get-tuple-element.114), channel_id=1, source_target_pairs={{0,8},{8,16},{16,24},{1,9},{9,17},{17,25},{2,10},{10,18},{18,26},{... | collective-permute-start | bytes 196616 | tf_op jit(solution)/shard_map/ppermute | solution.py:828
  6.4 18.2 %collective-permute-start.1 = (bf16[2,64,256]{2,1,0:T(8,128)(2,1)S(1)}, bf16[2,64,256]{2,1,0:T(8,128)(2,1)S(1)}, u32[]{:S(2)}, u32[]{:S(2)}) collective-permute-start(bf16[2,64,256]{2,1,0:T(8,128)(2,1)S(1)} %get-tuple-element.113), channel_id=1, source_target_pairs={{8,0},{16,8},{24,16},{9,1},{17,9},{25,17},{10,2},{18,10},{26,18},{... | collective-permute-start | bytes 196616 | tf_op jit(solution)/shard_map/ppermute | solution.py:828
  9.6 31.2 %all-to-all-start.1 = ((bf16[32,2,16,256]{3,2,1,0:T(8,128)(2,1)}), bf16[32,2,16,256]{3,2,1,0:T(8,128)(2,1)S(1)}, u32[]{:S(2)}, u32[]{:S(2)}) async-start(bf16[32,2,16,256]{3,2,1,0:T(8,128)(2,1)} %bitcast.3), calls=%async_computation.1 | async-start | bytes 1048576 | tf_op jit(solution)/shard_map/all_to_all | solution.py:969
  24.6 7.3 %copy-start.20 = (bf16[2,64,256]{2,1,0:T(8,128)(2,1)}, bf16[2,64,256]{2,1,0:T(8,128)(2,1)S(1)}, u32[]{:S(2)}) copy-start(bf16[2,64,256]{2,1,0:T(8,128)(2,1)S(1)} %collective-permute-done.up_ref) | copy-start | bytes 196612
  24.7 7.3 %copy-start.21 = (bf16[2,64,256]{2,1,0:T(8,128)(2,1)}, bf16[2,64,256]{2,1,0:T(8,128)(2,1)S(1)}, u32[]{:S(2)}) copy-start(bf16[2,64,256]{2,1,0:T(8,128)(2,1)S(1)} %collective-permute-done.1.down_ref) | copy-start | bytes 196612
  24.7 3.6 %collective-permute-start.3 = (bf16[20,2,256]{2,0,1:T(8,128)(2,1)S(1)}, bf16[20,2,256]{2,0,1:T(8,128)(2,1)S(1)}, u32[]{:S(2)}, u32[]{:S(2)}) collective-permute-start(bf16[20,2,256]{2,0,1:T(8,128)(2,1)S(1)} %pad_maximum_fusion.4), channel_id=1, source_target_pairs={{0,1},{1,2},{2,3},{3,4},{4,5},{5,6},{6,7},{8,9},{9,10},{10,11},{11... | collective-permute-start | bytes 61448 | tf_op jit(solution)/shard_map/ppermute | solution.py:828
  26.9 4.2 %collective-permute-start.2 = (bf16[20,2,256]{2,0,1:T(8,128)(2,1)S(1)}, bf16[20,2,256]{2,0,1:T(8,128)(2,1)S(1)}, u32[]{:S(2)}, u32[]{:S(2)}) collective-permute-start(bf16[20,2,256]{2,0,1:T(8,128)(2,1)S(1)} %pad_maximum_fusion.3), channel_id=1, source_target_pairs={{1,0},{2,1},{3,2},{4,3},{5,4},{6,5},{7,6},{9,8},{10,9},{11,10},{12... | collective-permute-start | bytes 61448 | tf_op jit(solution)/shard_map/ppermute | solution.py:828
  31.9 15.7 %copy-start.15 = (bf16[1024,64]{0,1:T(8,128)(2,1)S(1)}, bf16[1024,64]{0,1:T(8,128)(2,1)}, u32[]{:S(2)}) copy-start(bf16[1024,64]{0,1:T(8,128)(2,1)} %param.17) | copy-start | bytes 393220
  31.9 16.6 %copy-start.25 = (bf16[256]{0:T(256)(128)(2,1)S(1)}, bf16[256]{0:T(256)(128)(2,1)}, u32[]{:S(2)}) copy-start(bf16[256]{0:T(256)(128)(2,1)} %param.20) | copy-start | bytes 1540
  31.9 17.2 %copy-start.14 = (f32[8,64,64]{2,1,0:T(8,128)S(1)}, f32[8,64,64]{2,1,0:T(8,128)}, u32[]{:S(2)}) copy-start(f32[8,64,64]{2,1,0:T(8,128)} %param.23) | copy-start | bytes 393220
  40.9 15.0 %all-to-all-start = ((f32[32,1,1024]{2,1,0:T(1,128)}), f32[32,1,1024]{2,1,0:T(1,128)S(1)}, u32[]{:S(2)}, u32[]{:S(2)}) async-start(f32[32,1,1024]{2,1,0:T(1,128)} %get-tuple-element.62), calls=%async_computation | async-start | bytes 262144 | tf_op jit(solution)/shard_map/all_to_all | solution.py:851
  55.8 0.7 copy-start.16
  61.9 19.0 %all-to-all-start.2 = ((bf16[32,2,16,256]{3,2,1,0:T(8,128)(2,1)}), bf16[32,2,16,256]{3,2,1,0:T(8,128)(2,1)S(1)}, u32[]{:S(2)}, u32[]{:S(2)}) async-start(bf16[32,2,16,256]{3,2,1,0:T(8,128)(2,1)} %get-tuple-element.65), calls=%async_computation.2 | async-start | bytes 1048576 | tf_op jit(solution)/shard_map/all_to_all | solution.py:969
  64.5 13.7 %copy-start.6 = (bf16[16,4,2,8,256]{4,3,2,1,0:T(8,128)(2,1)S(1)}, bf16[16,4,2,8,256]{4,3,2,1,0:T(8,128)(2,1)}, u32[]{:S(2)}) copy-start(bf16[16,4,2,8,256]{4,3,2,1,0:T(8,128)(2,1)} %copy.46) | copy-start | bytes 1572868
  80.9 0.8 copy-start.13
  93.5 4.4 %copy-start.9 = (bf16[1024,256]{1,0:T(8,128)(2,1)S(1)}, bf16[1024,256]{1,0:T(8,128)(2,1)}, u32[]{:S(2)}) copy-start(bf16[1024,256]{1,0:T(8,128)(2,1)} %w_proj_ref.1) | copy-start | bytes 1572868
  93.5 5.5 %copy-start.12 = (bf16[1024,256]{1,0:T(8,128)(2,1)S(1)}, bf16[1024,256]{1,0:T(8,128)(2,1)}, u32[]{:S(2)}) copy-start(bf16[1024,256]{1,0:T(8,128)(2,1)} %get-tuple-element.72.att_ref) | copy-start | bytes 1572868
  93.5 20.7 %all-to-all-start.3 = ((bf16[32,2,16,256]{3,2,1,0:T(8,128)(2,1)}), bf16[32,2,16,256]{3,2,1,0:T(8,128)(2,1)S(1)}, u32[]{:S(2)}, u32[]{:S(2)}) async-start(bf16[32,2,16,256]{3,2,1,0:T(8,128)(2,1)} %bitcast.126), calls=%async_computation.3 | async-start | bytes 1048576 | tf_op jit(solution)/shard_map/all_to_all | solution.py:969
  114.2 0.8 copy-start.11
  123.0 9.4 %copy-start.7 = (bf16[256,1152]{1,0:T(8,128)(2,1)S(1)}, bf16[256,1152]{1,0:T(8,128)(2,1)}, u32[]{:S(2)}) copy-start(bf16[256,1152]{1,0:T(8,128)(2,1)} %attention_weights.1) | copy-start | bytes 1769476
  123.0 9.4 %copy-start.8 = (bf16[256,1024]{1,0:T(8,128)(2,1)S(1)}, bf16[256,1024]{1,0:T(8,128)(2,1)}, u32[]{:S(2)}) copy-start(bf16[256,1024]{1,0:T(8,128)(2,1)} %get-tuple-element.96) | copy-start | bytes 1572868
  124.9 33.3 %all-to-all-start.4 = ((bf16[32,40,256]{2,1,0:T(8,128)(2,1)}), bf16[32,40,256]{2,1,0:T(8,128)(2,1)S(1)}, u32[]{:S(2)}, u32[]{:S(2)}) async-start(bf16[32,40,256]{2,1,0:T(8,128)(2,1)} %pad_maximum_fusion.1), calls=%async_computation.4 | async-start | bytes 1310720 | tf_op jit(solution)/shard_map/all_to_all | solution.py:851
  127.5 5.1 %collective-permute-start.4 = (bf16[1,64,256]{2,1,0:T(8,128)(2,1)S(1)}, bf16[1,64,256]{2,1,0:T(8,128)(2,1)S(1)}, u32[]{:S(2)}, u32[]{:S(2)}) collective-permute-start(bf16[1,64,256]{2,1,0:T(8,128)(2,1)S(1)} %get-tuple-element.110), channel_id=1, source_target_pairs={{0,8},{8,16},{16,24},{1,9},{9,17},{17,25},{2,10},{10,18},{18,26},{... | collective-permute-start | bytes 98312 | tf_op jit(solution)/shard_map/ppermute | solution.py:828
  131.0 5.9 %collective-permute-start.5 = (bf16[1,64,256]{2,1,0:T(8,128)(2,1)S(1)}, bf16[1,64,256]{2,1,0:T(8,128)(2,1)S(1)}, u32[]{:S(2)}, u32[]{:S(2)}) collective-permute-start(bf16[1,64,256]{2,1,0:T(8,128)(2,1)S(1)} %get-tuple-element.109), channel_id=1, source_target_pairs={{8,0},{16,8},{24,16},{9,1},{17,9},{25,17},{10,2},{18,10},{26,18},{... | collective-permute-start | bytes 98312 | tf_op jit(solution)/shard_map/ppermute | solution.py:828
  132.6 7.3 %copy-start.22 = (bf16[1,64,256]{2,1,0:T(8,128)(2,1)}, bf16[1,64,256]{2,1,0:T(8,128)(2,1)S(1)}, u32[]{:S(2)}) copy-start(bf16[1,64,256]{2,1,0:T(8,128)(2,1)S(1)} %collective-permute-done.4.up_ref) | copy-start | bytes 98308
  132.7 7.1 %collective-permute-start.10 = (bf16[128,2176]{1,0:T(8,128)(2,1)S(1)}, bf16[128,2176]{1,0:T(8,128)(2,1)S(1)}, u32[]{:S(2)}, u32[]{:S(2)}) collective-permute-start(bf16[128,2176]{1,0:T(8,128)(2,1)S(1)} %dynamic-slice_bitcast_fusion), channel_id=1, source_target_pairs={{0,1},{1,0},{2,3},{3,2},{4,5},{5,4},{6,7},{7,6},{8,9},{9,8},{10,11... | collective-permute-start | bytes 1671176 | tf_op jit(solution)/shard_map/ppermute | solution.py:863
  136.9 7.8 %copy-start.23 = (bf16[1,64,256]{2,1,0:T(8,128)(2,1)}, bf16[1,64,256]{2,1,0:T(8,128)(2,1)S(1)}, u32[]{:S(2)}) copy-start(bf16[1,64,256]{2,1,0:T(8,128)(2,1)S(1)} %collective-permute-done.5.down_ref) | copy-start | bytes 98308
  137.0 7.0 %collective-permute-start.7 = (bf16[18,1,256]{2,1,0:T(2,128)(2,1)S(1)}, bf16[18,1,256]{2,1,0:T(2,128)(2,1)S(1)}, u32[]{:S(2)}, u32[]{:S(2)}) collective-permute-start(bf16[18,1,256]{2,1,0:T(2,128)(2,1)S(1)} %pad_maximum_fusion.6), channel_id=1, source_target_pairs={{0,1},{1,2},{2,3},{3,4},{4,5},{5,6},{6,7},{8,9},{9,10},{10,11},{11... | collective-permute-start | bytes 27656 | tf_op jit(solution)/shard_map/ppermute | solution.py:828
  138.3 5.7 %collective-permute-start.6 = (bf16[18,1,256]{2,1,0:T(2,128)(2,1)S(1)}, bf16[18,1,256]{2,1,0:T(2,128)(2,1)S(1)}, u32[]{:S(2)}, u32[]{:S(2)}) collective-permute-start(bf16[18,1,256]{2,1,0:T(2,128)(2,1)S(1)} %pad_maximum_fusion.5), channel_id=1, source_target_pairs={{1,0},{2,1},{3,2},{4,3},{5,4},{6,5},{7,6},{9,8},{10,9},{11,10},{12... | collective-permute-start | bytes 27656 | tf_op jit(solution)/shard_map/ppermute | solution.py:828
  140.0 6.2 %collective-permute-start.13 = (bf16[32,2176]{1,0:T(8,128)(2,1)S(1)}, bf16[32,2176]{1,0:T(8,128)(2,1)S(1)}, u32[]{:S(2)}, u32[]{:S(2)}) collective-permute-start(bf16[32,2176]{1,0:T(8,128)(2,1)S(1)} %get-tuple-element.105), channel_id=1, source_target_pairs={{0,24},{8,0},{16,8},{24,16},{1,25},{9,1},{17,9},{25,17},{2,26},{10... | collective-permute-start | bytes 417800 | tf_op jit(solution)/shard_map/ppermute | solution.py:863
  140.6 7.1 %collective-permute-start.12 = (bf16[32,2176]{1,0:T(8,128)(2,1)S(1)}, bf16[32,2176]{1,0:T(8,128)(2,1)S(1)}, u32[]{:S(2)}, u32[]{:S(2)}) collective-permute-start(bf16[32,2176]{1,0:T(8,128)(2,1)S(1)} %get-tuple-element.106), channel_id=1, source_target_pairs={{0,16},{8,24},{16,0},{24,8},{1,17},{9,25},{17,1},{25,9},{2,18},{10... | collective-permute-start | bytes 417800 | tf_op jit(solution)/shard_map/ppermute | solution.py:863
  144.0 6.1 %collective-permute-start.11 = (bf16[32,2176]{1,0:T(8,128)(2,1)S(1)}, bf16[32,2176]{1,0:T(8,128)(2,1)S(1)}, u32[]{:S(2)}, u32[]{:S(2)}) collective-permute-start(bf16[32,2176]{1,0:T(8,128)(2,1)S(1)} %get-tuple-element.104), channel_id=1, source_target_pairs={{0,8},{8,16},{16,24},{24,0},{1,9},{9,17},{17,25},{25,1},{2,10},{10... | collective-permute-start | bytes 417800 | tf_op jit(solution)/shard_map/ppermute | solution.py:863
  150.2 26.1 %collective-permute-start.16 = (bf16[8,2176]{1,0:T(8,128)(2,1)S(1)}, bf16[8,2176]{1,0:T(8,128)(2,1)S(1)}, u32[]{:S(2)}, u32[]{:S(2)}) collective-permute-start(bf16[8,2176]{1,0:T(8,128)(2,1)S(1)} %get-tuple-element.116), channel_id=1, source_target_pairs={{0,6},{1,7},{2,0},{3,1},{4,2},{5,3},{6,4},{7,5},{8,14},{9,15},{10,... | collective-permute-start | bytes 104456 | tf_op jit(solution)/shard_map/ppermute | solution.py:863
  156.6 19.7 %collective-permute-start.15 = (bf16[8,2176]{1,0:T(8,128)(2,1)S(1)}, bf16[8,2176]{1,0:T(8,128)(2,1)S(1)}, u32[]{:S(2)}, u32[]{:S(2)}) collective-permute-start(bf16[8,2176]{1,0:T(8,128)(2,1)S(1)} %get-tuple-element.117), channel_id=1, source_target_pairs={{0,4},{1,5},{2,6},{3,7},{4,0},{5,1},{6,2},{7,3},{8,12},{9,13},{10,... | collective-permute-start | bytes 104456 | tf_op jit(solution)/shard_map/ppermute | solution.py:863
  156.8 19.5 %collective-permute-start.14 = (bf16[8,2176]{1,0:T(8,128)(2,1)S(1)}, bf16[8,2176]{1,0:T(8,128)(2,1)S(1)}, u32[]{:S(2)}, u32[]{:S(2)}) collective-permute-start(bf16[8,2176]{1,0:T(8,128)(2,1)S(1)} %get-tuple-element.115), channel_id=1, source_target_pairs={{0,2},{1,3},{2,4},{3,5},{4,6},{5,7},{6,0},{7,1},{8,10},{9,11},{10,... | collective-permute-start | bytes 104456 | tf_op jit(solution)/shard_map/ppermute | solution.py:863
  158.1 0.8 copy-start.5
  175.2 11.4 %copy-start.26 = (f32[1,64]{1,0:T(1,128)S(1)}, f32[1,64]{1,0:T(1,128)}, u32[]{:S(2)}) copy-start(f32[1,64]{1,0:T(1,128)} %get-tuple-element.80.hidden_ref) | copy-start | bytes 772
  176.2 4.6 %collective-permute-start.8 = (bf16[128,1152]{1,0:T(8,128)(2,1)S(1)}, bf16[128,1152]{1,0:T(8,128)(2,1)S(1)}, u32[]{:S(2)}, u32[]{:S(2)}) collective-permute-start(bf16[128,1152]{1,0:T(8,128)(2,1)S(1)} %dynamic-slice_bitcast_fusion.1), channel_id=1, source_target_pairs={{0,1},{1,0},{2,3},{3,2},{4,5},{5,4},{6,7},{7,6},{8,9},{9,8},{10,11... | collective-permute-start | bytes 884744 | tf_op jit(solution)/shard_map/ppermute | solution.py:863
  176.3 10.3 %collective-permute-start.17 = (bf16[1,8,2176]{2,1,0:T(8,128)(2,1)S(1)}, bf16[1,8,2176]{2,1,0:T(8,128)(2,1)S(1)}, u32[]{:S(2)}, u32[]{:S(2)}) collective-permute-start(bf16[1,8,2176]{2,1,0:T(8,128)(2,1)S(1)} %bitcast.96), channel_id=1, source_target_pairs={{0,2},{1,3},{2,4},{3,5},{4,6},{5,7},{6,0},{7,1},{8,10},{9,11},{10,... | collective-permute-start | bytes 104456 | tf_op jit(solution)/shard_map/ppermute | solution.py:863
  178.4 8.3 %collective-permute-start.18 = (bf16[1,8,2176]{2,1,0:T(8,128)(2,1)S(1)}, bf16[1,8,2176]{2,1,0:T(8,128)(2,1)S(1)}, u32[]{:S(2)}, u32[]{:S(2)}) collective-permute-start(bf16[1,8,2176]{2,1,0:T(8,128)(2,1)S(1)} %bitcast.97), channel_id=1, source_target_pairs={{0,4},{1,5},{2,6},{3,7},{4,0},{5,1},{6,2},{7,3},{8,12},{9,13},{10,... | collective-permute-start | bytes 104456 | tf_op jit(solution)/shard_map/ppermute | solution.py:863
  179.5 7.2 %collective-permute-start.19 = (bf16[1,8,2176]{2,1,0:T(8,128)(2,1)S(1)}, bf16[1,8,2176]{2,1,0:T(8,128)(2,1)S(1)}, u32[]{:S(2)}, u32[]{:S(2)}) collective-permute-start(bf16[1,8,2176]{2,1,0:T(8,128)(2,1)S(1)} %bitcast.98), channel_id=1, source_target_pairs={{0,6},{1,7},{2,0},{3,1},{4,2},{5,3},{6,4},{7,5},{8,14},{9,15},{10,... | collective-permute-start | bytes 104456 | tf_op jit(solution)/shard_map/ppermute | solution.py:863
  182.6 15.3 %all-to-all-start.5 = ((bf16[16,8,1152]{2,1,0:T(8,128)(2,1)}), bf16[16,8,1152]{2,1,0:T(8,128)(2,1)S(1)}, u32[]{:S(2)}, u32[]{:S(2)}) async-start(bf16[16,8,1152]{2,1,0:T(8,128)(2,1)} %fusion.3), calls=%async_computation.5 | async-start | bytes 589824 | tf_op jit(solution)/shard_map/all_to_all | solution.py:884
  186.6 5.0 %copy-start.1 = (bf16[16,64,256]{2,1,0:T(8,128)(2,1)S(1)}, bf16[16,64,256]{2,1,0:T(8,128)(2,1)}, u32[]{:S(2)}) copy-start(bf16[16,64,256]{2,1,0:T(8,128)(2,1)} %image_ref.3) | copy-start | bytes 1572868
  186.6 5.0 %copy-start.2 = (bf16[16,64,256]{2,1,0:T(8,128)(2,1)S(1)}, bf16[16,64,256]{2,1,0:T(8,128)(2,1)}, u32[]{:S(2)}) copy-start(bf16[16,64,256]{2,1,0:T(8,128)(2,1)} %get-tuple-element.81.low_ref) | copy-start | bytes 1572868
  186.6 5.0 %copy-start.3 = (bf16[1,256]{1,0:T(2,128)(2,1)S(1)}, bf16[1,256]{1,0:T(2,128)(2,1)}, u32[]{:S(2)}) copy-start(bf16[1,256]{1,0:T(2,128)(2,1)} %reshape.133.gain_ref) | copy-start | bytes 1540
  186.6 5.0 %copy-start.4 = (f32[1024,256]{1,0:T(8,128)S(1)}, f32[1024,256]{1,0:T(8,128)}, u32[]{:S(2)}) copy-start(f32[1024,256]{1,0:T(8,128)} %get-tuple-element.87.first_ref) | copy-start | bytes 3145732
  186.7 15.5 %collective-permute-start.20 = (bf16[4,8,2176]{2,1,0:T(8,128)(2,1)S(1)}, bf16[4,8,2176]{2,1,0:T(8,128)(2,1)S(1)}, u32[]{:S(2)}, u32[]{:S(2)}) collective-permute-start(bf16[4,8,2176]{2,1,0:T(8,128)(2,1)S(1)} %bitcast.103), channel_id=1, source_target_pairs={{0,8},{8,16},{16,24},{24,0},{1,9},{9,17},{17,25},{25,1},{2,10},{10... | collective-permute-start | bytes 417800 | tf_op jit(solution)/shard_map/ppermute | solution.py:863
  188.7 13.5 %collective-permute-start.21 = (bf16[4,8,2176]{2,1,0:T(8,128)(2,1)S(1)}, bf16[4,8,2176]{2,1,0:T(8,128)(2,1)S(1)}, u32[]{:S(2)}, u32[]{:S(2)}) collective-permute-start(bf16[4,8,2176]{2,1,0:T(8,128)(2,1)S(1)} %bitcast.104), channel_id=1, source_target_pairs={{0,16},{8,24},{16,0},{24,8},{1,17},{9,25},{17,1},{25,9},{2,18},{10... | collective-permute-start | bytes 417800 | tf_op jit(solution)/shard_map/ppermute | solution.py:863
  190.2 12.1 %collective-permute-start.22 = (bf16[4,8,2176]{2,1,0:T(8,128)(2,1)S(1)}, bf16[4,8,2176]{2,1,0:T(8,128)(2,1)S(1)}, u32[]{:S(2)}, u32[]{:S(2)}) collective-permute-start(bf16[4,8,2176]{2,1,0:T(8,128)(2,1)S(1)} %bitcast.105), channel_id=1, source_target_pairs={{0,24},{8,0},{16,8},{24,16},{1,25},{9,1},{17,9},{25,17},{2,26},{10... | collective-permute-start | bytes 417800 | tf_op jit(solution)/shard_map/ppermute | solution.py:863
  198.7 13.4 %all-to-all-start.6 = ((bf16[16,8,1152]{2,1,0:T(8,128)(2,1)}), bf16[16,8,1152]{2,1,0:T(8,128)(2,1)S(1)}, u32[]{:S(2)}, u32[]{:S(2)}) async-start(bf16[16,8,1152]{2,1,0:T(8,128)(2,1)} %broadcast_in_dim.17), calls=%async_computation.6 | async-start | bytes 589824 | tf_op jit(solution)/shard_map/all_to_all | solution.py:884
  202.2 0.7 copy-start.17
  202.2 0.7 copy-start.19
  202.3 1.4 slice-start
  202.3 1.4 copy-start.10
  202.3 10.5 %collective-permute-start.23 = (bf16[16,8,2176]{2,1,0:T(8,128)(2,1)S(1)}, bf16[16,8,2176]{2,1,0:T(8,128)(2,1)S(1)}, u32[]{:S(2)}, u32[]{:S(2)}) collective-permute-start(bf16[16,8,2176]{2,1,0:T(8,128)(2,1)S(1)} %bitcast.101), channel_id=1, source_target_pairs={{0,1},{1,0},{2,3},{3,2},{4,5},{5,4},{6,7},{7,6},{8,9},{9,8},{10,11... | collective-permute-start | bytes 1671176 | tf_op jit(solution)/shard_map/ppermute | solution.py:863
  203.7 8.3 %copy-start.18 = (f32[1,1024]{1,0:T(1,128)S(1)}, f32[1,1024]{1,0:T(1,128)}, u32[]{:S(2)}) copy-start(f32[1,1024]{1,0:T(1,128)} %get-tuple-element.94) | copy-start | bytes 12292
  212.0 2.9 %collective-permute-start.9 = (bf16[128,1152]{1,0:T(8,128)(2,1)S(1)}, bf16[128,1152]{1,0:T(8,128)(2,1)S(1)}, u32[]{:S(2)}, u32[]{:S(2)}) collective-permute-start(bf16[128,1152]{1,0:T(8,128)(2,1)S(1)} %bitcast.93), channel_id=1, source_target_pairs={{0,1},{1,0},{2,3},{3,2},{4,5},{5,4},{6,7},{7,6},{8,9},{9,8},{10,11... | collective-permute-start | bytes 884744 | tf_op jit(solution)/shard_map/ppermute | solution.py:863

commit v6 on v5

--- a/solution.py
+++ b/solution.py
@@ -604,6 +604,10 @@
     )(recv, mixed, cot, gain, act, gate, w_project_t)
 
 
+def core_place():
+    return (lax.axis_index("col") % 2).astype(jnp.int32).reshape(1)
+
+
 def unpack_kernel(
     place_ref, near_ref, far_ref, expand_ref, depth_ref, norm0_ref, norm1_ref, tail_ref
 ):
@@ -630,7 +634,6 @@
 def run_unpack(near, far, expanded):
     rows = near.shape[0]
     channels = 2 * rows
-    place = (lax.axis_index("col") % 2).astype(jnp.int32).reshape(1)
     vmem = pl.BlockSpec(memory_space=pltpu.VMEM)
     return pl.pallas_call(
         unpack_kernel,
@@ -646,15 +649,15 @@
         compiler_params=SMALL,
         cost_estimate=estimate(2),
         name="unpack",
-    )(place, near, far)
+    )(core_place(), near, far)
 
 
 def expand_back_kernel(
     cells_total,
-    parts_ref, hidden_ref, gate_all_ref, w_sq_ref, w_ex_ref,
+    place_ref, parts_ref, hidden_ref, gate_all_ref, w_sq_ref, w_ex_ref,
     low_ref, up_ref, down_ref, side_ref, w_projt_ref, gate_ref, slope_ref, side_slope_ref,
     spread_slope_ref, spread_ref, w_dep_ref, turned_ref, w_exp_ref, gain_ref, norm1_ref,
-    weights_ref, first_ref, logit_ref, pre_ref,
+    mine_ref, other_ref, first_ref, logit_ref, pre_ref,
     main_ref, side_grad_ref, window_ref, expanded_ref, pool_ref, tail_ref, norm_ref,
 ):
     rows, cols, channels = low_ref.shape
@@ -734,7 +737,18 @@
     grad_expanded = expanded_ref[...]
     w_exp = w_exp_ref[...]
     weights = dot(turned_ref[...], grad_expanded)
-    weights_ref[:, pl.ds(pl.multiple_of(step * BLOCK, BLOCK), BLOCK)] = weights.astype(BF16)
+
+
+    def keep(at, values):
+        half = channels // 2
+        for place in range(2):
+
+            @pl.when(place_ref[0] == place)
+            def _():
+                mine_ref[:, at] = values[place * half : (place + 1) * half]
+                other_ref[:, at] = values[(1 - place) * half : (2 - place) * half]
+
+    keep(pl.ds(pl.multiple_of(step * BLOCK, BLOCK), BLOCK), weights.astype(BF16))
     norm_ref[...] += jnp.sum(weights * w_exp.astype(F32), axis=1, keepdims=True)
     first_ref[...] += dot(grad_expanded, w_exp, ((1,), (1,)))
 
@@ -747,7 +761,7 @@
             tail_ref[start + k : start + k + 1, :] = norm[:, piece]
             at = start + channels // LANES + k
             tail_ref[at : at + 1, :] = norm1_ref[:, piece]
-        weights_ref[:, steps * BLOCK :] = tail_ref[...].astype(BF16)
+        keep(slice(mine_ref.shape[1] - LANES, mine_ref.shape[1]), tail_ref[...].astype(BF16))
 
 
 def run_expand_back(
@@ -761,6 +775,7 @@
         functools.partial(expand_back_kernel, cells_total),
         grid=(steps,),
         in_specs=[
+            pl.BlockSpec(memory_space=pltpu.SMEM),
             pl.BlockSpec(
                 (parts.shape[0], 2 * steps, BLOCK), lambda e: (0, parts.shape[1] // (2 * steps) - 1, 0)
             ),
@@ -773,11 +788,13 @@
             whole(gain.shape), whole(norm1.shape),
         ],
         out_specs=[
-            whole((channels, expanded + LANES)), whole((rows * cols, channels)),
+            whole((channels // 2, expanded + LANES)), whole((channels // 2, expanded + LANES)),
+            whole((rows * cols, channels)),
             whole((1, expanded)), whole(hidden.shape),
         ],
         out_shape=[
-            jax.ShapeDtypeStruct((channels, expanded + LANES), BF16),
+            jax.ShapeDtypeStruct((channels // 2, expanded + LANES), BF16),
+            jax.ShapeDtypeStruct((channels // 2, expanded + LANES), BF16),
             jax.ShapeDtypeStruct((rows * cols, channels), F32),
             jax.ShapeDtypeStruct((1, expanded), F32),
             jax.ShapeDtypeStruct(hidden.shape, F32),
@@ -795,7 +812,7 @@
         cost_estimate=estimate(14),
         name="expand_back",
     )(
-        parts, hidden, gate, w_squeeze, w_excite, low, up, down, side, w_project_t, gate,
+        core_place(), parts, hidden, gate, w_squeeze, w_excite, low, up, down, side, w_project_t, gate,
         slope, side_slope, spread_slope, spread, w_depth, turned, w_expand, gain, norm1,
     )
 
@@ -873,11 +890,11 @@
     return total.astype(BF16)
 
 
-def sum_shares(matrix):
-    rows, columns = matrix.shape
+def sum_shares(mine, other):
+    rows, columns = 2 * mine.shape[0], mine.shape[1]
     count = lax.axis_size("row") * lax.axis_size("col")
     pair = ("col", 1, 2)
-    half = sum_parts(matrix, *pair)
+    half = (mine.astype(F32) + send_on(other, *pair, 1).astype(F32)).astype(BF16)
     same_core = [list(range(k, count, 2)) for k in range(2)]
 
     def around(blocks):
@@ -1046,13 +1063,15 @@
         parts = hand_around(gate_grad)
         attended_home = swap_groups(attended_sent, parity)
     up, down = halo_rows(grad_low, 1)
-    side = halo_sides(grad_low, up, down, 1)
+    edge_up, edge_down, parts = lax.optimization_barrier((up, down, parts))
+    side = halo_sides(grad_low, edge_up, edge_down, 1)
     weights = jnp.concatenate([weights, grad_project], axis=1)
     weights, _ = lax.optimization_barrier((weights, up))
     steps = sum_steps()
     for step in steps:
         weights = sum_parts(weights, *step)
-    late, grad_first, logit, pre = run_expand_back(
+    grad_low, weights = lax.optimization_barrier((grad_low, weights))
+    late, late_other, grad_first, logit, pre = run_expand_back(
         cells_total, parts, hidden, gate, w_squeeze, w_excite, grad_low, up, down, side,
         w_project_t, slope, side_slope, spread_slope, spread, w_depth, turned_first, w_expand,
         gain_first, grad_norm1,
@@ -1065,7 +1084,7 @@
     grad_qkv, grad_out_proj, grad_bias, grad_project = run_unpack_weights(
         steps, weights, other, channels, expanded, halves, members
     )
-    grad_expand, grad_depth, grad_norm0, grad_norm1 = run_unpack(*sum_shares(late), expanded)
+    grad_expand, grad_depth, grad_norm0, grad_norm1 = run_unpack(*sum_shares(late, late_other), expanded)
     grad_image = run_image_back(
         image.reshape(-1, channels), gain_first, grad_first, grad_low.reshape(-1, channels)
     )

time: 217 us -> 223 us (1.028)
  starting transfers between devices: 69.6 us -> 77.1 us
  waiting for transfers between devices: 40.7 us -> 38.3 us
    ppermute x16, waiting for transfers between devices: 5.36 us -> 13.6 us  [send_on(): return lax.ppermute(v, axis, pairs)]
    all_to_all x2, waiting for transfers between devices: 11.2 us -> 5.48 us  [around(): lax.all_to_all(blocks, AXES, split_axis=0, concat_axis=0, tiled=True, axi...]
    ppermute x8, waiting for transfers between devices: 7.18 us -> 1.83 us  [shift(): return lax.ppermute(cells, axis, pairs)]
    all_to_all x2, starting transfers between devices: 9.41 us -> 12.5 us  [hand_around(): return lax.all_to_all(blocks, AXES, split_axis=0, concat_axis=0, tiled=True)]
    ppermute x16, starting transfers between devices: 21.5 us -> 24.4 us  [send_on(): return lax.ppermute(v, axis, pairs)]
  transfers between devices with their start and end apart: 31 -> 31, of which waited for: 11 -> 13; matrix products, arithmetic and copies ran while one was open for 9% -> 8% of each run, Pallas kernels for 25% -> 17%
where the time goes in v6:
time: 223 us; the launch traced here: 222 us
  Pallas kernels  79.2 us (36%)
  starting transfers between devices  77.1 us (35%)
  waiting for transfers between devices  38.3 us (17%)
  local copies, waits for them, and re-layouts  14.8 us (7%)
  other arithmetic  8.81 us (4%)
    ppermute x16, starting transfers between devices, send_on(): return lax.ppermute(v, axis, pairs)  24.4 us
    pallas_call x1, Pallas kernels, run_expand_back(): pl.pallas_call(functools.partial(expand_back_kernel, cells_total), grid=(...  17.8 us
    ppermute x8, starting transfers between devices, shift(): return lax.ppermute(cells, axis, pairs)  17.6 us
    all_to_all x3, starting transfers between devices, swap_groups(): lax.all_to_all(blocks, AXES, split_axis=0, concat_axis=0, tiled=True, axi...  14 us
    pallas_call x1, Pallas kernels, run_slope(): pl.pallas_call(slope_kernel, grid=(expanded // BLOCK,), in_specs=[pl.Bloc...  13.7 us
    ppermute x16, waiting for transfers between devices, send_on(): return lax.ppermute(v, axis, pairs)  13.6 us
    all_to_all x3, waiting for transfers between devices, swap_groups(): lax.all_to_all(blocks, AXES, split_axis=0, concat_axis=0, tiled=True, axi...  13.4 us
    all_to_all x2, starting transfers between devices, hand_around(): return lax.all_to_all(blocks, AXES, split_axis=0, concat_axis=0, tiled=True)  12.5 us
  transfers between devices with their start and end apart: 31, of which 13 were waited for; matrix products, arithmetic and copies ran while one was open for 8% of the time, Pallas kernels for 17%

profile of v6, /device:TPU:0, one launch (start us, length us, event | category | flops | bytes accessed | tf_op | source)
XLA Modules:
  0.0 221.7 jit_solution(5833829800113360515)
XLA Ops:
  0.7 0.9 fusion.14
  1.6 4.8 %collective-permute-start = (bf16[2,64,256]{2,1,0:T(8,128)(2,1)S(1)}, bf16[2,64,256]{2,1,0:T(8,128)(2,1)S(1)}, u32[]{:S(2)}, u32[]{:S(2)}) collective-permute-start(bf16[2,64,256]{2,1,0:T(8,128)(2,1)S(1)} %get-tuple-element.126), channel_id=1, source_target_pairs={{0,8},{8,16},{16,24},{1,9},{9,17},{17,25},{2,10},{10,18},{18,26},{... | collective-permute-start | bytes 196616 | tf_op jit(solution)/shard_map/ppermute | solution.py:845
  6.4 1.3 collective-permute-start.1
  7.7 1.9 copy.45
  9.6 7.0 %all-to-all-start.1 = ((bf16[32,2,16,256]{3,2,1,0:T(8,128)(2,1)}), bf16[32,2,16,256]{3,2,1,0:T(8,128)(2,1)S(1)}, u32[]{:S(2)}, u32[]{:S(2)}) async-start(bf16[32,2,16,256]{3,2,1,0:T(8,128)(2,1)} %bitcast.3), calls=%async_computation.1 | async-start | bytes 1048576 | tf_op jit(solution)/shard_map/all_to_all | solution.py:986
  17.2 6.5 %expand.1 = (bf16[1024,256]{1,0:T(8,128)(2,1)}, bf16[16,64,1024]{2,1,0:T(8,128)(2,1)}, bf16[16,64,1024]{2,1,0:T(8,128)(2,1)}) custom-call(bf16[16,64,256]{2,1,0:T(8,128)(2,1)} %image_ref.3, bf16[1,256]{1,0:T(2,128)(2,1)} %reshape.129.gain_ref, bf16[256,1024]{1,0:T(8,128)(2,1)} %w_exp_ref.5), custom_call_target="tpu_custom_call" | custom-call | flops 15399999488 | bytes 50400000 | tf_op jit(solution)/shard_map/expand/pallas_call | solution.py:112
  23.7 0.9 fusion.13
  24.7 1.3 collective-permute-start.2
  26.1 3.0 %collective-permute-start.3 = (bf16[20,2,256]{2,0,1:T(8,128)(2,1)S(1)}, bf16[20,2,256]{2,0,1:T(8,128)(2,1)S(1)}, u32[]{:S(2)}, u32[]{:S(2)}) collective-permute-start(bf16[20,2,256]{2,0,1:T(8,128)(2,1)S(1)} %pad_maximum_fusion.4), channel_id=1, source_target_pairs={{0,1},{1,2},{2,3},{3,4},{4,5},{5,6},{6,7},{8,9},{9,10},{10,11},{11... | collective-permute-start | bytes 61448 | tf_op jit(solution)/shard_map/ppermute | solution.py:845
  30.7 8.9 %depthwise.1 = (bf16[416,1024]{1,0:T(8,128)(2,1)}, bf16[16,64,1024]{2,1,0:T(8,128)(2,1)}, f32[32,1,1024]{2,1,0:T(1,128)}) custom-call(bf16[2,64,256]{2,1,0:T(8,128)(2,1)} %copy-done.20, bf16[2,64,256]{2,1,0:T(8,128)(2,1)} %copy-done.21, bf16[160,256]{1,0:T(8,128)(2,1)} %maximum_bitcast_fusion.side_ref, bf16[1,256]{1,0:T(2,128)(2,1)} %reshape.129.gain_ref, ...), custom_call_target="tpu_custom_call" | custom-call | flops 1100000000 | bytes 3600000 | tf_op jit(solution)/shard_map/depthwise/pallas_call | solution.py:203
  39.6 8.0 %all-to-all-start = ((f32[32,1,1024]{2,1,0:T(1,128)}), f32[32,1,1024]{2,1,0:T(1,128)S(1)}, u32[]{:S(2)}, u32[]{:S(2)}) async-start(f32[32,1,1024]{2,1,0:T(1,128)} %get-tuple-element.68), calls=%async_computation | async-start | bytes 262144 | tf_op jit(solution)/shard_map/all_to_all | solution.py:868
  47.6 0.8 copy.47.w_sq_ref
  49.8 0.8 pad_maximum_fusion.2.bias_ref
  50.6 1.1 copy.46
  51.7 4.0 %all-to-all-done.parts_ref = f32[32,1,1024]{2,1,0:T(1,128)S(1)} async-done(((f32[32,1,1024]{2,1,0:T(1,128)}), f32[32,1,1024]{2,1,0:T(1,128)S(1)}, u32[]{:S(2)}, u32[]{:S(2)}) %all-to-all-start) | async-done | bytes 131104 | tf_op jit(solution)/shard_map/all_to_all | solution.py:868
  56.4 5.4 %mix.1 = (f32[1,1024]{1,0:T(1,128)}, f32[1,64]{1,0:T(1,128)}, f32[1,1024]{1,0:T(1,128)}, bf16[16,64,256]{2,1,0:T(8,128)(2,1)}, bf16[32,2,16,256]{3,2,1,0:T(8,128)(2,1)}) custom-call(f32[32,1,1024]{2,1,0:T(1,128)} %copy-done.16, bf16[1024,64]{1,0:T(8,128)(2,1)} %copy.47.w_sq_ref, bf16[64,1024]{1,0:T(8,128)(2,1)} %w_ex_ref.3, ...), custom_call_target="tpu_custom_call" | custom-call | flops 5500000256 | bytes 18000000 | tf_op jit(solution)/shard_map/mix/pallas_call | solution.py:343
  61.8 2.6 %all-to-all-start.2 = ((bf16[32,2,16,256]{3,2,1,0:T(8,128)(2,1)}), bf16[32,2,16,256]{3,2,1,0:T(8,128)(2,1)S(1)}, u32[]{:S(2)}, u32[]{:S(2)}) async-start(bf16[32,2,16,256]{3,2,1,0:T(8,128)(2,1)} %get-tuple-element.71), calls=%async_computation.2 | async-start | bytes 1048576 | tf_op jit(solution)/shard_map/all_to_all | solution.py:986
  64.5 13.7 %slope.1 = (bf16[18,64,1024]{2,1,0:T(8,128)(2,1)}, f32[18,8,1024]{2,1,0:T(8,128)}, bf16[16,64,1024]{2,1,0:T(8,128)(2,1)}, bf16[256,1024]{1,0:T(8,128)(2,1)}) custom-call(f32[4]{0:T(128)} %add_convert_fusion.1.flags_ref, bf16[416,1024]{1,0:T(8,128)(2,1)} %get-tuple-element.72.ring_ref, bf16[3,3,1024]{2,1,0:T(4,128)(2,1)} %w_dep_ref.5, ...), custom_call_target="tpu_custom_call" | custom-call | flops 14300000256 | bytes 46800000 | tf_op jit(solution)/shard_map/slope/pallas_call | solution.py:278
  78.2 1.1 convolution_convert_fusion.att_grad_ref
  79.3 1.5 all-to-all-done.2
  80.8 0.8 copy-done.12
  81.6 11.8 %attention.1 = (bf16[1024,256]{1,0:T(8,128)(2,1)}, bf16[1024,256]{1,0:T(8,128)(2,1)}, bf16[1024,256]{1,0:T(8,128)(2,1)}, bf16[1024,768]{1,0:T(8,128)(2,1)}, f32[2,256,64]{2,1,0:T(8,128)}) custom-call(bf16[1024,256]{1,0:T(8,128)(2,1)} %bitcast.120, bf16[1024,256]{1,0:T(8,128)(2,1)} %convolution_convert_fusion.att_grad_ref, bf16[256,768]{1,0:T(8,128)(2,1)} %w_qkv_ref.1, ...), custom_call_target="tpu_custom_call" | custom-call | flops 15399999488 | bytes 50400000 | tf_op jit(solution)/shard_map/attention/pallas_call | solution.py:480
  93.4 4.4 %all-to-all-start.3 = ((bf16[32,2,16,256]{3,2,1,0:T(8,128)(2,1)}), bf16[32,2,16,256]{3,2,1,0:T(8,128)(2,1)S(1)}, u32[]{:S(2)}, u32[]{:S(2)}) async-start(bf16[32,2,16,256]{3,2,1,0:T(8,128)(2,1)} %bitcast.119), calls=%async_computation.3 | async-start | bytes 1048576 | tf_op jit(solution)/shard_map/all_to_all | solution.py:986
  97.8 1.0 copy.50
  98.8 3.4 %attention_weights.1 = bf16[256,1152]{1,0:T(8,128)(2,1)} custom-call(bf16[1024,256]{1,0:T(8,128)(2,1)} %get-tuple-element.80.x_ref, bf16[1024,768]{1,0:T(8,128)(2,1)} %get-tuple-element.81.packed_grad_ref, bf16[1024,256]{1,0:T(8,128)(2,1)} %get-tuple-element.78.att_ref, bf16[1024,256]{1,0:T(8,128)(2,1)} %bitcast.108, f32[2,256,64]{2,1,0:T(8,128)} %get-tuple-element.82.bias_ref), custom_call_target="tpu_custom_call" | custom-call | flops 5500000256 | bytes 18000000 | tf_op jit(solution)/shard_map/attention_weights/pallas_call | solution.py:518
  102.2 11.9 %all-to-all-done.3.recv_ref = bf16[32,2,16,256]{3,2,1,0:T(8,128)(2,1)S(1)} async-done(((bf16[32,2,16,256]{3,2,1,0:T(8,128)(2,1)}), bf16[32,2,16,256]{3,2,1,0:T(8,128)(2,1)S(1)}, u32[]{:S(2)}, u32[]{:S(2)}) %all-to-all-start.3) | async-done | bytes 524320 | tf_op jit(solution)/shard_map/all_to_all | solution.py:986
  114.1 0.8 copy-done.11
  114.9 6.3 %mixed_back.1 = (bf16[16,64,256]{2,1,0:T(8,128)(2,1)}, f32[1,256]{1,0:T(1,128)}, bf16[256,1024]{1,0:T(8,128)(2,1)}, bf16[32,8,256]{2,1,0:T(8,128)(2,1)}) custom-call(bf16[32,2,16,256]{3,2,1,0:T(8,128)(2,1)} %copy-done.11, bf16[16,64,256]{2,1,0:T(8,128)(2,1)} %get-tuple-element.70.mixed_ref, bf16[16,64,256]{2,1,0:T(8,128)(2,1)} %cot_ref.1, ...), custom_call_target="tpu_custom_call" | custom-call | flops 7699999744 | bytes 25200000 | tf_op jit(solution)/shard_map/mixed_back/pallas_call | solution.py:580
  122.0 1.5 collective-permute-start.4
  123.6 1.2 pad_maximum_fusion
  126.2 0.9 pad_maximum_fusion.1
  127.1 4.5 %all-to-all-start.4 = ((bf16[32,40,256]{2,1,0:T(8,128)(2,1)}), bf16[32,40,256]{2,1,0:T(8,128)(2,1)S(1)}, u32[]{:S(2)}, u32[]{:S(2)}) async-start(bf16[32,40,256]{2,1,0:T(8,128)(2,1)} %pad_maximum_fusion.1), calls=%async_computation.4 | async-start | bytes 1310720 | tf_op jit(solution)/shard_map/all_to_all | solution.py:868
  131.6 1.3 collective-permute-start.5
  133.1 2.7 %collective-permute-start.7 = (bf16[32,2176]{1,0:T(8,128)(2,1)S(1)}, bf16[32,2176]{1,0:T(8,128)(2,1)S(1)}, u32[]{:S(2)}, u32[]{:S(2)}) collective-permute-start(bf16[32,2176]{1,0:T(8,128)(2,1)S(1)} %get-tuple-element.116), channel_id=1, source_target_pairs={{0,8},{8,16},{16,24},{24,0},{1,9},{9,17},{17,25},{25,1},{2,10},{10... | collective-permute-start | bytes 417800 | tf_op jit(solution)/shard_map/ppermute | solution.py:880
  135.8 1.8 collective-permute-start.8
  137.6 2.4 %collective-permute-start.9 = (bf16[32,2176]{1,0:T(8,128)(2,1)S(1)}, bf16[32,2176]{1,0:T(8,128)(2,1)S(1)}, u32[]{:S(2)}, u32[]{:S(2)}) collective-permute-start(bf16[32,2176]{1,0:T(8,128)(2,1)S(1)} %get-tuple-element.117), channel_id=1, source_target_pairs={{0,24},{8,0},{16,8},{24,16},{1,25},{9,1},{17,9},{25,17},{2,26},{10... | collective-permute-start | bytes 417800 | tf_op jit(solution)/shard_map/ppermute | solution.py:880
  140.0 0.9 fusion.11
  140.9 4.0 %collective-permute-done.7 = bf16[32,2176]{1,0:T(8,128)(2,1)S(1)} collective-permute-done((bf16[32,2176]{1,0:T(8,128)(2,1)S(1)}, bf16[32,2176]{1,0:T(8,128)(2,1)S(1)}, u32[]{:S(2)}, u32[]{:S(2)}) %collective-permute-start.7) | collective-permute-done | bytes 139296 | tf_op jit(solution)/shard_map/ppermute | solution.py:880
  144.8 2.5 %collective-permute-done.8 = bf16[32,2176]{1,0:T(8,128)(2,1)S(1)} collective-permute-done((bf16[32,2176]{1,0:T(8,128)(2,1)S(1)}, bf16[32,2176]{1,0:T(8,128)(2,1)S(1)}, u32[]{:S(2)}, u32[]{:S(2)}) %collective-permute-start.8) | collective-permute-done | bytes 139296 | tf_op jit(solution)/shard_map/ppermute | solution.py:880
  147.8 2.7 %collective-permute-start.10 = (bf16[8,2176]{1,0:T(8,128)(2,1)S(1)}, bf16[8,2176]{1,0:T(8,128)(2,1)S(1)}, u32[]{:S(2)}, u32[]{:S(2)}) collective-permute-start(bf16[8,2176]{1,0:T(8,128)(2,1)S(1)} %get-tuple-element.127), channel_id=1, source_target_pairs={{0,2},{1,3},{2,4},{3,5},{4,6},{5,7},{6,0},{7,1},{8,10},{9,11},{10,... | collective-permute-start | bytes 104456 | tf_op jit(solution)/shard_map/ppermute | solution.py:880
  150.5 1.9 collective-permute-start.11
  152.4 1.6 collective-permute-start.12
  154.1 1.3 collective-permute-start.13
  155.4 3.0 %collective-permute-start.14 = (bf16[18,1,256]{2,1,0:T(2,128)(2,1)S(1)}, bf16[18,1,256]{2,1,0:T(2,128)(2,1)S(1)}, u32[]{:S(2)}, u32[]{:S(2)}) collective-permute-start(bf16[18,1,256]{2,1,0:T(2,128)(2,1)S(1)} %pad_maximum_fusion.6), channel_id=1, source_target_pairs={{0,1},{1,2},{2,3},{3,4},{4,5},{5,6},{6,7},{8,9},{9,10},{10,11},{11... | collective-permute-start | bytes 27656 | tf_op jit(solution)/shard_map/ppermute | solution.py:845
  160.0 17.8 %expand_back.1 = (bf16[128,1152]{1,0:T(8,128)(2,1)}, bf16[128,1152]{1,0:T(8,128)(2,1)}, f32[1024,256]{1,0:T(8,128)}, f32[1,1024]{1,0:T(1,128)}, f32[1,64]{1,0:T(1,128)}) custom-call(s32[1]{0:T(128)} %bitcast.25.place_ref, bf16[32,40,256]{2,1,0:T(8,128)(2,1)} %copy-done.5, f32[1,64]{1,0:T(1,128)} %get-tuple-element.88.hidden_ref, ...), custom_call_target="tpu_custom_call" | custom-call | flops 15399999488 | bytes 50400000 | tf_op jit(solution)/shard_map/expand_back/pallas_call | solution.py:774
  178.3 1.4 collective-permute-done.15
  179.7 1.8 fusion.2
  181.4 5.1 %all-to-all-start.5 = ((bf16[16,8,1152]{2,1,0:T(8,128)(2,1)}), bf16[16,8,1152]{2,1,0:T(8,128)(2,1)S(1)}, u32[]{:S(2)}, u32[]{:S(2)}) async-start(bf16[16,8,1152]{2,1,0:T(8,128)(2,1)} %fusion.2), calls=%async_computation.5 | async-start | bytes 589824 | tf_op jit(solution)/shard_map/all_to_all | solution.py:901
  186.6 2.0 collective-permute-start.17
  188.6 2.4 %collective-permute-start.18 = (bf16[1,8,2176]{2,1,0:T(8,128)(2,1)S(1)}, bf16[1,8,2176]{2,1,0:T(8,128)(2,1)S(1)}, u32[]{:S(2)}, u32[]{:S(2)}) collective-permute-start(bf16[1,8,2176]{2,1,0:T(8,128)(2,1)S(1)} %bitcast.91), channel_id=1, source_target_pairs={{0,4},{1,5},{2,6},{3,7},{4,0},{5,1},{6,2},{7,3},{8,12},{9,13},{10,... | collective-permute-start | bytes 104456 | tf_op jit(solution)/shard_map/ppermute | solution.py:880
  190.9 1.5 collective-permute-start.19
  192.4 1.1 fusion
  193.5 3.6 %collective-permute-done.17.refs_1_ = bf16[1,8,2176]{2,1,0:T(8,128)(2,1)S(1)} collective-permute-done((bf16[1,8,2176]{2,1,0:T(8,128)(2,1)S(1)}, bf16[1,8,2176]{2,1,0:T(8,128)(2,1)S(1)}, u32[]{:S(2)}, u32[]{:S(2)}) %collective-permute-start.17) | collective-permute-done | bytes 34848 | tf_op jit(solution)/shard_map/ppermute | solution.py:880
  197.1 1.8 collective-permute-done.18.refs_2_
  198.9 1.5 collective-permute-start.20
  200.4 1.5 collective-permute-start.21
  201.9 1.5 collective-permute-start.22
  204.2 3.5 %all-to-all-start.6 = ((bf16[16,8,1152]{2,1,0:T(8,128)(2,1)}), bf16[16,8,1152]{2,1,0:T(8,128)(2,1)S(1)}, u32[]{:S(2)}, u32[]{:S(2)}) async-start(bf16[16,8,1152]{2,1,0:T(8,128)(2,1)} %broadcast_in_dim.17), calls=%async_computation.6 | async-start | bytes 589824 | tf_op jit(solution)/shard_map/all_to_all | solution.py:901
  207.7 0.8 broadcast_multiply_fusion
  208.7 0.9 copy-done.1
  210.1 2.2 %image_back.1 = bf16[1024,256]{1,0:T(8,128)(2,1)} custom-call(bf16[1024,256]{1,0:T(8,128)(2,1)S(1)} %bitcast.89, bf16[1,256]{1,0:T(2,128)(2,1)S(1)} %copy-done.3, f32[1024,256]{1,0:T(8,128)S(1)} %copy-done.4, bf16[1024,256]{1,0:T(8,128)(2,1)S(1)} %bitcast.94), custom_call_target="tpu_custom_call" | custom-call | flops 4400000000 | bytes 14400000 | tf_op jit(solution)/shard_map/image_back/pallas_call | solution.py:830
  212.3 5.5 %all-to-all-done.6 = bf16[16,8,1152]{2,1,0:T(8,128)(2,1)S(1)} async-done(((bf16[16,8,1152]{2,1,0:T(8,128)(2,1)}), bf16[16,8,1152]{2,1,0:T(8,128)(2,1)S(1)}, u32[]{:S(2)}, u32[]{:S(2)}) %all-to-all-start.6) | async-done | bytes 294944 | tf_op jit(solution)/shard_map/all_to_all | solution.py:901
  218.6 2.1 unpack_weights.1
  220.7 1.1 unpack.1
  (120 shorter events, 11.5 us)
Async XLA Ops:
  0.6 77.5 %copy-start = (bf16[256,256]{1,0:T(8,128)(2,1)S(1)}, bf16[256,256]{1,0:T(8,128)(2,1)}, u32[]{:S(2)}) copy-start(bf16[256,256]{1,0:T(8,128)(2,1)} %param.22) | copy-start | bytes 393220
  0.7 16.0 %copy-start.24 = (bf16[256]{0:T(256)(128)(2,1)S(1)}, bf16[256]{0:T(256)(128)(2,1)}, u32[]{:S(2)}) copy-start(bf16[256]{0:T(256)(128)(2,1)} %param.14) | copy-start | bytes 1540
  1.6 23.0 %collective-permute-start = (bf16[2,64,256]{2,1,0:T(8,128)(2,1)S(1)}, bf16[2,64,256]{2,1,0:T(8,128)(2,1)S(1)}, u32[]{:S(2)}, u32[]{:S(2)}) collective-permute-start(bf16[2,64,256]{2,1,0:T(8,128)(2,1)S(1)} %get-tuple-element.126), channel_id=1, source_target_pairs={{0,8},{8,16},{16,24},{1,9},{9,17},{17,25},{2,10},{10,18},{18,26},{... | collective-permute-start | bytes 196616 | tf_op jit(solution)/shard_map/ppermute | solution.py:845
  6.4 18.2 %collective-permute-start.1 = (bf16[2,64,256]{2,1,0:T(8,128)(2,1)S(1)}, bf16[2,64,256]{2,1,0:T(8,128)(2,1)S(1)}, u32[]{:S(2)}, u32[]{:S(2)}) collective-permute-start(bf16[2,64,256]{2,1,0:T(8,128)(2,1)S(1)} %get-tuple-element.125), channel_id=1, source_target_pairs={{8,0},{16,8},{24,16},{9,1},{17,9},{25,17},{10,2},{18,10},{26,18},{... | collective-permute-start | bytes 196616 | tf_op jit(solution)/shard_map/ppermute | solution.py:845
  9.6 30.0 %all-to-all-start.1 = ((bf16[32,2,16,256]{3,2,1,0:T(8,128)(2,1)}), bf16[32,2,16,256]{3,2,1,0:T(8,128)(2,1)S(1)}, u32[]{:S(2)}, u32[]{:S(2)}) async-start(bf16[32,2,16,256]{3,2,1,0:T(8,128)(2,1)} %bitcast.3), calls=%async_computation.1 | async-start | bytes 1048576 | tf_op jit(solution)/shard_map/all_to_all | solution.py:986
  24.6 6.1 %copy-start.20 = (bf16[2,64,256]{2,1,0:T(8,128)(2,1)}, bf16[2,64,256]{2,1,0:T(8,128)(2,1)S(1)}, u32[]{:S(2)}) copy-start(bf16[2,64,256]{2,1,0:T(8,128)(2,1)S(1)} %collective-permute-done.up_ref) | copy-start | bytes 196612
  24.7 6.0 %copy-start.21 = (bf16[2,64,256]{2,1,0:T(8,128)(2,1)}, bf16[2,64,256]{2,1,0:T(8,128)(2,1)S(1)}, u32[]{:S(2)}) copy-start(bf16[2,64,256]{2,1,0:T(8,128)(2,1)S(1)} %collective-permute-done.1.down_ref) | copy-start | bytes 196612
  24.7 4.5 %collective-permute-start.2 = (bf16[20,2,256]{2,0,1:T(8,128)(2,1)S(1)}, bf16[20,2,256]{2,0,1:T(8,128)(2,1)S(1)}, u32[]{:S(2)}, u32[]{:S(2)}) collective-permute-start(bf16[20,2,256]{2,0,1:T(8,128)(2,1)S(1)} %pad_maximum_fusion.3), channel_id=1, source_target_pairs={{1,0},{2,1},{3,2},{4,3},{5,4},{6,5},{7,6},{9,8},{10,9},{11,10},{12... | collective-permute-start | bytes 61448 | tf_op jit(solution)/shard_map/ppermute | solution.py:845
  26.1 3.9 %collective-permute-start.3 = (bf16[20,2,256]{2,0,1:T(8,128)(2,1)S(1)}, bf16[20,2,256]{2,0,1:T(8,128)(2,1)S(1)}, u32[]{:S(2)}, u32[]{:S(2)}) collective-permute-start(bf16[20,2,256]{2,0,1:T(8,128)(2,1)S(1)} %pad_maximum_fusion.4), channel_id=1, source_target_pairs={{0,1},{1,2},{2,3},{3,4},{4,5},{5,6},{6,7},{8,9},{9,10},{10,11},{11... | collective-permute-start | bytes 61448 | tf_op jit(solution)/shard_map/ppermute | solution.py:845
  30.7 16.9 %copy-start.14 = (bf16[1024,64]{0,1:T(8,128)(2,1)S(1)}, bf16[1024,64]{0,1:T(8,128)(2,1)}, u32[]{:S(2)}) copy-start(bf16[1024,64]{0,1:T(8,128)(2,1)} %param.17) | copy-start | bytes 393220
  30.7 17.7 %copy-start.25 = (bf16[256]{0:T(256)(128)(2,1)S(1)}, bf16[256]{0:T(256)(128)(2,1)}, u32[]{:S(2)}) copy-start(bf16[256]{0:T(256)(128)(2,1)} %param.20) | copy-start | bytes 1540
  30.7 18.3 %copy-start.13 = (f32[8,64,64]{2,1,0:T(8,128)S(1)}, f32[8,64,64]{2,1,0:T(8,128)}, u32[]{:S(2)}) copy-start(f32[8,64,64]{2,1,0:T(8,128)} %param.23) | copy-start | bytes 393220
  39.6 16.1 %all-to-all-start = ((f32[32,1,1024]{2,1,0:T(1,128)}), f32[32,1,1024]{2,1,0:T(1,128)S(1)}, u32[]{:S(2)}, u32[]{:S(2)}) async-start(f32[32,1,1024]{2,1,0:T(1,128)} %get-tuple-element.68), calls=%async_computation | async-start | bytes 262144 | tf_op jit(solution)/shard_map/all_to_all | solution.py:868
  55.7 0.7 copy-start.16
  61.8 19.0 %all-to-all-start.2 = ((bf16[32,2,16,256]{3,2,1,0:T(8,128)(2,1)}), bf16[32,2,16,256]{3,2,1,0:T(8,128)(2,1)S(1)}, u32[]{:S(2)}, u32[]{:S(2)}) async-start(bf16[32,2,16,256]{3,2,1,0:T(8,128)(2,1)} %get-tuple-element.71), calls=%async_computation.2 | async-start | bytes 1048576 | tf_op jit(solution)/shard_map/all_to_all | solution.py:986
  64.5 13.7 %copy-start.6 = (bf16[16,4,2,8,256]{4,3,2,1,0:T(8,128)(2,1)S(1)}, bf16[16,4,2,8,256]{4,3,2,1,0:T(8,128)(2,1)}, u32[]{:S(2)}) copy-start(bf16[16,4,2,8,256]{4,3,2,1,0:T(8,128)(2,1)} %copy.46) | copy-start | bytes 1572868
  80.8 0.8 copy-start.12
  93.4 4.4 %copy-start.8 = (bf16[1024,256]{1,0:T(8,128)(2,1)S(1)}, bf16[1024,256]{1,0:T(8,128)(2,1)}, u32[]{:S(2)}) copy-start(bf16[1024,256]{1,0:T(8,128)(2,1)} %w_proj_ref.1) | copy-start | bytes 1572868
  93.4 20.7 %all-to-all-start.3 = ((bf16[32,2,16,256]{3,2,1,0:T(8,128)(2,1)}), bf16[32,2,16,256]{3,2,1,0:T(8,128)(2,1)S(1)}, u32[]{:S(2)}, u32[]{:S(2)}) async-start(bf16[32,2,16,256]{3,2,1,0:T(8,128)(2,1)} %bitcast.119), calls=%async_computation.3 | async-start | bytes 1048576 | tf_op jit(solution)/shard_map/all_to_all | solution.py:986
  114.1 0.8 copy-start.11
  114.9 8.6 %copy-start.7 = (bf16[256,1152]{1,0:T(8,128)(2,1)S(1)}, bf16[256,1152]{1,0:T(8,128)(2,1)}, u32[]{:S(2)}) copy-start(bf16[256,1152]{1,0:T(8,128)(2,1)} %attention_weights.1) | copy-start | bytes 1769476
  122.0 3.1 %collective-permute-start.4 = (bf16[1,64,256]{2,1,0:T(8,128)(2,1)S(1)}, bf16[1,64,256]{2,1,0:T(8,128)(2,1)S(1)}, u32[]{:S(2)}, u32[]{:S(2)}) collective-permute-start(bf16[1,64,256]{2,1,0:T(8,128)(2,1)S(1)} %get-tuple-element.122), channel_id=1, source_target_pairs={{0,8},{8,16},{16,24},{1,9},{9,17},{17,25},{2,10},{10,18},{18,26},{... | collective-permute-start | bytes 98312 | tf_op jit(solution)/shard_map/ppermute | solution.py:845
  123.6 2.4 %copy-start.10 = (bf16[1024,256]{1,0:T(8,128)(2,1)S(1)}, bf16[1024,256]{1,0:T(8,128)(2,1)}, u32[]{:S(2)}) copy-start(bf16[1024,256]{1,0:T(8,128)(2,1)} %get-tuple-element.78.att_ref) | copy-start | bytes 1572868
  124.8 1.5 copy-start.15
  125.1 28.9 %copy-start.22 = (bf16[1,64,256]{2,1,0:T(8,128)(2,1)}, bf16[1,64,256]{2,1,0:T(8,128)(2,1)S(1)}, u32[]{:S(2)}) copy-start(bf16[1,64,256]{2,1,0:T(8,128)(2,1)S(1)} %collective-permute-done.4.up_ref) | copy-start | bytes 98308
  125.2 7.8 %collective-permute-start.6 = (bf16[128,2176]{1,0:T(8,128)(2,1)S(1)}, bf16[128,2176]{1,0:T(8,128)(2,1)S(1)}, u32[]{:S(2)}, u32[]{:S(2)}) collective-permute-start(bf16[128,2176]{1,0:T(8,128)(2,1)S(1)} %dynamic-slice_bitcast_fusion), channel_id=1, source_target_pairs={{0,1},{1,0},{2,3},{3,2},{4,5},{5,4},{6,7},{7,6},{8,9},{9,8},{10,11... | collective-permute-start | bytes 1671176 | tf_op jit(solution)/shard_map/ppermute | solution.py:880
  127.1 26.9 %all-to-all-start.4 = ((bf16[32,40,256]{2,1,0:T(8,128)(2,1)}), bf16[32,40,256]{2,1,0:T(8,128)(2,1)S(1)}, u32[]{:S(2)}, u32[]{:S(2)}) async-start(bf16[32,40,256]{2,1,0:T(8,128)(2,1)} %pad_maximum_fusion.1), calls=%async_computation.4 | async-start | bytes 1310720 | tf_op jit(solution)/shard_map/all_to_all | solution.py:868
  131.6 22.3 %collective-permute-start.5 = (bf16[1,64,256]{2,1,0:T(8,128)(2,1)S(1)}, bf16[1,64,256]{2,1,0:T(8,128)(2,1)S(1)}, u32[]{:S(2)}, u32[]{:S(2)}) collective-permute-start(bf16[1,64,256]{2,1,0:T(8,128)(2,1)S(1)} %get-tuple-element.121), channel_id=1, source_target_pairs={{8,0},{16,8},{24,16},{9,1},{17,9},{25,17},{10,2},{18,10},{26,18},{... | collective-permute-start | bytes 98312 | tf_op jit(solution)/shard_map/ppermute | solution.py:845
  133.1 11.7 %collective-permute-start.7 = (bf16[32,2176]{1,0:T(8,128)(2,1)S(1)}, bf16[32,2176]{1,0:T(8,128)(2,1)S(1)}, u32[]{:S(2)}, u32[]{:S(2)}) collective-permute-start(bf16[32,2176]{1,0:T(8,128)(2,1)S(1)} %get-tuple-element.116), channel_id=1, source_target_pairs={{0,8},{8,16},{16,24},{24,0},{1,9},{9,17},{17,25},{25,1},{2,10},{10... | collective-permute-start | bytes 417800 | tf_op jit(solution)/shard_map/ppermute | solution.py:880
  135.8 11.5 %collective-permute-start.8 = (bf16[32,2176]{1,0:T(8,128)(2,1)S(1)}, bf16[32,2176]{1,0:T(8,128)(2,1)S(1)}, u32[]{:S(2)}, u32[]{:S(2)}) collective-permute-start(bf16[32,2176]{1,0:T(8,128)(2,1)S(1)} %get-tuple-element.118), channel_id=1, source_target_pairs={{0,16},{8,24},{16,0},{24,8},{1,17},{9,25},{17,1},{25,9},{2,18},{10... | collective-permute-start | bytes 417800 | tf_op jit(solution)/shard_map/ppermute | solution.py:880
  137.6 10.1 %collective-permute-start.9 = (bf16[32,2176]{1,0:T(8,128)(2,1)S(1)}, bf16[32,2176]{1,0:T(8,128)(2,1)S(1)}, u32[]{:S(2)}, u32[]{:S(2)}) collective-permute-start(bf16[32,2176]{1,0:T(8,128)(2,1)S(1)} %get-tuple-element.117), channel_id=1, source_target_pairs={{0,24},{8,0},{16,8},{24,16},{1,25},{9,1},{17,9},{25,17},{2,26},{10... | collective-permute-start | bytes 417800 | tf_op jit(solution)/shard_map/ppermute | solution.py:880
  147.8 10.7 %collective-permute-start.10 = (bf16[8,2176]{1,0:T(8,128)(2,1)S(1)}, bf16[8,2176]{1,0:T(8,128)(2,1)S(1)}, u32[]{:S(2)}, u32[]{:S(2)}) collective-permute-start(bf16[8,2176]{1,0:T(8,128)(2,1)S(1)} %get-tuple-element.127), channel_id=1, source_target_pairs={{0,2},{1,3},{2,4},{3,5},{4,6},{5,7},{6,0},{7,1},{8,10},{9,11},{10,... | collective-permute-start | bytes 104456 | tf_op jit(solution)/shard_map/ppermute | solution.py:880
  150.5 8.0 %collective-permute-start.11 = (bf16[8,2176]{1,0:T(8,128)(2,1)S(1)}, bf16[8,2176]{1,0:T(8,128)(2,1)S(1)}, u32[]{:S(2)}, u32[]{:S(2)}) collective-permute-start(bf16[8,2176]{1,0:T(8,128)(2,1)S(1)} %get-tuple-element.129), channel_id=1, source_target_pairs={{0,4},{1,5},{2,6},{3,7},{4,0},{5,1},{6,2},{7,3},{8,12},{9,13},{10,... | collective-permute-start | bytes 104456 | tf_op jit(solution)/shard_map/ppermute | solution.py:880
  152.4 6.1 %collective-permute-start.12 = (bf16[8,2176]{1,0:T(8,128)(2,1)S(1)}, bf16[8,2176]{1,0:T(8,128)(2,1)S(1)}, u32[]{:S(2)}, u32[]{:S(2)}) collective-permute-start(bf16[8,2176]{1,0:T(8,128)(2,1)S(1)} %get-tuple-element.128), channel_id=1, source_target_pairs={{0,6},{1,7},{2,0},{3,1},{4,2},{5,3},{6,4},{7,5},{8,14},{9,15},{10,... | collective-permute-start | bytes 104456 | tf_op jit(solution)/shard_map/ppermute | solution.py:880
  154.0 6.0 %copy-start.23 = (bf16[1,64,256]{2,1,0:T(8,128)(2,1)}, bf16[1,64,256]{2,1,0:T(8,128)(2,1)S(1)}, u32[]{:S(2)}) copy-start(bf16[1,64,256]{2,1,0:T(8,128)(2,1)S(1)} %collective-permute-done.5.down_ref) | copy-start | bytes 98308
  154.0 6.0 %copy-start.5 = (bf16[32,40,256]{2,1,0:T(8,128)(2,1)}, bf16[32,40,256]{2,1,0:T(8,128)(2,1)S(1)}, u32[]{:S(2)}) copy-start(bf16[32,40,256]{2,1,0:T(8,128)(2,1)S(1)} %all-to-all-done.4.parts_ref) | copy-start | bytes 1966084
  154.1 4.5 %collective-permute-start.13 = (bf16[18,1,256]{2,1,0:T(2,128)(2,1)S(1)}, bf16[18,1,256]{2,1,0:T(2,128)(2,1)S(1)}, u32[]{:S(2)}, u32[]{:S(2)}) collective-permute-start(bf16[18,1,256]{2,1,0:T(2,128)(2,1)S(1)} %pad_maximum_fusion.5), channel_id=1, source_target_pairs={{1,0},{2,1},{3,2},{4,3},{5,4},{6,5},{7,6},{9,8},{10,9},{11,10},{12... | collective-permute-start | bytes 27656 | tf_op jit(solution)/shard_map/ppermute | solution.py:845
  155.4 3.9 %collective-permute-start.14 = (bf16[18,1,256]{2,1,0:T(2,128)(2,1)S(1)}, bf16[18,1,256]{2,1,0:T(2,128)(2,1)S(1)}, u32[]{:S(2)}, u32[]{:S(2)}) collective-permute-start(bf16[18,1,256]{2,1,0:T(2,128)(2,1)S(1)} %pad_maximum_fusion.6), channel_id=1, source_target_pairs={{0,1},{1,2},{2,3},{3,4},{4,5},{5,6},{6,7},{8,9},{9,10},{10,11},{11... | collective-permute-start | bytes 27656 | tf_op jit(solution)/shard_map/ppermute | solution.py:845
  177.8 8.7 %copy-start.26 = (f32[1,64]{1,0:T(1,128)S(1)}, f32[1,64]{1,0:T(1,128)}, u32[]{:S(2)}) copy-start(f32[1,64]{1,0:T(1,128)} %get-tuple-element.88.hidden_ref) | copy-start | bytes 772
  177.8 8.8 %slice-start = ((bf16[32,40,256]{2,1,0:T(8,128)(2,1)}), bf16[32,32,256]{2,1,0:T(8,128)(2,1)S(1)}, s32[]{:S(2)}) async-start(bf16[32,40,256]{2,1,0:T(8,128)(2,1)} %copy-done.5), calls=%async_computation.7 | async-start | bytes 1048576 | tf_op jit(solution)/shard_map/slice | solution.py:1061
  177.8 1.9 collective-permute-start.15
  181.4 11.0 %copy-start.9 = (bf16[16,64,256]{2,1,0:T(8,128)(2,1)S(1)}, bf16[16,64,256]{2,1,0:T(8,128)(2,1)}, u32[]{:S(2)}) copy-start(bf16[16,64,256]{2,1,0:T(8,128)(2,1)} %get-tuple-element.70.mixed_ref) | copy-start | bytes 1572868
  181.4 21.9 %all-to-all-start.5 = ((bf16[16,8,1152]{2,1,0:T(8,128)(2,1)}), bf16[16,8,1152]{2,1,0:T(8,128)(2,1)S(1)}, u32[]{:S(2)}, u32[]{:S(2)}) async-start(bf16[16,8,1152]{2,1,0:T(8,128)(2,1)} %fusion.2), calls=%async_computation.5 | async-start | bytes 589824 | tf_op jit(solution)/shard_map/all_to_all | solution.py:901
  186.6 10.5 %collective-permute-start.17 = (bf16[1,8,2176]{2,1,0:T(8,128)(2,1)S(1)}, bf16[1,8,2176]{2,1,0:T(8,128)(2,1)S(1)}, u32[]{:S(2)}, u32[]{:S(2)}) collective-permute-start(bf16[1,8,2176]{2,1,0:T(8,128)(2,1)S(1)} %bitcast.90), channel_id=1, source_target_pairs={{0,2},{1,3},{2,4},{3,5},{4,6},{5,7},{6,0},{7,1},{8,10},{9,11},{10,... | collective-permute-start | bytes 104456 | tf_op jit(solution)/shard_map/ppermute | solution.py:880
  188.6 10.3 %collective-permute-start.18 = (bf16[1,8,2176]{2,1,0:T(8,128)(2,1)S(1)}, bf16[1,8,2176]{2,1,0:T(8,128)(2,1)S(1)}, u32[]{:S(2)}, u32[]{:S(2)}) collective-permute-start(bf16[1,8,2176]{2,1,0:T(8,128)(2,1)S(1)} %bitcast.91), channel_id=1, source_target_pairs={{0,4},{1,5},{2,6},{3,7},{4,0},{5,1},{6,2},{7,3},{8,12},{9,13},{10,... | collective-permute-start | bytes 104456 | tf_op jit(solution)/shard_map/ppermute | solution.py:880
  190.9 8.0 %collective-permute-start.19 = (bf16[1,8,2176]{2,1,0:T(8,128)(2,1)S(1)}, bf16[1,8,2176]{2,1,0:T(8,128)(2,1)S(1)}, u32[]{:S(2)}, u32[]{:S(2)}) collective-permute-start(bf16[1,8,2176]{2,1,0:T(8,128)(2,1)S(1)} %bitcast.92), channel_id=1, source_target_pairs={{0,6},{1,7},{2,0},{3,1},{4,2},{5,3},{6,4},{7,5},{8,14},{9,15},{10,... | collective-permute-start | bytes 104456 | tf_op jit(solution)/shard_map/ppermute | solution.py:880
  193.5 14.2 %copy-start.18 = (f32[1,1024]{1,0:T(1,128)S(1)}, f32[1,1024]{1,0:T(1,128)}, u32[]{:S(2)}) copy-start(f32[1,1024]{1,0:T(1,128)} %get-tuple-element.108) | copy-start | bytes 12292
  198.9 9.6 %collective-permute-start.20 = (bf16[4,8,2176]{2,1,0:T(8,128)(2,1)S(1)}, bf16[4,8,2176]{2,1,0:T(8,128)(2,1)S(1)}, u32[]{:S(2)}, u32[]{:S(2)}) collective-permute-start(bf16[4,8,2176]{2,1,0:T(8,128)(2,1)S(1)} %bitcast.97), channel_id=1, source_target_pairs={{0,8},{8,16},{16,24},{24,0},{1,9},{9,17},{17,25},{25,1},{2,10},{10... | collective-permute-start | bytes 417800 | tf_op jit(solution)/shard_map/ppermute | solution.py:880
  200.4 8.1 %collective-permute-start.21 = (bf16[4,8,2176]{2,1,0:T(8,128)(2,1)S(1)}, bf16[4,8,2176]{2,1,0:T(8,128)(2,1)S(1)}, u32[]{:S(2)}, u32[]{:S(2)}) collective-permute-start(bf16[4,8,2176]{2,1,0:T(8,128)(2,1)S(1)} %bitcast.98), channel_id=1, source_target_pairs={{0,16},{8,24},{16,0},{24,8},{1,17},{9,25},{17,1},{25,9},{2,18},{10... | collective-permute-start | bytes 417800 | tf_op jit(solution)/shard_map/ppermute | solution.py:880
  201.9 6.6 %collective-permute-start.22 = (bf16[4,8,2176]{2,1,0:T(8,128)(2,1)S(1)}, bf16[4,8,2176]{2,1,0:T(8,128)(2,1)S(1)}, u32[]{:S(2)}, u32[]{:S(2)}) collective-permute-start(bf16[4,8,2176]{2,1,0:T(8,128)(2,1)S(1)} %bitcast.99), channel_id=1, source_target_pairs={{0,24},{8,0},{16,8},{24,16},{1,25},{9,1},{17,9},{25,17},{2,26},{10... | collective-permute-start | bytes 417800 | tf_op jit(solution)/shard_map/ppermute | solution.py:880
  204.2 13.6 %all-to-all-start.6 = ((bf16[16,8,1152]{2,1,0:T(8,128)(2,1)}), bf16[16,8,1152]{2,1,0:T(8,128)(2,1)S(1)}, u32[]{:S(2)}, u32[]{:S(2)}) async-start(bf16[16,8,1152]{2,1,0:T(8,128)(2,1)} %broadcast_in_dim.17), calls=%async_computation.6 | async-start | bytes 589824 | tf_op jit(solution)/shard_map/all_to_all | solution.py:901
  208.5 1.0 copy-start.1
  208.5 1.2 copy-start.2
  208.5 1.2 copy-start.3
  208.5 1.6 copy-start.4
  208.6 10.0 %collective-permute-start.23 = (bf16[16,8,2176]{2,1,0:T(8,128)(2,1)S(1)}, bf16[16,8,2176]{2,1,0:T(8,128)(2,1)S(1)}, u32[]{:S(2)}, u32[]{:S(2)}) collective-permute-start(bf16[16,8,2176]{2,1,0:T(8,128)(2,1)S(1)} %bitcast.95), channel_id=1, source_target_pairs={{0,1},{1,0},{2,3},{3,2},{4,5},{5,4},{6,7},{7,6},{8,9},{9,8},{10,11... | collective-permute-start | bytes 1671176 | tf_op jit(solution)/shard_map/ppermute | solution.py:880
  210.1 7.7 %copy-start.17 = (f32[1,1024]{1,0:T(1,128)S(1)}, f32[1,1024]{1,0:T(1,128)}, u32[]{:S(2)}) copy-start(f32[1,1024]{1,0:T(1,128)} %get-tuple-element.106) | copy-start | bytes 12292
  210.1 7.7 %copy-start.19 = (f32[1,64]{1,0:T(1,128)S(1)}, f32[1,64]{1,0:T(1,128)}, u32[]{:S(2)}) copy-start(f32[1,64]{1,0:T(1,128)} %get-tuple-element.107) | copy-start | bytes 772
  217.8 2.9 %collective-permute-start.16 = (bf16[128,1152]{1,0:T(8,128)(2,1)S(1)}, bf16[128,1152]{1,0:T(8,128)(2,1)S(1)}, u32[]{:S(2)}, u32[]{:S(2)}) collective-permute-start(bf16[128,1152]{1,0:T(8,128)(2,1)S(1)} %bitcast.87), channel_id=1, source_target_pairs={{0,1},{1,0},{2,3},{3,2},{4,5},{5,4},{6,7},{7,6},{8,9},{9,8},{10,11... | collective-permute-start | bytes 884744 | tf_op jit(solution)/shard_map/ppermute | solution.py:880

commit v7 on v6

--- a/solution.py
+++ b/solution.py
@@ -741,14 +741,12 @@
 
     def keep(at, values):
         half = channels // 2
-        for place in range(2):
-
-            @pl.when(place_ref[0] == place)
-            def _():
-                mine_ref[:, at] = values[place * half : (place + 1) * half]
-                other_ref[:, at] = values[(1 - place) * half : (2 - place) * half]
-
-    keep(pl.ds(pl.multiple_of(step * BLOCK, BLOCK), BLOCK), weights.astype(BF16))
+        upper, lower = values[:half], values[half:]
+        first_core = place_ref[0] == 0
+        mine_ref[:, at] = jnp.where(first_core, upper, lower).astype(BF16)
+        other_ref[:, at] = jnp.where(first_core, lower, upper).astype(BF16)
+
+    keep(pl.ds(pl.multiple_of(step * BLOCK, BLOCK), BLOCK), weights)
     norm_ref[...] += jnp.sum(weights * w_exp.astype(F32), axis=1, keepdims=True)
     first_ref[...] += dot(grad_expanded, w_exp, ((1,), (1,)))
 
@@ -761,7 +759,7 @@
             tail_ref[start + k : start + k + 1, :] = norm[:, piece]
             at = start + channels // LANES + k
             tail_ref[at : at + 1, :] = norm1_ref[:, piece]
-        keep(slice(mine_ref.shape[1] - LANES, mine_ref.shape[1]), tail_ref[...].astype(BF16))
+        keep(slice(mine_ref.shape[1] - LANES, mine_ref.shape[1]), tail_ref[...])
 
 
 def run_expand_back(
@@ -1063,14 +1061,12 @@
         parts = hand_around(gate_grad)
         attended_home = swap_groups(attended_sent, parity)
     up, down = halo_rows(grad_low, 1)
-    edge_up, edge_down, parts = lax.optimization_barrier((up, down, parts))
-    side = halo_sides(grad_low, edge_up, edge_down, 1)
+    side = halo_sides(grad_low, up, down, 1)
     weights = jnp.concatenate([weights, grad_project], axis=1)
     weights, _ = lax.optimization_barrier((weights, up))
     steps = sum_steps()
     for step in steps:
         weights = sum_parts(weights, *step)
-    grad_low, weights = lax.optimization_barrier((grad_low, weights))
     late, late_other, grad_first, logit, pre = run_expand_back(
         cells_total, parts, hidden, gate, w_squeeze, w_excite, grad_low, up, down, side,
         w_project_t, slope, side_slope, spread_slope, spread, w_depth, turned_first, w_expand,

time: 223 us -> 216 us (0.969)
  starting transfers between devices: 77.1 us -> 69.6 us
  waiting for transfers between devices: 38.3 us -> 40.7 us
    ppermute x16, waiting for transfers between devices: 13.6 us -> 5.36 us  [send_on(): return lax.ppermute(v, axis, pairs)]
    all_to_all x2, waiting for transfers between devices: 5.48 us -> 11.2 us  [around(): lax.all_to_all(blocks, AXES, split_axis=0, concat_axis=0, tiled=True, axi...]
    ppermute x8, waiting for transfers between devices: 1.83 us -> 7.18 us  [shift(): return lax.ppermute(cells, axis, pairs)]
    all_to_all x2, starting transfers between devices: 12.5 us -> 9.41 us  [hand_around(): return lax.all_to_all(blocks, AXES, split_axis=0, concat_axis=0, tiled=True)]
    ppermute x16, starting transfers between devices: 24.4 us -> 21.5 us  [send_on(): return lax.ppermute(v, axis, pairs)]
  transfers between devices with their start and end apart: 31 -> 31, of which waited for: 13 -> 11; matrix products, arithmetic and copies ran while one was open for 8% -> 8% of each run, Pallas kernels for 17% -> 25%
where the time goes in v7:
time: 216 us; the launch traced here: 215 us
  Pallas kernels  77.7 us (36%)
  starting transfers between devices  69.6 us (32%)
  waiting for transfers between devices  40.7 us (19%)
  local copies, waits for them, and re-layouts  14.7 us (7%)
  other arithmetic  8.71 us (4%)
  matrix products  2.23 us (1%)
    ppermute x16, starting transfers between devices, send_on(): return lax.ppermute(v, axis, pairs)  21.5 us
    ppermute x8, starting transfers between devices, shift(): return lax.ppermute(cells, axis, pairs)  17.2 us
    pallas_call x1, Pallas kernels, run_expand_back(): pl.pallas_call(functools.partial(expand_back_kernel, cells_total), grid=(...  16.2 us
    all_to_all x3, starting transfers between devices, swap_groups(): lax.all_to_all(blocks, AXES, split_axis=0, concat_axis=0, tiled=True, axi...  14 us
    pallas_call x1, Pallas kernels, run_slope(): pl.pallas_call(slope_kernel, grid=(expanded // BLOCK,), in_specs=[pl.Bloc...  13.7 us
    all_to_all x3, waiting for transfers between devices, swap_groups(): lax.all_to_all(blocks, AXES, split_axis=0, concat_axis=0, tiled=True, axi...  12.9 us
    pallas_call x1, Pallas kernels, run_attention(): pl.pallas_call(functools.partial(attention_kernel, members, heads, lines)...  11.8 us
    all_to_all x2, waiting for transfers between devices, around(): lax.all_to_all(blocks, AXES, split_axis=0, concat_axis=0, tiled=True, axi...  11.2 us
  transfers between devices with their start and end apart: 31, of which 11 were waited for; matrix products, arithmetic and copies ran while one was open for 8% of the time, Pallas kernels for 25%

profile of v7, /device:TPU:0, one launch (start us, length us, event | category | flops | bytes accessed | tf_op | source)
XLA Modules:
  0.0 214.9 jit_solution(14550341220200996556)
XLA Ops:
  0.7 0.9 fusion.14
  1.6 4.8 %collective-permute-start = (bf16[2,64,256]{2,1,0:T(8,128)(2,1)S(1)}, bf16[2,64,256]{2,1,0:T(8,128)(2,1)S(1)}, u32[]{:S(2)}, u32[]{:S(2)}) collective-permute-start(bf16[2,64,256]{2,1,0:T(8,128)(2,1)S(1)} %get-tuple-element.116), channel_id=1, source_target_pairs={{0,8},{8,16},{16,24},{1,9},{9,17},{17,25},{2,10},{10,18},{18,26},{... | collective-permute-start | bytes 196616 | tf_op jit(solution)/shard_map/ppermute | solution.py:843
  6.4 1.3 collective-permute-start.1
  7.7 1.9 copy.45
  9.6 7.0 %all-to-all-start.1 = ((bf16[32,2,16,256]{3,2,1,0:T(8,128)(2,1)}), bf16[32,2,16,256]{3,2,1,0:T(8,128)(2,1)S(1)}, u32[]{:S(2)}, u32[]{:S(2)}) async-start(bf16[32,2,16,256]{3,2,1,0:T(8,128)(2,1)} %bitcast.3), calls=%async_computation.1 | async-start | bytes 1048576 | tf_op jit(solution)/shard_map/all_to_all | solution.py:984
  17.2 6.5 %expand.1 = (bf16[1024,256]{1,0:T(8,128)(2,1)}, bf16[16,64,1024]{2,1,0:T(8,128)(2,1)}, bf16[16,64,1024]{2,1,0:T(8,128)(2,1)}) custom-call(bf16[16,64,256]{2,1,0:T(8,128)(2,1)} %image_ref.3, bf16[1,256]{1,0:T(2,128)(2,1)} %reshape.129.gain_ref, bf16[256,1024]{1,0:T(8,128)(2,1)} %w_exp_ref.5), custom_call_target="tpu_custom_call" | custom-call | flops 15399999488 | bytes 50400000 | tf_op jit(solution)/shard_map/expand/pallas_call | solution.py:112
  23.7 0.9 fusion.13
  24.7 2.1 collective-permute-start.3
  26.9 1.3 collective-permute-start.2
  28.3 2.8 %collective-permute-done.2 = bf16[20,2,256]{2,0,1:T(8,128)(2,1)S(1)} collective-permute-done((bf16[20,2,256]{2,0,1:T(8,128)(2,1)S(1)}, bf16[20,2,256]{2,0,1:T(8,128)(2,1)S(1)}, u32[]{:S(2)}, u32[]{:S(2)}) %collective-permute-start.2) | collective-permute-done | bytes 20512 | tf_op jit(solution)/shard_map/ppermute | solution.py:843
  31.9 8.9 %depthwise.1 = (bf16[416,1024]{1,0:T(8,128)(2,1)}, bf16[16,64,1024]{2,1,0:T(8,128)(2,1)}, f32[32,1,1024]{2,1,0:T(1,128)}) custom-call(bf16[2,64,256]{2,1,0:T(8,128)(2,1)} %copy-done.20, bf16[2,64,256]{2,1,0:T(8,128)(2,1)} %copy-done.21, bf16[160,256]{1,0:T(8,128)(2,1)} %maximum_bitcast_fusion.side_ref, bf16[1,256]{1,0:T(2,128)(2,1)} %reshape.129.gain_ref, ...), custom_call_target="tpu_custom_call" | custom-call | flops 1100000000 | bytes 3600000 | tf_op jit(solution)/shard_map/depthwise/pallas_call | solution.py:203
  40.9 6.8 %all-to-all-start = ((f32[32,1,1024]{2,1,0:T(1,128)}), f32[32,1,1024]{2,1,0:T(1,128)S(1)}, u32[]{:S(2)}, u32[]{:S(2)}) async-start(f32[32,1,1024]{2,1,0:T(1,128)} %get-tuple-element.63), calls=%async_computation | async-start | bytes 262144 | tf_op jit(solution)/shard_map/all_to_all | solution.py:866
  47.7 0.8 copy.47.w_sq_ref
  49.9 0.8 pad_maximum_fusion.2.bias_ref
  50.7 1.1 copy.46
  51.8 4.0 %all-to-all-done.parts_ref = f32[32,1,1024]{2,1,0:T(1,128)S(1)} async-done(((f32[32,1,1024]{2,1,0:T(1,128)}), f32[32,1,1024]{2,1,0:T(1,128)S(1)}, u32[]{:S(2)}, u32[]{:S(2)}) %all-to-all-start) | async-done | bytes 131104 | tf_op jit(solution)/shard_map/all_to_all | solution.py:866
  56.5 5.4 %mix.1 = (f32[1,1024]{1,0:T(1,128)}, f32[1,64]{1,0:T(1,128)}, f32[1,1024]{1,0:T(1,128)}, bf16[16,64,256]{2,1,0:T(8,128)(2,1)}, bf16[32,2,16,256]{3,2,1,0:T(8,128)(2,1)}) custom-call(f32[32,1,1024]{2,1,0:T(1,128)} %copy-done.16, bf16[1024,64]{1,0:T(8,128)(2,1)} %copy.47.w_sq_ref, bf16[64,1024]{1,0:T(8,128)(2,1)} %w_ex_ref.3, ...), custom_call_target="tpu_custom_call" | custom-call | flops 5500000256 | bytes 18000000 | tf_op jit(solution)/shard_map/mix/pallas_call | solution.py:343
  61.9 2.6 %all-to-all-start.2 = ((bf16[32,2,16,256]{3,2,1,0:T(8,128)(2,1)}), bf16[32,2,16,256]{3,2,1,0:T(8,128)(2,1)S(1)}, u32[]{:S(2)}, u32[]{:S(2)}) async-start(bf16[32,2,16,256]{3,2,1,0:T(8,128)(2,1)} %get-tuple-element.66), calls=%async_computation.2 | async-start | bytes 1048576 | tf_op jit(solution)/shard_map/all_to_all | solution.py:984
  64.6 13.7 %slope.1 = (bf16[18,64,1024]{2,1,0:T(8,128)(2,1)}, f32[18,8,1024]{2,1,0:T(8,128)}, bf16[16,64,1024]{2,1,0:T(8,128)(2,1)}, bf16[256,1024]{1,0:T(8,128)(2,1)}) custom-call(f32[4]{0:T(128)} %add_convert_fusion.1.flags_ref, bf16[416,1024]{1,0:T(8,128)(2,1)} %get-tuple-element.67.ring_ref, bf16[3,3,1024]{2,1,0:T(4,128)(2,1)} %w_dep_ref.5, ...), custom_call_target="tpu_custom_call" | custom-call | flops 14300000256 | bytes 46800000 | tf_op jit(solution)/shard_map/slope/pallas_call | solution.py:278
  78.3 1.1 convolution_convert_fusion.att_grad_ref
  79.4 1.5 all-to-all-done.2
  80.9 0.8 copy-done.13
  81.7 11.8 %attention.1 = (bf16[1024,256]{1,0:T(8,128)(2,1)}, bf16[1024,256]{1,0:T(8,128)(2,1)}, bf16[1024,256]{1,0:T(8,128)(2,1)}, bf16[1024,768]{1,0:T(8,128)(2,1)}, f32[2,256,64]{2,1,0:T(8,128)}) custom-call(bf16[1024,256]{1,0:T(8,128)(2,1)} %bitcast.120, bf16[1024,256]{1,0:T(8,128)(2,1)} %convolution_convert_fusion.att_grad_ref, bf16[256,768]{1,0:T(8,128)(2,1)} %w_qkv_ref.1, ...), custom_call_target="tpu_custom_call" | custom-call | flops 15399999488 | bytes 50400000 | tf_op jit(solution)/shard_map/attention/pallas_call | solution.py:480
  93.5 4.4 %all-to-all-start.3 = ((bf16[32,2,16,256]{3,2,1,0:T(8,128)(2,1)}), bf16[32,2,16,256]{3,2,1,0:T(8,128)(2,1)S(1)}, u32[]{:S(2)}, u32[]{:S(2)}) async-start(bf16[32,2,16,256]{3,2,1,0:T(8,128)(2,1)} %bitcast.118), calls=%async_computation.3 | async-start | bytes 1048576 | tf_op jit(solution)/shard_map/all_to_all | solution.py:984
  97.9 1.0 copy.50
  99.3 3.5 %attention_weights.1 = bf16[256,1152]{1,0:T(8,128)(2,1)} custom-call(bf16[1024,256]{1,0:T(8,128)(2,1)} %get-tuple-element.75.x_ref, bf16[1024,768]{1,0:T(8,128)(2,1)} %get-tuple-element.76.packed_grad_ref, bf16[1024,256]{1,0:T(8,128)(2,1)} %get-tuple-element.73.att_ref, bf16[1024,256]{1,0:T(8,128)(2,1)} %bitcast.107, f32[2,256,64]{2,1,0:T(8,128)} %get-tuple-element.77.bias_ref), custom_call_target="tpu_custom_call" | custom-call | flops 5500000256 | bytes 18000000 | tf_op jit(solution)/shard_map/attention_weights/pallas_call | solution.py:518
  102.8 11.4 %all-to-all-done.3.recv_ref = bf16[32,2,16,256]{3,2,1,0:T(8,128)(2,1)S(1)} async-done(((bf16[32,2,16,256]{3,2,1,0:T(8,128)(2,1)}), bf16[32,2,16,256]{3,2,1,0:T(8,128)(2,1)S(1)}, u32[]{:S(2)}, u32[]{:S(2)}) %all-to-all-start.3) | async-done | bytes 524320 | tf_op jit(solution)/shard_map/all_to_all | solution.py:984
  114.2 0.8 copy-done.11
  115.0 6.3 %mixed_back.1 = (bf16[16,64,256]{2,1,0:T(8,128)(2,1)}, f32[1,256]{1,0:T(1,128)}, bf16[256,1024]{1,0:T(8,128)(2,1)}, bf16[32,8,256]{2,1,0:T(8,128)(2,1)}) custom-call(bf16[32,2,16,256]{3,2,1,0:T(8,128)(2,1)} %copy-done.11, bf16[16,64,256]{2,1,0:T(8,128)(2,1)} %get-tuple-element.65.mixed_ref, bf16[16,64,256]{2,1,0:T(8,128)(2,1)} %cot_ref.1, ...), custom_call_target="tpu_custom_call" | custom-call | flops 7699999744 | bytes 25200000 | tf_op jit(solution)/shard_map/mixed_back/pallas_call | solution.py:580
  121.3 0.8 fusion.12
  122.1 0.9 fusion.11
  123.0 1.9 pad_maximum_fusion.1
  124.9 2.6 %all-to-all-start.4 = ((bf16[32,40,256]{2,1,0:T(8,128)(2,1)}), bf16[32,40,256]{2,1,0:T(8,128)(2,1)S(1)}, u32[]{:S(2)}, u32[]{:S(2)}) async-start(bf16[32,40,256]{2,1,0:T(8,128)(2,1)} %pad_maximum_fusion.1), calls=%async_computation.4 | async-start | bytes 1310720 | tf_op jit(solution)/shard_map/all_to_all | solution.py:866
  127.5 3.5 %collective-permute-start.4 = (bf16[1,64,256]{2,1,0:T(8,128)(2,1)S(1)}, bf16[1,64,256]{2,1,0:T(8,128)(2,1)S(1)}, u32[]{:S(2)}, u32[]{:S(2)}) collective-permute-start(bf16[1,64,256]{2,1,0:T(8,128)(2,1)S(1)} %get-tuple-element.112), channel_id=1, source_target_pairs={{0,8},{8,16},{16,24},{1,9},{9,17},{17,25},{2,10},{10,18},{18,26},{... | collective-permute-start | bytes 98312 | tf_op jit(solution)/shard_map/ppermute | solution.py:843
  131.0 1.3 collective-permute-start.5
  132.7 4.2 %collective-permute-done.5.down_ref = bf16[1,64,256]{2,1,0:T(8,128)(2,1)S(1)} collective-permute-done((bf16[1,64,256]{2,1,0:T(8,128)(2,1)S(1)}, bf16[1,64,256]{2,1,0:T(8,128)(2,1)S(1)}, u32[]{:S(2)}, u32[]{:S(2)}) %collective-permute-start.5) | collective-permute-done | bytes 32800 | tf_op jit(solution)/shard_map/ppermute | solution.py:843
  137.0 1.3 collective-permute-start.7
  138.3 1.5 collective-permute-start.6
  140.6 3.4 %collective-permute-start.12 = (bf16[32,2176]{1,0:T(8,128)(2,1)S(1)}, bf16[32,2176]{1,0:T(8,128)(2,1)S(1)}, u32[]{:S(2)}, u32[]{:S(2)}) collective-permute-start(bf16[32,2176]{1,0:T(8,128)(2,1)S(1)} %get-tuple-element.108), channel_id=1, source_target_pairs={{0,16},{8,24},{16,0},{24,8},{1,17},{9,25},{17,1},{25,9},{2,18},{10... | collective-permute-start | bytes 417800 | tf_op jit(solution)/shard_map/ppermute | solution.py:878
  144.8 1.5 collective-permute-done.13
  146.2 1.5 collective-permute-done.12
  147.7 2.4 %collective-permute-done.11 = bf16[32,2176]{1,0:T(8,128)(2,1)S(1)} collective-permute-done((bf16[32,2176]{1,0:T(8,128)(2,1)S(1)}, bf16[32,2176]{1,0:T(8,128)(2,1)S(1)}, u32[]{:S(2)}, u32[]{:S(2)}) %collective-permute-start.11) | collective-permute-done | bytes 139296 | tf_op jit(solution)/shard_map/ppermute | solution.py:878
  150.2 6.4 %collective-permute-start.16 = (bf16[8,2176]{1,0:T(8,128)(2,1)S(1)}, bf16[8,2176]{1,0:T(8,128)(2,1)S(1)}, u32[]{:S(2)}, u32[]{:S(2)}) collective-permute-start(bf16[8,2176]{1,0:T(8,128)(2,1)S(1)} %get-tuple-element.118), channel_id=1, source_target_pairs={{0,6},{1,7},{2,0},{3,1},{4,2},{5,3},{6,4},{7,5},{8,14},{9,15},{10,... | collective-permute-start | bytes 104456 | tf_op jit(solution)/shard_map/ppermute | solution.py:878
  156.8 1.3 collective-permute-start.14
  158.1 0.8 copy-done.5
  158.9 16.2 %expand_back.1 = (bf16[128,1152]{1,0:T(8,128)(2,1)}, bf16[128,1152]{1,0:T(8,128)(2,1)}, f32[1024,256]{1,0:T(8,128)}, f32[1,1024]{1,0:T(1,128)}, f32[1,64]{1,0:T(1,128)}) custom-call(s32[1]{0:T(128)} %bitcast.25.place_ref, bf16[32,40,256]{2,1,0:T(8,128)(2,1)} %copy-done.5, f32[1,64]{1,0:T(1,128)} %get-tuple-element.81.hidden_ref, ...), custom_call_target="tpu_custom_call" | custom-call | flops 15399999488 | bytes 50400000 | tf_op jit(solution)/shard_map/expand_back/pallas_call | solution.py:772
  175.3 2.0 collective-permute-start.17
  177.3 1.1 collective-permute-start.18
  178.4 1.3 collective-permute-start.19
  179.8 1.8 fusion.2
  181.5 4.0 %all-to-all-start.5 = ((bf16[16,8,1152]{2,1,0:T(8,128)(2,1)}), bf16[16,8,1152]{2,1,0:T(8,128)(2,1)S(1)}, u32[]{:S(2)}, u32[]{:S(2)}) async-start(bf16[16,8,1152]{2,1,0:T(8,128)(2,1)} %fusion.2), calls=%async_computation.5 | async-start | bytes 589824 | tf_op jit(solution)/shard_map/all_to_all | solution.py:899
  185.7 2.0 collective-permute-start.20
  187.6 1.5 collective-permute-start.21
  189.1 1.5 collective-permute-start.22
  190.6 2.2 %image_back.1 = bf16[1024,256]{1,0:T(8,128)(2,1)} custom-call(bf16[1024,256]{1,0:T(8,128)(2,1)S(1)} %bitcast.89, bf16[1,256]{1,0:T(2,128)(2,1)S(1)} %copy-done.3, f32[1024,256]{1,0:T(8,128)S(1)} %copy-done.4, bf16[1024,256]{1,0:T(8,128)(2,1)S(1)} %bitcast.94), custom_call_target="tpu_custom_call" | custom-call | flops 4400000000 | bytes 14400000 | tf_op jit(solution)/shard_map/image_back/pallas_call | solution.py:828
  192.8 4.0 %all-to-all-done.5 = bf16[16,8,1152]{2,1,0:T(8,128)(2,1)S(1)} async-done(((bf16[16,8,1152]{2,1,0:T(8,128)(2,1)}), bf16[16,8,1152]{2,1,0:T(8,128)(2,1)S(1)}, u32[]{:S(2)}, u32[]{:S(2)}) %all-to-all-start.5) | async-done | bytes 294944 | tf_op jit(solution)/shard_map/all_to_all | solution.py:899
  196.9 0.7 broadcast_in_dim.17
  197.6 3.5 %all-to-all-start.6 = ((bf16[16,8,1152]{2,1,0:T(8,128)(2,1)}), bf16[16,8,1152]{2,1,0:T(8,128)(2,1)S(1)}, u32[]{:S(2)}, u32[]{:S(2)}) async-start(bf16[16,8,1152]{2,1,0:T(8,128)(2,1)} %broadcast_in_dim.17), calls=%async_computation.6 | async-start | bytes 589824 | tf_op jit(solution)/shard_map/all_to_all | solution.py:899
  201.8 0.8 broadcast_multiply_fusion.1
  202.7 1.1 fusion
  203.8 7.2 %all-to-all-done.6 = bf16[16,8,1152]{2,1,0:T(8,128)(2,1)S(1)} async-done(((bf16[16,8,1152]{2,1,0:T(8,128)(2,1)}), bf16[16,8,1152]{2,1,0:T(8,128)(2,1)S(1)}, u32[]{:S(2)}, u32[]{:S(2)}) %all-to-all-start.6) | async-done | bytes 294944 | tf_op jit(solution)/shard_map/all_to_all | solution.py:899
  211.0 0.8 broadcast_multiply_fusion
  211.8 2.1 unpack_weights.1
  213.8 1.1 unpack.1
  (120 shorter events, 7.2 us)
Async XLA Ops:
  0.6 77.6 %copy-start = (bf16[256,256]{1,0:T(8,128)(2,1)S(1)}, bf16[256,256]{1,0:T(8,128)(2,1)}, u32[]{:S(2)}) copy-start(bf16[256,256]{1,0:T(8,128)(2,1)} %param.22) | copy-start | bytes 393220
  0.7 16.0 %copy-start.24 = (bf16[256]{0:T(256)(128)(2,1)S(1)}, bf16[256]{0:T(256)(128)(2,1)}, u32[]{:S(2)}) copy-start(bf16[256]{0:T(256)(128)(2,1)} %param.14) | copy-start | bytes 1540
  1.6 23.0 %collective-permute-start = (bf16[2,64,256]{2,1,0:T(8,128)(2,1)S(1)}, bf16[2,64,256]{2,1,0:T(8,128)(2,1)S(1)}, u32[]{:S(2)}, u32[]{:S(2)}) collective-permute-start(bf16[2,64,256]{2,1,0:T(8,128)(2,1)S(1)} %get-tuple-element.116), channel_id=1, source_target_pairs={{0,8},{8,16},{16,24},{1,9},{9,17},{17,25},{2,10},{10,18},{18,26},{... | collective-permute-start | bytes 196616 | tf_op jit(solution)/shard_map/ppermute | solution.py:843
  6.4 18.2 %collective-permute-start.1 = (bf16[2,64,256]{2,1,0:T(8,128)(2,1)S(1)}, bf16[2,64,256]{2,1,0:T(8,128)(2,1)S(1)}, u32[]{:S(2)}, u32[]{:S(2)}) collective-permute-start(bf16[2,64,256]{2,1,0:T(8,128)(2,1)S(1)} %get-tuple-element.115), channel_id=1, source_target_pairs={{8,0},{16,8},{24,16},{9,1},{17,9},{25,17},{10,2},{18,10},{26,18},{... | collective-permute-start | bytes 196616 | tf_op jit(solution)/shard_map/ppermute | solution.py:843
  9.6 31.2 %all-to-all-start.1 = ((bf16[32,2,16,256]{3,2,1,0:T(8,128)(2,1)}), bf16[32,2,16,256]{3,2,1,0:T(8,128)(2,1)S(1)}, u32[]{:S(2)}, u32[]{:S(2)}) async-start(bf16[32,2,16,256]{3,2,1,0:T(8,128)(2,1)} %bitcast.3), calls=%async_computation.1 | async-start | bytes 1048576 | tf_op jit(solution)/shard_map/all_to_all | solution.py:984
  24.6 7.3 %copy-start.20 = (bf16[2,64,256]{2,1,0:T(8,128)(2,1)}, bf16[2,64,256]{2,1,0:T(8,128)(2,1)S(1)}, u32[]{:S(2)}) copy-start(bf16[2,64,256]{2,1,0:T(8,128)(2,1)S(1)} %collective-permute-done.up_ref) | copy-start | bytes 196612
  24.7 7.3 %copy-start.21 = (bf16[2,64,256]{2,1,0:T(8,128)(2,1)}, bf16[2,64,256]{2,1,0:T(8,128)(2,1)S(1)}, u32[]{:S(2)}) copy-start(bf16[2,64,256]{2,1,0:T(8,128)(2,1)S(1)} %collective-permute-done.1.down_ref) | copy-start | bytes 196612
  24.7 3.6 %collective-permute-start.3 = (bf16[20,2,256]{2,0,1:T(8,128)(2,1)S(1)}, bf16[20,2,256]{2,0,1:T(8,128)(2,1)S(1)}, u32[]{:S(2)}, u32[]{:S(2)}) collective-permute-start(bf16[20,2,256]{2,0,1:T(8,128)(2,1)S(1)} %pad_maximum_fusion.4), channel_id=1, source_target_pairs={{0,1},{1,2},{2,3},{3,4},{4,5},{5,6},{6,7},{8,9},{9,10},{10,11},{11... | collective-permute-start | bytes 61448 | tf_op jit(solution)/shard_map/ppermute | solution.py:843
  26.9 4.2 %collective-permute-start.2 = (bf16[20,2,256]{2,0,1:T(8,128)(2,1)S(1)}, bf16[20,2,256]{2,0,1:T(8,128)(2,1)S(1)}, u32[]{:S(2)}, u32[]{:S(2)}) collective-permute-start(bf16[20,2,256]{2,0,1:T(8,128)(2,1)S(1)} %pad_maximum_fusion.3), channel_id=1, source_target_pairs={{1,0},{2,1},{3,2},{4,3},{5,4},{6,5},{7,6},{9,8},{10,9},{11,10},{12... | collective-permute-start | bytes 61448 | tf_op jit(solution)/shard_map/ppermute | solution.py:843
  31.9 15.7 %copy-start.15 = (bf16[1024,64]{0,1:T(8,128)(2,1)S(1)}, bf16[1024,64]{0,1:T(8,128)(2,1)}, u32[]{:S(2)}) copy-start(bf16[1024,64]{0,1:T(8,128)(2,1)} %param.17) | copy-start | bytes 393220
  31.9 16.6 %copy-start.25 = (bf16[256]{0:T(256)(128)(2,1)S(1)}, bf16[256]{0:T(256)(128)(2,1)}, u32[]{:S(2)}) copy-start(bf16[256]{0:T(256)(128)(2,1)} %param.20) | copy-start | bytes 1540
  31.9 17.2 %copy-start.14 = (f32[8,64,64]{2,1,0:T(8,128)S(1)}, f32[8,64,64]{2,1,0:T(8,128)}, u32[]{:S(2)}) copy-start(f32[8,64,64]{2,1,0:T(8,128)} %param.23) | copy-start | bytes 393220
  40.9 15.0 %all-to-all-start = ((f32[32,1,1024]{2,1,0:T(1,128)}), f32[32,1,1024]{2,1,0:T(1,128)S(1)}, u32[]{:S(2)}, u32[]{:S(2)}) async-start(f32[32,1,1024]{2,1,0:T(1,128)} %get-tuple-element.63), calls=%async_computation | async-start | bytes 262144 | tf_op jit(solution)/shard_map/all_to_all | solution.py:866
  55.8 0.7 copy-start.16
  61.9 19.0 %all-to-all-start.2 = ((bf16[32,2,16,256]{3,2,1,0:T(8,128)(2,1)}), bf16[32,2,16,256]{3,2,1,0:T(8,128)(2,1)S(1)}, u32[]{:S(2)}, u32[]{:S(2)}) async-start(bf16[32,2,16,256]{3,2,1,0:T(8,128)(2,1)} %get-tuple-element.66), calls=%async_computation.2 | async-start | bytes 1048576 | tf_op jit(solution)/shard_map/all_to_all | solution.py:984
  64.5 13.7 %copy-start.6 = (bf16[16,4,2,8,256]{4,3,2,1,0:T(8,128)(2,1)S(1)}, bf16[16,4,2,8,256]{4,3,2,1,0:T(8,128)(2,1)}, u32[]{:S(2)}) copy-start(bf16[16,4,2,8,256]{4,3,2,1,0:T(8,128)(2,1)} %copy.46) | copy-start | bytes 1572868
  80.9 0.8 copy-start.13
  93.5 4.4 %copy-start.9 = (bf16[1024,256]{1,0:T(8,128)(2,1)S(1)}, bf16[1024,256]{1,0:T(8,128)(2,1)}, u32[]{:S(2)}) copy-start(bf16[1024,256]{1,0:T(8,128)(2,1)} %w_proj_ref.1) | copy-start | bytes 1572868
  93.5 5.5 %copy-start.12 = (bf16[1024,256]{1,0:T(8,128)(2,1)S(1)}, bf16[1024,256]{1,0:T(8,128)(2,1)}, u32[]{:S(2)}) copy-start(bf16[1024,256]{1,0:T(8,128)(2,1)} %get-tuple-element.73.att_ref) | copy-start | bytes 1572868
  93.5 20.7 %all-to-all-start.3 = ((bf16[32,2,16,256]{3,2,1,0:T(8,128)(2,1)}), bf16[32,2,16,256]{3,2,1,0:T(8,128)(2,1)S(1)}, u32[]{:S(2)}, u32[]{:S(2)}) async-start(bf16[32,2,16,256]{3,2,1,0:T(8,128)(2,1)} %bitcast.118), calls=%async_computation.3 | async-start | bytes 1048576 | tf_op jit(solution)/shard_map/all_to_all | solution.py:984
  114.2 0.8 copy-start.11
  123.0 9.4 %copy-start.7 = (bf16[256,1152]{1,0:T(8,128)(2,1)S(1)}, bf16[256,1152]{1,0:T(8,128)(2,1)}, u32[]{:S(2)}) copy-start(bf16[256,1152]{1,0:T(8,128)(2,1)} %attention_weights.1) | copy-start | bytes 1769476
  123.0 9.4 %copy-start.8 = (bf16[256,1024]{1,0:T(8,128)(2,1)S(1)}, bf16[256,1024]{1,0:T(8,128)(2,1)}, u32[]{:S(2)}) copy-start(bf16[256,1024]{1,0:T(8,128)(2,1)} %get-tuple-element.98) | copy-start | bytes 1572868
  124.9 33.3 %all-to-all-start.4 = ((bf16[32,40,256]{2,1,0:T(8,128)(2,1)}), bf16[32,40,256]{2,1,0:T(8,128)(2,1)S(1)}, u32[]{:S(2)}, u32[]{:S(2)}) async-start(bf16[32,40,256]{2,1,0:T(8,128)(2,1)} %pad_maximum_fusion.1), calls=%async_computation.4 | async-start | bytes 1310720 | tf_op jit(solution)/shard_map/all_to_all | solution.py:866
  127.5 5.1 %collective-permute-start.4 = (bf16[1,64,256]{2,1,0:T(8,128)(2,1)S(1)}, bf16[1,64,256]{2,1,0:T(8,128)(2,1)S(1)}, u32[]{:S(2)}, u32[]{:S(2)}) collective-permute-start(bf16[1,64,256]{2,1,0:T(8,128)(2,1)S(1)} %get-tuple-element.112), channel_id=1, source_target_pairs={{0,8},{8,16},{16,24},{1,9},{9,17},{17,25},{2,10},{10,18},{18,26},{... | collective-permute-start | bytes 98312 | tf_op jit(solution)/shard_map/ppermute | solution.py:843
  131.0 5.9 %collective-permute-start.5 = (bf16[1,64,256]{2,1,0:T(8,128)(2,1)S(1)}, bf16[1,64,256]{2,1,0:T(8,128)(2,1)S(1)}, u32[]{:S(2)}, u32[]{:S(2)}) collective-permute-start(bf16[1,64,256]{2,1,0:T(8,128)(2,1)S(1)} %get-tuple-element.111), channel_id=1, source_target_pairs={{8,0},{16,8},{24,16},{9,1},{17,9},{25,17},{10,2},{18,10},{26,18},{... | collective-permute-start | bytes 98312 | tf_op jit(solution)/shard_map/ppermute | solution.py:843
  132.6 7.3 %copy-start.22 = (bf16[1,64,256]{2,1,0:T(8,128)(2,1)}, bf16[1,64,256]{2,1,0:T(8,128)(2,1)S(1)}, u32[]{:S(2)}) copy-start(bf16[1,64,256]{2,1,0:T(8,128)(2,1)S(1)} %collective-permute-done.4.up_ref) | copy-start | bytes 98308
  132.7 7.1 %collective-permute-start.10 = (bf16[128,2176]{1,0:T(8,128)(2,1)S(1)}, bf16[128,2176]{1,0:T(8,128)(2,1)S(1)}, u32[]{:S(2)}, u32[]{:S(2)}) collective-permute-start(bf16[128,2176]{1,0:T(8,128)(2,1)S(1)} %dynamic-slice_bitcast_fusion), channel_id=1, source_target_pairs={{0,1},{1,0},{2,3},{3,2},{4,5},{5,4},{6,7},{7,6},{8,9},{9,8},{10,11... | collective-permute-start | bytes 1671176 | tf_op jit(solution)/shard_map/ppermute | solution.py:878
  136.9 7.8 %copy-start.23 = (bf16[1,64,256]{2,1,0:T(8,128)(2,1)}, bf16[1,64,256]{2,1,0:T(8,128)(2,1)S(1)}, u32[]{:S(2)}) copy-start(bf16[1,64,256]{2,1,0:T(8,128)(2,1)S(1)} %collective-permute-done.5.down_ref) | copy-start | bytes 98308
  137.0 7.0 %collective-permute-start.7 = (bf16[18,1,256]{2,1,0:T(2,128)(2,1)S(1)}, bf16[18,1,256]{2,1,0:T(2,128)(2,1)S(1)}, u32[]{:S(2)}, u32[]{:S(2)}) collective-permute-start(bf16[18,1,256]{2,1,0:T(2,128)(2,1)S(1)} %pad_maximum_fusion.6), channel_id=1, source_target_pairs={{0,1},{1,2},{2,3},{3,4},{4,5},{5,6},{6,7},{8,9},{9,10},{10,11},{11... | collective-permute-start | bytes 27656 | tf_op jit(solution)/shard_map/ppermute | solution.py:843
  138.3 5.7 %collective-permute-start.6 = (bf16[18,1,256]{2,1,0:T(2,128)(2,1)S(1)}, bf16[18,1,256]{2,1,0:T(2,128)(2,1)S(1)}, u32[]{:S(2)}, u32[]{:S(2)}) collective-permute-start(bf16[18,1,256]{2,1,0:T(2,128)(2,1)S(1)} %pad_maximum_fusion.5), channel_id=1, source_target_pairs={{1,0},{2,1},{3,2},{4,3},{5,4},{6,5},{7,6},{9,8},{10,9},{11,10},{12... | collective-permute-start | bytes 27656 | tf_op jit(solution)/shard_map/ppermute | solution.py:843
  140.0 6.2 %collective-permute-start.13 = (bf16[32,2176]{1,0:T(8,128)(2,1)S(1)}, bf16[32,2176]{1,0:T(8,128)(2,1)S(1)}, u32[]{:S(2)}, u32[]{:S(2)}) collective-permute-start(bf16[32,2176]{1,0:T(8,128)(2,1)S(1)} %get-tuple-element.107), channel_id=1, source_target_pairs={{0,24},{8,0},{16,8},{24,16},{1,25},{9,1},{17,9},{25,17},{2,26},{10... | collective-permute-start | bytes 417800 | tf_op jit(solution)/shard_map/ppermute | solution.py:878
  140.6 7.1 %collective-permute-start.12 = (bf16[32,2176]{1,0:T(8,128)(2,1)S(1)}, bf16[32,2176]{1,0:T(8,128)(2,1)S(1)}, u32[]{:S(2)}, u32[]{:S(2)}) collective-permute-start(bf16[32,2176]{1,0:T(8,128)(2,1)S(1)} %get-tuple-element.108), channel_id=1, source_target_pairs={{0,16},{8,24},{16,0},{24,8},{1,17},{9,25},{17,1},{25,9},{2,18},{10... | collective-permute-start | bytes 417800 | tf_op jit(solution)/shard_map/ppermute | solution.py:878
  144.0 6.1 %collective-permute-start.11 = (bf16[32,2176]{1,0:T(8,128)(2,1)S(1)}, bf16[32,2176]{1,0:T(8,128)(2,1)S(1)}, u32[]{:S(2)}, u32[]{:S(2)}) collective-permute-start(bf16[32,2176]{1,0:T(8,128)(2,1)S(1)} %get-tuple-element.106), channel_id=1, source_target_pairs={{0,8},{8,16},{16,24},{24,0},{1,9},{9,17},{17,25},{25,1},{2,10},{10... | collective-permute-start | bytes 417800 | tf_op jit(solution)/shard_map/ppermute | solution.py:878
  150.2 25.0 %collective-permute-start.16 = (bf16[8,2176]{1,0:T(8,128)(2,1)S(1)}, bf16[8,2176]{1,0:T(8,128)(2,1)S(1)}, u32[]{:S(2)}, u32[]{:S(2)}) collective-permute-start(bf16[8,2176]{1,0:T(8,128)(2,1)S(1)} %get-tuple-element.118), channel_id=1, source_target_pairs={{0,6},{1,7},{2,0},{3,1},{4,2},{5,3},{6,4},{7,5},{8,14},{9,15},{10,... | collective-permute-start | bytes 104456 | tf_op jit(solution)/shard_map/ppermute | solution.py:878
  156.6 18.6 %collective-permute-start.15 = (bf16[8,2176]{1,0:T(8,128)(2,1)S(1)}, bf16[8,2176]{1,0:T(8,128)(2,1)S(1)}, u32[]{:S(2)}, u32[]{:S(2)}) collective-permute-start(bf16[8,2176]{1,0:T(8,128)(2,1)S(1)} %get-tuple-element.119), channel_id=1, source_target_pairs={{0,4},{1,5},{2,6},{3,7},{4,0},{5,1},{6,2},{7,3},{8,12},{9,13},{10,... | collective-permute-start | bytes 104456 | tf_op jit(solution)/shard_map/ppermute | solution.py:878
  156.8 18.4 %collective-permute-start.14 = (bf16[8,2176]{1,0:T(8,128)(2,1)S(1)}, bf16[8,2176]{1,0:T(8,128)(2,1)S(1)}, u32[]{:S(2)}, u32[]{:S(2)}) collective-permute-start(bf16[8,2176]{1,0:T(8,128)(2,1)S(1)} %get-tuple-element.117), channel_id=1, source_target_pairs={{0,2},{1,3},{2,4},{3,5},{4,6},{5,7},{6,0},{7,1},{8,10},{9,11},{10,... | collective-permute-start | bytes 104456 | tf_op jit(solution)/shard_map/ppermute | solution.py:878
  158.1 0.8 copy-start.5
  175.1 10.4 %copy-start.26 = (f32[1,64]{1,0:T(1,128)S(1)}, f32[1,64]{1,0:T(1,128)}, u32[]{:S(2)}) copy-start(f32[1,64]{1,0:T(1,128)} %get-tuple-element.81.hidden_ref) | copy-start | bytes 772
  175.2 4.6 %collective-permute-start.8 = (bf16[128,1152]{1,0:T(8,128)(2,1)}, bf16[128,1152]{1,0:T(8,128)(2,1)S(1)}, u32[]{:S(2)}, u32[]{:S(2)}) collective-permute-start(bf16[128,1152]{1,0:T(8,128)(2,1)} %get-tuple-element.90), channel_id=1, source_target_pairs={{0,1},{1,0},{2,3},{3,2},{4,5},{5,4},{6,7},{7,6},{8,9},{9,8},{10,11... | collective-permute-start | bytes 884744 | tf_op jit(solution)/shard_map/ppermute | solution.py:878
  175.3 10.3 %collective-permute-start.17 = (bf16[1,8,2176]{2,1,0:T(8,128)(2,1)S(1)}, bf16[1,8,2176]{2,1,0:T(8,128)(2,1)S(1)}, u32[]{:S(2)}, u32[]{:S(2)}) collective-permute-start(bf16[1,8,2176]{2,1,0:T(8,128)(2,1)S(1)} %bitcast.90), channel_id=1, source_target_pairs={{0,2},{1,3},{2,4},{3,5},{4,6},{5,7},{6,0},{7,1},{8,10},{9,11},{10,... | collective-permute-start | bytes 104456 | tf_op jit(solution)/shard_map/ppermute | solution.py:878
  177.3 8.3 %collective-permute-start.18 = (bf16[1,8,2176]{2,1,0:T(8,128)(2,1)S(1)}, bf16[1,8,2176]{2,1,0:T(8,128)(2,1)S(1)}, u32[]{:S(2)}, u32[]{:S(2)}) collective-permute-start(bf16[1,8,2176]{2,1,0:T(8,128)(2,1)S(1)} %bitcast.91), channel_id=1, source_target_pairs={{0,4},{1,5},{2,6},{3,7},{4,0},{5,1},{6,2},{7,3},{8,12},{9,13},{10,... | collective-permute-start | bytes 104456 | tf_op jit(solution)/shard_map/ppermute | solution.py:878
  178.4 7.2 %collective-permute-start.19 = (bf16[1,8,2176]{2,1,0:T(8,128)(2,1)S(1)}, bf16[1,8,2176]{2,1,0:T(8,128)(2,1)S(1)}, u32[]{:S(2)}, u32[]{:S(2)}) collective-permute-start(bf16[1,8,2176]{2,1,0:T(8,128)(2,1)S(1)} %bitcast.92), channel_id=1, source_target_pairs={{0,6},{1,7},{2,0},{3,1},{4,2},{5,3},{6,4},{7,5},{8,14},{9,15},{10,... | collective-permute-start | bytes 104456 | tf_op jit(solution)/shard_map/ppermute | solution.py:878
  181.5 15.3 %all-to-all-start.5 = ((bf16[16,8,1152]{2,1,0:T(8,128)(2,1)}), bf16[16,8,1152]{2,1,0:T(8,128)(2,1)S(1)}, u32[]{:S(2)}, u32[]{:S(2)}) async-start(bf16[16,8,1152]{2,1,0:T(8,128)(2,1)} %fusion.2), calls=%async_computation.5 | async-start | bytes 589824 | tf_op jit(solution)/shard_map/all_to_all | solution.py:899
  185.6 5.0 %copy-start.1 = (bf16[16,64,256]{2,1,0:T(8,128)(2,1)S(1)}, bf16[16,64,256]{2,1,0:T(8,128)(2,1)}, u32[]{:S(2)}) copy-start(bf16[16,64,256]{2,1,0:T(8,128)(2,1)} %image_ref.3) | copy-start | bytes 1572868
  185.6 5.0 %copy-start.2 = (bf16[16,64,256]{2,1,0:T(8,128)(2,1)S(1)}, bf16[16,64,256]{2,1,0:T(8,128)(2,1)}, u32[]{:S(2)}) copy-start(bf16[16,64,256]{2,1,0:T(8,128)(2,1)} %get-tuple-element.82.low_ref) | copy-start | bytes 1572868
  185.6 5.0 %copy-start.3 = (bf16[1,256]{1,0:T(2,128)(2,1)S(1)}, bf16[1,256]{1,0:T(2,128)(2,1)}, u32[]{:S(2)}) copy-start(bf16[1,256]{1,0:T(2,128)(2,1)} %reshape.129.gain_ref) | copy-start | bytes 1540
  185.6 5.0 %copy-start.4 = (f32[1024,256]{1,0:T(8,128)S(1)}, f32[1024,256]{1,0:T(8,128)}, u32[]{:S(2)}) copy-start(f32[1024,256]{1,0:T(8,128)} %get-tuple-element.88.first_ref) | copy-start | bytes 3145732
  185.7 15.5 %collective-permute-start.20 = (bf16[4,8,2176]{2,1,0:T(8,128)(2,1)S(1)}, bf16[4,8,2176]{2,1,0:T(8,128)(2,1)S(1)}, u32[]{:S(2)}, u32[]{:S(2)}) collective-permute-start(bf16[4,8,2176]{2,1,0:T(8,128)(2,1)S(1)} %bitcast.97), channel_id=1, source_target_pairs={{0,8},{8,16},{16,24},{24,0},{1,9},{9,17},{17,25},{25,1},{2,10},{10... | collective-permute-start | bytes 417800 | tf_op jit(solution)/shard_map/ppermute | solution.py:878
  187.6 13.5 %collective-permute-start.21 = (bf16[4,8,2176]{2,1,0:T(8,128)(2,1)S(1)}, bf16[4,8,2176]{2,1,0:T(8,128)(2,1)S(1)}, u32[]{:S(2)}, u32[]{:S(2)}) collective-permute-start(bf16[4,8,2176]{2,1,0:T(8,128)(2,1)S(1)} %bitcast.98), channel_id=1, source_target_pairs={{0,16},{8,24},{16,0},{24,8},{1,17},{9,25},{17,1},{25,9},{2,18},{10... | collective-permute-start | bytes 417800 | tf_op jit(solution)/shard_map/ppermute | solution.py:878
  189.1 12.1 %collective-permute-start.22 = (bf16[4,8,2176]{2,1,0:T(8,128)(2,1)S(1)}, bf16[4,8,2176]{2,1,0:T(8,128)(2,1)S(1)}, u32[]{:S(2)}, u32[]{:S(2)}) collective-permute-start(bf16[4,8,2176]{2,1,0:T(8,128)(2,1)S(1)} %bitcast.99), channel_id=1, source_target_pairs={{0,24},{8,0},{16,8},{24,16},{1,25},{9,1},{17,9},{25,17},{2,26},{10... | collective-permute-start | bytes 417800 | tf_op jit(solution)/shard_map/ppermute | solution.py:878
  197.6 13.4 %all-to-all-start.6 = ((bf16[16,8,1152]{2,1,0:T(8,128)(2,1)}), bf16[16,8,1152]{2,1,0:T(8,128)(2,1)S(1)}, u32[]{:S(2)}, u32[]{:S(2)}) async-start(bf16[16,8,1152]{2,1,0:T(8,128)(2,1)} %broadcast_in_dim.17), calls=%async_computation.6 | async-start | bytes 589824 | tf_op jit(solution)/shard_map/all_to_all | solution.py:899
  201.1 0.7 copy-start.17
  201.2 0.7 copy-start.19
  201.3 1.4 slice-start
  201.3 1.4 copy-start.10
  201.3 10.5 %collective-permute-start.23 = (bf16[16,8,2176]{2,1,0:T(8,128)(2,1)S(1)}, bf16[16,8,2176]{2,1,0:T(8,128)(2,1)S(1)}, u32[]{:S(2)}, u32[]{:S(2)}) collective-permute-start(bf16[16,8,2176]{2,1,0:T(8,128)(2,1)S(1)} %bitcast.95), channel_id=1, source_target_pairs={{0,1},{1,0},{2,3},{3,2},{4,5},{5,4},{6,7},{7,6},{8,9},{9,8},{10,11... | collective-permute-start | bytes 1671176 | tf_op jit(solution)/shard_map/ppermute | solution.py:878
  202.6 8.3 %copy-start.18 = (f32[1,1024]{1,0:T(1,128)S(1)}, f32[1,1024]{1,0:T(1,128)}, u32[]{:S(2)}) copy-start(f32[1,1024]{1,0:T(1,128)} %get-tuple-element.96) | copy-start | bytes 12292
  211.0 2.9 %collective-permute-start.9 = (bf16[128,1152]{1,0:T(8,128)(2,1)S(1)}, bf16[128,1152]{1,0:T(8,128)(2,1)S(1)}, u32[]{:S(2)}, u32[]{:S(2)}) collective-permute-start(bf16[128,1152]{1,0:T(8,128)(2,1)S(1)} %bitcast.87), channel_id=1, source_target_pairs={{0,1},{1,0},{2,3},{3,2},{4,5},{5,4},{6,7},{7,6},{8,9},{9,8},{10,11... | collective-permute-start | bytes 884744 | tf_op jit(solution)/shard_map/ppermute | solution.py:878
